TPU v7x, 32 devices: a whole 2x2x4 slice. The times are simulated.
32 devices in a mesh: groups: 2 (over y), seq: 4 (over z), seg: 4 (over x, core).
Axes of the slice: x: 2, y: 2, z: 4, core: 2. Of those that a mesh axis runs over, the one named last changes fastest.
Arguments:
- layer_input: bfloat16 [8, 1024, 2048], P(('groups', 'seq'), 'seg'), parts along dimension 0, may hold values from -6 to 6
- out_cot: bfloat16 [8, 1024, 512], P(('groups', 'seq'), 'seg'), parts along dimension 0, may hold values from -6 to 6
- w_proj: bfloat16 [2048, 1536], P('seq'), may hold values from -0.125 to 0.125
- inner_start: float32 [8, 4, 2, 8, 64, 256], P(('groups', 'seq'), 'seg'), parts along dimension 0, may hold values from -1.5 to 1.5
- rates: float32 [8], replicated, may hold values from 0.01 to 0.06
Outputs:
- grad_input: bfloat16 [8, 1024, 2048], P(('groups', 'seq'), 'seg'), parts along dimension 0
- grad_proj: float32 [4096, 1536], P(('groups', 'seq')), parts along dimension 0
- grad_inner: float32 [8, 4, 2, 8, 64, 256], P(('groups', 'seq'), 'seg'), parts along dimension 0
There are 2 independent parts, one for each index of `groups`. A program takes and returns all parts, laid end to end along the dimension named above; an argument that names none is the same for every part. Nothing has to cross between parts.
All inputs are finite; a program needn't handle non-finite values.
Results may differ from a plain program's by a relative error of at most 0.008.
Values may be sent and summed in bfloat16 or wider, within the bound.
No kernel may reach another device: no remote copies, remote signals or barrier semaphores. Data moves between devices by JAX's collectives and lax.ppermute only.
A program may use at most 128 MiB of HBM per device.

v0:
```python
import jax
import jax.numpy as jnp
from jax import lax
from jax.sharding import PartitionSpec as P

MB = 256


HIGH = lax.Precision.HIGHEST


def shifted(value, axis, steps):
    count = lax.axis_size(axis)
    first, last = (max(0, -steps), min(count, count - steps))
    return lax.ppermute(value, axis, [(source, source + steps) for source in range(first, last)])


def predict(first, second, inputs):
    hidden = jax.nn.gelu(jnp.einsum("thf,hfk->thk", inputs, first, precision=HIGH))
    return jnp.einsum("thk,hfk->thf", hidden, second, precision=HIGH)


def segment_map(inner, queries, keys, values, rates):
    first = inner[0]
    second = inner[1]

    def inner_loss(first_w, second_w):
        resid = keys + predict(first_w, second_w, keys) - values
        return 0.5 * jnp.sum(resid * resid) / MB

    grad_first, grad_second = jax.grad(inner_loss, argnums=(0, 1))(first, second)
    first = first - rates[:, None, None] * grad_first
    second = second - rates[:, None, None] * grad_second
    outputs = [queries + predict(first, second, queries)]
    return (jnp.stack([first, second]), jnp.concatenate(outputs, 0))


def pull_back(inner_a, qkv_a, cot_a, rates_a, incoming):

    def local(inner_b, queries, keys, values):
        return segment_map(inner_b, queries, keys, values, rates_a)

    _, pull = jax.vjp(local, inner_a, qkv_a[:, 0], qkv_a[:, 1], qkv_a[:, 2])
    grad_seg, grad_q, grad_k, grad_v = pull((incoming, cot_a))
    return (grad_seg, jnp.stack([grad_q, grad_k, grad_v], 1))


def run_chain(start, qkv_float, cot_float, rates, place, length, group, sender):
    heads = rates.shape[0]
    blocks = heads // group
    feats = start.shape[2]

    def turn(index, state):
        incoming, grad_inner, grad_qkv = state
        block = index - (length - 1 - place)
        active = jnp.logical_and(block >= 0, block < blocks)
        pick = jnp.clip(block, 0, blocks - 1) * group
        inner_part = lax.dynamic_slice_in_dim(start, pick, group, 1)
        qkv_part = lax.dynamic_slice_in_dim(qkv_float, pick, group, 2)
        cot_part = lax.dynamic_slice_in_dim(cot_float, pick, group, 1)
        rate_part = lax.dynamic_slice_in_dim(rates, pick, group, 0)

        def work(carry):
            return pull_back(inner_part, qkv_part, cot_part, rate_part, carry)

        def resting(carry):
            return (jnp.zeros_like(inner_part), jnp.zeros_like(qkv_part))

        result = lax.cond(active, work, resting, incoming)
        old_inner = lax.dynamic_slice_in_dim(grad_inner, pick, group, 1)
        old_qkv = lax.dynamic_slice_in_dim(grad_qkv, pick, group, 2)
        grad_inner = lax.dynamic_update_slice_in_dim(
            grad_inner, jnp.where(active, result[0], old_inner), pick, 1
        )
        grad_qkv = lax.dynamic_update_slice_in_dim(
            grad_qkv, jnp.where(active, result[1], old_qkv), pick, 2
        )
        incoming = sender(result[0])
        return (incoming, grad_inner, grad_qkv)

    first_state = (
        jnp.zeros((2, group, feats, start.shape[3]), jnp.float32),
        jnp.zeros_like(start),
        jnp.zeros_like(qkv_float),
    )
    _, grad_inner, grad_qkv = lax.fori_loop(0, length + blocks - 1, turn, first_state)
    return (grad_inner, grad_qkv)


def per_device(layer_input, out_cot, w_proj, inner_start, rates):
    rows = layer_input[0]
    tokens = rows.shape[0]
    heads = rates.shape[0]
    feats = inner_start.shape[4]
    weights = lax.all_gather(w_proj, "seq", axis=0, tiled=True)
    qkv = jnp.dot(rows, weights, preferred_element_type=jnp.float32).astype(jnp.bfloat16)
    qkv_float = qkv.astype(jnp.float32).reshape(tokens, 3, heads, feats)
    cot_float = out_cot[0].astype(jnp.float32).reshape(tokens, heads, feats)
    start = inner_start[0, 0]
    place = lax.axis_index("seg")
    length = lax.axis_size("seg")

    def send_single(piece):
        return shifted(piece, "seg", -1)

    grad_inner, grad_qkv = run_chain(
        start, qkv_float, cot_float, rates, place, length, 1, send_single
    )
    qkv_grad = grad_qkv.reshape(tokens, 3 * heads * feats).astype(jnp.bfloat16)
    grad_input = lax.dot_general(
        qkv_grad, weights, (((1,), (1,)), ((), ())), preferred_element_type=jnp.float32
    ).astype(jnp.bfloat16)
    shard = lax.psum_scatter(
        lax.dot_general(
            rows, qkv_grad, (((0,), (0,)), ((), ())), preferred_element_type=jnp.float32
        ),
        "seq",
        scatter_dimension=0,
        tiled=True,
    )
    grad_proj = lax.psum(shard, "seg")
    return (grad_input[None], grad_proj, grad_inner[None, None])


def solution(mesh):
    placed = (
        P(("groups", "seq"), "seg", None),
        P(("groups", "seq"), "seg", None),
        P("seq", None),
        P(("groups", "seq"), "seg", None, None, None, None),
        P(),
    )
    return jax.shard_map(
        per_device,
        mesh=mesh,
        in_specs=placed,
        out_specs=(
            P(("groups", "seq"), "seg", None),
            P(("groups", "seq"), None),
            P(("groups", "seq"), "seg", None, None, None, None),
        ),
        check_vma=False,
    )
```

profile of v0, /device:TPU:9, one launch (start us, length us, event | category | flops | bytes accessed | tf_op | source)
XLA Modules:
  0.0 706.8 jit_solution(11672201555846113761)
XLA Ops:
  8.4 115.0 %all-gather.2.cloned.1.call-done = bf16[2048,1536]{1,0:T(8,128)(2,1)} async-done(((bf16[512,1536]{1,0:T(8,128)(2,1)}), bf16[2048,1536]{1,0:T(8,128)(2,1)}) %all-gather.2.cloned.1.call-update) | async-done | bytes 6291472 | tf_op jit(solution)/shard_map/all_gather | solution.py:95
  123.3 5.7 fusion.102
  129.0 1.9 copy.18
  133.0 272.7 %while.19 = (s32[]{:T(128)}, f32[2,1,64,256]{3,2,1,0:T(8,128)S(1)}, f32[2,8,64,256]{3,2,1,0:T(8,128)}, bf16[256,3,8,64]{0,3,2,1:T(8,128)(2,1)}, s32[]{:T(128)}, ...) while((s32[]{:T(128)}, f32[2,1,64,256]{3,2,1,0:T(8,128)S(1)}, ...), condition=%wide.region_3.4_spmd, body=%wide.region_0.3_spmd.sunk | while | flops 1016528896 | bytes 12788125 | solution.py:86
  133.0 2.4 collective-permute-start
  139.4 1.9 collective-permute-start
  141.4 1.6 select_dynamic-update-slice_fusion.4
  144.5 35.4 %collective-permute-done = f32[2,1,64,256]{3,2,1,0:T(8,128)S(1)} collective-permute-done((f32[2,1,64,256]{3,2,1,0:T(8,128)S(1)}, f32[2,1,64,256]{3,2,1,0:T(8,128)S(1)}, u32[]{:S(2)}, u32[]{:S(2)}) %collective-permute-start) | collective-permute-done | bytes 131104 | tf_op jit(solution)/shard_map/while/body/eval_jaxpr/ppermute | solution.py:15
  179.9 19.3 %conditional.2 = (f32[2,1,64,256]{3,2,1,0:T(8,128)S(1)}, bf16[256,3,1,64]{0,3,2,1:T(8,128)(2,1)S(1)}) conditional(s32[]{:T(128)} %convert_element_type.44, () %tuple.59, (f32[2,1,64,256]{3,2,1,0:T(8,128)S(1)}, f32[256,8,64]{0,2,1:T(8,128)S(1)}, s32[]{:T(128)}, f32[2,8,64,256]{3,2,1,0:T(8,128)}, f32[8]{0:T(128)S(1)}, ...), branch_computations={%region_1.1_spmd, %region_2.2_spmd} | conditional | flops 1016446976 | bytes 11574408 | solution.py:69
  182.9 1.9 fusion.21
  186.2 1.9 fusion.24
  199.2 1.9 collective-permute-start
  205.5 19.3 %conditional.2 = (f32[2,1,64,256]{3,2,1,0:T(8,128)S(1)}, bf16[256,3,1,64]{0,3,2,1:T(8,128)(2,1)S(1)}) conditional(s32[]{:T(128)} %convert_element_type.44, () %tuple.59, (f32[2,1,64,256]{3,2,1,0:T(8,128)S(1)}, f32[256,8,64]{0,2,1:T(8,128)S(1)}, s32[]{:T(128)}, f32[2,8,64,256]{3,2,1,0:T(8,128)}, f32[8]{0:T(128)S(1)}, ...), branch_computations={%region_1.1_spmd, %region_2.2_spmd} | conditional | flops 1016446976 | bytes 11574408 | solution.py:69
  208.5 1.9 fusion.21
  211.8 1.9 fusion.24
  224.7 1.9 collective-permute-start
  231.0 19.3 %conditional.2 = (f32[2,1,64,256]{3,2,1,0:T(8,128)S(1)}, bf16[256,3,1,64]{0,3,2,1:T(8,128)(2,1)S(1)}) conditional(s32[]{:T(128)} %convert_element_type.44, () %tuple.59, (f32[2,1,64,256]{3,2,1,0:T(8,128)S(1)}, f32[256,8,64]{0,2,1:T(8,128)S(1)}, s32[]{:T(128)}, f32[2,8,64,256]{3,2,1,0:T(8,128)}, f32[8]{0:T(128)S(1)}, ...), branch_computations={%region_1.1_spmd, %region_2.2_spmd} | conditional | flops 1016446976 | bytes 11574408 | solution.py:69
  234.1 1.9 fusion.21
  237.3 1.9 fusion.24
  250.3 1.9 collective-permute-start
  252.2 1.6 select_dynamic-update-slice_fusion.4
  256.6 19.3 %conditional.2 = (f32[2,1,64,256]{3,2,1,0:T(8,128)S(1)}, bf16[256,3,1,64]{0,3,2,1:T(8,128)(2,1)S(1)}) conditional(s32[]{:T(128)} %convert_element_type.44, () %tuple.59, (f32[2,1,64,256]{3,2,1,0:T(8,128)S(1)}, f32[256,8,64]{0,2,1:T(8,128)S(1)}, s32[]{:T(128)}, f32[2,8,64,256]{3,2,1,0:T(8,128)}, f32[8]{0:T(128)S(1)}, ...), branch_computations={%region_1.1_spmd, %region_2.2_spmd} | conditional | flops 1016446976 | bytes 11574408 | solution.py:69
  259.6 1.9 fusion.21
  262.9 1.9 fusion.24
  275.9 1.9 collective-permute-start
  277.8 1.6 select_dynamic-update-slice_fusion.4
  282.2 19.3 %conditional.2 = (f32[2,1,64,256]{3,2,1,0:T(8,128)S(1)}, bf16[256,3,1,64]{0,3,2,1:T(8,128)(2,1)S(1)}) conditional(s32[]{:T(128)} %convert_element_type.44, () %tuple.59, (f32[2,1,64,256]{3,2,1,0:T(8,128)S(1)}, f32[256,8,64]{0,2,1:T(8,128)S(1)}, s32[]{:T(128)}, f32[2,8,64,256]{3,2,1,0:T(8,128)}, f32[8]{0:T(128)S(1)}, ...), branch_computations={%region_1.1_spmd, %region_2.2_spmd} | conditional | flops 1016446976 | bytes 11574408 | solution.py:69
  285.2 1.9 fusion.21
  288.5 1.9 fusion.24
  301.4 1.9 collective-permute-start
  307.7 19.3 %conditional.2 = (f32[2,1,64,256]{3,2,1,0:T(8,128)S(1)}, bf16[256,3,1,64]{0,3,2,1:T(8,128)(2,1)S(1)}) conditional(s32[]{:T(128)} %convert_element_type.44, () %tuple.59, (f32[2,1,64,256]{3,2,1,0:T(8,128)S(1)}, f32[256,8,64]{0,2,1:T(8,128)S(1)}, s32[]{:T(128)}, f32[2,8,64,256]{3,2,1,0:T(8,128)}, f32[8]{0:T(128)S(1)}, ...), branch_computations={%region_1.1_spmd, %region_2.2_spmd} | conditional | flops 1016446976 | bytes 11574408 | solution.py:69
  310.8 1.9 fusion.21
  314.0 1.9 fusion.24
  327.0 1.9 collective-permute-start
  333.3 19.3 %conditional.2 = (f32[2,1,64,256]{3,2,1,0:T(8,128)S(1)}, bf16[256,3,1,64]{0,3,2,1:T(8,128)(2,1)S(1)}) conditional(s32[]{:T(128)} %convert_element_type.44, () %tuple.59, (f32[2,1,64,256]{3,2,1,0:T(8,128)S(1)}, f32[256,8,64]{0,2,1:T(8,128)S(1)}, s32[]{:T(128)}, f32[2,8,64,256]{3,2,1,0:T(8,128)}, f32[8]{0:T(128)S(1)}, ...), branch_computations={%region_1.1_spmd, %region_2.2_spmd} | conditional | flops 1016446976 | bytes 11574408 | solution.py:69
  336.3 1.9 fusion.21
  339.6 1.9 fusion.24
  352.6 1.9 collective-permute-start
  358.9 19.3 %conditional.2 = (f32[2,1,64,256]{3,2,1,0:T(8,128)S(1)}, bf16[256,3,1,64]{0,3,2,1:T(8,128)(2,1)S(1)}) conditional(s32[]{:T(128)} %convert_element_type.44, () %tuple.59, (f32[2,1,64,256]{3,2,1,0:T(8,128)S(1)}, f32[256,8,64]{0,2,1:T(8,128)S(1)}, s32[]{:T(128)}, f32[2,8,64,256]{3,2,1,0:T(8,128)}, f32[8]{0:T(128)S(1)}, ...), branch_computations={%region_1.1_spmd, %region_2.2_spmd} | conditional | flops 1016446976 | bytes 11574408 | solution.py:69
  361.9 1.9 fusion.21
  365.2 1.9 fusion.24
  378.1 1.9 collective-permute-start
  384.5 18.1 %collective-permute-start = (f32[2,1,64,256]{3,2,1,0:T(8,128)S(1)}, f32[2,1,64,256]{3,2,1,0:T(8,128)S(1)}, u32[]{:S(2)}, u32[]{:S(2)}) collective-permute-start(f32[2,1,64,256]{3,2,1,0:T(8,128)S(1)} %get-tuple-element.373), channel_id=1, source_target_pairs={{1,0},{2,1},{3,2},{5,4},{6,5},{7,6},{9,8},{10,9},{11,10},{13,12},{... | collective-permute-start | bytes 393224 | tf_op jit(solution)/shard_map/while/body/eval_jaxpr/ppermute | solution.py:15
  405.7 7.5 %convolution_bitcast_fusion.17 = f32[2048,1536]{0,1:T(8,128)} fusion(bf16[256,1536]{0,1:T(8,128)(2,1)} %bitcast.257, bf16[1,256,2048]{2,1,0:T(8,128)(2,1)S(1)} %copy-done), kind=kOutput, calls=%fused_computation.139 | convolution fusion | flops 1610612736 | bytes 14417920 | tf_op jit(solution)/shard_map/dot_general | solution.py:114
  413.3 211.7 %reduce-scatter.2.cloned.1.call-done = f32[512,1536]{0,1:T(8,128)} async-done(((f32[2048,1536]{0,1:T(8,128)}), f32[512,1536]{0,1:T(8,128)}) %reduce-scatter.2.cloned.1.call-update) | async-done | bytes 3145744 | tf_op jit(solution)/shard_map/reduce_scatter | solution.py:113
  626.1 5.6 fusion.103
  631.7 65.0 %all-reduce.4.cloned.1.call-done = f32[512,1536]{0,1:T(8,128)} async-done(((f32[512,1536]{0,1:T(8,128)}), f32[512,1536]{0,1:T(8,128)}) %all-reduce.4.cloned.1.call-update) | async-done | bytes 3145744 | tf_op jit(solution)/shard_map/psum | solution.py:121
  696.7 3.5 copy.19
  (232 shorter events, 168.4 us)
Async XLA Ops:
  7.2 116.2 %copy-start = (bf16[1,256,2048]{2,1,0:T(8,128)(2,1)S(1)}, bf16[1,256,2048]{2,1,0:T(8,128)(2,1)}, u32[]{:S(2)}) copy-start(bf16[1,256,2048]{2,1,0:T(8,128)(2,1)} %param.9) | copy-start | bytes 3145732
  7.2 1.0 copy-start.2
  7.2 116.1 %all-gather.2.cloned.1.call-start = ((), (), s32[]{:S(2)}) async-start(), calls=%async_computation.1 | async-start | bytes 7864320 | tf_op jit(solution)/shard_map/all_gather | solution.py:95
  7.9 617.0 %reduce-scatter.2.cloned.1.call-start = ((), (), s32[]{:S(2)}) async-start(), calls=%async_computation.2 | async-start | bytes 15728640 | tf_op jit(solution)/shard_map/reduce_scatter | solution.py:113
  130.9 2.1 copy-start.3
  133.0 6.4 collective-permute-start
  139.4 40.4 %collective-permute-start = (f32[2,1,64,256]{3,2,1,0:T(8,128)S(1)}, f32[2,1,64,256]{3,2,1,0:T(8,128)S(1)}, u32[]{:S(2)}, u32[]{:S(2)}) collective-permute-start(f32[2,1,64,256]{3,2,1,0:T(8,128)S(1)} %get-tuple-element.373), channel_id=1, source_target_pairs={{1,0},{2,1},{3,2},{5,4},{6,5},{7,6},{9,8},{10,9},{11,10},{13,12},{... | collective-permute-start | bytes 393224 | tf_op jit(solution)/shard_map/while/body/eval_jaxpr/ppermute | solution.py:15
  199.2 6.3 collective-permute-start
  224.7 6.3 collective-permute-start
  250.3 6.3 collective-permute-start
  275.9 6.3 collective-permute-start
  301.4 6.3 collective-permute-start
  327.0 6.3 collective-permute-start
  352.6 6.3 collective-permute-start
  378.1 6.3 collective-permute-start
  384.5 21.3 %collective-permute-start = (f32[2,1,64,256]{3,2,1,0:T(8,128)S(1)}, f32[2,1,64,256]{3,2,1,0:T(8,128)S(1)}, u32[]{:S(2)}, u32[]{:S(2)}) collective-permute-start(f32[2,1,64,256]{3,2,1,0:T(8,128)S(1)} %get-tuple-element.373), channel_id=1, source_target_pairs={{1,0},{2,1},{3,2},{5,4},{6,5},{7,6},{9,8},{10,9},{11,10},{13,12},{... | collective-permute-start | bytes 393224 | tf_op jit(solution)/shard_map/while/body/eval_jaxpr/ppermute | solution.py:15
  413.2 283.5 %all-reduce.4.cloned.1.call-start = ((), (), s32[]{:S(2)}) async-start(), calls=%async_computation.3 | async-start | bytes 6291456 | tf_op jit(solution)/shard_map/psum | solution.py:121
  625.0 1.1 copy-start.1
Sparse Core Ops, SparseCore 0:
  9.6 113.6 all-gather.1
  413.3 211.5 reduce-scatter.1
  627.3 69.3 all-reduce.3
where the time goes:
time: 713 us; the launch traced here: 707 us
  waiting for transfers between devices  438 us (61%)
  matrix products  167 us (23%)
  starting transfers between devices  37.9 us (5%)
  other arithmetic  34.8 us (5%)
  local copies, waits for them, and re-layouts  13.9 us (2%)
  between operations  13.8 us (2%)
    reduce_scatter x1, waiting for transfers between devices, per_device(): lax.psum_scatter(lax.dot_general(rows, qkv_grad, (((0,), (0,)), ((), ()))...  212 us
    all_gather x1, waiting for transfers between devices, per_device(): weights = lax.all_gather(w_proj, 'seq', axis=0, tiled=True)  115 us
    dot_general x88, matrix products, predict(): return jnp.einsum('thk,hfk->thf', hidden, second, precision=HIGH)  86.7 us
    psum x1, waiting for transfers between devices, per_device(): grad_proj = lax.psum(shard, 'seg')  65 us
    dot_general x72, matrix products, predict(): jnp.einsum('thf,hfk->thk', inputs, first, precision=HIGH)  61.7 us
    ppermute x11, waiting for transfers between devices, shifted(): lax.ppermute(value, axis, [(source, source + steps) for source in range(f...  45.9 us
    ppermute x11, starting transfers between devices, shifted(): lax.ppermute(value, axis, [(source, source + steps) for source in range(f...  37.8 us
    dynamic_update_slice x11, other arithmetic, turn(): lax.dynamic_update_slice_in_dim(grad_inner, jnp.where(active, result[0],...  17.4 us
  transfers between devices with their start and end apart: 14, of which 13 were waited for; matrix products, arithmetic and copies ran while one was open for 6% of the time, Pallas kernels for 0%

commit v1 on v0

v1 whole, which is shorter than its diff:
```python
import functools

import jax
import jax.numpy as jnp
from jax import lax
from jax.experimental import pallas as pl
from jax.experimental.pallas import tpu as pltpu
from jax.sharding import PartitionSpec as P

MB = 256
BF = jnp.bfloat16
F32 = jnp.float32
CORES = 2
GELU_A = 0.7978845608028654
GELU_B = 0.044715
VMEM = 56 * 1024 * 1024


def dot(a, b, ca, cb):
    return lax.dot_general(a, b, (((ca,), (cb,)), ((), ())), preferred_element_type=F32)


def gelu_parts(u):
    square = u * u
    tanh = jnp.tanh(u * (GELU_A + (GELU_A * GELU_B) * square))
    half = 0.5 * (1.0 + tanh)
    sech = 1.0 - tanh * tanh
    slope = GELU_A + (3.0 * GELU_A * GELU_B) * square
    return square, tanh, half, sech, slope


def inner_kernel(dims, table, rates, *refs):
    nseg, nseq, hpd, feats, hid, tokens, chunk = dims
    li = refs[:nseg]
    wt = refs[nseg : nseg + nseq]
    inner = refs[nseg + nseq : 2 * nseg + nseq]
    cot = refs[2 * nseg + nseq : 3 * nseg + nseq]
    gp, gq, gi = refs[3 * nseg + nseq : 3 * nseg + nseq + 3]
    qkv, wts, cts, ht, rt, g1, g2p, gu, gab = refs[3 * nseg + nseq + 3 :]
    rows = 3 * hpd * feats

    for slot in range(nseg):
        total = jnp.zeros((rows, tokens), F32)
        for back in range(nseq):
            at = pl.multiple_of(table[nseg + back] * chunk, chunk)
            total += dot(wt[back][...], li[slot][:, pl.ds(at, chunk)], 1, 1)
        qkv[slot] = total.astype(BF).reshape(3, hpd, feats, tokens)
        wts[slot] = inner[slot][...].reshape(2, hpd, feats, hid)
        cts[slot] = cot[slot][...].reshape(hpd, feats, tokens)

    def local(index, carry):
        slot = index // hpd
        head = index % hpd
        rate = rates[table[nseg + nseq] + head] * (1.0 / MB)
        a_b, b_b = wts[slot, 0, head], wts[slot, 1, head]
        q_b, k_b, v_b = qkv[slot, 0, head], qkv[slot, 1, head], qkv[slot, 2, head]
        c_b = cts[slot, head]
        u = dot(a_b, k_b, 0, 0)
        square, tanh, half, sech, slope = gelu_parts(u)
        h_b = (u * half).astype(BF)
        first = half + 0.5 * u * sech * slope
        second = sech * (GELU_A + (6.0 * GELU_A * GELU_B) * square - u * tanh * slope * slope)
        ht[slot, head] = h_b
        g1[slot, head] = first
        resid = k_b.astype(F32) - v_b.astype(F32) + dot(b_b, h_b, 1, 0)
        r_b = resid.astype(BF)
        rt[slot, head] = r_b
        p = dot(b_b, r_b, 0, 0)
        g2p[slot, head] = second * p
        gu_b = (first * p).astype(BF)
        gu[slot, head] = gu_b
        new_a = (a_b.astype(F32) - rate * dot(k_b, gu_b, 1, 1)).astype(BF)
        new_b = (b_b.astype(F32) - rate * dot(r_b, h_b, 1, 1)).astype(BF)
        uq = dot(new_a, q_b, 0, 0)
        square, tanh, half, sech, slope = gelu_parts(uq)
        hq_b = (uq * half).astype(BF)
        guq_b = ((half + 0.5 * uq * sech * slope) * dot(new_b, c_b, 0, 0)).astype(BF)
        gab[slot, 0, head] = dot(q_b, guq_b, 1, 1)
        gab[slot, 1, head] = dot(c_b, hq_b, 1, 1)
        gq[slot, 0, head] = (c_b.astype(F32) + dot(new_a, guq_b, 1, 0)).astype(BF)
        return carry

    lax.fori_loop(0, nseg * hpd, local, 0)

    def step(turn, carry):
        slot = table[nseg - 1 - turn]
        result = []
        for head in range(hpd):
            rate = rates[table[nseg + nseq] + head] * (1.0 / MB)
            t_a = carry[head][0] + gab[slot, 0, head]
            t_b = carry[head][1] + gab[slot, 1, head]
            a_b, b_b = wts[slot, 0, head], wts[slot, 1, head]
            k_b = qkv[slot, 1, head]
            h_b, r_b, gu_b = ht[slot, head], rt[slot, head], gu[slot, head]
            ta_b, tb_b = t_a.astype(BF), t_b.astype(BF)
            du = dot(ta_b, k_b, 0, 0)
            dh_b = (g1[slot, head] * du).astype(BF)
            dr = dot(b_b, dh_b, 1, 0) + dot(tb_b, h_b, 1, 0)
            dr_b = dr.astype(BF)
            dp = dot(b_b, dr_b, 0, 0) + dot(tb_b, r_b, 0, 0)
            dgu_b = (g2p[slot, head] * du + g1[slot, head] * dp).astype(BF)
            c_a = t_a - rate * dot(k_b, dgu_b, 1, 1)
            c_b = t_b - rate * (dot(dr_b, h_b, 1, 1) + dot(r_b, dh_b, 1, 1))
            left = jnp.concatenate([a_b, ta_b], 1)
            gk = dr + dot(left, jnp.concatenate([dgu_b, gu_b], 0), 1, 0)
            gq[slot, 1, head] = (-rate * gk).astype(BF)
            gq[slot, 2, head] = (rate * dr).astype(BF)
            gi[slot, 0, head] = c_a.astype(BF)
            gi[slot, 1, head] = c_b.astype(BF)
            result.append((c_a, c_b))
        return tuple(result)

    zero = jnp.zeros((feats, hid), F32)
    lax.fori_loop(0, nseg, step, tuple((zero, zero) for _ in range(hpd)))

    for piece in range(nseq):
        total = jnp.zeros((rows, chunk), F32)
        for slot in range(nseg):
            part = li[slot][:, piece * chunk : (piece + 1) * chunk]
            total += dot(gq[slot].reshape(rows, tokens), part, 1, 0)
        gp[piece] = total.astype(BF)


def input_kernel(nseg, nseq, chunk, table, gq, *refs):
    wt = refs[:nseq]
    out = refs[nseq]
    for back in range(nseq):
        at = pl.multiple_of(table[nseg + back] * chunk, chunk)
        for slot in range(nseg):
            value = dot(gq[slot].reshape(-1, gq.shape[-1]), wt[back][...], 0, 0)
            out[slot, :, pl.ds(at, chunk)] = value.astype(BF)


def per_device(layer_input, out_cot, w_proj, inner_start, rates):
    rows = layer_input[0]
    tokens, width = rows.shape
    heads = rates.shape[0]
    feats, hid = inner_start.shape[4:]
    nseg, nseq = lax.axis_size("seg"), lax.axis_size("seq")
    chips = nseg // CORES
    hpd = heads // nseg
    own = hpd * feats
    chunk = width // nseq
    me, place = lax.axis_index("seg"), lax.axis_index("seq")
    chip, core = me // CORES, me % CORES
    slots = [(dx, dc) for dx in range(chips) for dc in range(CORES)]

    def other(index, dx, dc):
        return ((index // CORES + dx) % chips) * CORES + (index % CORES + dc) % CORES

    def to_seg(value, dx, dc):
        if dx % chips == 0 and dc == 0:
            return value
        return lax.ppermute(value, "seg", [(i, other(i, dx, dc)) for i in range(nseg)])

    def to_seq(value, dz):
        return lax.ppermute(value, "seq", [(i, (i + dz) % nseq) for i in range(nseq)])

    def pick(values, order):
        return jnp.stack(
            [lax.dynamic_index_in_dim(values, order[i], 0, keepdims=False) for i in range(nseg)]
        )

    columns = w_proj.reshape(chunk, 3, nseg, own)
    mine = lax.dynamic_index_in_dim(columns, me, 2, keepdims=False)
    mine = mine.transpose(1, 2, 0).reshape(3 * own, chunk)
    wt = [mine] + [to_seq(mine, dz) for dz in range(1, nseq)]

    far = [to_seg(rows, dx, 0) for dx in range(chips)]
    near = [to_seg(value, 0, 1) for value in far]
    li = [value for pair in zip(far, near) for value in pair]

    start = inner_start[0, 0].astype(BF).reshape(2, nseg, own, hid)
    cots = out_cot[0].T.reshape(nseg, own, tokens)
    inner, cot = [], []
    for dx, dc in slots:
        dest = other(me, dx, dc)
        piece = lax.dynamic_index_in_dim(start, dest, 1, keepdims=False)
        inner.append(to_seg(piece, dx, dc))
        cot.append(to_seg(lax.dynamic_index_in_dim(cots, dest, 0, keepdims=False), dx, dc))

    segs = jnp.arange(nseg, dtype=jnp.int32)
    slot_of = ((chip - segs // CORES) % chips) * CORES + (core + segs) % CORES
    back = (place - jnp.arange(nseq, dtype=jnp.int32)) % nseq
    table = jnp.concatenate([slot_of, back, (me * hpd)[None]]).astype(jnp.int32)

    dims = (nseg, nseq, hpd, feats, hid, tokens, chunk)
    smem = pl.BlockSpec(memory_space=pltpu.SMEM)
    vmem = pl.BlockSpec(memory_space=pltpu.VMEM)
    gp, gq, gi = pl.pallas_call(
        functools.partial(inner_kernel, dims),
        in_specs=[smem, smem] + [vmem] * (3 * nseg + nseq),
        out_specs=[vmem] * 3,
        out_shape=[
            jax.ShapeDtypeStruct((nseq, 3 * own, chunk), BF),
            jax.ShapeDtypeStruct((nseg, 3, hpd, feats, tokens), BF),
            jax.ShapeDtypeStruct((nseg, 2, hpd, feats, hid), BF),
        ],
        scratch_shapes=[
            pltpu.VMEM((nseg, 3, hpd, feats, tokens), BF),
            pltpu.VMEM((nseg, 2, hpd, feats, hid), BF),
            pltpu.VMEM((nseg, hpd, feats, tokens), BF),
            pltpu.VMEM((nseg, hpd, hid, tokens), BF),
            pltpu.VMEM((nseg, hpd, feats, tokens), BF),
            pltpu.VMEM((nseg, hpd, hid, tokens), F32),
            pltpu.VMEM((nseg, hpd, hid, tokens), F32),
            pltpu.VMEM((nseg, hpd, hid, tokens), BF),
            pltpu.VMEM((nseg, 2, hpd, feats, hid), F32),
        ],
        compiler_params=pltpu.CompilerParams(vmem_limit_bytes=VMEM),
        cost_estimate=pl.CostEstimate(
            flops=40 * 10**9, bytes_accessed=10**7, transcendentals=10**6
        ),
        name="inner",
    )(table, rates, *li, *wt, *inner, *cot)

    total = lax.dynamic_index_in_dim(gp, place, 0, keepdims=False).astype(F32)
    for dz in range(1, nseq):
        piece = lax.dynamic_index_in_dim(gp, (place + dz) % nseq, 0, keepdims=False)
        total += to_seq(piece, dz).astype(F32)
    far = jnp.stack([to_seg(total, dx, 0) for dx in range(chips)])
    near = to_seg(far, 0, 1)
    both = jnp.stack([far, near], 1).reshape(nseg, 3, hpd, feats, chunk)
    ordered = pick(both, slot_of)
    grad_proj = ordered.transpose(4, 1, 0, 2, 3).reshape(chunk, 3 * heads * feats)

    part = pl.pallas_call(
        functools.partial(input_kernel, nseg, nseq, chunk),
        in_specs=[smem] + [vmem] * (1 + nseq),
        out_specs=vmem,
        out_shape=jax.ShapeDtypeStruct((nseg, tokens, width), BF),
        compiler_params=pltpu.CompilerParams(vmem_limit_bytes=VMEM),
        cost_estimate=pl.CostEstimate(flops=3 * 10**9, bytes_accessed=10**7, transcendentals=0),
        name="input",
    )(table, gq, *wt)
    part = part.reshape(chips, CORES, tokens, width)
    summed = part[:, 0].astype(F32) + to_seg(part[:, 1], 0, 1).astype(F32)
    grad_input = summed[0]
    for dx in range(1, chips):
        grad_input += to_seg(summed[dx].astype(BF), -dx, 0).astype(F32)

    pieces = jnp.stack([to_seg(gi[i], -dx, dc) for i, (dx, dc) in enumerate(slots)])
    source = ((segs // CORES - chip) % chips) * CORES + (core + segs) % CORES
    grad_inner = pick(pieces, source).transpose(1, 0, 2, 3, 4)
    grad_inner = grad_inner.reshape(2, heads, feats, hid).astype(F32)
    return (grad_input.astype(BF)[None], grad_proj, grad_inner[None, None])


def solution(mesh):
    placed = (
        P(("groups", "seq"), "seg", None),
        P(("groups", "seq"), "seg", None),
        P("seq", None),
        P(("groups", "seq"), "seg", None, None, None, None),
        P(),
    )
    return jax.shard_map(
        per_device,
        mesh=mesh,
        in_specs=placed,
        out_specs=(
            P(("groups", "seq"), "seg", None),
            P(("groups", "seq"), None),
            P(("groups", "seq"), "seg", None, None, None, None),
        ),
        check_vma=False,
    )
```

time: 713 us -> 207 us (0.29)
  waiting for transfers between devices: 438 us -> 102 us
  matrix products: 167 us -> 0 us
  Pallas kernels: 0 us -> 28.8 us
  other arithmetic: 34.8 us -> 10.9 us
  starting transfers between devices: 37.9 us -> 23.2 us
  local copies, waits for them, and re-layouts: 13.9 us -> 22.9 us
    reduce_scatter x1 -> x0, waiting for transfers between devices: 212 us -> none  [per_device(): lax.psum_scatter(lax.dot_general(rows, qkv_grad, (((0,), (0,)), ((), ()))...]
    dot_general x163 -> x0, matrix products: 167 us -> none  [the longest x88 86.7 us: predict(): return jnp.einsum('thk,hfk->thf', hidden, second, precision=HIGH)]
    all_gather x1 -> x0, waiting for transfers between devices: 115 us -> none  [per_device(): weights = lax.all_gather(w_proj, 'seq', axis=0, tiled=True)]
    psum x1 -> x0, waiting for transfers between devices: 65 us -> none  [per_device(): grad_proj = lax.psum(shard, 'seg')]
    ppermute x11 -> x22, waiting for transfers between devices: 45.9 us -> 102 us  [the longest x6 63.9 us: to_seq(): lax.ppermute(value, 'seq', [(i, (i + dz) % nseq) for i in range(nseq)])]
    dynamic_update_slice x22 -> x0, other arithmetic: 34.6 us -> none  [the longest x11 17.4 us: turn(): lax.dynamic_update_slice_in_dim(grad_inner, jnp.where(active, result[0],...]
    pallas_call x0 -> x2, Pallas kernels: none -> 28.8 us  [the longest x1 22.8 us: per_device(): pl.pallas_call(functools.partial(inner_kernel, dims), in_specs=[smem, sme...]
    ppermute x11 -> x22, starting transfers between devices: 37.8 us -> 23.2 us  [the longest x16 16.4 us: to_seg(): lax.ppermute(value, 'seg', [(i, other(i, dx, dc)) for i in range(nseg)])]
  transfers between devices with their start and end apart: 14 -> 22, of which waited for: 13 -> 10; matrix products, arithmetic and copies ran while one was open for 6% -> 12% of each run, Pallas kernels for 0% -> 0%
where the time goes in v1:
time: 207 us; the launch traced here: 203 us
  waiting for transfers between devices  102 us (49%)
  Pallas kernels  28.8 us (14%)
  starting transfers between devices  23.2 us (11%)
  local copies, waits for them, and re-layouts  22.9 us (11%)
  between operations  15.6 us (8%)
  other arithmetic  10.9 us (5%)
    ppermute x6, waiting for transfers between devices, to_seq(): lax.ppermute(value, 'seq', [(i, (i + dz) % nseq) for i in range(nseq)])  63.9 us
    ppermute x16, waiting for transfers between devices, to_seg(): lax.ppermute(value, 'seg', [(i, other(i, dx, dc)) for i in range(nseg)])  37.7 us
    pallas_call x1, Pallas kernels, per_device(): pl.pallas_call(functools.partial(inner_kernel, dims), in_specs=[smem, sme...  22.8 us
    ppermute x16, starting transfers between devices, to_seg(): lax.ppermute(value, 'seg', [(i, other(i, dx, dc)) for i in range(nseg)])  16.4 us
    ppermute x6, starting transfers between devices, to_seq(): lax.ppermute(value, 'seq', [(i, (i + dz) % nseq) for i in range(nseq)])  6.78 us
    pallas_call x1, Pallas kernels, per_device(): pl.pallas_call(functools.partial(input_kernel, nseg, nseq, chunk), in_spe...  5.93 us
    unnamed x25, local copies, waits for them, and re-layouts  5.69 us
  transfers between devices with their start and end apart: 22, of which 10 were waited for; matrix products, arithmetic and copies ran while one was open for 12% of the time, Pallas kernels for 0%

profile of v1, /device:TPU:9, one launch (start us, length us, event | category | flops | bytes accessed | tf_op | source)
XLA Modules:
  0.0 202.9 jit_solution(17957138449446876817)
XLA Ops:
  0.6 1.3 collective-permute-start.1
  1.9 1.0 collective-permute-start
  2.9 22.2 %collective-permute-done.1.refs_2_ = bf16[256,2048]{1,0:T(8,128)(2,1)} collective-permute-done((bf16[256,2048]{1,0:T(8,128)(2,1)}, bf16[256,2048]{1,0:T(8,128)(2,1)}, u32[]{:S(2)}, u32[]{:S(2)}) %collective-permute-start.1) | collective-permute-done | bytes 1048608 | tf_op jit(solution)/shard_map/ppermute | solution.py:154
  25.0 1.5 collective-permute-start.2
  26.6 1.1 copy.34
  27.7 0.7 dynamic-slice_bitcast_fusion.7
  28.4 1.2 collective-permute-start.10
  29.6 0.9 collective-permute-start.11
  30.5 3.0 %reshape.45 = bf16[512,3,4,128]{3,2,1,0:T(4,128)(2,1)S(1)} reshape(bf16[512,1536]{1,0:T(8,128)(2,1)} %param.7) | data formatting | bytes 3145728 | tf_op jit(solution)/shard_map/reshape | solution.py:164
  33.6 0.7 dynamic-slice_bitcast_fusion.3
  34.3 0.6 copy-done.11
  34.9 1.2 collective-permute-start.7
  36.2 0.9 collective-permute-start.8
  37.1 0.8 constant_dynamic-slice_fusion.8
  37.9 1.0 copy.19
  38.9 1.3 collective-permute-start.3
  40.3 1.5 collective-permute-start.4
  41.8 1.4 collective-permute-done.8.refs_11_
  43.9 5.9 %collective-permute-done.3.refs_5_.refs_1_ = bf16[384,512]{1,0:T(8,128)(2,1)S(1)} collective-permute-done((bf16[384,512]{1,0:T(8,128)(2,1)S(1)}, bf16[384,512]{1,0:T(8,128)(2,1)S(1)}, u32[]{:S(2)}, u32[]{:S(2)}) %collective-permute-start.3) | collective-permute-done | bytes 393248 | tf_op jit(solution)/shard_map/ppermute | solution.py:157
  49.8 24.4 %collective-permute-done.4.refs_6_.refs_2_ = bf16[384,512]{1,0:T(8,128)(2,1)S(1)} collective-permute-done((bf16[384,512]{1,0:T(8,128)(2,1)S(1)}, bf16[384,512]{1,0:T(8,128)(2,1)S(1)}, u32[]{:S(2)}, u32[]{:S(2)}) %collective-permute-start.4) | collective-permute-done | bytes 393248 | tf_op jit(solution)/shard_map/ppermute | solution.py:157
  74.2 2.0 collective-permute-done.5.refs_7_.refs_3_
  76.3 0.7 copy-done.7
  77.0 22.8 %inner.1 = (bf16[4,384,512]{2,1,0:T(8,128)(2,1)}, bf16[4,3,2,64,256]{4,3,2,1,0:T(8,128)(2,1)}, bf16[4,2,2,64,256]{4,3,2,1,0:T(8,128)(2,1)}) custom-call(s32[9]{0:T(128)} %pad_add_fusion.table, f32[8]{0:T(128)} %rates.1, bf16[256,2048]{1,0:T(8,128)(2,1)} %bitcast.117, bf16[256,2048]{1,0:T(8,128)(2,1)} %collective-permute-done.refs_1_, ...), custom_call_target="tpu_custom_call" | custom-call | flops 40000000000 | bytes 10000000 | tf_op jit(solution)/shard_map/inner/pallas_call | solution.py:190
  99.8 5.9 %input.1 = bf16[4,256,2048]{2,1,0:T(8,128)(2,1)} custom-call(s32[9]{0:T(128)} %pad_add_fusion.table, bf16[4,3,2,64,256]{4,3,2,1,0:T(8,128)(2,1)} %get-tuple-element.6.gq, bf16[384,512]{1,0:T(8,128)(2,1)} %bitcast.112, bf16[384,512]{1,0:T(8,128)(2,1)} %copy-done.5, bf16[384,512]{1,0:T(8,128)(2,1)} %copy-done.6, bf16[384,512]{1,0:T(8,128)(2,1)} %copy-done.7), custom_call_target="tpu_custom_call" | custom-call | flops 3000000000 | bytes 10000000 | tf_op jit(solution)/shard_map/input/pallas_call | solution.py:227
  105.7 3.3 %slice_bitcast_fusion.1 = bf16[2,256,2048]{2,1,0:T(8,128)(2,1)} fusion(bf16[2,2,256,2048]{3,2,1,0:T(8,128)(2,1)} %bitcast.100), kind=kLoop, calls=%fused_computation.7 | loop fusion | bytes 4194304 | tf_op jit(solution)/shard_map/squeeze | solution.py:237
  109.6 1.5 collective-permute-start.15
  111.2 2.3 %collective-permute-start.14 = (bf16[384,512]{1,0:T(8,128)(2,1)S(1)}, bf16[384,512]{1,0:T(8,128)(2,1)}, u32[]{:S(2)}, u32[]{:S(2)}) collective-permute-start(bf16[384,512]{1,0:T(8,128)(2,1)S(1)} %get-tuple-element.18), channel_id=1, source_target_pairs={{0,4},{4,8},{8,12},{12,0},{1,5},{5,9},{9,13},{13,1},{2,6},{6,10},{... | collective-permute-start | bytes 1179656 | tf_op jit(solution)/shard_map/ppermute | solution.py:157
  113.5 6.9 %collective-permute-done.16 = bf16[384,512]{1,0:T(8,128)(2,1)S(1)} collective-permute-done((bf16[384,512]{1,0:T(8,128)(2,1)S(1)}, bf16[384,512]{1,0:T(8,128)(2,1)S(1)}, u32[]{:S(2)}, u32[]{:S(2)}) %collective-permute-start.16) | collective-permute-done | bytes 393248 | tf_op jit(solution)/shard_map/ppermute | solution.py:157
  120.4 16.3 %collective-permute-done.15 = bf16[384,512]{1,0:T(8,128)(2,1)S(1)} collective-permute-done((bf16[384,512]{1,0:T(8,128)(2,1)S(1)}, bf16[384,512]{1,0:T(8,128)(2,1)S(1)}, u32[]{:S(2)}, u32[]{:S(2)}) %collective-permute-start.15) | collective-permute-done | bytes 393248 | tf_op jit(solution)/shard_map/ppermute | solution.py:157
  136.6 8.4 %collective-permute-done.14 = bf16[384,512]{1,0:T(8,128)(2,1)} collective-permute-done((bf16[384,512]{1,0:T(8,128)(2,1)S(1)}, bf16[384,512]{1,0:T(8,128)(2,1)}, u32[]{:S(2)}, u32[]{:S(2)}) %collective-permute-start.14) | collective-permute-done | bytes 393248 | tf_op jit(solution)/shard_map/ppermute | solution.py:157
  145.1 1.2 fusion.5
  146.2 1.3 collective-permute-start.17
  147.5 0.7 fusion.17
  153.1 2.0 fusion.15
  155.1 1.2 collective-permute-start.21
  156.3 1.2 collective-permute-start.20
  157.5 7.1 %collective-permute-done.17 = f32[384,512]{1,0:T(8,128)S(1)} collective-permute-done((f32[384,512]{1,0:T(8,128)S(1)}, f32[384,512]{1,0:T(8,128)S(1)}, u32[]{:S(2)}, u32[]{:S(2)}) %collective-permute-start.17) | collective-permute-done | bytes 786464 | tf_op jit(solution)/shard_map/ppermute | solution.py:154
  164.6 1.6 fusion.14
  166.2 2.9 %collective-permute-start.18 = (f32[2,384,512]{2,1,0:T(8,128)}, f32[2,384,512]{2,1,0:T(8,128)S(1)}, u32[]{:S(2)}, u32[]{:S(2)}) collective-permute-start(f32[2,384,512]{2,1,0:T(8,128)} %get-tuple-element.17), channel_id=1, source_target_pairs={{0,1},{1,0},{2,3},{3,2},{4,5},{5,4},{6,7},{7,6},{8,9},{9,8},{10,11... | collective-permute-start | bytes 4718600 | tf_op jit(solution)/shard_map/ppermute | solution.py:154
  169.1 2.3 %convert_add_fusion = f32[2,256,2048]{2,1,0:T(8,128)S(1)} fusion(bf16[2,256,2048]{2,1,0:T(8,128)(2,1)} %collective-permute-done.12, bf16[2,2,256,2048]{3,2,1,0:T(8,128)(2,1)S(1)} %bitcast.101), kind=kLoop, calls=%fused_computation | loop fusion | flops 3145728 | bytes 8388608 | tf_op jit(solution)/shard_map/add | solution.py:237
  171.5 2.0 copy-done
  173.5 1.1 fusion.3
  174.6 1.2 collective-permute-start.13
  186.2 1.0 pad_maximum_fusion.2
  187.4 1.1 copy.32
  190.4 2.4 %copy.33 = f32[512,1536]{1,0:T(8,128)} copy(f32[512,1536]{0,1:T(8,128)S(1)} %bitcast.99) | data formatting | bytes 6291456
  192.7 6.9 %collective-permute-done.13 = bf16[256,2048]{1,0:T(8,128)(2,1)} collective-permute-done((bf16[256,2048]{1,0:T(8,128)(2,1)}, bf16[256,2048]{1,0:T(8,128)(2,1)}, u32[]{:S(2)}, u32[]{:S(2)}) %collective-permute-start.13) | collective-permute-done | bytes 1048608 | tf_op jit(solution)/shard_map/ppermute | solution.py:154
  199.7 3.2 %fusion.2 = bf16[1,256,2048]{2,1,0:T(8,128)(2,1)} fusion(bf16[256,2048]{1,0:T(8,128)(2,1)} %collective-permute-done.13, f32[2,256,2048]{2,1,0:T(8,128)} %copy-done), kind=kLoop, calls=%fused_computation.10 | loop fusion | flops 1572864 | bytes 4194304 | tf_op jit(solution)/shard_map/broadcast_in_dim | solution.py:246
  (52 shorter events, 4.0 us)
Async XLA Ops:
  0.6 32.9 %copy-start.3 = (f32[1,1,2,8,64,256]{5,4,3,2,1,0:T(8,128)S(1)}, f32[1,1,2,8,64,256]{5,4,3,2,1,0:T(8,128)}, u32[]{:S(2)}) copy-start(f32[1,1,2,8,64,256]{5,4,3,2,1,0:T(8,128)} %param.8) | copy-start | bytes 3145732
  0.6 24.4 %collective-permute-start.1 = (bf16[256,2048]{1,0:T(8,128)(2,1)}, bf16[256,2048]{1,0:T(8,128)(2,1)}, u32[]{:S(2)}, u32[]{:S(2)}) collective-permute-start(bf16[256,2048]{1,0:T(8,128)(2,1)} %bitcast.115), channel_id=1, source_target_pairs={{0,2},{1,3},{2,0},{3,1},{4,6},{5,7},{6,4},{7,5},{8,10},{9,11},{10,... | collective-permute-start | bytes 3145736 | tf_op jit(solution)/shard_map/ppermute | solution.py:154
  1.9 74.3 %collective-permute-start = (bf16[256,2048]{1,0:T(8,128)(2,1)}, bf16[256,2048]{1,0:T(8,128)(2,1)}, u32[]{:S(2)}, u32[]{:S(2)}) collective-permute-start(bf16[256,2048]{1,0:T(8,128)(2,1)} %bitcast.116), channel_id=1, source_target_pairs={{0,1},{1,0},{2,3},{3,2},{4,5},{5,4},{6,7},{7,6},{8,9},{9,8},{10,11... | collective-permute-start | bytes 3145736 | tf_op jit(solution)/shard_map/ppermute | solution.py:154
  25.0 51.2 %collective-permute-start.2 = (bf16[256,2048]{1,0:T(8,128)(2,1)}, bf16[256,2048]{1,0:T(8,128)(2,1)}, u32[]{:S(2)}, u32[]{:S(2)}) collective-permute-start(bf16[256,2048]{1,0:T(8,128)(2,1)} %collective-permute-done.1.refs_2_), channel_id=1, source_target_pairs={{0,1},{1,0},{2,3},{3,2},{4,5},{5,4},{6,7},{7,6},{8,9},{9,8},{10,11... | collective-permute-start | bytes 3145736 | tf_op jit(solution)/shard_map/ppermute | solution.py:154
  28.4 5.9 %collective-permute-start.9 = (bf16[128,256]{1,0:T(8,128)(2,1)S(1)}, bf16[128,256]{1,0:T(8,128)(2,1)S(1)}, u32[]{:S(2)}, u32[]{:S(2)}) collective-permute-start(bf16[128,256]{1,0:T(8,128)(2,1)S(1)} %get-tuple-element.35), channel_id=1, source_target_pairs={{0,1},{1,0},{2,3},{3,2},{4,5},{5,4},{6,7},{7,6},{8,9},{9,8},{10,11... | collective-permute-start | bytes 196616 | tf_op jit(solution)/shard_map/ppermute | solution.py:154
  28.4 5.9 %collective-permute-start.10 = (bf16[128,256]{1,0:T(8,128)(2,1)S(1)}, bf16[128,256]{1,0:T(8,128)(2,1)S(1)}, u32[]{:S(2)}, u32[]{:S(2)}) collective-permute-start(bf16[128,256]{1,0:T(8,128)(2,1)S(1)} %get-tuple-element.34), channel_id=1, source_target_pairs={{0,2},{1,3},{2,0},{3,1},{4,6},{5,7},{6,4},{7,5},{8,10},{9,11},{10,... | collective-permute-start | bytes 196616 | tf_op jit(solution)/shard_map/ppermute | solution.py:154
  29.6 6.6 %collective-permute-start.11 = (bf16[128,256]{1,0:T(8,128)(2,1)S(1)}, bf16[128,256]{1,0:T(8,128)(2,1)}, u32[]{:S(2)}, u32[]{:S(2)}) collective-permute-start(bf16[128,256]{1,0:T(8,128)(2,1)S(1)} %get-tuple-element.33), channel_id=1, source_target_pairs={{0,3},{1,2},{2,1},{3,0},{4,7},{5,6},{6,5},{7,4},{8,11},{9,10},{10,... | collective-permute-start | bytes 196616 | tf_op jit(solution)/shard_map/ppermute | solution.py:154
  34.3 4.6 %copy-start.10 = (bf16[128,256]{1,0:T(8,128)(2,1)}, bf16[128,256]{1,0:T(8,128)(2,1)S(1)}, u32[]{:S(2)}) copy-start(bf16[128,256]{1,0:T(8,128)(2,1)S(1)} %collective-permute-done.9.refs_13_) | copy-start | bytes 196612
  34.3 4.6 %collective-permute-start.6 = (bf16[2,128,256]{2,1,0:T(8,128)(2,1)S(1)}, bf16[2,128,256]{2,1,0:T(8,128)(2,1)S(1)}, u32[]{:S(2)}, u32[]{:S(2)}) collective-permute-start(bf16[2,128,256]{2,1,0:T(8,128)(2,1)S(1)} %get-tuple-element.31), channel_id=1, source_target_pairs={{0,1},{1,0},{2,3},{3,2},{4,5},{5,4},{6,7},{7,6},{8,9},{9,8},{10,11... | collective-permute-start | bytes 393224 | tf_op jit(solution)/shard_map/ppermute | solution.py:154
  34.3 0.6 copy-start.11
  34.9 5.3 %collective-permute-start.7 = (bf16[2,128,256]{2,1,0:T(8,128)(2,1)S(1)}, bf16[2,128,256]{2,1,0:T(8,128)(2,1)S(1)}, u32[]{:S(2)}, u32[]{:S(2)}) collective-permute-start(bf16[2,128,256]{2,1,0:T(8,128)(2,1)S(1)} %get-tuple-element.30), channel_id=1, source_target_pairs={{0,2},{1,3},{2,0},{3,1},{4,6},{5,7},{6,4},{7,5},{8,10},{9,11},{10,... | collective-permute-start | bytes 393224 | tf_op jit(solution)/shard_map/ppermute | solution.py:154
  36.2 7.1 %collective-permute-start.8 = (bf16[2,128,256]{2,1,0:T(8,128)(2,1)S(1)}, bf16[2,128,256]{2,1,0:T(8,128)(2,1)}, u32[]{:S(2)}, u32[]{:S(2)}) collective-permute-start(bf16[2,128,256]{2,1,0:T(8,128)(2,1)S(1)} %get-tuple-element.29), channel_id=1, source_target_pairs={{0,3},{1,2},{2,1},{3,0},{4,7},{5,6},{6,5},{7,4},{8,11},{9,10},{10,... | collective-permute-start | bytes 393224 | tf_op jit(solution)/shard_map/ppermute | solution.py:154
  38.9 37.3 %copy-start.4 = (bf16[512,3,1,128]{0,3,1,2:T(8,128)(2,1)}, bf16[512,3,1,128]{0,3,1,2:T(8,128)(2,1)S(1)}, u32[]{:S(2)}) copy-start(bf16[512,3,1,128]{0,3,1,2:T(8,128)(2,1)S(1)} %copy.19) | copy-start | bytes 1179652
  38.9 37.3 %copy-start.8 = (bf16[2,128,256]{2,1,0:T(8,128)(2,1)}, bf16[2,128,256]{2,1,0:T(8,128)(2,1)S(1)}, u32[]{:S(2)}) copy-start(bf16[2,128,256]{2,1,0:T(8,128)(2,1)S(1)} %collective-permute-done.6.refs_9_) | copy-start | bytes 393220
  38.9 10.9 %collective-permute-start.3 = (bf16[384,512]{1,0:T(8,128)(2,1)S(1)}, bf16[384,512]{1,0:T(8,128)(2,1)S(1)}, u32[]{:S(2)}, u32[]{:S(2)}) collective-permute-start(bf16[384,512]{1,0:T(8,128)(2,1)S(1)} %bitcast.108), channel_id=1, source_target_pairs={{0,4},{4,8},{8,12},{12,0},{1,5},{5,9},{9,13},{13,1},{2,6},{6,10},{... | collective-permute-start | bytes 1179656 | tf_op jit(solution)/shard_map/ppermute | solution.py:157
  40.3 35.9 %copy-start.9 = (bf16[2,128,256]{2,1,0:T(8,128)(2,1)}, bf16[2,128,256]{2,1,0:T(8,128)(2,1)S(1)}, u32[]{:S(2)}) copy-start(bf16[2,128,256]{2,1,0:T(8,128)(2,1)S(1)} %collective-permute-done.7.refs_10_) | copy-start | bytes 393220
  40.3 33.9 %collective-permute-start.4 = (bf16[384,512]{1,0:T(8,128)(2,1)S(1)}, bf16[384,512]{1,0:T(8,128)(2,1)S(1)}, u32[]{:S(2)}, u32[]{:S(2)}) collective-permute-start(bf16[384,512]{1,0:T(8,128)(2,1)S(1)} %bitcast.109), channel_id=1, source_target_pairs={{0,8},{4,12},{8,0},{12,4},{1,9},{5,13},{9,1},{13,5},{2,10},{6,14},... | collective-permute-start | bytes 1179656 | tf_op jit(solution)/shard_map/ppermute | solution.py:157
  43.3 32.9 %collective-permute-start.5 = (bf16[384,512]{1,0:T(8,128)(2,1)S(1)}, bf16[384,512]{1,0:T(8,128)(2,1)S(1)}, u32[]{:S(2)}, u32[]{:S(2)}) collective-permute-start(bf16[384,512]{1,0:T(8,128)(2,1)S(1)} %bitcast.110), channel_id=1, source_target_pairs={{0,12},{4,0},{8,4},{12,8},{1,13},{5,1},{9,5},{13,9},{2,14},{6,2},{... | collective-permute-start | bytes 1179656 | tf_op jit(solution)/shard_map/ppermute | solution.py:157
  49.8 26.4 %copy-start.5 = (bf16[384,512]{1,0:T(8,128)(2,1)}, bf16[384,512]{1,0:T(8,128)(2,1)S(1)}, u32[]{:S(2)}) copy-start(bf16[384,512]{1,0:T(8,128)(2,1)S(1)} %collective-permute-done.3.refs_5_.refs_1_) | copy-start | bytes 1179652
  74.2 2.1 %copy-start.6 = (bf16[384,512]{1,0:T(8,128)(2,1)}, bf16[384,512]{1,0:T(8,128)(2,1)S(1)}, u32[]{:S(2)}) copy-start(bf16[384,512]{1,0:T(8,128)(2,1)S(1)} %collective-permute-done.4.refs_6_.refs_2_) | copy-start | bytes 1179652
  76.2 0.8 copy-start.7
  105.7 3.8 %copy-start.2 = (bf16[4,384,512]{2,1,0:T(8,128)(2,1)S(1)}, bf16[4,384,512]{2,1,0:T(8,128)(2,1)}, u32[]{:S(2)}) copy-start(bf16[4,384,512]{2,1,0:T(8,128)(2,1)} %get-tuple-element.7) | copy-start | bytes 4718596
  109.0 60.1 %collective-permute-start.12 = (bf16[2,256,2048]{2,1,0:T(8,128)(2,1)}, bf16[2,256,2048]{2,1,0:T(8,128)(2,1)}, u32[]{:S(2)}, u32[]{:S(2)}) collective-permute-start(bf16[2,256,2048]{2,1,0:T(8,128)(2,1)} %slice_bitcast_fusion.1), channel_id=1, source_target_pairs={{0,1},{1,0},{2,3},{3,2},{4,5},{5,4},{6,7},{7,6},{8,9},{9,8},{10,11... | collective-permute-start | bytes 6291464 | tf_op jit(solution)/shard_map/ppermute | solution.py:154
  109.6 10.8 %collective-permute-start.16 = (bf16[384,512]{1,0:T(8,128)(2,1)S(1)}, bf16[384,512]{1,0:T(8,128)(2,1)S(1)}, u32[]{:S(2)}, u32[]{:S(2)}) collective-permute-start(bf16[384,512]{1,0:T(8,128)(2,1)S(1)} %get-tuple-element.19), channel_id=1, source_target_pairs={{0,12},{4,0},{8,4},{12,8},{1,13},{5,1},{9,5},{13,9},{2,14},{6,2},{... | collective-permute-start | bytes 1179656 | tf_op jit(solution)/shard_map/ppermute | solution.py:157
  109.6 27.0 %collective-permute-start.15 = (bf16[384,512]{1,0:T(8,128)(2,1)S(1)}, bf16[384,512]{1,0:T(8,128)(2,1)S(1)}, u32[]{:S(2)}, u32[]{:S(2)}) collective-permute-start(bf16[384,512]{1,0:T(8,128)(2,1)S(1)} %get-tuple-element.20), channel_id=1, source_target_pairs={{0,8},{4,12},{8,0},{12,4},{1,9},{5,13},{9,1},{13,5},{2,10},{6,14},... | collective-permute-start | bytes 1179656 | tf_op jit(solution)/shard_map/ppermute | solution.py:157
  111.2 33.9 %collective-permute-start.14 = (bf16[384,512]{1,0:T(8,128)(2,1)S(1)}, bf16[384,512]{1,0:T(8,128)(2,1)}, u32[]{:S(2)}, u32[]{:S(2)}) collective-permute-start(bf16[384,512]{1,0:T(8,128)(2,1)S(1)} %get-tuple-element.18), channel_id=1, source_target_pairs={{0,4},{4,8},{8,12},{12,0},{1,5},{5,9},{9,13},{13,1},{2,6},{6,10},{... | collective-permute-start | bytes 1179656 | tf_op jit(solution)/shard_map/ppermute | solution.py:157
  146.2 18.3 %collective-permute-start.17 = (f32[384,512]{1,0:T(8,128)S(1)}, f32[384,512]{1,0:T(8,128)S(1)}, u32[]{:S(2)}, u32[]{:S(2)}) collective-permute-start(f32[384,512]{1,0:T(8,128)S(1)} %fusion.5), channel_id=1, source_target_pairs={{0,2},{1,3},{2,0},{3,1},{4,6},{5,7},{6,4},{7,5},{8,10},{9,11},{10,... | collective-permute-start | bytes 2359304 | tf_op jit(solution)/shard_map/ppermute | solution.py:154
  153.0 16.1 %copy-start.1 = (bf16[4,256,2048]{2,1,0:T(8,128)(2,1)S(1)}, bf16[4,256,2048]{2,1,0:T(8,128)(2,1)}, u32[]{:S(2)}) copy-start(bf16[4,256,2048]{2,1,0:T(8,128)(2,1)} %input.1) | copy-start | bytes 12582916
  155.1 31.1 %collective-permute-start.21 = (bf16[2,2,64,256]{3,2,1,0:T(8,128)(2,1)}, bf16[2,2,64,256]{3,2,1,0:T(8,128)(2,1)S(1)}, u32[]{:S(2)}, u32[]{:S(2)}) collective-permute-start(bf16[2,2,64,256]{3,2,1,0:T(8,128)(2,1)} %get-tuple-element.26), channel_id=1, source_target_pairs={{0,3},{1,2},{2,1},{3,0},{4,7},{5,6},{6,5},{7,4},{8,11},{9,10},{10,... | collective-permute-start | bytes 393224 | tf_op jit(solution)/shard_map/ppermute | solution.py:154
  156.3 29.9 %collective-permute-start.20 = (bf16[2,2,64,256]{3,2,1,0:T(8,128)(2,1)}, bf16[2,2,64,256]{3,2,1,0:T(8,128)(2,1)}, u32[]{:S(2)}, u32[]{:S(2)}) collective-permute-start(bf16[2,2,64,256]{3,2,1,0:T(8,128)(2,1)} %get-tuple-element.27), channel_id=1, source_target_pairs={{0,2},{1,3},{2,0},{3,1},{4,6},{5,7},{6,4},{7,5},{8,10},{9,11},{10,... | collective-permute-start | bytes 393224 | tf_op jit(solution)/shard_map/ppermute | solution.py:154
  157.5 28.7 %collective-permute-start.19 = (bf16[2,2,64,256]{3,2,1,0:T(8,128)(2,1)S(1)}, bf16[2,2,64,256]{3,2,1,0:T(8,128)(2,1)}, u32[]{:S(2)}, u32[]{:S(2)}) collective-permute-start(bf16[2,2,64,256]{3,2,1,0:T(8,128)(2,1)S(1)} %get-tuple-element.28), channel_id=1, source_target_pairs={{0,1},{1,0},{2,3},{3,2},{4,5},{5,4},{6,7},{7,6},{8,9},{9,8},{10,11... | collective-permute-start | bytes 393224 | tf_op jit(solution)/shard_map/ppermute | solution.py:154
  166.2 22.3 %collective-permute-start.18 = (f32[2,384,512]{2,1,0:T(8,128)}, f32[2,384,512]{2,1,0:T(8,128)S(1)}, u32[]{:S(2)}, u32[]{:S(2)}) collective-permute-start(f32[2,384,512]{2,1,0:T(8,128)} %get-tuple-element.17), channel_id=1, source_target_pairs={{0,1},{1,0},{2,3},{3,2},{4,5},{5,4},{6,7},{7,6},{8,9},{9,8},{10,11... | collective-permute-start | bytes 4718600 | tf_op jit(solution)/shard_map/ppermute | solution.py:154
  171.5 2.0 copy-start
  174.6 25.1 %collective-permute-start.13 = (bf16[256,2048]{1,0:T(8,128)(2,1)}, bf16[256,2048]{1,0:T(8,128)(2,1)}, u32[]{:S(2)}, u32[]{:S(2)}) collective-permute-start(bf16[256,2048]{1,0:T(8,128)(2,1)} %fusion.3), channel_id=1, source_target_pairs={{0,2},{1,3},{2,0},{3,1},{4,6},{5,7},{6,4},{7,5},{8,10},{9,11},{10,... | collective-permute-start | bytes 3145736 | tf_op jit(solution)/shard_map/ppermute | solution.py:154

commit v2 on v1

--- a/solution.py
+++ b/solution.py
@@ -29,15 +29,39 @@
     return square, tanh, half, sech, slope
 
 
+def prep_kernel(dims, table, w, cots, start, mine, *refs):
+    nseg, nseq, hpd, feats, hid, tokens, chunk = dims
+    packs = refs[:nseg]
+    block, turned = refs[nseg:]
+    own = hpd * feats
+    total = own * nseg
+    wide = block.shape[0]
+    me = table[nseg + nseq + 1]
+    base = me * own // wide * wide
+    for part in range(3):
+        at = pl.multiple_of(part * total + base, wide)
+        block[...] = w[:, pl.ds(at, wide)].T
+        rest = pl.multiple_of(me * own - base, own)
+        mine[part * own : (part + 1) * own] = block[pl.ds(rest, own)]
+    turned[...] = cots[...].T
+    for slot in range(nseg):
+        dest = table[nseg + nseq + 2 + slot]
+        piece = start[:, pl.ds(dest * hpd, hpd)].astype(BF)
+        packs[slot][: 2 * own] = piece.reshape(2 * own, hid)
+        packs[slot][2 * own :] = turned[pl.ds(pl.multiple_of(dest * own, own), own)]
+
+
 def inner_kernel(dims, table, rates, *refs):
     nseg, nseq, hpd, feats, hid, tokens, chunk = dims
-    li = refs[:nseg]
-    wt = refs[nseg : nseg + nseq]
-    inner = refs[nseg + nseq : 2 * nseg + nseq]
-    cot = refs[2 * nseg + nseq : 3 * nseg + nseq]
-    gp, gq, gi = refs[3 * nseg + nseq : 3 * nseg + nseq + 3]
-    qkv, wts, cts, ht, rt, g1, g2p, gu, gab = refs[3 * nseg + nseq + 3 :]
-    rows = 3 * hpd * feats
+    li, refs = refs[:nseg], refs[nseg:]
+    wt, refs = refs[:nseq], refs[nseq:]
+    packs, refs = refs[:nseg], refs[nseg:]
+    gp, refs = refs[:nseq], refs[nseq:]
+    gq, refs = refs[0], refs[1:]
+    gi, refs = refs[:nseg], refs[nseg:]
+    qkv, wts, cts, ht, rt, g1, g2p, gu, gab, gis = refs
+    own = hpd * feats
+    rows = 3 * own
 
     for slot in range(nseg):
         total = jnp.zeros((rows, tokens), F32)
@@ -45,8 +69,8 @@
             at = pl.multiple_of(table[nseg + back] * chunk, chunk)
             total += dot(wt[back][...], li[slot][:, pl.ds(at, chunk)], 1, 1)
         qkv[slot] = total.astype(BF).reshape(3, hpd, feats, tokens)
-        wts[slot] = inner[slot][...].reshape(2, hpd, feats, hid)
-        cts[slot] = cot[slot][...].reshape(hpd, feats, tokens)
+        wts[slot] = packs[slot][: 2 * own].reshape(2, hpd, feats, hid)
+        cts[slot] = packs[slot][2 * own :].reshape(hpd, feats, tokens)
 
     def local(index, carry):
         slot = index // hpd
@@ -105,30 +129,66 @@
             gk = dr + dot(left, jnp.concatenate([dgu_b, gu_b], 0), 1, 0)
             gq[slot, 1, head] = (-rate * gk).astype(BF)
             gq[slot, 2, head] = (rate * dr).astype(BF)
-            gi[slot, 0, head] = c_a.astype(BF)
-            gi[slot, 1, head] = c_b.astype(BF)
+            gis[slot, 0, head] = c_a.astype(BF)
+            gis[slot, 1, head] = c_b.astype(BF)
             result.append((c_a, c_b))
         return tuple(result)
 
     zero = jnp.zeros((feats, hid), F32)
     lax.fori_loop(0, nseg, step, tuple((zero, zero) for _ in range(hpd)))
 
-    for piece in range(nseq):
+    for slot in range(nseg):
+        gi[slot][...] = gis[slot]
+    for dz in range(nseq):
+        at = pl.multiple_of(table[nseg + (nseq - dz) % nseq] * chunk, chunk)
         total = jnp.zeros((rows, chunk), F32)
         for slot in range(nseg):
-            part = li[slot][:, piece * chunk : (piece + 1) * chunk]
-            total += dot(gq[slot].reshape(rows, tokens), part, 1, 0)
-        gp[piece] = total.astype(BF)
+            total += dot(gq[slot].reshape(rows, tokens), li[slot][:, pl.ds(at, chunk)], 1, 0)
+        gp[dz][...] = total.astype(gp[dz].dtype)
 
 
 def input_kernel(nseg, nseq, chunk, table, gq, *refs):
     wt = refs[:nseq]
-    out = refs[nseq]
-    for back in range(nseq):
-        at = pl.multiple_of(table[nseg + back] * chunk, chunk)
-        for slot in range(nseg):
-            value = dot(gq[slot].reshape(-1, gq.shape[-1]), wt[back][...], 0, 0)
-            out[slot, :, pl.ds(at, chunk)] = value.astype(BF)
+    outs = refs[nseq:]
+    for slot in range(nseg):
+        left = gq[slot].reshape(-1, gq.shape[-1])
+        for back in range(nseq):
+            at = pl.multiple_of(table[nseg + back] * chunk, chunk)
+            value = dot(left, wt[back][...], 0, 0)
+            outs[slot % CORES][slot // CORES, :, pl.ds(at, chunk)] = value.astype(BF)
+
+
+def sum_kernel(*refs):
+    total = refs[0][...]
+    for ref in refs[1:-1]:
+        total += ref[...].astype(F32)
+    refs[-1][...] = total.T.astype(BF)
+
+
+def join_kernel(dims, table, *refs):
+    nseg, nseq, hpd, feats, hid, tokens, chunk = dims
+    chips = nseg // CORES
+    far, near, out = refs[:chips], refs[chips], refs[chips + 1]
+    own = hpd * feats
+    me = table[nseg + nseq + 1]
+    chip = me // CORES
+    even = me % CORES == 0
+    for dx in range(chips):
+        source = (chip - dx + chips) % chips
+        for part in range(3):
+            a = far[dx][:, part * own : (part + 1) * own].astype(F32)
+            b = near[dx, :, part * own : (part + 1) * own].astype(F32)
+            left, right = jnp.where(even, a, b), jnp.where(even, b, a)
+            at = pl.multiple_of(part * nseg * own + source * CORES * own, CORES * own)
+            out[:, pl.ds(at, CORES * own)] = jnp.concatenate([left, right], 1)
+
+
+def weights_kernel(dims, table, *refs):
+    nseg, nseq, hpd = dims[:3]
+    out = refs[nseg]
+    for slot in range(nseg):
+        source = table[nseg + nseq + 2 + slot]
+        out[:, pl.ds(source * hpd, hpd)] = refs[slot][...].astype(F32)
 
 
 def per_device(layer_input, out_cot, w_proj, inner_start, rates):
@@ -156,47 +216,56 @@
     def to_seq(value, dz):
         return lax.ppermute(value, "seq", [(i, (i + dz) % nseq) for i in range(nseq)])
 
-    def pick(values, order):
-        return jnp.stack(
-            [lax.dynamic_index_in_dim(values, order[i], 0, keepdims=False) for i in range(nseg)]
-        )
-
-    columns = w_proj.reshape(chunk, 3, nseg, own)
-    mine = lax.dynamic_index_in_dim(columns, me, 2, keepdims=False)
-    mine = mine.transpose(1, 2, 0).reshape(3 * own, chunk)
+    def kernel(body, name, outs, scratch, flops, *operands):
+        smem = pl.BlockSpec(memory_space=pltpu.SMEM)
+        vmem = pl.BlockSpec(memory_space=pltpu.VMEM)
+        moved = sum(o.size * o.dtype.itemsize for o in [*operands, *outs])
+        return pl.pallas_call(
+            body,
+            in_specs=[smem if o.ndim == 1 else vmem for o in operands],
+            out_specs=[vmem] * len(outs),
+            out_shape=outs,
+            scratch_shapes=scratch,
+            compiler_params=pltpu.CompilerParams(vmem_limit_bytes=VMEM),
+            cost_estimate=pl.CostEstimate(flops=flops, bytes_accessed=moved, transcendentals=0),
+            name=name,
+        )(*operands)
+
+    def array(shape, dtype):
+        return jax.ShapeDtypeStruct(shape, dtype)
+
+    segs = jnp.arange(nseg, dtype=jnp.int32)
+    slot_of = ((chip - segs // CORES) % chips) * CORES + (core + segs) % CORES
+    back = (place - jnp.arange(nseq, dtype=jnp.int32)) % nseq
+    dest = ((chip + segs // CORES) % chips) * CORES + (core + segs) % CORES
+    table = jnp.concatenate([slot_of, back, jnp.stack([me * hpd, me]), dest]).astype(jnp.int32)
+    dims = (nseg, nseq, hpd, feats, hid, tokens, chunk)
+
+    mine, *packs = kernel(
+        functools.partial(prep_kernel, dims),
+        "prep",
+        [array((3 * own, chunk), BF)] + [array((3 * own, tokens), BF)] * nseg,
+        [pltpu.VMEM((max(own, 128), chunk), BF), pltpu.VMEM((heads * feats, tokens), BF)],
+        10**6,
+        table,
+        w_proj,
+        out_cot[0],
+        inner_start[0, 0],
+    )
+    rows, mine, *packs = lax.optimization_barrier((rows, mine, *packs))
     wt = [mine] + [to_seq(mine, dz) for dz in range(1, nseq)]
-
     far = [to_seg(rows, dx, 0) for dx in range(chips)]
     near = [to_seg(value, 0, 1) for value in far]
     li = [value for pair in zip(far, near) for value in pair]
-
-    start = inner_start[0, 0].astype(BF).reshape(2, nseg, own, hid)
-    cots = out_cot[0].T.reshape(nseg, own, tokens)
-    inner, cot = [], []
-    for dx, dc in slots:
-        dest = other(me, dx, dc)
-        piece = lax.dynamic_index_in_dim(start, dest, 1, keepdims=False)
-        inner.append(to_seg(piece, dx, dc))
-        cot.append(to_seg(lax.dynamic_index_in_dim(cots, dest, 0, keepdims=False), dx, dc))
-
-    segs = jnp.arange(nseg, dtype=jnp.int32)
-    slot_of = ((chip - segs // CORES) % chips) * CORES + (core + segs) % CORES
-    back = (place - jnp.arange(nseq, dtype=jnp.int32)) % nseq
-    table = jnp.concatenate([slot_of, back, (me * hpd)[None]]).astype(jnp.int32)
-
-    dims = (nseg, nseq, hpd, feats, hid, tokens, chunk)
-    smem = pl.BlockSpec(memory_space=pltpu.SMEM)
-    vmem = pl.BlockSpec(memory_space=pltpu.VMEM)
-    gp, gq, gi = pl.pallas_call(
+    packs = [to_seg(packs[i], dx, dc) for i, (dx, dc) in enumerate(slots)]
+
+    outs = kernel(
         functools.partial(inner_kernel, dims),
-        in_specs=[smem, smem] + [vmem] * (3 * nseg + nseq),
-        out_specs=[vmem] * 3,
-        out_shape=[
-            jax.ShapeDtypeStruct((nseq, 3 * own, chunk), BF),
-            jax.ShapeDtypeStruct((nseg, 3, hpd, feats, tokens), BF),
-            jax.ShapeDtypeStruct((nseg, 2, hpd, feats, hid), BF),
-        ],
-        scratch_shapes=[
+        "inner",
+        [array((3 * own, chunk), BF if dz else F32) for dz in range(nseq)]
+        + [array((nseg, 3, hpd, feats, tokens), BF)]
+        + [array((2, hpd, feats, hid), BF)] * nseg,
+        [
             pltpu.VMEM((nseg, 3, hpd, feats, tokens), BF),
             pltpu.VMEM((nseg, 2, hpd, feats, hid), BF),
             pltpu.VMEM((nseg, hpd, feats, tokens), BF),
@@ -206,43 +275,57 @@
             pltpu.VMEM((nseg, hpd, hid, tokens), F32),
             pltpu.VMEM((nseg, hpd, hid, tokens), BF),
             pltpu.VMEM((nseg, 2, hpd, feats, hid), F32),
+            pltpu.VMEM((nseg, 2, hpd, feats, hid), BF),
         ],
-        compiler_params=pltpu.CompilerParams(vmem_limit_bytes=VMEM),
-        cost_estimate=pl.CostEstimate(
-            flops=40 * 10**9, bytes_accessed=10**7, transcendentals=10**6
-        ),
-        name="inner",
-    )(table, rates, *li, *wt, *inner, *cot)
-
-    total = lax.dynamic_index_in_dim(gp, place, 0, keepdims=False).astype(F32)
-    for dz in range(1, nseq):
-        piece = lax.dynamic_index_in_dim(gp, (place + dz) % nseq, 0, keepdims=False)
-        total += to_seq(piece, dz).astype(F32)
-    far = jnp.stack([to_seg(total, dx, 0) for dx in range(chips)])
-    near = to_seg(far, 0, 1)
-    both = jnp.stack([far, near], 1).reshape(nseg, 3, hpd, feats, chunk)
-    ordered = pick(both, slot_of)
-    grad_proj = ordered.transpose(4, 1, 0, 2, 3).reshape(chunk, 3 * heads * feats)
-
-    part = pl.pallas_call(
+        20 * 10**9,
+        table,
+        rates,
+        *li,
+        *wt,
+        *packs,
+    )
+    gp, gq, gi = outs[:nseq], outs[nseq], outs[nseq + 1 :]
+
+    got = [to_seq(gp[dz], dz) for dz in range(1, nseq)]
+
+    keep, send = kernel(
         functools.partial(input_kernel, nseg, nseq, chunk),
-        in_specs=[smem] + [vmem] * (1 + nseq),
-        out_specs=vmem,
-        out_shape=jax.ShapeDtypeStruct((nseg, tokens, width), BF),
-        compiler_params=pltpu.CompilerParams(vmem_limit_bytes=VMEM),
-        cost_estimate=pl.CostEstimate(flops=3 * 10**9, bytes_accessed=10**7, transcendentals=0),
-        name="input",
-    )(table, gq, *wt)
-    part = part.reshape(chips, CORES, tokens, width)
-    summed = part[:, 0].astype(F32) + to_seg(part[:, 1], 0, 1).astype(F32)
+        "input",
+        [array((chips, tokens, width), BF)] * CORES,
+        [],
+        3 * 10**9,
+        table,
+        gq,
+        *wt,
+    )
+    summed = keep.astype(F32) + to_seg(send, 0, 1).astype(F32)
     grad_input = summed[0]
     for dx in range(1, chips):
         grad_input += to_seg(summed[dx].astype(BF), -dx, 0).astype(F32)
 
-    pieces = jnp.stack([to_seg(gi[i], -dx, dc) for i, (dx, dc) in enumerate(slots)])
-    source = ((segs // CORES - chip) % chips) * CORES + (core + segs) % CORES
-    grad_inner = pick(pieces, source).transpose(1, 0, 2, 3, 4)
-    grad_inner = grad_inner.reshape(2, heads, feats, hid).astype(F32)
+    (grad_inner,) = kernel(
+        functools.partial(weights_kernel, dims),
+        "weights",
+        [array((2, heads, feats, hid), F32)],
+        [],
+        10**6,
+        table,
+        *[to_seg(gi[i], -dx, dc) for i, (dx, dc) in enumerate(slots)],
+    )
+
+    (total,) = kernel(sum_kernel, "sum", [array((chunk, 3 * own), BF)], [], 10**6, gp[0], *got)
+    far = [to_seg(total, dx, 0) for dx in range(chips)]
+    near = to_seg(jnp.stack(far), 0, 1)
+    (grad_proj,) = kernel(
+        functools.partial(join_kernel, dims),
+        "join",
+        [array((chunk, 3 * heads * feats), F32)],
+        [],
+        10**6,
+        table,
+        *far,
+        near,
+    )
     return (grad_input.astype(BF)[None], grad_proj, grad_inner[None, None])
 
 

time: 207 us -> 188 us (0.908); the launches traced: 203 us -> 187 us
  local copies, waits for them, and re-layouts: 22.9 us -> 5.84 us
  waiting for transfers between devices: 102 us -> 119 us
  between operations: 15.6 us -> 0.86 us
  Pallas kernels: 28.8 us -> 39.3 us
  other arithmetic: 10.9 us -> 3.77 us
  starting transfers between devices: 23.2 us -> 18.9 us
    ppermute x16 -> x13, waiting for transfers between devices: 37.7 us -> 56.7 us  [to_seg(): lax.ppermute(value, 'seg', [(i, other(i, dx, dc)) for i in range(nseg)])]
    pallas_call x2 -> x6, Pallas kernels: 28.8 us -> 39.3 us  [kernel(): pl.pallas_call(body, in_specs=[smem if o.ndim == 1 else vmem for o in ope...]
    squeeze x4 -> x0, local copies, waits for them, and re-layouts: 4.74 us -> none  [the longest x1 3.28 us: per_device(): summed = part[:, 0].astype(F32) + to_seg(part[:, 1], 0, 1).astype(F32)]
    ppermute x16 -> x13, starting transfers between devices: 16.4 us -> 12.3 us  [to_seg(): lax.ppermute(value, 'seg', [(i, other(i, dx, dc)) for i in range(nseg)])]
    reshape x2 -> x0, local copies, waits for them, and re-layouts: 4.05 us -> none  [the longest x1 2.97 us: per_device(): columns = w_proj.reshape(chunk, 3, nseg, own)]
    slice x3 -> x0, local copies, waits for them, and re-layouts: 3.26 us -> none  [the longest x1 1.98 us: per_device(): gi[i]]
    another operation x3 -> x1, other arithmetic: 2.94 us -> 0.09 us  [per_device(): near = to_seg(jnp.stack(far), 0, 1)]
    dynamic_slice x4 -> x0, local copies, waits for them, and re-layouts: 2.33 us -> none  [the longest x2 1.81 us: per_device(): mine = lax.dynamic_index_in_dim(columns, me, 2, keepdims=False)]
  transfers between devices with their start and end apart: 22 -> 19, of which waited for: 10 -> 13; matrix products, arithmetic and copies ran while one was open for 12% -> 1% of each run, Pallas kernels for 0% -> 4%
where the time goes in v2:
time: 188 us; the launch traced here: 187 us
  waiting for transfers between devices  119 us (63%)
  Pallas kernels  39.3 us (21%)
  starting transfers between devices  18.9 us (10%)
  local copies, waits for them, and re-layouts  5.84 us (3%)
  other arithmetic  3.77 us (2%)
    ppermute x6, waiting for transfers between devices, to_seq(): lax.ppermute(value, 'seq', [(i, (i + dz) % nseq) for i in range(nseq)])  62.1 us
    ppermute x13, waiting for transfers between devices, to_seg(): lax.ppermute(value, 'seg', [(i, other(i, dx, dc)) for i in range(nseg)])  56.7 us
    pallas_call x6, Pallas kernels, kernel(): pl.pallas_call(body, in_specs=[smem if o.ndim == 1 else vmem for o in ope...  39.3 us
    ppermute x13, starting transfers between devices, to_seg(): lax.ppermute(value, 'seg', [(i, other(i, dx, dc)) for i in range(nseg)])  12.3 us
    ppermute x6, starting transfers between devices, to_seq(): lax.ppermute(value, 'seq', [(i, (i + dz) % nseq) for i in range(nseq)])  6.54 us
    unnamed x48, local copies, waits for them, and re-layouts  5.03 us
  transfers between devices with their start and end apart: 19, of which 13 were waited for; matrix products, arithmetic and copies ran while one was open for 1% of the time, Pallas kernels for 4%

profile of v2, /device:TPU:9, one launch (start us, length us, event | category | flops | bytes accessed | tf_op | source)
XLA Modules:
  0.0 187.5 jit_solution(9927102050895126940)
XLA Ops:
  0.6 0.0 copy-start.8
  0.7 0.7 concatenate.3.table
  1.4 3.0 %prep.1 = (bf16[384,512]{1,0:T(8,128)(2,1)}, bf16[384,256]{1,0:T(8,128)(2,1)}, bf16[384,256]{1,0:T(8,128)(2,1)}, bf16[384,256]{1,0:T(8,128)(2,1)}, bf16[384,256]{1,0:T(8,128)(2,1)}) custom-call(s32[14]{0:T(128)} %concatenate.3.table, bf16[512,1536]{1,0:T(8,128)(2,1)} %w.1, bf16[256,512]{1,0:T(8,128)(2,1)} %bitcast.24, f32[2,8,64,256]{3,2,1,0:T(8,128)} %bitcast.22), custom_call_target="tpu_custom_call" | custom-call | flops 1000000 | bytes 4063288 | tf_op jit(solution)/shard_map/prep/pallas_call | solution.py:223
  4.4 1.2 collective-permute-start.1
  5.6 1.0 collective-permute-start
  6.5 21.9 %collective-permute-done.1.refs_2_ = bf16[256,2048]{1,0:T(8,128)(2,1)S(1)} collective-permute-done((bf16[256,2048]{1,0:T(8,128)(2,1)S(1)}, bf16[256,2048]{1,0:T(8,128)(2,1)S(1)}, u32[]{:S(2)}, u32[]{:S(2)}) %collective-permute-start.1) | collective-permute-done | bytes 1048608 | tf_op jit(solution)/shard_map/ppermute | solution.py:214
  28.4 1.5 collective-permute-start.2
  30.0 1.2 collective-permute-start.7
  31.2 0.9 collective-permute-start.8
  32.1 0.5 collective-permute-done.6.refs_9_
  32.6 1.3 collective-permute-start.3
  33.9 2.2 %collective-permute-done.7.refs_10_ = bf16[384,256]{1,0:T(8,128)(2,1)S(1)} collective-permute-done((bf16[384,256]{1,0:T(8,128)(2,1)}, bf16[384,256]{1,0:T(8,128)(2,1)S(1)}, u32[]{:S(2)}, u32[]{:S(2)}) %collective-permute-start.7) | collective-permute-done | bytes 196640 | tf_op jit(solution)/shard_map/ppermute | solution.py:214
  36.1 2.3 %collective-permute-start.4 = (bf16[384,512]{1,0:T(8,128)(2,1)}, bf16[384,512]{1,0:T(8,128)(2,1)S(1)}, u32[]{:S(2)}, u32[]{:S(2)}) collective-permute-start(bf16[384,512]{1,0:T(8,128)(2,1)} %get-tuple-element.31.refs_4_.refs_0_), channel_id=1, source_target_pairs={{0,8},{4,12},{8,0},{12,4},{1,9},{5,13},{9,1},{13,5},{2,10},{6,14},... | collective-permute-start | bytes 1179656 | tf_op jit(solution)/shard_map/ppermute | solution.py:217
  38.4 2.9 %collective-permute-done.8.refs_11_ = bf16[384,256]{1,0:T(8,128)(2,1)S(1)} collective-permute-done((bf16[384,256]{1,0:T(8,128)(2,1)}, bf16[384,256]{1,0:T(8,128)(2,1)S(1)}, u32[]{:S(2)}, u32[]{:S(2)}) %collective-permute-start.8) | collective-permute-done | bytes 196640 | tf_op jit(solution)/shard_map/ppermute | solution.py:214
  41.3 2.1 %collective-permute-done.3.refs_5_.refs_1_ = bf16[384,512]{1,0:T(8,128)(2,1)S(1)} collective-permute-done((bf16[384,512]{1,0:T(8,128)(2,1)}, bf16[384,512]{1,0:T(8,128)(2,1)S(1)}, u32[]{:S(2)}, u32[]{:S(2)}) %collective-permute-start.3) | collective-permute-done | bytes 393248 | tf_op jit(solution)/shard_map/ppermute | solution.py:217
  43.4 24.5 %collective-permute-done.4.refs_6_.refs_2_ = bf16[384,512]{1,0:T(8,128)(2,1)S(1)} collective-permute-done((bf16[384,512]{1,0:T(8,128)(2,1)}, bf16[384,512]{1,0:T(8,128)(2,1)S(1)}, u32[]{:S(2)}, u32[]{:S(2)}) %collective-permute-start.4) | collective-permute-done | bytes 393248 | tf_op jit(solution)/shard_map/ppermute | solution.py:217
  67.9 2.1 %collective-permute-done.5.refs_7_.refs_3_ = bf16[384,512]{1,0:T(8,128)(2,1)S(1)} collective-permute-done((bf16[384,512]{1,0:T(8,128)(2,1)}, bf16[384,512]{1,0:T(8,128)(2,1)S(1)}, u32[]{:S(2)}, u32[]{:S(2)}) %collective-permute-start.5) | collective-permute-done | bytes 393248 | tf_op jit(solution)/shard_map/ppermute | solution.py:217
  70.1 0.7 copy-done.17
  70.8 0.3 copy-done.10
  71.1 1.0 copy-done.11
  72.1 22.9 %inner.1 = (f32[384,512]{1,0:T(8,128)}, bf16[384,512]{1,0:T(8,128)(2,1)}, bf16[384,512]{1,0:T(8,128)(2,1)}, bf16[384,512]{1,0:T(8,128)(2,1)}, bf16[4,3,2,64,256]...) custom-call(s32[14]{0:T(128)} %concatenate.3.table, ...), custom_call_target="tpu_custom_call" | custom-call | flops 20000000000 | bytes 9830488 | tf_op jit(solution)/shard_map/inner/pallas_call | solution.py:223
  95.0 5.5 %input.1 = (bf16[2,256,2048]{2,1,0:T(8,128)(2,1)}, bf16[2,256,2048]{2,1,0:T(8,128)(2,1)}) custom-call(s32[14]{0:T(128)} %concatenate.3.table, bf16[4,3,2,64,256]{4,3,2,1,0:T(8,128)(2,1)} %get-tuple-element.36.gq, bf16[384,512]{1,0:T(8,128)(2,1)} %get-tuple-element.31.refs_4_.refs_0_, bf16[384,512]{1,0:T(8,128)(2,1)} %copy-done.12, ...), custom_call_target="tpu_custom_call" | custom-call | flops 3000000000 | bytes 6553656 | tf_op jit(solution)/shard_map/input/pallas_call | solution.py:223
  100.5 0.5 collective-permute-start.9
  101.0 1.5 collective-permute-start.12
  102.6 1.4 collective-permute-start.13
  104.0 7.7 %collective-permute-done.11.refs_1_ = bf16[384,512]{1,0:T(8,128)(2,1)S(1)} collective-permute-done((bf16[384,512]{1,0:T(8,128)(2,1)S(1)}, bf16[384,512]{1,0:T(8,128)(2,1)S(1)}, u32[]{:S(2)}, u32[]{:S(2)}) %collective-permute-start.11) | collective-permute-done | bytes 393248 | tf_op jit(solution)/shard_map/ppermute | solution.py:217
  111.7 23.3 %collective-permute-done.12.refs_2_ = bf16[384,512]{1,0:T(8,128)(2,1)S(1)} collective-permute-done((bf16[384,512]{1,0:T(8,128)(2,1)S(1)}, bf16[384,512]{1,0:T(8,128)(2,1)S(1)}, u32[]{:S(2)}, u32[]{:S(2)}) %collective-permute-start.12) | collective-permute-done | bytes 393248 | tf_op jit(solution)/shard_map/ppermute | solution.py:217
  135.0 2.4 %collective-permute-done.13.refs_3_ = bf16[384,512]{1,0:T(8,128)(2,1)S(1)} collective-permute-done((bf16[384,512]{1,0:T(8,128)(2,1)S(1)}, bf16[384,512]{1,0:T(8,128)(2,1)S(1)}, u32[]{:S(2)}, u32[]{:S(2)}) %collective-permute-start.13) | collective-permute-done | bytes 393248 | tf_op jit(solution)/shard_map/ppermute | solution.py:217
  137.4 0.7 copy-done.7
  138.1 2.5 %sum.1.refs_0_ = bf16[512,384]{1,0:T(8,128)(2,1)} custom-call(f32[384,512]{1,0:T(8,128)} %get-tuple-element.39.refs_0_, bf16[384,512]{1,0:T(8,128)(2,1)} %copy-done.5, bf16[384,512]{1,0:T(8,128)(2,1)} %copy-done.6, bf16[384,512]{1,0:T(8,128)(2,1)} %copy-done.7), custom_call_target="tpu_custom_call" | custom-call | flops 1000000 | bytes 2359296 | tf_op jit(solution)/shard_map/sum/pallas_call | solution.py:223
  140.6 1.2 collective-permute-start.14
  141.8 1.3 copy-done.2
  143.2 2.4 %convert_add_fusion = f32[2,256,2048]{2,1,0:T(8,128)S(1)} fusion(bf16[2,256,2048]{2,1,0:T(8,128)(2,1)} %copy-done.2, bf16[2,256,2048]{2,1,0:T(8,128)(2,1)S(1)} %copy-done.1), kind=kLoop, calls=%fused_computation | loop fusion | flops 3145728 | bytes 8388608 | tf_op jit(solution)/shard_map/add | solution.py:301
  145.6 0.1 fusion.3
  145.8 0.3 collective-permute-start.10
  146.1 4.9 %collective-permute-done.14.refs_1_ = bf16[512,384]{1,0:T(8,128)(2,1)S(1)} collective-permute-done((bf16[512,384]{1,0:T(8,128)(2,1)}, bf16[512,384]{1,0:T(8,128)(2,1)S(1)}, u32[]{:S(2)}, u32[]{:S(2)}) %collective-permute-start.14) | collective-permute-done | bytes 393248 | tf_op jit(solution)/shard_map/ppermute | solution.py:214
  151.0 0.1 pad_maximum_fusion
  151.1 2.3 %collective-permute-start.15 = (bf16[2,512,384]{2,1,0:T(8,128)(2,1)S(1)}, bf16[2,512,384]{2,1,0:T(8,128)(2,1)S(1)}, u32[]{:S(2)}, u32[]{:S(2)}) collective-permute-start(bf16[2,512,384]{2,1,0:T(8,128)(2,1)S(1)} %pad_maximum_fusion), channel_id=1, source_target_pairs={{0,1},{1,0},{2,3},{3,2},{4,5},{5,4},{6,7},{7,6},{8,9},{9,8},{10,11... | collective-permute-start | bytes 2359304 | tf_op jit(solution)/shard_map/ppermute | solution.py:214
  153.4 0.1 collective-permute-start.16
  153.5 1.2 collective-permute-start.17
  154.7 0.8 collective-permute-start.18
  155.6 0.0 collective-permute-done.16.refs_1_
  155.6 20.8 %collective-permute-done.17.refs_2_ = bf16[2,2,64,256]{3,2,1,0:T(8,128)(2,1)} collective-permute-done((bf16[2,2,64,256]{3,2,1,0:T(8,128)(2,1)S(1)}, bf16[2,2,64,256]{3,2,1,0:T(8,128)(2,1)}, u32[]{:S(2)}, u32[]{:S(2)}) %collective-permute-start.17) | collective-permute-done | bytes 131104 | tf_op jit(solution)/shard_map/ppermute | solution.py:214
  176.4 3.4 %collective-permute-done.18.refs_3_ = bf16[2,2,64,256]{3,2,1,0:T(8,128)(2,1)} collective-permute-done((bf16[2,2,64,256]{3,2,1,0:T(8,128)(2,1)S(1)}, bf16[2,2,64,256]{3,2,1,0:T(8,128)(2,1)}, u32[]{:S(2)}, u32[]{:S(2)}) %collective-permute-start.18) | collective-permute-done | bytes 131104 | tf_op jit(solution)/shard_map/ppermute | solution.py:214
  179.9 2.1 %weights.1 = f32[2,8,64,256]{3,2,1,0:T(8,128)} custom-call(s32[14]{0:T(128)} %concatenate.3.table, bf16[2,2,64,256]{3,2,1,0:T(8,128)(2,1)} %get-tuple-element.43.refs_0_, bf16[2,2,64,256]{3,2,1,0:T(8,128)(2,1)} %collective-permute-done.16.refs_1_, bf16[2,2,64,256]{3,2,1,0:T(8,128)(2,1)} %collective-permute-done.17.refs_2_, ...), custom_call_target="tpu_custom_call" | custom-call | flops 1000000 | bytes 1572920 | tf_op jit(solution)/shard_map/weights/pallas_call | solution.py:223
  182.0 0.9 copy-done.4
  182.9 3.3 %join.1 = f32[512,1536]{1,0:T(8,128)} custom-call(s32[14]{0:T(128)} %concatenate.3.table, bf16[512,384]{1,0:T(8,128)(2,1)} %sum.1.refs_0_, bf16[512,384]{1,0:T(8,128)(2,1)} %copy-done.3, bf16[2,512,384]{2,1,0:T(8,128)(2,1)} %copy-done.4), custom_call_target="tpu_custom_call" | custom-call | flops 1000000 | bytes 4718648 | tf_op jit(solution)/shard_map/join/pallas_call | solution.py:223
  186.2 1.3 fusion.2
  (51 shorter events, 0.1 us)
Async XLA Ops:
  0.6 3.8 %copy-start.8 = (bf16[1,256,2048]{2,1,0:T(8,128)(2,1)S(1)}, bf16[1,256,2048]{2,1,0:T(8,128)(2,1)}, u32[]{:S(2)}) copy-start(bf16[1,256,2048]{2,1,0:T(8,128)(2,1)} %param.5) | copy-start | bytes 3145732
  4.4 24.0 %collective-permute-start.1 = (bf16[256,2048]{1,0:T(8,128)(2,1)S(1)}, bf16[256,2048]{1,0:T(8,128)(2,1)S(1)}, u32[]{:S(2)}, u32[]{:S(2)}) collective-permute-start(bf16[256,2048]{1,0:T(8,128)(2,1)S(1)} %bitcast.26), channel_id=1, source_target_pairs={{0,2},{1,3},{2,0},{3,1},{4,6},{5,7},{6,4},{7,5},{8,10},{9,11},{10,... | collective-permute-start | bytes 3145736 | tf_op jit(solution)/shard_map/ppermute | solution.py:214
  5.6 64.4 %collective-permute-start = (bf16[256,2048]{1,0:T(8,128)(2,1)S(1)}, bf16[256,2048]{1,0:T(8,128)(2,1)S(1)}, u32[]{:S(2)}, u32[]{:S(2)}) collective-permute-start(bf16[256,2048]{1,0:T(8,128)(2,1)S(1)} %bitcast.27), channel_id=1, source_target_pairs={{0,1},{1,0},{2,3},{3,2},{4,5},{5,4},{6,7},{7,6},{8,9},{9,8},{10,11... | collective-permute-start | bytes 3145736 | tf_op jit(solution)/shard_map/ppermute | solution.py:214
  28.4 41.6 %copy-start.9 = (bf16[256,2048]{1,0:T(8,128)(2,1)}, bf16[256,2048]{1,0:T(8,128)(2,1)S(1)}, u32[]{:S(2)}) copy-start(bf16[256,2048]{1,0:T(8,128)(2,1)S(1)} %collective-permute-done.1.refs_2_) | copy-start | bytes 3145732
  28.4 41.6 %collective-permute-start.2 = (bf16[256,2048]{1,0:T(8,128)(2,1)S(1)}, bf16[256,2048]{1,0:T(8,128)(2,1)S(1)}, u32[]{:S(2)}, u32[]{:S(2)}) collective-permute-start(bf16[256,2048]{1,0:T(8,128)(2,1)S(1)} %collective-permute-done.1.refs_2_), channel_id=1, source_target_pairs={{0,1},{1,0},{2,3},{3,2},{4,5},{5,4},{6,7},{7,6},{8,9},{9,8},{10,11... | collective-permute-start | bytes 3145736 | tf_op jit(solution)/shard_map/ppermute | solution.py:214
  30.0 2.6 %collective-permute-start.6 = (bf16[384,256]{1,0:T(8,128)(2,1)}, bf16[384,256]{1,0:T(8,128)(2,1)S(1)}, u32[]{:S(2)}, u32[]{:S(2)}) collective-permute-start(bf16[384,256]{1,0:T(8,128)(2,1)} %get-tuple-element.33), channel_id=1, source_target_pairs={{0,1},{1,0},{2,3},{3,2},{4,5},{5,4},{6,7},{7,6},{8,9},{9,8},{10,11... | collective-permute-start | bytes 589832 | tf_op jit(solution)/shard_map/ppermute | solution.py:214
  30.0 6.2 %collective-permute-start.7 = (bf16[384,256]{1,0:T(8,128)(2,1)}, bf16[384,256]{1,0:T(8,128)(2,1)S(1)}, u32[]{:S(2)}, u32[]{:S(2)}) collective-permute-start(bf16[384,256]{1,0:T(8,128)(2,1)} %get-tuple-element.34), channel_id=1, source_target_pairs={{0,2},{1,3},{2,0},{3,1},{4,6},{5,7},{6,4},{7,5},{8,10},{9,11},{10,... | collective-permute-start | bytes 589832 | tf_op jit(solution)/shard_map/ppermute | solution.py:214
  31.2 10.1 %collective-permute-start.8 = (bf16[384,256]{1,0:T(8,128)(2,1)}, bf16[384,256]{1,0:T(8,128)(2,1)S(1)}, u32[]{:S(2)}, u32[]{:S(2)}) collective-permute-start(bf16[384,256]{1,0:T(8,128)(2,1)} %get-tuple-element.35), channel_id=1, source_target_pairs={{0,3},{1,2},{2,1},{3,0},{4,7},{5,6},{6,5},{7,4},{8,11},{9,10},{10,... | collective-permute-start | bytes 589832 | tf_op jit(solution)/shard_map/ppermute | solution.py:214
  32.6 37.4 %copy-start.18 = (bf16[384,256]{1,0:T(8,128)(2,1)}, bf16[384,256]{1,0:T(8,128)(2,1)S(1)}, u32[]{:S(2)}) copy-start(bf16[384,256]{1,0:T(8,128)(2,1)S(1)} %collective-permute-done.6.refs_9_) | copy-start | bytes 589828
  32.6 10.8 %collective-permute-start.3 = (bf16[384,512]{1,0:T(8,128)(2,1)}, bf16[384,512]{1,0:T(8,128)(2,1)S(1)}, u32[]{:S(2)}, u32[]{:S(2)}) collective-permute-start(bf16[384,512]{1,0:T(8,128)(2,1)} %get-tuple-element.31.refs_4_.refs_0_), channel_id=1, source_target_pairs={{0,4},{4,8},{8,12},{12,0},{1,5},{5,9},{9,13},{13,1},{2,6},{6,10},{... | collective-permute-start | bytes 1179656 | tf_op jit(solution)/shard_map/ppermute | solution.py:217
  36.1 33.9 %copy-start.19 = (bf16[384,256]{1,0:T(8,128)(2,1)}, bf16[384,256]{1,0:T(8,128)(2,1)S(1)}, u32[]{:S(2)}) copy-start(bf16[384,256]{1,0:T(8,128)(2,1)S(1)} %collective-permute-done.7.refs_10_) | copy-start | bytes 589828
  36.1 31.7 %collective-permute-start.4 = (bf16[384,512]{1,0:T(8,128)(2,1)}, bf16[384,512]{1,0:T(8,128)(2,1)S(1)}, u32[]{:S(2)}, u32[]{:S(2)}) collective-permute-start(bf16[384,512]{1,0:T(8,128)(2,1)} %get-tuple-element.31.refs_4_.refs_0_), channel_id=1, source_target_pairs={{0,8},{4,12},{8,0},{12,4},{1,9},{5,13},{9,1},{13,5},{2,10},{6,14},... | collective-permute-start | bytes 1179656 | tf_op jit(solution)/shard_map/ppermute | solution.py:217
  41.3 28.7 %copy-start.20 = (bf16[384,256]{1,0:T(8,128)(2,1)}, bf16[384,256]{1,0:T(8,128)(2,1)S(1)}, u32[]{:S(2)}) copy-start(bf16[384,256]{1,0:T(8,128)(2,1)S(1)} %collective-permute-done.8.refs_11_) | copy-start | bytes 589828
  41.3 28.7 %collective-permute-start.5 = (bf16[384,512]{1,0:T(8,128)(2,1)}, bf16[384,512]{1,0:T(8,128)(2,1)S(1)}, u32[]{:S(2)}, u32[]{:S(2)}) collective-permute-start(bf16[384,512]{1,0:T(8,128)(2,1)} %get-tuple-element.31.refs_4_.refs_0_), channel_id=1, source_target_pairs={{0,12},{4,0},{8,4},{12,8},{1,13},{5,1},{9,5},{13,9},{2,14},{6,2},{... | collective-permute-start | bytes 1179656 | tf_op jit(solution)/shard_map/ppermute | solution.py:217
  43.4 26.6 %copy-start.12 = (bf16[384,512]{1,0:T(8,128)(2,1)}, bf16[384,512]{1,0:T(8,128)(2,1)S(1)}, u32[]{:S(2)}) copy-start(bf16[384,512]{1,0:T(8,128)(2,1)S(1)} %collective-permute-done.3.refs_5_.refs_1_) | copy-start | bytes 1179652
  67.9 2.2 %copy-start.13 = (bf16[384,512]{1,0:T(8,128)(2,1)}, bf16[384,512]{1,0:T(8,128)(2,1)S(1)}, u32[]{:S(2)}) copy-start(bf16[384,512]{1,0:T(8,128)(2,1)S(1)} %collective-permute-done.4.refs_6_.refs_2_) | copy-start | bytes 1179652
  70.0 0.8 copy-start.17
  70.0 1.1 copy-start.10
  71.1 1.0 copy-start.11
  94.9 6.1 %copy-start.16 = (bf16[384,512]{1,0:T(8,128)(2,1)S(1)}, bf16[384,512]{1,0:T(8,128)(2,1)}, u32[]{:S(2)}) copy-start(bf16[384,512]{1,0:T(8,128)(2,1)} %get-tuple-element.40) | copy-start | bytes 1179652
  94.9 6.1 %copy-start.15 = (bf16[384,512]{1,0:T(8,128)(2,1)S(1)}, bf16[384,512]{1,0:T(8,128)(2,1)}, u32[]{:S(2)}) copy-start(bf16[384,512]{1,0:T(8,128)(2,1)} %get-tuple-element.41) | copy-start | bytes 1179652
  95.0 7.6 %copy-start.14 = (bf16[384,512]{1,0:T(8,128)(2,1)S(1)}, bf16[384,512]{1,0:T(8,128)(2,1)}, u32[]{:S(2)}) copy-start(bf16[384,512]{1,0:T(8,128)(2,1)} %get-tuple-element.42) | copy-start | bytes 1179652
  100.5 42.7 %copy-start.1 = (bf16[2,256,2048]{2,1,0:T(8,128)(2,1)S(1)}, bf16[2,256,2048]{2,1,0:T(8,128)(2,1)}, u32[]{:S(2)}) copy-start(bf16[2,256,2048]{2,1,0:T(8,128)(2,1)} %get-tuple-element.37) | copy-start | bytes 6291460
  100.5 41.3 %collective-permute-start.9 = (bf16[2,256,2048]{2,1,0:T(8,128)(2,1)}, bf16[2,256,2048]{2,1,0:T(8,128)(2,1)S(1)}, u32[]{:S(2)}, u32[]{:S(2)}) collective-permute-start(bf16[2,256,2048]{2,1,0:T(8,128)(2,1)} %get-tuple-element.38), channel_id=1, source_target_pairs={{0,1},{1,0},{2,3},{3,2},{4,5},{5,4},{6,7},{7,6},{8,9},{9,8},{10,11... | collective-permute-start | bytes 6291464 | tf_op jit(solution)/shard_map/ppermute | solution.py:214
  101.0 10.7 %collective-permute-start.11 = (bf16[384,512]{1,0:T(8,128)(2,1)S(1)}, bf16[384,512]{1,0:T(8,128)(2,1)S(1)}, u32[]{:S(2)}, u32[]{:S(2)}) collective-permute-start(bf16[384,512]{1,0:T(8,128)(2,1)S(1)} %copy-done.16), channel_id=1, source_target_pairs={{0,4},{4,8},{8,12},{12,0},{1,5},{5,9},{9,13},{13,1},{2,6},{6,10},{... | collective-permute-start | bytes 1179656 | tf_op jit(solution)/shard_map/ppermute | solution.py:217
  101.0 34.0 %collective-permute-start.12 = (bf16[384,512]{1,0:T(8,128)(2,1)S(1)}, bf16[384,512]{1,0:T(8,128)(2,1)S(1)}, u32[]{:S(2)}, u32[]{:S(2)}) collective-permute-start(bf16[384,512]{1,0:T(8,128)(2,1)S(1)} %copy-done.15), channel_id=1, source_target_pairs={{0,8},{4,12},{8,0},{12,4},{1,9},{5,13},{9,1},{13,5},{2,10},{6,14},... | collective-permute-start | bytes 1179656 | tf_op jit(solution)/shard_map/ppermute | solution.py:217
  102.6 34.8 %collective-permute-start.13 = (bf16[384,512]{1,0:T(8,128)(2,1)S(1)}, bf16[384,512]{1,0:T(8,128)(2,1)S(1)}, u32[]{:S(2)}, u32[]{:S(2)}) collective-permute-start(bf16[384,512]{1,0:T(8,128)(2,1)S(1)} %copy-done.14), channel_id=1, source_target_pairs={{0,12},{4,0},{8,4},{12,8},{1,13},{5,1},{9,5},{13,9},{2,14},{6,2},{... | collective-permute-start | bytes 1179656 | tf_op jit(solution)/shard_map/ppermute | solution.py:217
  111.7 25.7 %copy-start.5 = (bf16[384,512]{1,0:T(8,128)(2,1)}, bf16[384,512]{1,0:T(8,128)(2,1)S(1)}, u32[]{:S(2)}) copy-start(bf16[384,512]{1,0:T(8,128)(2,1)S(1)} %collective-permute-done.11.refs_1_) | copy-start | bytes 1179652
  135.0 2.4 %copy-start.6 = (bf16[384,512]{1,0:T(8,128)(2,1)}, bf16[384,512]{1,0:T(8,128)(2,1)S(1)}, u32[]{:S(2)}) copy-start(bf16[384,512]{1,0:T(8,128)(2,1)S(1)} %collective-permute-done.12.refs_2_) | copy-start | bytes 1179652
  137.4 0.7 copy-start.7
  140.6 10.4 %collective-permute-start.14 = (bf16[512,384]{1,0:T(8,128)(2,1)}, bf16[512,384]{1,0:T(8,128)(2,1)S(1)}, u32[]{:S(2)}, u32[]{:S(2)}) collective-permute-start(bf16[512,384]{1,0:T(8,128)(2,1)} %sum.1.refs_0_), channel_id=1, source_target_pairs={{0,2},{1,3},{2,0},{3,1},{4,6},{5,7},{6,4},{7,5},{8,10},{9,11},{10,... | collective-permute-start | bytes 1179656 | tf_op jit(solution)/shard_map/ppermute | solution.py:214
  141.8 1.3 copy-start.2
  145.6 5.5 %copy-start = (bf16[512,384]{1,0:T(8,128)(2,1)S(1)}, bf16[512,384]{1,0:T(8,128)(2,1)}, u32[]{:S(2)}) copy-start(bf16[512,384]{1,0:T(8,128)(2,1)} %sum.1.refs_0_) | copy-start | bytes 1179652
  145.6 7.8 %copy-start.23 = (bf16[2,2,64,256]{3,2,1,0:T(8,128)(2,1)S(1)}, bf16[2,2,64,256]{3,2,1,0:T(8,128)(2,1)}, u32[]{:S(2)}) copy-start(bf16[2,2,64,256]{3,2,1,0:T(8,128)(2,1)} %get-tuple-element.44) | copy-start | bytes 393220
  145.6 7.9 %copy-start.22 = (bf16[2,2,64,256]{3,2,1,0:T(8,128)(2,1)S(1)}, bf16[2,2,64,256]{3,2,1,0:T(8,128)(2,1)}, u32[]{:S(2)}) copy-start(bf16[2,2,64,256]{3,2,1,0:T(8,128)(2,1)} %get-tuple-element.45) | copy-start | bytes 393220
  145.6 9.1 %copy-start.21 = (bf16[2,2,64,256]{3,2,1,0:T(8,128)(2,1)S(1)}, bf16[2,2,64,256]{3,2,1,0:T(8,128)(2,1)}, u32[]{:S(2)}) copy-start(bf16[2,2,64,256]{3,2,1,0:T(8,128)(2,1)} %get-tuple-element.46) | copy-start | bytes 393220
  145.8 40.4 %collective-permute-start.10 = (bf16[256,2048]{1,0:T(8,128)(2,1)S(1)}, bf16[256,2048]{1,0:T(8,128)(2,1)S(1)}, u32[]{:S(2)}, u32[]{:S(2)}) collective-permute-start(bf16[256,2048]{1,0:T(8,128)(2,1)S(1)} %fusion.3), channel_id=1, source_target_pairs={{0,2},{1,3},{2,0},{3,1},{4,6},{5,7},{6,4},{7,5},{8,10},{9,11},{10,... | collective-permute-start | bytes 3145736 | tf_op jit(solution)/shard_map/ppermute | solution.py:214
  151.0 31.0 %copy-start.3 = (bf16[512,384]{1,0:T(8,128)(2,1)}, bf16[512,384]{1,0:T(8,128)(2,1)S(1)}, u32[]{:S(2)}) copy-start(bf16[512,384]{1,0:T(8,128)(2,1)S(1)} %collective-permute-done.14.refs_1_) | copy-start | bytes 1179652
  151.1 30.9 %collective-permute-start.15 = (bf16[2,512,384]{2,1,0:T(8,128)(2,1)S(1)}, bf16[2,512,384]{2,1,0:T(8,128)(2,1)S(1)}, u32[]{:S(2)}, u32[]{:S(2)}) collective-permute-start(bf16[2,512,384]{2,1,0:T(8,128)(2,1)S(1)} %pad_maximum_fusion), channel_id=1, source_target_pairs={{0,1},{1,0},{2,3},{3,2},{4,5},{5,4},{6,7},{7,6},{8,9},{9,8},{10,11... | collective-permute-start | bytes 2359304 | tf_op jit(solution)/shard_map/ppermute | solution.py:214
  153.4 2.2 %collective-permute-start.16 = (bf16[2,2,64,256]{3,2,1,0:T(8,128)(2,1)S(1)}, bf16[2,2,64,256]{3,2,1,0:T(8,128)(2,1)}, u32[]{:S(2)}, u32[]{:S(2)}) collective-permute-start(bf16[2,2,64,256]{3,2,1,0:T(8,128)(2,1)S(1)} %copy-done.23), channel_id=1, source_target_pairs={{0,1},{1,0},{2,3},{3,2},{4,5},{5,4},{6,7},{7,6},{8,9},{9,8},{10,11... | collective-permute-start | bytes 393224 | tf_op jit(solution)/shard_map/ppermute | solution.py:214
  153.5 22.9 %collective-permute-start.17 = (bf16[2,2,64,256]{3,2,1,0:T(8,128)(2,1)S(1)}, bf16[2,2,64,256]{3,2,1,0:T(8,128)(2,1)}, u32[]{:S(2)}, u32[]{:S(2)}) collective-permute-start(bf16[2,2,64,256]{3,2,1,0:T(8,128)(2,1)S(1)} %copy-done.22), channel_id=1, source_target_pairs={{0,2},{1,3},{2,0},{3,1},{4,6},{5,7},{6,4},{7,5},{8,10},{9,11},{10,... | collective-permute-start | bytes 393224 | tf_op jit(solution)/shard_map/ppermute | solution.py:214
  154.7 25.1 %collective-permute-start.18 = (bf16[2,2,64,256]{3,2,1,0:T(8,128)(2,1)S(1)}, bf16[2,2,64,256]{3,2,1,0:T(8,128)(2,1)}, u32[]{:S(2)}, u32[]{:S(2)}) collective-permute-start(bf16[2,2,64,256]{3,2,1,0:T(8,128)(2,1)S(1)} %copy-done.21), channel_id=1, source_target_pairs={{0,3},{1,2},{2,1},{3,0},{4,7},{5,6},{6,5},{7,4},{8,11},{9,10},{10,... | collective-permute-start | bytes 393224 | tf_op jit(solution)/shard_map/ppermute | solution.py:214
  182.0 0.9 copy-start.4

commit v3 on v2

v3 whole, which is shorter than its diff:
```python
import functools

import jax
import jax.numpy as jnp
from jax import lax
from jax.experimental import pallas as pl
from jax.experimental.pallas import tpu as pltpu
from jax.sharding import PartitionSpec as P

MB = 256
BF = jnp.bfloat16
F32 = jnp.float32
CORES = 2
GELU_A = 0.7978845608028654
GELU_B = 0.044715
MIB = 1024 * 1024


def dot(a, b, ca, cb):
    return lax.dot_general(a, b, (((ca,), (cb,)), ((), ())), preferred_element_type=F32)


def gelu_parts(u):
    square = u * u
    tanh = jnp.tanh(u * (GELU_A + (GELU_A * GELU_B) * square))
    half = 0.5 * (1.0 + tanh)
    sech = 1.0 - tanh * tanh
    slope = GELU_A + (3.0 * GELU_A * GELU_B) * square
    return square, tanh, half, sech, slope


def prep_kernel(dims, table, w, cots, start, mine, keep, send, block, turned):
    nseg, nseq, hpd, feats, hid, tokens, chunk = dims
    own = hpd * feats
    total = own * nseg
    wide = block.shape[0]
    me = table[nseg + nseq + 1]
    base = me * own // wide * wide
    for part in range(3):
        at = pl.multiple_of(part * total + base, wide)
        block[...] = w[:, pl.ds(at, wide)].T
        rest = pl.multiple_of(me * own - base, own)
        mine[part * own : (part + 1) * own] = block[pl.ds(rest, own)]
    turned[...] = cots[...].T
    for slot in range(nseg):
        dest = table[nseg + nseq + 2 + slot]
        piece = start[:, pl.ds(dest * hpd, hpd)].astype(BF)
        pack = (keep, send)[slot % CORES]
        pack[slot // CORES, : 2 * own] = piece.reshape(2 * own, hid)
        pack[slot // CORES, 2 * own :] = turned[pl.ds(pl.multiple_of(dest * own, own), own)]


def inner_kernel(dims, head, before, table, rates, *refs):
    nseg, nseq, hpd, feats, hid, tokens, chunk = dims
    chips = nseg // CORES
    li, refs = refs[:nseg], refs[nseg:]
    wt, refs = refs[:nseq], refs[nseq:]
    keep, got, refs = refs[0], refs[1], refs[2:]
    hops, refs = refs[: chips - 1], refs[chips - 1 :]
    earlier, refs = refs[:before], refs[before:]
    gp, refs = refs[:nseq], refs[nseq:]
    gq, stay, leave, qkv, wts, cts, ht, rt, g1, g2p, gu, gab = refs
    own = hpd * feats
    rows = 3 * feats

    for slot in range(nseg):
        dx, dc = slot // CORES, slot % CORES
        pack = ((keep, got)[dc].at[0]) if dx == 0 else hops[dx - 1].at[dc]
        total = jnp.zeros((rows, tokens), F32)
        for back in range(nseq):
            at = pl.multiple_of(table[nseg + back] * chunk, chunk)
            left = jnp.concatenate(
                [wt[back][p * own + head * feats : p * own + (head + 1) * feats] for p in range(3)]
            )
            total += dot(left, li[slot][:, pl.ds(at, chunk)], 1, 1)
        qkv[slot] = total.astype(BF).reshape(3, feats, tokens)
        wts[slot, 0] = pack[head * feats : (head + 1) * feats]
        wts[slot, 1] = pack[own + head * feats : own + (head + 1) * feats]
        cts[slot] = pack[2 * own + head * feats : 2 * own + (head + 1) * feats]
    rate = rates[table[nseg + nseq] + head] * (1.0 / MB)

    def local(slot):
        a_b, b_b = wts[slot, 0], wts[slot, 1]
        q_b, k_b, v_b = qkv[slot, 0], qkv[slot, 1], qkv[slot, 2]
        c_b = cts[slot]
        u = dot(a_b, k_b, 0, 0)
        square, tanh, half, sech, slope = gelu_parts(u)
        h_b = (u * half).astype(BF)
        first = half + 0.5 * u * sech * slope
        second = sech * (GELU_A + (6.0 * GELU_A * GELU_B) * square - u * tanh * slope * slope)
        ht[slot] = h_b
        g1[slot] = first
        resid = k_b.astype(F32) - v_b.astype(F32) + dot(b_b, h_b, 1, 0)
        r_b = resid.astype(BF)
        rt[slot] = r_b
        p = dot(b_b, r_b, 0, 0)
        g2p[slot] = second * p
        gu_b = (first * p).astype(BF)
        gu[slot] = gu_b
        new_a = (a_b.astype(F32) - rate * dot(k_b, gu_b, 1, 1)).astype(BF)
        new_b = (b_b.astype(F32) - rate * dot(r_b, h_b, 1, 1)).astype(BF)
        uq = dot(new_a, q_b, 0, 0)
        square, tanh, half, sech, slope = gelu_parts(uq)
        hq_b = (uq * half).astype(BF)
        guq_b = ((half + 0.5 * uq * sech * slope) * dot(new_b, c_b, 0, 0)).astype(BF)
        gab[slot, 0] = dot(q_b, guq_b, 1, 1)
        gab[slot, 1] = dot(c_b, hq_b, 1, 1)
        gq[slot, 0] = (c_b.astype(F32) + dot(new_a, guq_b, 1, 0)).astype(BF)

    for slot in range(nseg):
        local(slot)

    def step(turn, carry):
        slot = table[nseg - 1 - turn]
        t_a = carry[0] + gab[slot, 0]
        t_b = carry[1] + gab[slot, 1]
        a_b, b_b = wts[slot, 0], wts[slot, 1]
        k_b = qkv[slot, 1]
        h_b, r_b, gu_b = ht[slot], rt[slot], gu[slot]
        ta_b, tb_b = t_a.astype(BF), t_b.astype(BF)
        du = dot(ta_b, k_b, 0, 0)
        dh_b = (g1[slot] * du).astype(BF)
        dr = dot(b_b, dh_b, 1, 0) + dot(tb_b, h_b, 1, 0)
        dr_b = dr.astype(BF)
        dp = dot(b_b, dr_b, 0, 0) + dot(tb_b, r_b, 0, 0)
        dgu_b = (g2p[slot] * du + g1[slot] * dp).astype(BF)
        c_a = t_a - rate * dot(k_b, dgu_b, 1, 1)
        c_b = t_b - rate * (dot(dr_b, h_b, 1, 1) + dot(r_b, dh_b, 1, 1))
        left = jnp.concatenate([a_b, ta_b], 1)
        gk = dr + dot(left, jnp.concatenate([dgu_b, gu_b], 0), 1, 0)
        gq[slot, 1] = (-rate * gk).astype(BF)
        gq[slot, 2] = (rate * dr).astype(BF)
        wts[slot, 0] = c_a.astype(BF)
        wts[slot, 1] = c_b.astype(BF)
        return (c_a, c_b)

    zero = jnp.zeros((feats, hid), F32)
    carry = (zero, zero)
    for turn in range(nseg):
        carry = step(turn, carry)

    for dx in range(chips):
        for dc, out in enumerate((stay, leave)):
            if before:
                for i in range(head):
                    out[dx, :, i] = earlier[CORES * i + dc][dx, :, 0]
                out[dx, :, head] = wts[dx * CORES + dc]
            else:
                out[dx, :, 0] = wts[dx * CORES + dc]
    for dz in range(nseq):
        at = pl.multiple_of(table[nseg + (nseq - dz) % nseq] * chunk, chunk)
        total = jnp.zeros((rows, chunk), F32)
        for slot in range(nseg):
            total += dot(gq[slot].reshape(rows, tokens), li[slot][:, pl.ds(at, chunk)], 1, 0)
        gp[dz][...] = total.astype(gp[dz].dtype)


def input_kernel(dims, slots, table, *refs):
    nseg, nseq, hpd, feats, hid, tokens, chunk = dims
    gq, wt, outs = refs[:hpd], refs[hpd : hpd + nseq], refs[hpd + nseq :]
    own = hpd * feats
    for i, slot in enumerate(slots):
        left = jnp.concatenate([gq[h][slot, p] for p in range(3) for h in range(hpd)])
        for back in range(nseq):
            at = pl.multiple_of(table[nseg + back] * chunk, chunk)
            value = dot(left, wt[back][...], 0, 0)
            outs[slot % CORES][i // CORES, :, pl.ds(at, chunk)] = value.astype(BF)


def sum_kernel(dims, *refs):
    nseg, nseq, hpd, feats, hid, tokens, chunk = dims
    out = refs[-1]
    for head in range(hpd):
        total = refs[head * nseq][...]
        for ref in refs[head * nseq + 1 : (head + 1) * nseq]:
            total += ref[...].astype(F32)
        for part in range(3):
            at = (part * hpd + head) * feats
            out[:, at : at + feats] = total[part * feats : (part + 1) * feats].T.astype(BF)


def join_kernel(dims, table, *refs):
    nseg, nseq, hpd, feats, hid, tokens, chunk = dims
    chips = nseg // CORES
    far, near, out = refs[:chips], refs[chips], refs[chips + 1]
    own = hpd * feats
    me = table[nseg + nseq + 1]
    chip = me // CORES
    even = me % CORES == 0
    for dx in range(chips):
        source = (chip - dx + chips) % chips
        for part in range(3):
            a = far[dx][:, part * own : (part + 1) * own].astype(F32)
            b = near[dx, :, part * own : (part + 1) * own].astype(F32)
            left, right = jnp.where(even, a, b), jnp.where(even, b, a)
            at = pl.multiple_of(part * nseg * own + source * CORES * own, CORES * own)
            out[:, pl.ds(at, CORES * own)] = jnp.concatenate([left, right], 1)


def weights_kernel(dims, table, stay, got, *refs):
    nseg, nseq, hpd = dims[:3]
    hops, out = refs[:-1], refs[-1]
    for slot in range(nseg):
        dx, dc = slot // CORES, slot % CORES
        source = table[nseg + nseq + 2 + slot]
        piece = (stay, got)[dc][0] if dx == 0 else hops[dx - 1][dc]
        out[:, pl.ds(source * hpd, hpd)] = piece.astype(F32)


def per_device(layer_input, out_cot, w_proj, inner_start, rates):
    rows = layer_input[0]
    tokens, width = rows.shape
    heads = rates.shape[0]
    feats, hid = inner_start.shape[4:]
    nseg, nseq = lax.axis_size("seg"), lax.axis_size("seq")
    chips = nseg // CORES
    hpd = heads // nseg
    own = hpd * feats
    chunk = width // nseq
    me, place = lax.axis_index("seg"), lax.axis_index("seq")
    chip, core = me // CORES, me % CORES
    barrier = lax.optimization_barrier

    def to_chip(value, dx):
        pairs = [(i, (i + dx * CORES) % nseg) for i in range(nseg)]
        return lax.ppermute(value, "seg", pairs)

    def to_core(value):
        return lax.ppermute(value, "seg", [(i, i ^ 1) for i in range(nseg)])

    def to_seq(value, dz):
        return lax.ppermute(value, "seq", [(i, (i + dz) % nseq) for i in range(nseq)])

    def kernel(body, name, limit, cost, outs, scratch, *operands):
        smem = pl.BlockSpec(memory_space=pltpu.SMEM)
        vmem = pl.BlockSpec(memory_space=pltpu.VMEM)
        return pl.pallas_call(
            body,
            in_specs=[smem if o.ndim == 1 else vmem for o in operands],
            out_specs=[vmem] * len(outs),
            out_shape=[jax.ShapeDtypeStruct(*o) for o in outs],
            scratch_shapes=[pltpu.VMEM(*o) for o in scratch],
            compiler_params=pltpu.CompilerParams(vmem_limit_bytes=limit * MIB),
            cost_estimate=pl.CostEstimate(flops=0, bytes_accessed=cost, transcendentals=0),
            name=name,
        )(*operands)

    segs = jnp.arange(nseg, dtype=jnp.int32)
    slot_of = ((chip - segs // CORES) % chips) * CORES + (core + segs) % CORES
    back = (place - jnp.arange(nseq, dtype=jnp.int32)) % nseq
    dest = ((chip + segs // CORES) % chips) * CORES + (core + segs) % CORES
    table = jnp.concatenate([slot_of, back, jnp.stack([me * hpd, me]), dest]).astype(jnp.int32)
    dims = (nseg, nseq, hpd, feats, hid, tokens, chunk)

    mine, keep, send = kernel(
        functools.partial(prep_kernel, dims),
        "prep",
        16,
        0,
        [((3 * own, chunk), BF)] + [((chips, 3 * own, tokens), BF)] * CORES,
        [((max(own, 128), chunk), BF), ((heads * feats, tokens), BF)],
        table,
        w_proj,
        out_cot[0],
        inner_start[0, 0],
    )
    rows, mine, keep, send = barrier((rows, mine, keep, send))
    far = [to_chip(rows, dx) for dx in range(1, chips)]
    near = to_core(rows)
    got = to_core(send)
    wt = [to_seq(mine, dz) for dz in range(1, nseq - 1)]
    near, got, keep, mine = barrier((near, got, keep, mine))
    wt = [mine] + wt + [to_seq(mine, nseq - 1)]
    hops = [to_chip(jnp.stack([keep[dx], got[dx]]), dx) for dx in range(1, chips)]
    wt, far, hops = barrier((wt, far, hops))
    li = [rows, near]
    for value in far:
        li += [value, to_core(value)]

    pieces, grads, inners = [], [], []
    for head in range(hpd):
        last = head == hpd - 1
        before = len(inners) if last else 0
        sent = hpd if last else 1
        outs = kernel(
            functools.partial(inner_kernel, dims, head, before),
            "inner",
            36,
            40 * MIB,
            [((3 * feats, chunk), BF if dz else F32) for dz in range(nseq)]
            + [((nseg, 3, feats, tokens), BF)]
            + [((chips, 2, sent, feats, hid), BF)] * CORES,
            [
                ((nseg, 3, feats, tokens), BF),
                ((nseg, 2, feats, hid), BF),
                ((nseg, feats, tokens), BF),
                ((nseg, hid, tokens), BF),
                ((nseg, feats, tokens), BF),
                ((nseg, hid, tokens), F32),
                ((nseg, hid, tokens), F32),
                ((nseg, hid, tokens), BF),
                ((nseg, 2, feats, hid), F32),
            ],
            table,
            rates,
            *li,
            *wt,
            keep,
            got,
            *hops,
            *(inners if last else []),
        )
        gp = outs[:nseq]
        grads.append(outs[nseq])
        inners += outs[nseq + 1 :]
        if pieces:
            pieces, gp, grads = barrier((pieces, gp, grads))
        pieces += [gp[0]] + [to_seq(gp[dz], dz) for dz in range(1, nseq)]

    stay, leave = inners[-CORES:]
    two = range(nseg)[:CORES]
    rest = range(nseg)[CORES:]

    def partial_input(name, limit, slots, grads):
        return kernel(
            functools.partial(input_kernel, dims, slots),
            name,
            limit,
            10 * MIB,
            [((len(slots) // CORES, tokens, width), BF)] * CORES,
            [],
            table,
            *grads,
            *wt,
        )

    out, cross = partial_input("far", 16, rest, grads)
    cross, leave = to_core(cross), to_core(leave)
    cross, leave, grads = barrier((cross, leave, grads))
    out = (out.astype(F32) + cross.astype(F32)).astype(BF)
    hops = [to_chip(out[dx - 1], -dx) for dx in range(1, chips)]
    backs = [to_chip(jnp.stack([stay[dx], leave[dx]]), -dx) for dx in range(1, chips)]
    home, aside = partial_input("home", 16, two, grads)
    aside = to_core(aside)
    pieces, hops, backs, aside = barrier((pieces, hops, backs, aside))
    grad_input = home[0].astype(F32) + aside[0].astype(F32)
    for hop in hops:
        grad_input += hop.astype(F32)

    (total,) = kernel(
        functools.partial(sum_kernel, dims),
        "sum",
        12,
        0,
        [((chunk, 3 * own), BF)],
        [],
        *pieces,
    )
    far = [total] + [to_chip(total, dx) for dx in range(1, chips)]
    near = to_core(jnp.stack(far))
    (grad_inner,) = kernel(
        functools.partial(weights_kernel, dims),
        "weights",
        8,
        10 * MIB,
        [((2, heads, feats, hid), F32)],
        [],
        table,
        stay,
        leave,
        *backs,
    )
    (grad_proj,) = kernel(
        functools.partial(join_kernel, dims),
        "join",
        16,
        0,
        [((chunk, 3 * heads * feats), F32)],
        [],
        table,
        *far,
        near,
    )
    return (grad_input.astype(BF)[None], grad_proj, grad_inner[None, None])


def solution(mesh):
    placed = (
        P(("groups", "seq"), "seg", None),
        P(("groups", "seq"), "seg", None),
        P("seq", None),
        P(("groups", "seq"), "seg", None, None, None, None),
        P(),
    )
    return jax.shard_map(
        per_device,
        mesh=mesh,
        in_specs=placed,
        out_specs=(
            P(("groups", "seq"), "seg", None),
            P(("groups", "seq"), None),
            P(("groups", "seq"), "seg", None, None, None, None),
        ),
        check_vma=False,
    )
```

time: 188 us -> 133 us (0.71)
  waiting for transfers between devices: 119 us -> 74 us
  Pallas kernels: 39.3 us -> 29.2 us
  starting transfers between devices: 18.9 us -> 22.3 us
  local copies, waits for them, and re-layouts: 5.84 us -> 3.81 us
    ppermute x13 -> x12, waiting for transfers between devices: 56.7 us -> 23.1 us  [the longest x5 18.3 us: to_chip(): return lax.ppermute(value, 'seg', pairs)]
    ppermute x6 -> x9, waiting for transfers between devices: 62.1 us -> 50.9 us  [to_seq(): lax.ppermute(value, 'seq', [(i, (i + dz) % nseq) for i in range(nseq)])]
    pallas_call x6 -> x8, Pallas kernels: 39.3 us -> 29.2 us  [kernel(): pl.pallas_call(body, in_specs=[smem if o.ndim == 1 else vmem for o in ope...]
    ppermute x6 -> x9, starting transfers between devices: 6.54 us -> 13.6 us  [to_seq(): lax.ppermute(value, 'seq', [(i, (i + dz) % nseq) for i in range(nseq)])]
    ppermute x13 -> x12, starting transfers between devices: 12.3 us -> 8.79 us  [the longest x7 5.34 us: to_core(): return lax.ppermute(value, 'seg', [(i, i ^ 1) for i in range(nseg)])]
    add x1 -> x0, other arithmetic: 2.39 us -> none  [per_device(): summed = keep.astype(F32) + to_seg(send, 0, 1).astype(F32)]
    unnamed x48 -> x10, local copies, waits for them, and re-layouts: 5.03 us -> 3.67 us
  transfers between devices with their start and end apart: 19 -> 21, of which waited for: 13 -> 10; matrix products, arithmetic and copies ran while one was open for 1% -> 2% of each run, Pallas kernels for 4% -> 9%
where the time goes in v3:
time: 133 us; the launch traced here: 132 us
  waiting for transfers between devices  74 us (56%)
  Pallas kernels  29.2 us (22%)
  starting transfers between devices  22.3 us (17%)
  local copies, waits for them, and re-layouts  3.81 us (3%)
  other arithmetic  2.08 us (2%)
    ppermute x9, waiting for transfers between devices, to_seq(): lax.ppermute(value, 'seq', [(i, (i + dz) % nseq) for i in range(nseq)])  50.9 us
    pallas_call x8, Pallas kernels, kernel(): pl.pallas_call(body, in_specs=[smem if o.ndim == 1 else vmem for o in ope...  29.2 us
    ppermute x5, waiting for transfers between devices, to_chip(): return lax.ppermute(value, 'seg', pairs)  18.3 us
    ppermute x9, starting transfers between devices, to_seq(): lax.ppermute(value, 'seq', [(i, (i + dz) % nseq) for i in range(nseq)])  13.6 us
    ppermute x7, starting transfers between devices, to_core(): return lax.ppermute(value, 'seg', [(i, i ^ 1) for i in range(nseg)])  5.34 us
    ppermute x7, waiting for transfers between devices, to_core(): return lax.ppermute(value, 'seg', [(i, i ^ 1) for i in range(nseg)])  4.88 us
    unnamed x10, local copies, waits for them, and re-layouts  3.67 us
    ppermute x5, starting transfers between devices, to_chip(): return lax.ppermute(value, 'seg', pairs)  3.46 us
  transfers between devices with their start and end apart: 21, of which 10 were waited for; matrix products, arithmetic and copies ran while one was open for 2% of the time, Pallas kernels for 9%

profile of v3, /device:TPU:9, one launch (start us, length us, event | category | flops | bytes accessed | tf_op | source)
XLA Modules:
  0.0 132.3 jit_solution(6134350178832082353)
XLA Ops:
  0.7 0.1 concatenate.3.table
  0.8 1.5 %copy-done.1 = bf16[512,1536]{1,0:T(8,128)(2,1)S(1)} copy-done((bf16[512,1536]{1,0:T(8,128)(2,1)S(1)}, bf16[512,1536]{1,0:T(8,128)(2,1)}, u32[]{:S(2)}) %copy-start.1) | copy-done | bytes 1572888
  2.3 1.2 copy-done.2
  3.5 0.9 copy-done.3
  4.5 0.8 prep.1
  5.3 0.7 collective-permute-start
  6.0 1.2 collective-permute-start.5
  7.2 0.3 collective-permute-start.1
  7.6 2.3 %collective-permute-start.3 = (bf16[384,512]{1,0:T(8,128)(2,1)S(1)}, bf16[384,512]{1,0:T(8,128)(2,1)S(1)}, u32[]{:S(2)}, u32[]{:S(2)}) collective-permute-start(bf16[384,512]{1,0:T(8,128)(2,1)S(1)} %get-tuple-element.75.refs_4_.refs_2_), channel_id=1, source_target_pairs={{0,8},{4,12},{8,0},{12,4},{1,9},{5,13},{9,1},{13,5},{2,10},{6,14},... | collective-permute-start | bytes 1179656 | tf_op jit(solution)/shard_map/ppermute | solution.py:232
  9.9 0.0 collective-permute-start.2
  9.9 0.0 collective-permute-done.1.refs_9_
  10.0 0.3 collective-permute-start.6
  10.3 1.5 %collective-permute-start.4 = (bf16[384,512]{1,0:T(8,128)(2,1)S(1)}, bf16[384,512]{1,0:T(8,128)(2,1)S(1)}, u32[]{:S(2)}, u32[]{:S(2)}) collective-permute-start(bf16[384,512]{1,0:T(8,128)(2,1)S(1)} %get-tuple-element.75.refs_4_.refs_2_), channel_id=1, source_target_pairs={{0,12},{4,0},{8,4},{12,8},{1,13},{5,1},{9,5},{13,9},{2,14},{6,2},{... | collective-permute-start | bytes 1179656 | tf_op jit(solution)/shard_map/ppermute | solution.py:232
  11.8 15.3 %collective-permute-done.3.refs_6_.refs_4_ = bf16[384,512]{1,0:T(8,128)(2,1)S(1)} collective-permute-done((bf16[384,512]{1,0:T(8,128)(2,1)S(1)}, bf16[384,512]{1,0:T(8,128)(2,1)S(1)}, u32[]{:S(2)}, u32[]{:S(2)}) %collective-permute-start.3) | collective-permute-done | bytes 393248 | tf_op jit(solution)/shard_map/ppermute | solution.py:232
  27.1 16.9 %collective-permute-done.2.refs_5_.refs_3_ = bf16[384,512]{1,0:T(8,128)(2,1)S(1)} collective-permute-done((bf16[384,512]{1,0:T(8,128)(2,1)S(1)}, bf16[384,512]{1,0:T(8,128)(2,1)S(1)}, u32[]{:S(2)}, u32[]{:S(2)}) %collective-permute-start.2) | collective-permute-done | bytes 393248 | tf_op jit(solution)/shard_map/ppermute | solution.py:232
  44.0 0.5 collective-permute-start.7
  44.5 2.3 %collective-permute-done.7.refs_3_ = bf16[256,2048]{1,0:T(8,128)(2,1)S(1)} collective-permute-done((bf16[256,2048]{1,0:T(8,128)(2,1)S(1)}, bf16[256,2048]{1,0:T(8,128)(2,1)S(1)}, u32[]{:S(2)}, u32[]{:S(2)}) %collective-permute-start.7) | collective-permute-done | bytes 1048608 | tf_op jit(solution)/shard_map/ppermute | solution.py:229
  46.8 10.1 %inner.2 = (f32[192,512]{1,0:T(8,128)S(1)}, bf16[192,512]{1,0:T(8,128)(2,1)S(1)}, bf16[192,512]{1,0:T(8,128)(2,1)S(1)}, bf16[192,512]{1,0:T(8,128)(2,1)S(1)}, bf...) custom-call(s32[14]{0:T(128)S(1)} %concatenate.3.table, ...), custom_call_target="tpu_custom_call" | custom-call | bytes 41943040 | tf_op jit(solution)/shard_map/inner/pallas_call | solution.py:237
  56.9 2.2 %collective-permute-start.8 = (bf16[192,512]{1,0:T(8,128)(2,1)S(1)}, bf16[192,512]{1,0:T(8,128)(2,1)S(1)}, u32[]{:S(2)}, u32[]{:S(2)}) collective-permute-start(bf16[192,512]{1,0:T(8,128)(2,1)S(1)} %get-tuple-element.81), channel_id=1, source_target_pairs={{0,4},{4,8},{8,12},{12,0},{1,5},{5,9},{9,13},{13,1},{2,6},{6,10},{... | collective-permute-start | bytes 589832 | tf_op jit(solution)/shard_map/ppermute | solution.py:232
  59.1 1.3 collective-permute-start.10
  60.4 10.1 %inner.3 = (f32[192,512]{1,0:T(8,128)S(1)}, bf16[192,512]{1,0:T(8,128)(2,1)S(1)}, bf16[192,512]{1,0:T(8,128)(2,1)S(1)}, bf16[192,512]{1,0:T(8,128)(2,1)S(1)}, bf...) custom-call(s32[14]{0:T(128)S(1)} %concatenate.3.table, ...), custom_call_target="tpu_custom_call" | custom-call | bytes 41943040 | tf_op jit(solution)/shard_map/inner/pallas_call | solution.py:237
  70.5 5.2 %collective-permute-done.9.refs_2_ = bf16[192,512]{1,0:T(8,128)(2,1)S(1)} collective-permute-done((bf16[192,512]{1,0:T(8,128)(2,1)S(1)}, bf16[192,512]{1,0:T(8,128)(2,1)S(1)}, u32[]{:S(2)}, u32[]{:S(2)}) %collective-permute-start.9) | collective-permute-done | bytes 196640 | tf_op jit(solution)/shard_map/ppermute | solution.py:232
  75.7 0.0 collective-permute-done.10.refs_3_
  75.7 1.8 %far.1 = (bf16[1,256,2048]{2,1,0:T(8,128)(2,1)S(1)}, bf16[1,256,2048]{2,1,0:T(8,128)(2,1)S(1)}) custom-call(s32[14]{0:T(128)S(1)} %concatenate.3.table, bf16[4,3,64,256]{3,2,1,0:T(8,128)(2,1)S(1)} %get-tuple-element.96.refs_0_, bf16[4,3,64,256]{3,2,1,0:T(8,128)(2,1)S(1)} %get-tuple-element.97.refs_1_, ...), custom_call_target="tpu_custom_call" | custom-call | bytes 10485760 | tf_op jit(solution)/shard_map/far/pallas_call | solution.py:237
  77.5 1.3 collective-permute-start.11
  78.7 0.1 collective-permute-start.12
  78.8 2.6 %collective-permute-done.12.got = bf16[2,2,2,64,256]{4,3,2,1,0:T(8,128)(2,1)S(1)} collective-permute-done((bf16[2,2,2,64,256]{4,3,2,1,0:T(8,128)(2,1)S(1)}, bf16[2,2,2,64,256]{4,3,2,1,0:T(8,128)(2,1)S(1)}, u32[]{:S(2)}, u32[]{:S(2)}) %collective-permute-start.12) | collective-permute-done | bytes 262176 | tf_op jit(solution)/shard_map/ppermute | solution.py:229
  81.4 0.0 collective-permute-done.11
  81.4 1.8 %home.1 = (bf16[1,256,2048]{2,1,0:T(8,128)(2,1)S(1)}, bf16[1,256,2048]{2,1,0:T(8,128)(2,1)S(1)}) custom-call(s32[14]{0:T(128)S(1)} %concatenate.3.table, bf16[4,3,64,256]{3,2,1,0:T(8,128)(2,1)S(1)} %get-tuple-element.96.refs_0_, bf16[4,3,64,256]{3,2,1,0:T(8,128)(2,1)S(1)} %get-tuple-element.97.refs_1_, ...), custom_call_target="tpu_custom_call" | custom-call | bytes 10485760 | tf_op jit(solution)/shard_map/home/pallas_call | solution.py:237
  83.2 0.4 collective-permute-start.18
  83.7 0.4 fusion.1
  84.1 0.3 collective-permute-start.16
  84.4 0.0 collective-permute-start.13
  84.5 1.3 collective-permute-start.17
  85.7 3.1 %collective-permute-start.14 = (bf16[192,512]{1,0:T(8,128)(2,1)S(1)}, bf16[192,512]{1,0:T(8,128)(2,1)S(1)}, u32[]{:S(2)}, u32[]{:S(2)}) collective-permute-start(bf16[192,512]{1,0:T(8,128)(2,1)S(1)} %get-tuple-element.105), channel_id=1, source_target_pairs={{0,8},{4,12},{8,0},{12,4},{1,9},{5,13},{9,1},{13,5},{2,10},{6,14},... | collective-permute-start | bytes 589832 | tf_op jit(solution)/shard_map/ppermute | solution.py:232
  88.9 1.6 %collective-permute-done.13.refs_5_ = bf16[192,512]{1,0:T(8,128)(2,1)S(1)} collective-permute-done((bf16[192,512]{1,0:T(8,128)(2,1)S(1)}, bf16[192,512]{1,0:T(8,128)(2,1)S(1)}, u32[]{:S(2)}, u32[]{:S(2)}) %collective-permute-start.13) | collective-permute-done | bytes 196640 | tf_op jit(solution)/shard_map/ppermute | solution.py:232
  90.4 3.2 %collective-permute-start.15 = (bf16[192,512]{1,0:T(8,128)(2,1)S(1)}, bf16[192,512]{1,0:T(8,128)(2,1)S(1)}, u32[]{:S(2)}, u32[]{:S(2)}) collective-permute-start(bf16[192,512]{1,0:T(8,128)(2,1)S(1)} %get-tuple-element.106), channel_id=1, source_target_pairs={{0,12},{4,0},{8,4},{12,8},{1,13},{5,1},{9,5},{13,9},{2,14},{6,2},{... | collective-permute-start | bytes 589832 | tf_op jit(solution)/shard_map/ppermute | solution.py:232
  93.6 7.1 %collective-permute-done.14.refs_6_ = bf16[192,512]{1,0:T(8,128)(2,1)S(1)} collective-permute-done((bf16[192,512]{1,0:T(8,128)(2,1)S(1)}, bf16[192,512]{1,0:T(8,128)(2,1)S(1)}, u32[]{:S(2)}, u32[]{:S(2)}) %collective-permute-start.14) | collective-permute-done | bytes 196640 | tf_op jit(solution)/shard_map/ppermute | solution.py:232
  100.8 4.8 %collective-permute-done.15.refs_7_ = bf16[192,512]{1,0:T(8,128)(2,1)S(1)} collective-permute-done((bf16[192,512]{1,0:T(8,128)(2,1)S(1)}, bf16[192,512]{1,0:T(8,128)(2,1)S(1)}, u32[]{:S(2)}, u32[]{:S(2)}) %collective-permute-start.15) | collective-permute-done | bytes 196640 | tf_op jit(solution)/shard_map/ppermute | solution.py:232
  105.5 8.8 %collective-permute-done.17.refs_0_ = bf16[2,2,2,64,256]{4,3,2,1,0:T(8,128)(2,1)S(1)} collective-permute-done((bf16[2,2,2,64,256]{4,3,2,1,0:T(8,128)(2,1)S(1)}, bf16[2,2,2,64,256]{4,3,2,1,0:T(8,128)(2,1)S(1)}, u32[]{:S(2)}, u32[]{:S(2)}) %collective-permute-start.17) | collective-permute-done | bytes 262176 | tf_op jit(solution)/shard_map/ppermute | solution.py:226
  114.4 0.6 sum.1.refs_0_
  115.0 0.3 collective-permute-start.19
  115.3 9.4 %collective-permute-done.19.refs_1_ = bf16[512,384]{1,0:T(8,128)(2,1)S(1)} collective-permute-done((bf16[512,384]{1,0:T(8,128)(2,1)S(1)}, bf16[512,384]{1,0:T(8,128)(2,1)S(1)}, u32[]{:S(2)}, u32[]{:S(2)}) %collective-permute-start.19) | collective-permute-done | bytes 393248 | tf_op jit(solution)/shard_map/ppermute | solution.py:226
  124.7 0.1 pad_maximum_fusion
  124.8 1.9 %collective-permute-start.20 = (bf16[2,512,384]{2,1,0:T(8,128)(2,1)S(1)}, bf16[2,512,384]{2,1,0:T(8,128)(2,1)S(1)}, u32[]{:S(2)}, u32[]{:S(2)}) collective-permute-start(bf16[2,512,384]{2,1,0:T(8,128)(2,1)S(1)} %pad_maximum_fusion), channel_id=1, source_target_pairs={{0,1},{1,0},{2,3},{3,2},{4,5},{5,4},{6,7},{7,6},{8,9},{9,8},{10,11... | collective-permute-start | bytes 2359304 | tf_op jit(solution)/shard_map/ppermute | solution.py:229
  126.7 1.6 %weights.1 = f32[2,8,64,256]{3,2,1,0:T(8,128)} custom-call(s32[14]{0:T(128)S(1)} %concatenate.3.table, bf16[2,2,2,64,256]{4,3,2,1,0:T(8,128)(2,1)S(1)} %get-tuple-element.109.stay, bf16[2,2,2,64,256]{4,3,2,1,0:T(8,128)(2,1)S(1)} %collective-permute-done.12.got, bf16[2,2,2,64,256]{4,3,2,1,0:T(8,128)(2,1)S(1)} %collective-permute-done.17.refs_0_), custom_call_target="tpu_custom_call" | custom-call | bytes 10485760 | tf_op jit(solution)/shard_map/weights/pallas_call | solution.py:237
  128.3 1.5 %fusion.2 = bf16[1,256,2048]{2,1,0:T(8,128)(2,1)} fusion(bf16[256,2048]{1,0:T(8,128)(2,1)S(1)} %collective-permute-done.16, bf16[1,256,2048]{2,1,0:T(8,128)(2,1)S(1)} %collective-permute-done.18, bf16[1,256,2048]{2,1,0:T(8,128)(2,1)S(1)} %get-tuple-element.98), kind=kLoop, calls=%fused_computation.4 | loop fusion | flops 3145728 | bytes 4194304 | tf_op jit(solution)/shard_map/broadcast_in_dim | solution.py:384
  129.8 2.5 %join.1 = f32[512,1536]{1,0:T(8,128)} custom-call(s32[14]{0:T(128)S(1)} %concatenate.3.table, bf16[512,384]{1,0:T(8,128)(2,1)S(1)} %sum.1.refs_0_, bf16[512,384]{1,0:T(8,128)(2,1)S(1)} %collective-permute-done.19.refs_1_, bf16[2,512,384]{2,1,0:T(8,128)(2,1)S(1)} %collective-permute-done.20.refs_2_), custom_call_target="tpu_custom_call" | custom-call | tf_op jit(solution)/shard_map/join/pallas_call | solution.py:237
  (24 shorter events, 0.2 us)
Async XLA Ops:
  0.6 4.6 %copy-start = (bf16[1,256,2048]{2,1,0:T(8,128)(2,1)S(1)}, bf16[1,256,2048]{2,1,0:T(8,128)(2,1)}, u32[]{:S(2)}) copy-start(bf16[1,256,2048]{2,1,0:T(8,128)(2,1)} %param.5) | copy-start | bytes 3145732
  0.8 1.5 %copy-start.1 = (bf16[512,1536]{1,0:T(8,128)(2,1)S(1)}, bf16[512,1536]{1,0:T(8,128)(2,1)}, u32[]{:S(2)}) copy-start(bf16[512,1536]{1,0:T(8,128)(2,1)} %w.1) | copy-start | bytes 4718596
  2.3 1.2 copy-start.2
  3.5 0.9 copy-start.3
  4.5 42.3 %copy-start.4 = (f32[8]{0:T(128)S(1)}, f32[8]{0:T(128)}, u32[]{:S(2)}) copy-start(f32[8]{0:T(128)} %rates.3) | copy-start | bytes 100
  5.3 4.6 %collective-permute-start = (bf16[256,2048]{1,0:T(8,128)(2,1)S(1)}, bf16[256,2048]{1,0:T(8,128)(2,1)S(1)}, u32[]{:S(2)}, u32[]{:S(2)}) collective-permute-start(bf16[256,2048]{1,0:T(8,128)(2,1)S(1)} %bitcast.18), channel_id=1, source_target_pairs={{0,1},{1,0},{2,3},{3,2},{4,5},{5,4},{6,7},{7,6},{8,9},{9,8},{10,11... | collective-permute-start | bytes 3145736 | tf_op jit(solution)/shard_map/ppermute | solution.py:229
  6.0 37.9 %collective-permute-start.5 = (bf16[256,2048]{1,0:T(8,128)(2,1)S(1)}, bf16[256,2048]{1,0:T(8,128)(2,1)S(1)}, u32[]{:S(2)}, u32[]{:S(2)}) collective-permute-start(bf16[256,2048]{1,0:T(8,128)(2,1)S(1)} %bitcast.19), channel_id=1, source_target_pairs={{0,2},{1,3},{2,0},{3,1},{4,6},{5,7},{6,4},{7,5},{8,10},{9,11},{10,... | collective-permute-start | bytes 3145736 | tf_op jit(solution)/shard_map/ppermute | solution.py:226
  7.2 2.7 %collective-permute-start.1 = (bf16[2,384,256]{2,1,0:T(8,128)(2,1)S(1)}, bf16[2,384,256]{2,1,0:T(8,128)(2,1)S(1)}, u32[]{:S(2)}, u32[]{:S(2)}) collective-permute-start(bf16[2,384,256]{2,1,0:T(8,128)(2,1)S(1)} %get-tuple-element.67), channel_id=1, source_target_pairs={{0,1},{1,0},{2,3},{3,2},{4,5},{5,4},{6,7},{7,6},{8,9},{9,8},{10,11... | collective-permute-start | bytes 1179656 | tf_op jit(solution)/shard_map/ppermute | solution.py:229
  7.6 19.5 %collective-permute-start.3 = (bf16[384,512]{1,0:T(8,128)(2,1)S(1)}, bf16[384,512]{1,0:T(8,128)(2,1)S(1)}, u32[]{:S(2)}, u32[]{:S(2)}) collective-permute-start(bf16[384,512]{1,0:T(8,128)(2,1)S(1)} %get-tuple-element.75.refs_4_.refs_2_), channel_id=1, source_target_pairs={{0,8},{4,12},{8,0},{12,4},{1,9},{5,13},{9,1},{13,5},{2,10},{6,14},... | collective-permute-start | bytes 1179656 | tf_op jit(solution)/shard_map/ppermute | solution.py:232
  9.9 34.0 %collective-permute-start.2 = (bf16[384,512]{1,0:T(8,128)(2,1)S(1)}, bf16[384,512]{1,0:T(8,128)(2,1)S(1)}, u32[]{:S(2)}, u32[]{:S(2)}) collective-permute-start(bf16[384,512]{1,0:T(8,128)(2,1)S(1)} %get-tuple-element.75.refs_4_.refs_2_), channel_id=1, source_target_pairs={{0,4},{4,8},{8,12},{12,0},{1,5},{5,9},{9,13},{13,1},{2,6},{6,10},{... | collective-permute-start | bytes 1179656 | tf_op jit(solution)/shard_map/ppermute | solution.py:232
  10.0 33.9 %collective-permute-start.6 = (bf16[2,384,256]{2,1,0:T(8,128)(2,1)S(1)}, bf16[2,384,256]{2,1,0:T(8,128)(2,1)S(1)}, u32[]{:S(2)}, u32[]{:S(2)}) collective-permute-start(bf16[2,384,256]{2,1,0:T(8,128)(2,1)S(1)} %pad_maximum_fusion.1), channel_id=1, source_target_pairs={{0,2},{1,3},{2,0},{3,1},{4,6},{5,7},{6,4},{7,5},{8,10},{9,11},{10,... | collective-permute-start | bytes 1179656 | tf_op jit(solution)/shard_map/ppermute | solution.py:226
  10.3 33.6 %collective-permute-start.4 = (bf16[384,512]{1,0:T(8,128)(2,1)S(1)}, bf16[384,512]{1,0:T(8,128)(2,1)S(1)}, u32[]{:S(2)}, u32[]{:S(2)}) collective-permute-start(bf16[384,512]{1,0:T(8,128)(2,1)S(1)} %get-tuple-element.75.refs_4_.refs_2_), channel_id=1, source_target_pairs={{0,12},{4,0},{8,4},{12,8},{1,13},{5,1},{9,5},{13,9},{2,14},{6,2},{... | collective-permute-start | bytes 1179656 | tf_op jit(solution)/shard_map/ppermute | solution.py:232
  44.0 2.8 %collective-permute-start.7 = (bf16[256,2048]{1,0:T(8,128)(2,1)S(1)}, bf16[256,2048]{1,0:T(8,128)(2,1)S(1)}, u32[]{:S(2)}, u32[]{:S(2)}) collective-permute-start(bf16[256,2048]{1,0:T(8,128)(2,1)S(1)} %collective-permute-done.5.refs_2_), channel_id=1, source_target_pairs={{0,1},{1,0},{2,3},{3,2},{4,5},{5,4},{6,7},{7,6},{8,9},{9,8},{10,11... | collective-permute-start | bytes 3145736 | tf_op jit(solution)/shard_map/ppermute | solution.py:229
  56.9 13.6 %collective-permute-start.8 = (bf16[192,512]{1,0:T(8,128)(2,1)S(1)}, bf16[192,512]{1,0:T(8,128)(2,1)S(1)}, u32[]{:S(2)}, u32[]{:S(2)}) collective-permute-start(bf16[192,512]{1,0:T(8,128)(2,1)S(1)} %get-tuple-element.81), channel_id=1, source_target_pairs={{0,4},{4,8},{8,12},{12,0},{1,5},{5,9},{9,13},{13,1},{2,6},{6,10},{... | collective-permute-start | bytes 589832 | tf_op jit(solution)/shard_map/ppermute | solution.py:232
  59.1 16.6 %collective-permute-start.9 = (bf16[192,512]{1,0:T(8,128)(2,1)S(1)}, bf16[192,512]{1,0:T(8,128)(2,1)S(1)}, u32[]{:S(2)}, u32[]{:S(2)}) collective-permute-start(bf16[192,512]{1,0:T(8,128)(2,1)S(1)} %get-tuple-element.82), channel_id=1, source_target_pairs={{0,8},{4,12},{8,0},{12,4},{1,9},{5,13},{9,1},{13,5},{2,10},{6,14},... | collective-permute-start | bytes 589832 | tf_op jit(solution)/shard_map/ppermute | solution.py:232
  59.1 16.6 %collective-permute-start.10 = (bf16[192,512]{1,0:T(8,128)(2,1)S(1)}, bf16[192,512]{1,0:T(8,128)(2,1)S(1)}, u32[]{:S(2)}, u32[]{:S(2)}) collective-permute-start(bf16[192,512]{1,0:T(8,128)(2,1)S(1)} %get-tuple-element.83), channel_id=1, source_target_pairs={{0,12},{4,0},{8,4},{12,8},{1,13},{5,1},{9,5},{13,9},{2,14},{6,2},{... | collective-permute-start | bytes 589832 | tf_op jit(solution)/shard_map/ppermute | solution.py:232
  77.5 3.9 %collective-permute-start.11 = (bf16[1,256,2048]{2,1,0:T(8,128)(2,1)S(1)}, bf16[1,256,2048]{2,1,0:T(8,128)(2,1)S(1)}, u32[]{:S(2)}, u32[]{:S(2)}) collective-permute-start(bf16[1,256,2048]{2,1,0:T(8,128)(2,1)S(1)} %get-tuple-element.94), channel_id=1, source_target_pairs={{0,1},{1,0},{2,3},{3,2},{4,5},{5,4},{6,7},{7,6},{8,9},{9,8},{10,11... | collective-permute-start | bytes 3145736 | tf_op jit(solution)/shard_map/ppermute | solution.py:229
  78.7 2.7 %collective-permute-start.12 = (bf16[2,2,2,64,256]{4,3,2,1,0:T(8,128)(2,1)S(1)}, bf16[2,2,2,64,256]{4,3,2,1,0:T(8,128)(2,1)S(1)}, u32[]{:S(2)}, u32[]{:S(2)}) collective-permute-start(bf16[2,2,2,64,256]{4,3,2,1,0:T(8,128)(2,1)S(1)} %get-tuple-element.95), channel_id=1, source_target_pairs={{0,1},{1,0},{2,3},{3,2},{4,5},{5,4},{6,7},{7,6},{8,9},{9,8},{10,11... | collective-permute-start | bytes 786440 | tf_op jit(solution)/shard_map/ppermute | solution.py:229
  83.2 31.2 %collective-permute-start.18 = (bf16[1,256,2048]{2,1,0:T(8,128)(2,1)S(1)}, bf16[1,256,2048]{2,1,0:T(8,128)(2,1)S(1)}, u32[]{:S(2)}, u32[]{:S(2)}) collective-permute-start(bf16[1,256,2048]{2,1,0:T(8,128)(2,1)S(1)} %get-tuple-element.111), channel_id=1, source_target_pairs={{0,1},{1,0},{2,3},{3,2},{4,5},{5,4},{6,7},{7,6},{8,9},{9,8},{10,11... | collective-permute-start | bytes 3145736 | tf_op jit(solution)/shard_map/ppermute | solution.py:229
  84.1 30.3 %collective-permute-start.16 = (bf16[256,2048]{1,0:T(8,128)(2,1)S(1)}, bf16[256,2048]{1,0:T(8,128)(2,1)S(1)}, u32[]{:S(2)}, u32[]{:S(2)}) collective-permute-start(bf16[256,2048]{1,0:T(8,128)(2,1)S(1)} %fusion.1), channel_id=1, source_target_pairs={{0,2},{1,3},{2,0},{3,1},{4,6},{5,7},{6,4},{7,5},{8,10},{9,11},{10,... | collective-permute-start | bytes 3145736 | tf_op jit(solution)/shard_map/ppermute | solution.py:226
  84.4 6.0 %collective-permute-start.13 = (bf16[192,512]{1,0:T(8,128)(2,1)S(1)}, bf16[192,512]{1,0:T(8,128)(2,1)S(1)}, u32[]{:S(2)}, u32[]{:S(2)}) collective-permute-start(bf16[192,512]{1,0:T(8,128)(2,1)S(1)} %get-tuple-element.104), channel_id=1, source_target_pairs={{0,4},{4,8},{8,12},{12,0},{1,5},{5,9},{9,13},{13,1},{2,6},{6,10},{... | collective-permute-start | bytes 589832 | tf_op jit(solution)/shard_map/ppermute | solution.py:232
  84.5 29.9 %collective-permute-start.17 = (bf16[2,2,2,64,256]{4,3,2,1,0:T(8,128)(2,1)S(1)}, bf16[2,2,2,64,256]{4,3,2,1,0:T(8,128)(2,1)S(1)}, u32[]{:S(2)}, u32[]{:S(2)}) collective-permute-start(bf16[2,2,2,64,256]{4,3,2,1,0:T(8,128)(2,1)S(1)} %pad_maximum_fusion.2), channel_id=1, source_target_pairs={{0,2},{1,3},{2,0},{3,1},{4,6},{5,7},{6,4},{7,5},{8,10},{9,11},{10,... | collective-permute-start | bytes 786440 | tf_op jit(solution)/shard_map/ppermute | solution.py:226
  85.7 15.0 %collective-permute-start.14 = (bf16[192,512]{1,0:T(8,128)(2,1)S(1)}, bf16[192,512]{1,0:T(8,128)(2,1)S(1)}, u32[]{:S(2)}, u32[]{:S(2)}) collective-permute-start(bf16[192,512]{1,0:T(8,128)(2,1)S(1)} %get-tuple-element.105), channel_id=1, source_target_pairs={{0,8},{4,12},{8,0},{12,4},{1,9},{5,13},{9,1},{13,5},{2,10},{6,14},... | collective-permute-start | bytes 589832 | tf_op jit(solution)/shard_map/ppermute | solution.py:232
  90.4 15.1 %collective-permute-start.15 = (bf16[192,512]{1,0:T(8,128)(2,1)S(1)}, bf16[192,512]{1,0:T(8,128)(2,1)S(1)}, u32[]{:S(2)}, u32[]{:S(2)}) collective-permute-start(bf16[192,512]{1,0:T(8,128)(2,1)S(1)} %get-tuple-element.106), channel_id=1, source_target_pairs={{0,12},{4,0},{8,4},{12,8},{1,13},{5,1},{9,5},{13,9},{2,14},{6,2},{... | collective-permute-start | bytes 589832 | tf_op jit(solution)/shard_map/ppermute | solution.py:232
  115.0 9.7 %collective-permute-start.19 = (bf16[512,384]{1,0:T(8,128)(2,1)S(1)}, bf16[512,384]{1,0:T(8,128)(2,1)S(1)}, u32[]{:S(2)}, u32[]{:S(2)}) collective-permute-start(bf16[512,384]{1,0:T(8,128)(2,1)S(1)} %sum.1.refs_0_), channel_id=1, source_target_pairs={{0,2},{1,3},{2,0},{3,1},{4,6},{5,7},{6,4},{7,5},{8,10},{9,11},{10,... | collective-permute-start | bytes 1179656 | tf_op jit(solution)/shard_map/ppermute | solution.py:226
  124.8 5.0 %collective-permute-start.20 = (bf16[2,512,384]{2,1,0:T(8,128)(2,1)S(1)}, bf16[2,512,384]{2,1,0:T(8,128)(2,1)S(1)}, u32[]{:S(2)}, u32[]{:S(2)}) collective-permute-start(bf16[2,512,384]{2,1,0:T(8,128)(2,1)S(1)} %pad_maximum_fusion), channel_id=1, source_target_pairs={{0,1},{1,0},{2,3},{3,2},{4,5},{5,4},{6,7},{7,6},{8,9},{9,8},{10,11... | collective-permute-start | bytes 2359304 | tf_op jit(solution)/shard_map/ppermute | solution.py:229

commit v4 on v3

--- a/solution.py
+++ b/solution.py
@@ -29,54 +29,55 @@
     return square, tanh, half, sech, slope
 
 
-def prep_kernel(dims, table, w, cots, start, mine, keep, send, block, turned):
+def columns_kernel(dims, table, w, *refs):
     nseg, nseq, hpd, feats, hid, tokens, chunk = dims
+    outs, block = refs[:hpd], refs[hpd]
     own = hpd * feats
-    total = own * nseg
     wide = block.shape[0]
     me = table[nseg + nseq + 1]
-    base = me * own // wide * wide
-    for part in range(3):
-        at = pl.multiple_of(part * total + base, wide)
-        block[...] = w[:, pl.ds(at, wide)].T
-        rest = pl.multiple_of(me * own - base, own)
-        mine[part * own : (part + 1) * own] = block[pl.ds(rest, own)]
+    block[...] = w[...].T
+    for head in range(hpd):
+        at = me * own % wide + head * feats
+        outs[head][...] = block[pl.ds(pl.multiple_of(at, feats), feats)]
+
+
+def packs_kernel(dims, table, cots, start, keep, send, turned):
+    nseg, nseq, hpd, feats, hid, tokens, chunk = dims
     turned[...] = cots[...].T
     for slot in range(nseg):
         dest = table[nseg + nseq + 2 + slot]
-        piece = start[:, pl.ds(dest * hpd, hpd)].astype(BF)
         pack = (keep, send)[slot % CORES]
-        pack[slot // CORES, : 2 * own] = piece.reshape(2 * own, hid)
-        pack[slot // CORES, 2 * own :] = turned[pl.ds(pl.multiple_of(dest * own, own), own)]
-
-
-def inner_kernel(dims, head, before, table, rates, *refs):
+        for head in range(hpd):
+            index = dest * hpd + head
+            for half in range(2):
+                rows = pl.ds(half * feats, feats)
+                pack[head, slot // CORES, rows] = start[half, index].astype(BF)
+            at = pl.multiple_of(index * feats, feats)
+            pack[head, slot // CORES, 2 * feats :] = turned[pl.ds(at, feats)]
+
+
+def inner_kernel(dims, head, table, rates, *refs):
     nseg, nseq, hpd, feats, hid, tokens, chunk = dims
     chips = nseg // CORES
     li, refs = refs[:nseg], refs[nseg:]
     wt, refs = refs[:nseq], refs[nseq:]
     keep, got, refs = refs[0], refs[1], refs[2:]
     hops, refs = refs[: chips - 1], refs[chips - 1 :]
-    earlier, refs = refs[:before], refs[before:]
     gp, refs = refs[:nseq], refs[nseq:]
     gq, stay, leave, qkv, wts, cts, ht, rt, g1, g2p, gu, gab = refs
-    own = hpd * feats
     rows = 3 * feats
 
     for slot in range(nseg):
         dx, dc = slot // CORES, slot % CORES
-        pack = ((keep, got)[dc].at[0]) if dx == 0 else hops[dx - 1].at[dc]
+        pack = ((keep, got)[dc].at[head, 0]) if dx == 0 else hops[dx - 1].at[dc]
         total = jnp.zeros((rows, tokens), F32)
         for back in range(nseq):
             at = pl.multiple_of(table[nseg + back] * chunk, chunk)
-            left = jnp.concatenate(
-                [wt[back][p * own + head * feats : p * own + (head + 1) * feats] for p in range(3)]
-            )
-            total += dot(left, li[slot][:, pl.ds(at, chunk)], 1, 1)
+            total += dot(wt[back][...], li[slot][:, pl.ds(at, chunk)], 1, 1)
         qkv[slot] = total.astype(BF).reshape(3, feats, tokens)
-        wts[slot, 0] = pack[head * feats : (head + 1) * feats]
-        wts[slot, 1] = pack[own + head * feats : own + (head + 1) * feats]
-        cts[slot] = pack[2 * own + head * feats : 2 * own + (head + 1) * feats]
+        wts[slot, 0] = pack[:feats]
+        wts[slot, 1] = pack[feats : 2 * feats]
+        cts[slot] = pack[2 * feats :]
     rate = rates[table[nseg + nseq] + head] * (1.0 / MB)
 
     def local(slot):
@@ -141,12 +142,7 @@
 
     for dx in range(chips):
         for dc, out in enumerate((stay, leave)):
-            if before:
-                for i in range(head):
-                    out[dx, :, i] = earlier[CORES * i + dc][dx, :, 0]
-                out[dx, :, head] = wts[dx * CORES + dc]
-            else:
-                out[dx, :, 0] = wts[dx * CORES + dc]
+            out[dx] = wts[dx * CORES + dc]
     for dz in range(nseq):
         at = pl.multiple_of(table[nseg + (nseq - dz) % nseq] * chunk, chunk)
         total = jnp.zeros((rows, chunk), F32)
@@ -157,54 +153,63 @@
 
 def input_kernel(dims, slots, table, *refs):
     nseg, nseq, hpd, feats, hid, tokens, chunk = dims
-    gq, wt, outs = refs[:hpd], refs[hpd : hpd + nseq], refs[hpd + nseq :]
-    own = hpd * feats
+    gq, wt, outs = refs[:hpd], refs[hpd : hpd + hpd * nseq], refs[hpd + hpd * nseq :]
     for i, slot in enumerate(slots):
-        left = jnp.concatenate([gq[h][slot, p] for p in range(3) for h in range(hpd)])
+        left = jnp.concatenate([gq[h][slot].reshape(3 * feats, tokens) for h in range(hpd)])
         for back in range(nseq):
             at = pl.multiple_of(table[nseg + back] * chunk, chunk)
-            value = dot(left, wt[back][...], 0, 0)
+            right = jnp.concatenate([wt[h * nseq + back][...] for h in range(hpd)])
+            value = dot(left, right, 0, 0)
             outs[slot % CORES][i // CORES, :, pl.ds(at, chunk)] = value.astype(BF)
 
 
-def sum_kernel(dims, *refs):
-    nseg, nseq, hpd, feats, hid, tokens, chunk = dims
-    out = refs[-1]
-    for head in range(hpd):
-        total = refs[head * nseq][...]
-        for ref in refs[head * nseq + 1 : (head + 1) * nseq]:
-            total += ref[...].astype(F32)
-        for part in range(3):
-            at = (part * hpd + head) * feats
-            out[:, at : at + feats] = total[part * feats : (part + 1) * feats].T.astype(BF)
+def sum_kernel(*refs):
+    total = refs[0][...]
+    for ref in refs[1:-1]:
+        total += ref[...].astype(F32)
+    total = total.T.astype(BF)
+    half = total.shape[0] // 2
+    refs[-1][...] = jnp.concatenate([total[:half], total[half:]], 1)
 
 
 def join_kernel(dims, table, *refs):
     nseg, nseq, hpd, feats, hid, tokens, chunk = dims
     chips = nseg // CORES
-    far, near, out = refs[:chips], refs[chips], refs[chips + 1]
-    own = hpd * feats
+    out = refs[-1]
+    wide = CORES * hpd * feats
+    half = chunk // 2
     me = table[nseg + nseq + 1]
     chip = me // CORES
     even = me % CORES == 0
     for dx in range(chips):
         source = (chip - dx + chips) % chips
-        for part in range(3):
-            a = far[dx][:, part * own : (part + 1) * own].astype(F32)
-            b = near[dx, :, part * own : (part + 1) * own].astype(F32)
-            left, right = jnp.where(even, a, b), jnp.where(even, b, a)
-            at = pl.multiple_of(part * nseg * own + source * CORES * own, CORES * own)
-            out[:, pl.ds(at, CORES * own)] = jnp.concatenate([left, right], 1)
-
-
-def weights_kernel(dims, table, stay, got, *refs):
+        for side in range(2):
+            mine, other = [], []
+            for head in range(hpd):
+                far, near = refs[head * (chips + 1) + dx], refs[head * (chips + 1) + chips]
+                mine.append(far[:, side * 3 * feats : (side + 1) * 3 * feats].astype(F32))
+                other.append(near[dx, :, side * 3 * feats : (side + 1) * 3 * feats].astype(F32))
+            for part in range(3):
+                cut = slice(part * feats, (part + 1) * feats)
+                a = jnp.concatenate([value[:, cut] for value in mine + other], 1)
+                b = jnp.concatenate([value[:, cut] for value in other + mine], 1)
+                at = pl.multiple_of((part * nseg * hpd * feats) + source * wide, wide)
+                rows = pl.ds(side * half, half)
+                out[rows, pl.ds(at, wide)] = jnp.where(even, a, b)
+
+
+def weights_kernel(dims, table, *refs):
     nseg, nseq, hpd = dims[:3]
-    hops, out = refs[:-1], refs[-1]
-    for slot in range(nseg):
-        dx, dc = slot // CORES, slot % CORES
-        source = table[nseg + nseq + 2 + slot]
-        piece = (stay, got)[dc][0] if dx == 0 else hops[dx - 1][dc]
-        out[:, pl.ds(source * hpd, hpd)] = piece.astype(F32)
+    chips = nseg // CORES
+    out = refs[-1]
+    for head in range(hpd):
+        stay, got, *hops = refs[head * (chips + 1) : (head + 1) * (chips + 1)]
+        for slot in range(nseg):
+            dx, dc = slot // CORES, slot % CORES
+            source = table[nseg + nseq + 2 + slot]
+            piece = (stay, got)[dc][0] if dx == 0 else hops[dx - 1][dc]
+            for half in range(2):
+                out[half, source * hpd + head] = piece[half].astype(F32)
 
 
 def per_device(layer_input, out_cot, w_proj, inner_start, rates):
@@ -252,44 +257,69 @@
     table = jnp.concatenate([slot_of, back, jnp.stack([me * hpd, me]), dest]).astype(jnp.int32)
     dims = (nseg, nseq, hpd, feats, hid, tokens, chunk)
 
-    mine, keep, send = kernel(
-        functools.partial(prep_kernel, dims),
-        "prep",
+    wide = max(own, 128)
+    mine = pl.pallas_call(
+        functools.partial(columns_kernel, dims),
+        grid_spec=pltpu.PrefetchScalarGridSpec(
+            num_scalar_prefetch=1,
+            grid=(3,),
+            in_specs=[
+                pl.BlockSpec(
+                    (chunk, wide),
+                    lambda part, table: (0, (part * nseg + table[nseg + nseq + 1]) * own // wide),
+                )
+            ],
+            out_specs=[pl.BlockSpec((feats, chunk), lambda part, table: (part, 0))] * hpd,
+            scratch_shapes=[pltpu.VMEM((wide, chunk), BF)],
+        ),
+        out_shape=[jax.ShapeDtypeStruct((3 * feats, chunk), BF)] * hpd,
+        compiler_params=pltpu.CompilerParams(vmem_limit_bytes=8 * MIB),
+        cost_estimate=pl.CostEstimate(flops=0, bytes_accessed=0, transcendentals=0),
+        name="columns",
+    )(table, w_proj)
+    mine, after = barrier((mine, table))
+    keep, send = kernel(
+        functools.partial(packs_kernel, dims),
+        "packs",
         16,
         0,
-        [((3 * own, chunk), BF)] + [((chips, 3 * own, tokens), BF)] * CORES,
-        [((max(own, 128), chunk), BF), ((heads * feats, tokens), BF)],
-        table,
-        w_proj,
+        [((hpd, chips, 3 * feats, tokens), BF)] * CORES,
+        [((heads * feats, tokens), BF)],
+        after,
         out_cot[0],
         inner_start[0, 0],
     )
-    rows, mine, keep, send = barrier((rows, mine, keep, send))
     far = [to_chip(rows, dx) for dx in range(1, chips)]
     near = to_core(rows)
     got = to_core(send)
-    wt = [to_seq(mine, dz) for dz in range(1, nseq - 1)]
+    wt = [[block] for block in mine]
+    wt[0] += [to_seq(mine[0], dz) for dz in range(1, nseq - 1)]
     near, got, keep, mine = barrier((near, got, keep, mine))
-    wt = [mine] + wt + [to_seq(mine, nseq - 1)]
-    hops = [to_chip(jnp.stack([keep[dx], got[dx]]), dx) for dx in range(1, chips)]
-    wt, far, hops = barrier((wt, far, hops))
+    wt[0] += [to_seq(mine[0], nseq - 1)]
+
+    def pack_hops(head):
+        return [
+            to_chip(jnp.stack([keep[head, dx], got[head, dx]]), dx) for dx in range(1, chips)
+        ]
+
+    hops = [pack_hops(0)]
+    wt[0], far, hops, mine, keep, got = barrier((wt[0], far, hops, mine, keep, got))
     li = [rows, near]
     for value in far:
         li += [value, to_core(value)]
-
-    pieces, grads, inners = [], [], []
-    for head in range(hpd):
-        last = head == hpd - 1
-        before = len(inners) if last else 0
-        sent = hpd if last else 1
+    for head in range(1, hpd):
+        wt[head] += [to_seq(mine[head], dz) for dz in range(1, nseq)]
+        hops.append(pack_hops(head))
+
+    def inner(head):
         outs = kernel(
-            functools.partial(inner_kernel, dims, head, before),
+            functools.partial(inner_kernel, dims, head),
             "inner",
             36,
             40 * MIB,
             [((3 * feats, chunk), BF if dz else F32) for dz in range(nseq)]
             + [((nseg, 3, feats, tokens), BF)]
-            + [((chips, 2, sent, feats, hid), BF)] * CORES,
+            + [((chips, 2, feats, hid), BF)] * CORES,
             [
                 ((nseg, 3, feats, tokens), BF),
                 ((nseg, 2, feats, hid), BF),
@@ -304,22 +334,41 @@
             table,
             rates,
             *li,
-            *wt,
+            *wt[head],
             keep,
             got,
-            *hops,
-            *(inners if last else []),
+            *hops[head],
         )
-        gp = outs[:nseq]
-        grads.append(outs[nseq])
-        inners += outs[nseq + 1 :]
-        if pieces:
-            pieces, gp, grads = barrier((pieces, gp, grads))
-        pieces += [gp[0]] + [to_seq(gp[dz], dz) for dz in range(1, nseq)]
-
-    stay, leave = inners[-CORES:]
-    two = range(nseg)[:CORES]
-    rest = range(nseg)[CORES:]
+        return outs[:nseq], outs[nseq], outs[nseq + 1], outs[nseq + 2]
+
+    def to_rows(gp):
+        return [gp[0]] + [to_seq(gp[dz], dz) for dz in range(1, nseq)]
+
+    def summed(head, pieces):
+        return kernel(sum_kernel, "sum", 12, 0, [((chunk // 2, 6 * feats), BF)], [], *pieces)[0]
+
+    def to_owner(stay, leave):
+        return [to_chip(jnp.stack([stay[dx], leave[dx]]), -dx) for dx in range(1, chips)]
+
+    grads, projs, inners = [], [], []
+    for head in range(hpd):
+        gp, gq, stay, leave = inner(head)
+        grads.append(gq)
+        if head < hpd - 1:
+            gp, leave, wt[head + 1], hops[head + 1] = barrier(
+                (gp, leave, wt[head + 1], hops[head + 1])
+            )
+            pieces = to_rows(gp)
+            leave = to_core(leave)
+            backs = to_owner(stay, leave)
+        if head > 0:
+            gp, grads, stay, leave, pieces, backs = barrier(
+                (gp, grads, stay, leave, pieces, backs)
+            )
+            total = summed(head - 1, pieces)
+            projs.append([total] + [to_chip(total, dx) for dx in range(1, chips)])
+            inners += [inners_stay, inners_leave, *backs]
+        inners_stay, inners_leave = stay, leave
 
     def partial_input(name, limit, slots, grads):
         return kernel(
@@ -331,33 +380,26 @@
             [],
             table,
             *grads,
-            *wt,
+            *[block for blocks in wt for block in blocks],
         )
 
-    out, cross = partial_input("far", 16, rest, grads)
+    out, cross = partial_input("far", 20, range(nseg)[CORES:], grads)
     cross, leave = to_core(cross), to_core(leave)
-    cross, leave, grads = barrier((cross, leave, grads))
+    cross, leave, grads, projs, gp = barrier((cross, leave, grads, projs, gp))
     out = (out.astype(F32) + cross.astype(F32)).astype(BF)
-    hops = [to_chip(out[dx - 1], -dx) for dx in range(1, chips)]
-    backs = [to_chip(jnp.stack([stay[dx], leave[dx]]), -dx) for dx in range(1, chips)]
-    home, aside = partial_input("home", 16, two, grads)
+    arrived = [to_chip(out[dx - 1], -dx) for dx in range(1, chips)]
+    pieces = to_rows(gp)
+    home, aside = partial_input("home", 20, range(CORES), grads)
     aside = to_core(aside)
-    pieces, hops, backs, aside = barrier((pieces, hops, backs, aside))
+    backs = to_owner(stay, leave)
+
+    total = summed(hpd - 1, pieces)
+    projs.append([total] + [to_chip(total, dx) for dx in range(1, chips)])
+    projs, arrived, aside, backs = barrier((projs, arrived, aside, backs))
+    projs = [value for far in projs for value in [*far, to_core(jnp.stack(far))]]
     grad_input = home[0].astype(F32) + aside[0].astype(F32)
-    for hop in hops:
-        grad_input += hop.astype(F32)
-
-    (total,) = kernel(
-        functools.partial(sum_kernel, dims),
-        "sum",
-        12,
-        0,
-        [((chunk, 3 * own), BF)],
-        [],
-        *pieces,
-    )
-    far = [total] + [to_chip(total, dx) for dx in range(1, chips)]
-    near = to_core(jnp.stack(far))
+    for value in arrived:
+        grad_input += value.astype(F32)
     (grad_inner,) = kernel(
         functools.partial(weights_kernel, dims),
         "weights",
@@ -366,6 +408,7 @@
         [((2, heads, feats, hid), F32)],
         [],
         table,
+        *inners,
         stay,
         leave,
         *backs,
@@ -378,8 +421,7 @@
         [((chunk, 3 * heads * feats), F32)],
         [],
         table,
-        *far,
-        near,
+        *projs,
     )
     return (grad_input.astype(BF)[None], grad_proj, grad_inner[None, None])
 

time: 133 us -> 131 us (0.985)
  waiting for transfers between devices: 74 us -> 66.3 us
  starting transfers between devices: 22.3 us -> 26.9 us
    ppermute x9 -> x12, waiting for transfers between devices: 50.9 us -> 42.6 us  [to_seq(): lax.ppermute(value, 'seq', [(i, (i + dz) % nseq) for i in range(nseq)])]
    ppermute x5 -> x8, waiting for transfers between devices: 18.3 us -> 22 us  [to_chip(): return lax.ppermute(value, 'seg', pairs)]
    ppermute x7 -> x9, waiting for transfers between devices: 4.88 us -> 1.62 us  [to_core(): return lax.ppermute(value, 'seg', [(i, i ^ 1) for i in range(nseg)])]
    ppermute x5 -> x8, starting transfers between devices: 3.46 us -> 5.36 us  [to_chip(): return lax.ppermute(value, 'seg', pairs)]
    ppermute x9 -> x12, starting transfers between devices: 13.6 us -> 15.2 us  [to_seq(): lax.ppermute(value, 'seq', [(i, (i + dz) % nseq) for i in range(nseq)])]
    ppermute x7 -> x9, starting transfers between devices: 5.34 us -> 6.3 us  [to_core(): return lax.ppermute(value, 'seg', [(i, i ^ 1) for i in range(nseg)])]
    pallas_call x8 -> x9, Pallas kernels: 29.2 us -> 29.5 us  [kernel(): pl.pallas_call(body, in_specs=[smem if o.ndim == 1 else vmem for o in ope...]
  transfers between devices with their start and end apart: 21 -> 29, of which waited for: 10 -> 14; matrix products, arithmetic and copies ran while one was open for 2% -> 2% of each run, Pallas kernels for 9% -> 18%
where the time goes in v4:
time: 131 us; the launch traced here: 130 us
  waiting for transfers between devices  66.3 us (51%)
  Pallas kernels  30.5 us (23%)
  starting transfers between devices  26.9 us (21%)
  local copies, waits for them, and re-layouts  3.73 us (3%)
  other arithmetic  2.09 us (2%)
    ppermute x12, waiting for transfers between devices, to_seq(): lax.ppermute(value, 'seq', [(i, (i + dz) % nseq) for i in range(nseq)])  42.6 us
    pallas_call x9, Pallas kernels, kernel(): pl.pallas_call(body, in_specs=[smem if o.ndim == 1 else vmem for o in ope...  29.5 us
    ppermute x8, waiting for transfers between devices, to_chip(): return lax.ppermute(value, 'seg', pairs)  22 us
    ppermute x12, starting transfers between devices, to_seq(): lax.ppermute(value, 'seq', [(i, (i + dz) % nseq) for i in range(nseq)])  15.2 us
    ppermute x9, starting transfers between devices, to_core(): return lax.ppermute(value, 'seg', [(i, i ^ 1) for i in range(nseg)])  6.3 us
    ppermute x8, starting transfers between devices, to_chip(): return lax.ppermute(value, 'seg', pairs)  5.36 us
    unnamed x10, local copies, waits for them, and re-layouts  3.59 us
  transfers between devices with their start and end apart: 29, of which 14 were waited for; matrix products, arithmetic and copies ran while one was open for 2% of the time, Pallas kernels for 18%

profile of v4, /device:TPU:9, one launch (start us, length us, event | category | flops | bytes accessed | tf_op | source)
XLA Modules:
  0.0 130.4 jit_solution(13911137977194988415)
XLA Ops:
  0.6 0.7 collective-permute-start
  1.5 1.4 %copy-done.1 = bf16[512,1536]{1,0:T(8,128)(2,1)S(1)} copy-done((bf16[512,1536]{1,0:T(8,128)(2,1)S(1)}, bf16[512,1536]{1,0:T(8,128)(2,1)}, u32[]{:S(2)}) %copy-start.1) | copy-done | bytes 1572888
  2.9 1.1 columns.1
  4.0 1.2 copy-done.2
  5.2 0.9 copy-done.3
  6.1 0.7 packs.1
  7.0 1.2 collective-permute-start.5
  8.2 2.3 %collective-permute-start.3 = (bf16[192,512]{1,0:T(8,128)(2,1)S(1)}, bf16[192,512]{1,0:T(8,128)(2,1)S(1)}, u32[]{:S(2)}, u32[]{:S(2)}) collective-permute-start(bf16[192,512]{1,0:T(8,128)(2,1)S(1)} %get-tuple-element.95.refs_4_.refs_2_), channel_id=1, source_target_pairs={{0,8},{4,12},{8,0},{12,4},{1,9},{5,13},{9,1},{13,5},{2,10},{6,14},... | collective-permute-start | bytes 589832 | tf_op jit(solution)/shard_map/ppermute | solution.py:237
  10.6 0.3 collective-permute-start.6
  10.9 1.5 %collective-permute-start.4 = (bf16[192,512]{1,0:T(8,128)(2,1)S(1)}, bf16[192,512]{1,0:T(8,128)(2,1)S(1)}, u32[]{:S(2)}, u32[]{:S(2)}) collective-permute-start(bf16[192,512]{1,0:T(8,128)(2,1)S(1)} %get-tuple-element.95.refs_4_.refs_2_), channel_id=1, source_target_pairs={{0,12},{4,0},{8,4},{12,8},{1,13},{5,1},{9,5},{13,9},{2,14},{6,2},{... | collective-permute-start | bytes 589832 | tf_op jit(solution)/shard_map/ppermute | solution.py:237
  12.4 7.4 %collective-permute-done.3.refs_6_.refs_4_ = bf16[192,512]{1,0:T(8,128)(2,1)S(1)} collective-permute-done((bf16[192,512]{1,0:T(8,128)(2,1)S(1)}, bf16[192,512]{1,0:T(8,128)(2,1)S(1)}, u32[]{:S(2)}, u32[]{:S(2)}) %collective-permute-start.3) | collective-permute-done | bytes 196640 | tf_op jit(solution)/shard_map/ppermute | solution.py:237
  19.8 7.9 %collective-permute-done.2.refs_5_.refs_3_ = bf16[192,512]{1,0:T(8,128)(2,1)S(1)} collective-permute-done((bf16[192,512]{1,0:T(8,128)(2,1)S(1)}, bf16[192,512]{1,0:T(8,128)(2,1)S(1)}, u32[]{:S(2)}, u32[]{:S(2)}) %collective-permute-start.2) | collective-permute-done | bytes 196640 | tf_op jit(solution)/shard_map/ppermute | solution.py:237
  27.7 3.7 %collective-permute-done.5.refs_2_ = bf16[256,2048]{1,0:T(8,128)(2,1)S(1)} collective-permute-done((bf16[256,2048]{1,0:T(8,128)(2,1)S(1)}, bf16[256,2048]{1,0:T(8,128)(2,1)S(1)}, u32[]{:S(2)}, u32[]{:S(2)}) %collective-permute-start.5) | collective-permute-done | bytes 1048608 | tf_op jit(solution)/shard_map/ppermute | solution.py:231
  31.4 4.2 %collective-permute-done.6.refs_10_ = bf16[2,192,256]{2,1,0:T(8,128)(2,1)S(1)} collective-permute-done((bf16[2,192,256]{2,1,0:T(8,128)(2,1)S(1)}, bf16[2,192,256]{2,1,0:T(8,128)(2,1)S(1)}, u32[]{:S(2)}, u32[]{:S(2)}) %collective-permute-start.6) | collective-permute-done | bytes 196640 | tf_op jit(solution)/shard_map/ppermute | solution.py:231
  35.6 1.2 collective-permute-start.7
  36.9 1.3 collective-permute-start.11
  38.3 2.3 %collective-permute-start.9 = (bf16[192,512]{1,0:T(8,128)(2,1)S(1)}, bf16[192,512]{1,0:T(8,128)(2,1)S(1)}, u32[]{:S(2)}, u32[]{:S(2)}) collective-permute-start(bf16[192,512]{1,0:T(8,128)(2,1)S(1)} %get-tuple-element.108.refs_4_.refs_6_), channel_id=1, source_target_pairs={{0,8},{4,12},{8,0},{12,4},{1,9},{5,13},{9,1},{13,5},{2,10},{6,14},... | collective-permute-start | bytes 589832 | tf_op jit(solution)/shard_map/ppermute | solution.py:237
  40.6 2.2 %collective-permute-start.8 = (bf16[192,512]{1,0:T(8,128)(2,1)S(1)}, bf16[192,512]{1,0:T(8,128)(2,1)S(1)}, u32[]{:S(2)}, u32[]{:S(2)}) collective-permute-start(bf16[192,512]{1,0:T(8,128)(2,1)S(1)} %get-tuple-element.108.refs_4_.refs_6_), channel_id=1, source_target_pairs={{0,4},{4,8},{8,12},{12,0},{1,5},{5,9},{9,13},{13,1},{2,6},{6,10},{... | collective-permute-start | bytes 589832 | tf_op jit(solution)/shard_map/ppermute | solution.py:237
  42.8 10.1 %inner.2 = (f32[192,512]{1,0:T(8,128)S(1)}, bf16[192,512]{1,0:T(8,128)(2,1)S(1)}, bf16[192,512]{1,0:T(8,128)(2,1)S(1)}, bf16[192,512]{1,0:T(8,128)(2,1)S(1)}, bf...) custom-call(s32[14]{0:T(128)S(1)} %concatenate.3.table, ...), custom_call_target="tpu_custom_call" | custom-call | bytes 41943040 | tf_op jit(solution)/shard_map/inner/pallas_call | solution.py:242
  53.0 4.2 %collective-permute-done.8.refs_5_.refs_7_ = bf16[192,512]{1,0:T(8,128)(2,1)S(1)} collective-permute-done((bf16[192,512]{1,0:T(8,128)(2,1)S(1)}, bf16[192,512]{1,0:T(8,128)(2,1)S(1)}, u32[]{:S(2)}, u32[]{:S(2)}) %collective-permute-start.8) | collective-permute-done | bytes 196640 | tf_op jit(solution)/shard_map/ppermute | solution.py:237
  57.2 1.2 collective-permute-start.15
  58.4 2.2 %collective-permute-start.12 = (bf16[192,512]{1,0:T(8,128)(2,1)S(1)}, bf16[192,512]{1,0:T(8,128)(2,1)S(1)}, u32[]{:S(2)}, u32[]{:S(2)}) collective-permute-start(bf16[192,512]{1,0:T(8,128)(2,1)S(1)} %get-tuple-element.122), channel_id=1, source_target_pairs={{0,4},{4,8},{8,12},{12,0},{1,5},{5,9},{9,13},{13,1},{2,6},{6,10},{... | collective-permute-start | bytes 589832 | tf_op jit(solution)/shard_map/ppermute | solution.py:237
  60.6 0.7 collective-permute-start.13
  61.4 0.5 collective-permute-start.14
  61.9 0.3 collective-permute-start.16
  62.2 10.1 %inner.3 = (f32[192,512]{1,0:T(8,128)S(1)}, bf16[192,512]{1,0:T(8,128)(2,1)S(1)}, bf16[192,512]{1,0:T(8,128)(2,1)S(1)}, bf16[192,512]{1,0:T(8,128)(2,1)S(1)}, bf...) custom-call(s32[14]{0:T(128)S(1)} %concatenate.3.table, ...), custom_call_target="tpu_custom_call" | custom-call | bytes 41943040 | tf_op jit(solution)/shard_map/inner/pallas_call | solution.py:242
  72.3 0.9 collective-permute-done.12.refs_1_
  73.2 4.4 %collective-permute-done.13.refs_2_ = bf16[192,512]{1,0:T(8,128)(2,1)S(1)} collective-permute-done((bf16[192,512]{1,0:T(8,128)(2,1)S(1)}, bf16[192,512]{1,0:T(8,128)(2,1)S(1)}, u32[]{:S(2)}, u32[]{:S(2)}) %collective-permute-start.13) | collective-permute-done | bytes 196640 | tf_op jit(solution)/shard_map/ppermute | solution.py:237
  77.5 1.3 %collective-permute-done.14.refs_3_ = bf16[192,512]{1,0:T(8,128)(2,1)S(1)} collective-permute-done((bf16[192,512]{1,0:T(8,128)(2,1)S(1)}, bf16[192,512]{1,0:T(8,128)(2,1)S(1)}, u32[]{:S(2)}, u32[]{:S(2)}) %collective-permute-start.14) | collective-permute-done | bytes 196640 | tf_op jit(solution)/shard_map/ppermute | solution.py:237
  78.9 1.8 %far.1 = (bf16[1,256,2048]{2,1,0:T(8,128)(2,1)S(1)}, bf16[1,256,2048]{2,1,0:T(8,128)(2,1)S(1)}) custom-call(s32[14]{0:T(128)S(1)} %concatenate.3.table, bf16[4,3,64,256]{3,2,1,0:T(8,128)(2,1)S(1)} %get-tuple-element.139.refs_0_, bf16[4,3,64,256]{3,2,1,0:T(8,128)(2,1)S(1)} %get-tuple-element.140.refs_1_, ...), custom_call_target="tpu_custom_call" | custom-call | bytes 10485760 | tf_op jit(solution)/shard_map/far/pallas_call | solution.py:242
  80.7 0.8 collective-permute-start.17
  82.4 1.6 %collective-permute-done.18.refs_4_ = bf16[2,2,64,256]{3,2,1,0:T(8,128)(2,1)S(1)} collective-permute-done((bf16[2,2,64,256]{3,2,1,0:T(8,128)(2,1)S(1)}, bf16[2,2,64,256]{3,2,1,0:T(8,128)(2,1)S(1)}, u32[]{:S(2)}, u32[]{:S(2)}) %collective-permute-start.18) | collective-permute-done | bytes 131104 | tf_op jit(solution)/shard_map/ppermute | solution.py:234
  84.0 4.4 %collective-permute-done.19.refs_1_ = bf16[256,384]{1,0:T(8,128)(2,1)S(1)} collective-permute-done((bf16[256,384]{1,0:T(8,128)(2,1)S(1)}, bf16[256,384]{1,0:T(8,128)(2,1)S(1)}, u32[]{:S(2)}, u32[]{:S(2)}) %collective-permute-start.19) | collective-permute-done | bytes 196640 | tf_op jit(solution)/shard_map/ppermute | solution.py:231
  88.3 1.8 %home.1 = (bf16[1,256,2048]{2,1,0:T(8,128)(2,1)S(1)}, bf16[1,256,2048]{2,1,0:T(8,128)(2,1)S(1)}) custom-call(s32[14]{0:T(128)S(1)} %concatenate.3.table, bf16[4,3,64,256]{3,2,1,0:T(8,128)(2,1)S(1)} %get-tuple-element.139.refs_0_, bf16[4,3,64,256]{3,2,1,0:T(8,128)(2,1)S(1)} %get-tuple-element.140.refs_1_, ...), custom_call_target="tpu_custom_call" | custom-call | bytes 10485760 | tf_op jit(solution)/shard_map/home/pallas_call | solution.py:242
  90.2 0.9 collective-permute-start.25
  91.0 0.4 fusion.1
  91.8 1.9 %collective-permute-start.21 = (bf16[192,512]{1,0:T(8,128)(2,1)S(1)}, bf16[192,512]{1,0:T(8,128)(2,1)S(1)}, u32[]{:S(2)}, u32[]{:S(2)}) collective-permute-start(bf16[192,512]{1,0:T(8,128)(2,1)S(1)} %get-tuple-element.146), channel_id=1, source_target_pairs={{0,8},{4,12},{8,0},{12,4},{1,9},{5,13},{9,1},{13,5},{2,10},{6,14},... | collective-permute-start | bytes 589832 | tf_op jit(solution)/shard_map/ppermute | solution.py:237
  93.6 1.5 %collective-permute-start.22 = (bf16[192,512]{1,0:T(8,128)(2,1)S(1)}, bf16[192,512]{1,0:T(8,128)(2,1)S(1)}, u32[]{:S(2)}, u32[]{:S(2)}) collective-permute-start(bf16[192,512]{1,0:T(8,128)(2,1)S(1)} %get-tuple-element.147), channel_id=1, source_target_pairs={{0,12},{4,0},{8,4},{12,8},{1,13},{5,1},{9,5},{13,9},{2,14},{6,2},{... | collective-permute-start | bytes 589832 | tf_op jit(solution)/shard_map/ppermute | solution.py:237
  95.1 2.8 %collective-permute-done.20.refs_1_ = bf16[192,512]{1,0:T(8,128)(2,1)S(1)} collective-permute-done((bf16[192,512]{1,0:T(8,128)(2,1)S(1)}, bf16[192,512]{1,0:T(8,128)(2,1)S(1)}, u32[]{:S(2)}, u32[]{:S(2)}) %collective-permute-start.20) | collective-permute-done | bytes 196640 | tf_op jit(solution)/shard_map/ppermute | solution.py:237
  98.0 10.8 %collective-permute-done.21.refs_2_ = bf16[192,512]{1,0:T(8,128)(2,1)S(1)} collective-permute-done((bf16[192,512]{1,0:T(8,128)(2,1)S(1)}, bf16[192,512]{1,0:T(8,128)(2,1)S(1)}, u32[]{:S(2)}, u32[]{:S(2)}) %collective-permute-start.21) | collective-permute-done | bytes 196640 | tf_op jit(solution)/shard_map/ppermute | solution.py:237
  108.7 3.0 %collective-permute-done.22.refs_3_ = bf16[192,512]{1,0:T(8,128)(2,1)S(1)} collective-permute-done((bf16[192,512]{1,0:T(8,128)(2,1)S(1)}, bf16[192,512]{1,0:T(8,128)(2,1)S(1)}, u32[]{:S(2)}, u32[]{:S(2)}) %collective-permute-start.22) | collective-permute-done | bytes 196640 | tf_op jit(solution)/shard_map/ppermute | solution.py:237
  111.9 1.3 collective-permute-start.23
  113.2 0.3 collective-permute-start.26
  113.6 9.8 %collective-permute-done.26.refs_5_ = bf16[2,2,64,256]{3,2,1,0:T(8,128)(2,1)S(1)} collective-permute-done((bf16[2,2,64,256]{3,2,1,0:T(8,128)(2,1)S(1)}, bf16[2,2,64,256]{3,2,1,0:T(8,128)(2,1)S(1)}, u32[]{:S(2)}, u32[]{:S(2)}) %collective-permute-start.26) | collective-permute-done | bytes 131104 | tf_op jit(solution)/shard_map/ppermute | solution.py:231
  123.4 0.9 collective-permute-start.27
  124.4 1.6 %weights.1 = f32[2,8,64,256]{3,2,1,0:T(8,128)} custom-call(s32[14]{0:T(128)S(1)} %concatenate.3.table, bf16[2,2,64,256]{3,2,1,0:T(8,128)(2,1)S(1)} %get-tuple-element.125.refs_0_, bf16[2,2,64,256]{3,2,1,0:T(8,128)(2,1)S(1)} %collective-permute-done.15.refs_1_, bf16[2,2,64,256]{3,2,1,0:T(8,128)(2,1)S(1)} %collective-permute-done.16.refs_2_, ...), custom_call_target="tpu_custom_call" | custom-call | bytes 10485760 | tf_op jit(solution)/shard_map/weights/pallas_call | solution.py:242
  126.0 1.5 %fusion.2 = bf16[1,256,2048]{2,1,0:T(8,128)(2,1)} fusion(bf16[256,2048]{1,0:T(8,128)(2,1)S(1)} %collective-permute-done.24, bf16[1,256,2048]{2,1,0:T(8,128)(2,1)S(1)} %collective-permute-done.25, bf16[1,256,2048]{2,1,0:T(8,128)(2,1)S(1)} %get-tuple-element.141), kind=kLoop, calls=%fused_computation.4 | loop fusion | flops 3145728 | bytes 4194304 | tf_op jit(solution)/shard_map/broadcast_in_dim | solution.py:426
  127.5 2.9 %join.1 = f32[512,1536]{1,0:T(8,128)} custom-call(s32[14]{0:T(128)S(1)} %concatenate.3.table, bf16[256,384]{1,0:T(8,128)(2,1)S(1)} %sum.2.refs_0_, bf16[256,384]{1,0:T(8,128)(2,1)S(1)} %collective-permute-done.19.refs_1_, bf16[2,256,384]{2,1,0:T(8,128)(2,1)S(1)} %collective-permute-done.27.refs_2_, bf16[256,384]{1,0:T(8,128)(2,1)S(1)} %sum.3.refs_3_, ...), custom_call_target="tpu_custom_call" | custom-call | tf_op jit(solution)/shard_map/join/pallas_call | solution.py:242
  (49 shorter events, 2.3 us)
Async XLA Ops:
  0.6 6.4 %copy-start = (bf16[1,256,2048]{2,1,0:T(8,128)(2,1)S(1)}, bf16[1,256,2048]{2,1,0:T(8,128)(2,1)}, u32[]{:S(2)}) copy-start(bf16[1,256,2048]{2,1,0:T(8,128)(2,1)} %param.5) | copy-start | bytes 3145732
  0.6 9.9 %collective-permute-start = (bf16[256,2048]{1,0:T(8,128)(2,1)}, bf16[256,2048]{1,0:T(8,128)(2,1)S(1)}, u32[]{:S(2)}, u32[]{:S(2)}) collective-permute-start(bf16[256,2048]{1,0:T(8,128)(2,1)} %bitcast.28), channel_id=1, source_target_pairs={{0,1},{1,0},{2,3},{3,2},{4,5},{5,4},{6,7},{7,6},{8,9},{9,8},{10,11... | collective-permute-start | bytes 3145736 | tf_op jit(solution)/shard_map/ppermute | solution.py:234
  1.5 1.4 %copy-start.1 = (bf16[512,1536]{1,0:T(8,128)(2,1)S(1)}, bf16[512,1536]{1,0:T(8,128)(2,1)}, u32[]{:S(2)}) copy-start(bf16[512,1536]{1,0:T(8,128)(2,1)} %w.1) | copy-start | bytes 4718596
  2.9 39.9 %copy-start.4 = (f32[8]{0:T(128)S(1)}, f32[8]{0:T(128)}, u32[]{:S(2)}) copy-start(f32[8]{0:T(128)} %rates.3) | copy-start | bytes 100
  4.0 1.2 copy-start.2
  5.2 0.9 copy-start.3
  6.8 3.7 %collective-permute-start.1 = (bf16[2,2,192,256]{3,2,1,0:T(8,128)(2,1)S(1)}, bf16[2,2,192,256]{3,2,1,0:T(8,128)(2,1)S(1)}, u32[]{:S(2)}, u32[]{:S(2)}) collective-permute-start(bf16[2,2,192,256]{3,2,1,0:T(8,128)(2,1)S(1)} %get-tuple-element.85), channel_id=1, source_target_pairs={{0,1},{1,0},{2,3},{3,2},{4,5},{5,4},{6,7},{7,6},{8,9},{9,8},{10,11... | collective-permute-start | bytes 1179656 | tf_op jit(solution)/shard_map/ppermute | solution.py:234
  7.0 24.4 %collective-permute-start.5 = (bf16[256,2048]{1,0:T(8,128)(2,1)S(1)}, bf16[256,2048]{1,0:T(8,128)(2,1)S(1)}, u32[]{:S(2)}, u32[]{:S(2)}) collective-permute-start(bf16[256,2048]{1,0:T(8,128)(2,1)S(1)} %bitcast.29), channel_id=1, source_target_pairs={{0,2},{1,3},{2,0},{3,1},{4,6},{5,7},{6,4},{7,5},{8,10},{9,11},{10,... | collective-permute-start | bytes 3145736 | tf_op jit(solution)/shard_map/ppermute | solution.py:231
  8.2 11.5 %collective-permute-start.3 = (bf16[192,512]{1,0:T(8,128)(2,1)S(1)}, bf16[192,512]{1,0:T(8,128)(2,1)S(1)}, u32[]{:S(2)}, u32[]{:S(2)}) collective-permute-start(bf16[192,512]{1,0:T(8,128)(2,1)S(1)} %get-tuple-element.95.refs_4_.refs_2_), channel_id=1, source_target_pairs={{0,8},{4,12},{8,0},{12,4},{1,9},{5,13},{9,1},{13,5},{2,10},{6,14},... | collective-permute-start | bytes 589832 | tf_op jit(solution)/shard_map/ppermute | solution.py:237
  10.5 17.1 %collective-permute-start.2 = (bf16[192,512]{1,0:T(8,128)(2,1)S(1)}, bf16[192,512]{1,0:T(8,128)(2,1)S(1)}, u32[]{:S(2)}, u32[]{:S(2)}) collective-permute-start(bf16[192,512]{1,0:T(8,128)(2,1)S(1)} %get-tuple-element.95.refs_4_.refs_2_), channel_id=1, source_target_pairs={{0,4},{4,8},{8,12},{12,0},{1,5},{5,9},{9,13},{13,1},{2,6},{6,10},{... | collective-permute-start | bytes 589832 | tf_op jit(solution)/shard_map/ppermute | solution.py:237
  10.6 25.0 %collective-permute-start.6 = (bf16[2,192,256]{2,1,0:T(8,128)(2,1)S(1)}, bf16[2,192,256]{2,1,0:T(8,128)(2,1)S(1)}, u32[]{:S(2)}, u32[]{:S(2)}) collective-permute-start(bf16[2,192,256]{2,1,0:T(8,128)(2,1)S(1)} %pad_maximum_fusion.2), channel_id=1, source_target_pairs={{0,2},{1,3},{2,0},{3,1},{4,6},{5,7},{6,4},{7,5},{8,10},{9,11},{10,... | collective-permute-start | bytes 589832 | tf_op jit(solution)/shard_map/ppermute | solution.py:231
  10.9 24.7 %collective-permute-start.4 = (bf16[192,512]{1,0:T(8,128)(2,1)S(1)}, bf16[192,512]{1,0:T(8,128)(2,1)S(1)}, u32[]{:S(2)}, u32[]{:S(2)}) collective-permute-start(bf16[192,512]{1,0:T(8,128)(2,1)S(1)} %get-tuple-element.95.refs_4_.refs_2_), channel_id=1, source_target_pairs={{0,12},{4,0},{8,4},{12,8},{1,13},{5,1},{9,5},{13,9},{2,14},{6,2},{... | collective-permute-start | bytes 589832 | tf_op jit(solution)/shard_map/ppermute | solution.py:237
  35.6 7.2 %collective-permute-start.7 = (bf16[256,2048]{1,0:T(8,128)(2,1)S(1)}, bf16[256,2048]{1,0:T(8,128)(2,1)S(1)}, u32[]{:S(2)}, u32[]{:S(2)}) collective-permute-start(bf16[256,2048]{1,0:T(8,128)(2,1)S(1)} %collective-permute-done.5.refs_2_), channel_id=1, source_target_pairs={{0,1},{1,0},{2,3},{3,2},{4,5},{5,4},{6,7},{7,6},{8,9},{9,8},{10,11... | collective-permute-start | bytes 3145736 | tf_op jit(solution)/shard_map/ppermute | solution.py:234
  36.9 16.1 %collective-permute-start.11 = (bf16[2,192,256]{2,1,0:T(8,128)(2,1)S(1)}, bf16[2,192,256]{2,1,0:T(8,128)(2,1)S(1)}, u32[]{:S(2)}, u32[]{:S(2)}) collective-permute-start(bf16[2,192,256]{2,1,0:T(8,128)(2,1)S(1)} %pad_maximum_fusion.3), channel_id=1, source_target_pairs={{0,2},{1,3},{2,0},{3,1},{4,6},{5,7},{6,4},{7,5},{8,10},{9,11},{10,... | collective-permute-start | bytes 589832 | tf_op jit(solution)/shard_map/ppermute | solution.py:231
  38.1 14.8 %collective-permute-start.10 = (bf16[192,512]{1,0:T(8,128)(2,1)S(1)}, bf16[192,512]{1,0:T(8,128)(2,1)S(1)}, u32[]{:S(2)}, u32[]{:S(2)}) collective-permute-start(bf16[192,512]{1,0:T(8,128)(2,1)S(1)} %get-tuple-element.108.refs_4_.refs_6_), channel_id=1, source_target_pairs={{0,12},{4,0},{8,4},{12,8},{1,13},{5,1},{9,5},{13,9},{2,14},{6,2},{... | collective-permute-start | bytes 589832 | tf_op jit(solution)/shard_map/ppermute | solution.py:237
  38.3 14.7 %collective-permute-start.9 = (bf16[192,512]{1,0:T(8,128)(2,1)S(1)}, bf16[192,512]{1,0:T(8,128)(2,1)S(1)}, u32[]{:S(2)}, u32[]{:S(2)}) collective-permute-start(bf16[192,512]{1,0:T(8,128)(2,1)S(1)} %get-tuple-element.108.refs_4_.refs_6_), channel_id=1, source_target_pairs={{0,8},{4,12},{8,0},{12,4},{1,9},{5,13},{9,1},{13,5},{2,10},{6,14},... | collective-permute-start | bytes 589832 | tf_op jit(solution)/shard_map/ppermute | solution.py:237
  40.6 16.6 %collective-permute-start.8 = (bf16[192,512]{1,0:T(8,128)(2,1)S(1)}, bf16[192,512]{1,0:T(8,128)(2,1)S(1)}, u32[]{:S(2)}, u32[]{:S(2)}) collective-permute-start(bf16[192,512]{1,0:T(8,128)(2,1)S(1)} %get-tuple-element.108.refs_4_.refs_6_), channel_id=1, source_target_pairs={{0,4},{4,8},{8,12},{12,0},{1,5},{5,9},{9,13},{13,1},{2,6},{6,10},{... | collective-permute-start | bytes 589832 | tf_op jit(solution)/shard_map/ppermute | solution.py:237
  57.2 4.7 %collective-permute-start.15 = (bf16[2,2,64,256]{3,2,1,0:T(8,128)(2,1)S(1)}, bf16[2,2,64,256]{3,2,1,0:T(8,128)(2,1)S(1)}, u32[]{:S(2)}, u32[]{:S(2)}) collective-permute-start(bf16[2,2,64,256]{3,2,1,0:T(8,128)(2,1)S(1)} %get-tuple-element.126), channel_id=1, source_target_pairs={{0,1},{1,0},{2,3},{3,2},{4,5},{5,4},{6,7},{7,6},{8,9},{9,8},{10,11... | collective-permute-start | bytes 393224 | tf_op jit(solution)/shard_map/ppermute | solution.py:234
  58.4 14.8 %collective-permute-start.12 = (bf16[192,512]{1,0:T(8,128)(2,1)S(1)}, bf16[192,512]{1,0:T(8,128)(2,1)S(1)}, u32[]{:S(2)}, u32[]{:S(2)}) collective-permute-start(bf16[192,512]{1,0:T(8,128)(2,1)S(1)} %get-tuple-element.122), channel_id=1, source_target_pairs={{0,4},{4,8},{8,12},{12,0},{1,5},{5,9},{9,13},{13,1},{2,6},{6,10},{... | collective-permute-start | bytes 589832 | tf_op jit(solution)/shard_map/ppermute | solution.py:237
  60.6 16.9 %collective-permute-start.13 = (bf16[192,512]{1,0:T(8,128)(2,1)S(1)}, bf16[192,512]{1,0:T(8,128)(2,1)S(1)}, u32[]{:S(2)}, u32[]{:S(2)}) collective-permute-start(bf16[192,512]{1,0:T(8,128)(2,1)S(1)} %get-tuple-element.123), channel_id=1, source_target_pairs={{0,8},{4,12},{8,0},{12,4},{1,9},{5,13},{9,1},{13,5},{2,10},{6,14},... | collective-permute-start | bytes 589832 | tf_op jit(solution)/shard_map/ppermute | solution.py:237
  61.4 17.5 %collective-permute-start.14 = (bf16[192,512]{1,0:T(8,128)(2,1)S(1)}, bf16[192,512]{1,0:T(8,128)(2,1)S(1)}, u32[]{:S(2)}, u32[]{:S(2)}) collective-permute-start(bf16[192,512]{1,0:T(8,128)(2,1)S(1)} %get-tuple-element.124), channel_id=1, source_target_pairs={{0,12},{4,0},{8,4},{12,8},{1,13},{5,1},{9,5},{13,9},{2,14},{6,2},{... | collective-permute-start | bytes 589832 | tf_op jit(solution)/shard_map/ppermute | solution.py:237
  61.9 16.9 %collective-permute-start.16 = (bf16[2,2,64,256]{3,2,1,0:T(8,128)(2,1)S(1)}, bf16[2,2,64,256]{3,2,1,0:T(8,128)(2,1)S(1)}, u32[]{:S(2)}, u32[]{:S(2)}) collective-permute-start(bf16[2,2,64,256]{3,2,1,0:T(8,128)(2,1)S(1)} %pad_maximum_fusion.4), channel_id=1, source_target_pairs={{0,2},{1,3},{2,0},{3,1},{4,6},{5,7},{6,4},{7,5},{8,10},{9,11},{10,... | collective-permute-start | bytes 393224 | tf_op jit(solution)/shard_map/ppermute | solution.py:231
  80.7 7.7 %collective-permute-start.17 = (bf16[1,256,2048]{2,1,0:T(8,128)(2,1)S(1)}, bf16[1,256,2048]{2,1,0:T(8,128)(2,1)S(1)}, u32[]{:S(2)}, u32[]{:S(2)}) collective-permute-start(bf16[1,256,2048]{2,1,0:T(8,128)(2,1)S(1)} %get-tuple-element.129), channel_id=1, source_target_pairs={{0,1},{1,0},{2,3},{3,2},{4,5},{5,4},{6,7},{7,6},{8,9},{9,8},{10,11... | collective-permute-start | bytes 3145736 | tf_op jit(solution)/shard_map/ppermute | solution.py:234
  81.8 6.6 %collective-permute-start.19 = (bf16[256,384]{1,0:T(8,128)(2,1)S(1)}, bf16[256,384]{1,0:T(8,128)(2,1)S(1)}, u32[]{:S(2)}, u32[]{:S(2)}) collective-permute-start(bf16[256,384]{1,0:T(8,128)(2,1)S(1)} %sum.2.refs_0_), channel_id=1, source_target_pairs={{0,2},{1,3},{2,0},{3,1},{4,6},{5,7},{6,4},{7,5},{8,10},{9,11},{10,... | collective-permute-start | bytes 589832 | tf_op jit(solution)/shard_map/ppermute | solution.py:231
  82.1 1.9 %collective-permute-start.18 = (bf16[2,2,64,256]{3,2,1,0:T(8,128)(2,1)S(1)}, bf16[2,2,64,256]{3,2,1,0:T(8,128)(2,1)S(1)}, u32[]{:S(2)}, u32[]{:S(2)}) collective-permute-start(bf16[2,2,64,256]{3,2,1,0:T(8,128)(2,1)S(1)} %get-tuple-element.130), channel_id=1, source_target_pairs={{0,1},{1,0},{2,3},{3,2},{4,5},{5,4},{6,7},{7,6},{8,9},{9,8},{10,11... | collective-permute-start | bytes 393224 | tf_op jit(solution)/shard_map/ppermute | solution.py:234
  90.2 33.1 %collective-permute-start.25 = (bf16[1,256,2048]{2,1,0:T(8,128)(2,1)S(1)}, bf16[1,256,2048]{2,1,0:T(8,128)(2,1)S(1)}, u32[]{:S(2)}, u32[]{:S(2)}) collective-permute-start(bf16[1,256,2048]{2,1,0:T(8,128)(2,1)S(1)} %get-tuple-element.150), channel_id=1, source_target_pairs={{0,1},{1,0},{2,3},{3,2},{4,5},{5,4},{6,7},{7,6},{8,9},{9,8},{10,11... | collective-permute-start | bytes 3145736 | tf_op jit(solution)/shard_map/ppermute | solution.py:234
  91.4 31.9 %collective-permute-start.24 = (bf16[256,2048]{1,0:T(8,128)(2,1)S(1)}, bf16[256,2048]{1,0:T(8,128)(2,1)S(1)}, u32[]{:S(2)}, u32[]{:S(2)}) collective-permute-start(bf16[256,2048]{1,0:T(8,128)(2,1)S(1)} %fusion.1), channel_id=1, source_target_pairs={{0,2},{1,3},{2,0},{3,1},{4,6},{5,7},{6,4},{7,5},{8,10},{9,11},{10,... | collective-permute-start | bytes 3145736 | tf_op jit(solution)/shard_map/ppermute | solution.py:231
  91.8 6.2 %collective-permute-start.20 = (bf16[192,512]{1,0:T(8,128)(2,1)S(1)}, bf16[192,512]{1,0:T(8,128)(2,1)S(1)}, u32[]{:S(2)}, u32[]{:S(2)}) collective-permute-start(bf16[192,512]{1,0:T(8,128)(2,1)S(1)} %get-tuple-element.145), channel_id=1, source_target_pairs={{0,4},{4,8},{8,12},{12,0},{1,5},{5,9},{9,13},{13,1},{2,6},{6,10},{... | collective-permute-start | bytes 589832 | tf_op jit(solution)/shard_map/ppermute | solution.py:237
  91.8 17.0 %collective-permute-start.21 = (bf16[192,512]{1,0:T(8,128)(2,1)S(1)}, bf16[192,512]{1,0:T(8,128)(2,1)S(1)}, u32[]{:S(2)}, u32[]{:S(2)}) collective-permute-start(bf16[192,512]{1,0:T(8,128)(2,1)S(1)} %get-tuple-element.146), channel_id=1, source_target_pairs={{0,8},{4,12},{8,0},{12,4},{1,9},{5,13},{9,1},{13,5},{2,10},{6,14},... | collective-permute-start | bytes 589832 | tf_op jit(solution)/shard_map/ppermute | solution.py:237
  93.6 18.0 %collective-permute-start.22 = (bf16[192,512]{1,0:T(8,128)(2,1)S(1)}, bf16[192,512]{1,0:T(8,128)(2,1)S(1)}, u32[]{:S(2)}, u32[]{:S(2)}) collective-permute-start(bf16[192,512]{1,0:T(8,128)(2,1)S(1)} %get-tuple-element.147), channel_id=1, source_target_pairs={{0,12},{4,0},{8,4},{12,8},{1,13},{5,1},{9,5},{13,9},{2,14},{6,2},{... | collective-permute-start | bytes 589832 | tf_op jit(solution)/shard_map/ppermute | solution.py:237
  111.9 11.4 %collective-permute-start.23 = (bf16[256,384]{1,0:T(8,128)(2,1)S(1)}, bf16[256,384]{1,0:T(8,128)(2,1)S(1)}, u32[]{:S(2)}, u32[]{:S(2)}) collective-permute-start(bf16[256,384]{1,0:T(8,128)(2,1)S(1)} %sum.3.refs_3_), channel_id=1, source_target_pairs={{0,2},{1,3},{2,0},{3,1},{4,6},{5,7},{6,4},{7,5},{8,10},{9,11},{10,... | collective-permute-start | bytes 589832 | tf_op jit(solution)/shard_map/ppermute | solution.py:231
  113.2 10.1 %collective-permute-start.26 = (bf16[2,2,64,256]{3,2,1,0:T(8,128)(2,1)S(1)}, bf16[2,2,64,256]{3,2,1,0:T(8,128)(2,1)S(1)}, u32[]{:S(2)}, u32[]{:S(2)}) collective-permute-start(bf16[2,2,64,256]{3,2,1,0:T(8,128)(2,1)S(1)} %pad_maximum_fusion.5), channel_id=1, source_target_pairs={{0,2},{1,3},{2,0},{3,1},{4,6},{5,7},{6,4},{7,5},{8,10},{9,11},{10,... | collective-permute-start | bytes 393224 | tf_op jit(solution)/shard_map/ppermute | solution.py:231
  123.4 4.1 %collective-permute-start.27 = (bf16[2,256,384]{2,1,0:T(8,128)(2,1)S(1)}, bf16[2,256,384]{2,1,0:T(8,128)(2,1)S(1)}, u32[]{:S(2)}, u32[]{:S(2)}) collective-permute-start(bf16[2,256,384]{2,1,0:T(8,128)(2,1)S(1)} %pad_maximum_fusion), channel_id=1, source_target_pairs={{0,1},{1,0},{2,3},{3,2},{4,5},{5,4},{6,7},{7,6},{8,9},{9,8},{10,11... | collective-permute-start | bytes 1179656 | tf_op jit(solution)/shard_map/ppermute | solution.py:234
  124.3 3.2 %collective-permute-start.28 = (bf16[2,256,384]{2,1,0:T(8,128)(2,1)S(1)}, bf16[2,256,384]{2,1,0:T(8,128)(2,1)S(1)}, u32[]{:S(2)}, u32[]{:S(2)}) collective-permute-start(bf16[2,256,384]{2,1,0:T(8,128)(2,1)S(1)} %pad_maximum_fusion.1), channel_id=1, source_target_pairs={{0,1},{1,0},{2,3},{3,2},{4,5},{5,4},{6,7},{7,6},{8,9},{9,8},{10,11... | collective-permute-start | bytes 1179656 | tf_op jit(solution)/shard_map/ppermute | solution.py:234

commit v5 on v4

v5 whole, which is shorter than its diff:
```python
import functools

import jax
import jax.numpy as jnp
from jax import lax
from jax.experimental import pallas as pl
from jax.experimental.pallas import tpu as pltpu
from jax.sharding import PartitionSpec as P

MB = 256
BF = jnp.bfloat16
F32 = jnp.float32
CORES = 2
GELU_A = 0.7978845608028654
GELU_B = 0.044715
MIB = 1024 * 1024


def dot(a, b, ca, cb):
    return lax.dot_general(a, b, (((ca,), (cb,)), ((), ())), preferred_element_type=F32)


def gelu_parts(u):
    square = u * u
    tanh = jnp.tanh(u * (GELU_A + (GELU_A * GELU_B) * square))
    half = 0.5 * (1.0 + tanh)
    sech = 1.0 - tanh * tanh
    slope = GELU_A + (3.0 * GELU_A * GELU_B) * square
    return square, tanh, half, sech, slope


def prep_kernel(dims, table, rows, w, cots, start, mine, pack, *refs):
    nseg, nseq, hpd, feats, hid, tokens, chunk = dims
    ships, refs = refs[: nseg // CORES], refs[nseg // CORES :]
    cut, held, weights, turned, sem = refs
    own = hpd * feats
    wide = cut.shape[2]
    per = rows.shape[1] // hid
    deep = pack.shape[0]
    me = table[nseg + nseq + 1]
    base = me * own // wide * wide
    copies = []
    for part in range(3):
        at = pl.multiple_of(part * nseg * own + base, wide)
        copies.append(pltpu.make_async_copy(w.at[:, pl.ds(at, wide)], cut.at[part], sem.at[part]))
    copies.append(pltpu.make_async_copy(cots, held, sem.at[3]))
    copies.append(pltpu.make_async_copy(start, weights, sem.at[4]))
    for i, ship in enumerate(ships):
        copies.append(pltpu.make_async_copy(rows, ship.at[pl.ds(0, tokens)], sem.at[5 + i]))
    for copy in copies:
        copy.start()
    for part in range(3):
        copies[part].wait()
        block = cut[part].T
        even = block[:own]
        for i in range(1, wide // own):
            even = jnp.where(me * own % wide == i * own, block[i * own : (i + 1) * own], even)
        mine[part * own : (part + 1) * own] = even
    copies[3].wait()
    turned[...] = held[...].T
    copies[4].wait()
    for slot in range(nseg):
        dest = table[nseg + nseq + 2 + slot]
        dx, dc = slot // CORES, slot % CORES
        target, low = (pack, 0) if slot == 0 else (ships[dx], tokens + (deep * dc if dx else 0))
        for i in range(3 * hpd):
            kind, head = i // hpd, i % hpd
            if kind < 2:
                value = weights[kind, dest * hpd + head].astype(BF)
            else:
                value = turned[pl.ds(pl.multiple_of((dest * hpd + head) * feats, feats), feats)]
            top, left = low + i // per * feats, i % per * hid
            target[top : top + feats, left : left + hid] = value
    for copy in copies[5:]:
        copy.wait()


def inner_kernel(dims, head, table, rates, *refs):
    nseg, nseq, hpd, feats, hid, tokens, chunk = dims
    chips = nseg // CORES
    li, refs = refs[:nseg], refs[nseg:]
    wt, refs = refs[:nseq], refs[nseq:]
    pack, refs = refs[0], refs[1:]
    gp, refs = refs[:nseq], refs[nseq:]
    gq, sent, kept, qkv, wts, cts, ht, rt, g1, g2p, gu, gab = refs
    rows = 3 * feats
    own = hpd * feats
    first = head * feats

    per = li[0].shape[1] // hid
    deep = pack.shape[0]

    for slot in range(nseg):
        dx, dc = slot // CORES, slot % CORES
        source, low = (pack, 0) if slot == 0 else (li[slot], tokens + (deep * dc if dx else 0))
        pieces = []
        for i in range(head, 3 * hpd, hpd):
            top, left = low + i // per * feats, i % per * hid
            pieces.append(source[top : top + feats, left : left + hid])
        total = jnp.zeros((rows, tokens), F32)
        for back in range(nseq):
            at = pl.multiple_of(table[nseg + back] * chunk, chunk)
            left = jnp.concatenate(
                [wt[back][p * own + first : p * own + first + feats] for p in range(3)]
            )
            total += dot(left, li[slot][:tokens, pl.ds(at, chunk)], 1, 1)
        qkv[slot] = total.astype(BF).reshape(3, feats, tokens)
        wts[slot, 0], wts[slot, 1], cts[slot] = pieces
    rate = rates[table[nseg + nseq] + head] * (1.0 / MB)

    def local(slot):
        a_b, b_b = wts[slot, 0], wts[slot, 1]
        q_b, k_b, v_b = qkv[slot, 0], qkv[slot, 1], qkv[slot, 2]
        c_b = cts[slot]
        u = dot(a_b, k_b, 0, 0)
        square, tanh, half, sech, slope = gelu_parts(u)
        h_b = (u * half).astype(BF)
        slope1 = half + 0.5 * u * sech * slope
        second = sech * (GELU_A + (6.0 * GELU_A * GELU_B) * square - u * tanh * slope * slope)
        ht[slot] = h_b
        g1[slot] = slope1
        resid = k_b.astype(F32) - v_b.astype(F32) + dot(b_b, h_b, 1, 0)
        r_b = resid.astype(BF)
        rt[slot] = r_b
        p = dot(b_b, r_b, 0, 0)
        g2p[slot] = second * p
        gu_b = (slope1 * p).astype(BF)
        gu[slot] = gu_b
        new_a = (a_b.astype(F32) - rate * dot(k_b, gu_b, 1, 1)).astype(BF)
        new_b = (b_b.astype(F32) - rate * dot(r_b, h_b, 1, 1)).astype(BF)
        uq = dot(new_a, q_b, 0, 0)
        square, tanh, half, sech, slope = gelu_parts(uq)
        hq_b = (uq * half).astype(BF)
        guq_b = ((half + 0.5 * uq * sech * slope) * dot(new_b, c_b, 0, 0)).astype(BF)
        gab[slot, 0] = dot(q_b, guq_b, 1, 1)
        gab[slot, 1] = dot(c_b, hq_b, 1, 1)
        gq[slot, 0] = (c_b.astype(F32) + dot(new_a, guq_b, 1, 0)).astype(BF)

    for slot in range(nseg):
        local(slot)

    def step(turn, carry):
        slot = table[nseg - 1 - turn]
        t_a = carry[0] + gab[slot, 0]
        t_b = carry[1] + gab[slot, 1]
        a_b, b_b = wts[slot, 0], wts[slot, 1]
        k_b = qkv[slot, 1]
        h_b, r_b, gu_b = ht[slot], rt[slot], gu[slot]
        ta_b, tb_b = t_a.astype(BF), t_b.astype(BF)
        du = dot(ta_b, k_b, 0, 0)
        dh_b = (g1[slot] * du).astype(BF)
        dr = dot(b_b, dh_b, 1, 0) + dot(tb_b, h_b, 1, 0)
        dr_b = dr.astype(BF)
        dp = dot(b_b, dr_b, 0, 0) + dot(tb_b, r_b, 0, 0)
        dgu_b = (g2p[slot] * du + g1[slot] * dp).astype(BF)
        c_a = t_a - rate * dot(k_b, dgu_b, 1, 1)
        c_b = t_b - rate * (dot(dr_b, h_b, 1, 1) + dot(r_b, dh_b, 1, 1))
        left = jnp.concatenate([a_b, ta_b], 1)
        gk = dr + dot(left, jnp.concatenate([dgu_b, gu_b], 0), 1, 0)
        gq[slot, 1] = (-rate * gk).astype(BF)
        gq[slot, 2] = (rate * dr).astype(BF)
        wts[slot, 0] = c_a.astype(BF)
        wts[slot, 1] = c_b.astype(BF)
        return (c_a, c_b)

    zero = jnp.zeros((feats, hid), F32)
    carry = (zero, zero)
    for turn in range(nseg):
        carry = step(turn, carry)

    for slot in range(nseg):
        dx, dc = slot // CORES, slot % CORES
        if dx == 0:
            kept[dc] = wts[slot]
        else:
            sent[dx - 1, dc * rows : (dc + 1) * rows] = gq[slot].reshape(rows, tokens)
            at = CORES * rows + dc * 2 * feats
            sent[dx - 1, at : at + 2 * feats] = wts[slot].reshape(2 * feats, hid)
    for dz in range(nseq):
        at = pl.multiple_of(table[nseg + (nseq - dz) % nseq] * chunk, chunk)
        total = jnp.zeros((rows, chunk), F32)
        for slot in range(nseg):
            part = li[slot][:tokens, pl.ds(at, chunk)]
            total += dot(gq[slot].reshape(rows, tokens), part, 1, 0)
        gp[dz][...] = total.astype(gp[dz].dtype)


def input_kernel(dims, table, *refs):
    nseg, nseq, hpd, feats, hid, tokens, chunk = dims
    chips = nseg // CORES
    rows = 3 * feats
    gq, refs = refs[:hpd], refs[hpd:]
    kept, refs = refs[:hpd], refs[hpd:]
    sent, refs = refs[: hpd * (chips - 1)], refs[hpd * (chips - 1) :]
    wt, refs = refs[: chips * nseq], refs[chips * nseq :]
    home, aside, leave = refs
    for dc in range(CORES):
        left = [gq[h][dc, p] for p in range(3) for h in range(hpd)]
        for dx in range(chips - 1):
            for p in range(3):
                at = dc * rows + p * feats
                left += [sent[h * (chips - 1) + dx][at : at + feats] for h in range(hpd)]
        left = jnp.concatenate(left)
        for back in range(nseq):
            at = pl.multiple_of(table[nseg + back] * chunk, chunk)
            right = jnp.concatenate([wt[dx * nseq + back][...] for dx in range(chips)])
            value = dot(left, right, 0, 0)
            out = (home, aside)[dc]
            out[:, pl.ds(at, chunk)] = value.astype(out.dtype)
    at = CORES * rows + 2 * feats
    for head in range(hpd):
        leave[head * chips] = kept[head][1].reshape(2 * feats, hid)
        for dx in range(1, chips):
            leave[head * chips + dx] = sent[head * (chips - 1) + dx - 1][at : at + 2 * feats]


def sum_kernel(*refs):
    total = refs[0][...]
    for ref in refs[1:-1]:
        total += ref[...].astype(F32)
    total = total.T.astype(BF)
    half = total.shape[0] // 2
    refs[-1][...] = jnp.concatenate([total[:half], total[half:]], 1)


def join_kernel(dims, table, *refs):
    nseg, nseq, hpd, feats, hid, tokens, chunk = dims
    chips = nseg // CORES
    far, near, out = refs[: hpd * chips], refs[hpd * chips], refs[hpd * chips + 1]
    wide = CORES * hpd * feats
    half = chunk // 2
    me = table[nseg + nseq + 1]
    chip = me // CORES
    even = me % CORES == 0
    for dx in range(chips):
        source = (chip - dx + chips) % chips
        for side in range(2):
            cut = slice(side * 3 * feats, (side + 1) * 3 * feats)
            mine = [far[h * chips + dx][:, cut].astype(F32) for h in range(hpd)]
            other = [near[h * chips + dx, :, cut].astype(F32) for h in range(hpd)]
            for part in range(3):
                cut = slice(part * feats, (part + 1) * feats)
                a = jnp.concatenate([value[:, cut] for value in mine + other], 1)
                b = jnp.concatenate([value[:, cut] for value in other + mine], 1)
                at = pl.multiple_of((part * nseg * hpd * feats) + source * wide, wide)
                rows = pl.ds(side * half, half)
                out[rows, pl.ds(at, wide)] = jnp.where(even, a, b)


def weights_kernel(dims, table, *refs):
    nseg, nseq, hpd, feats, hid, tokens, chunk = dims
    chips = nseg // CORES
    kept, refs = refs[:hpd], refs[hpd:]
    sent, refs = refs[: hpd * (chips - 1)], refs[hpd * (chips - 1) :]
    got, out = refs
    at = CORES * 3 * feats
    for head in range(hpd):
        for slot in range(nseg):
            dx, dc = slot // CORES, slot % CORES
            if dc == 1:
                piece = got[head * chips + dx]
            elif dx == 0:
                piece = kept[head][0].reshape(2 * feats, hid)
            else:
                piece = sent[head * (chips - 1) + dx - 1][at : at + 2 * feats]
            index = table[nseg + nseq + 2 + slot] * hpd + head
            out[0, index] = piece[:feats].astype(F32)
            out[1, index] = piece[feats:].astype(F32)


def per_device(layer_input, out_cot, w_proj, inner_start, rates):
    rows = layer_input[0]
    tokens, width = rows.shape
    heads = rates.shape[0]
    feats, hid = inner_start.shape[4:]
    nseg, nseq = lax.axis_size("seg"), lax.axis_size("seq")
    chips = nseg // CORES
    hpd = heads // nseg
    own = hpd * feats
    chunk = width // nseq
    me, place = lax.axis_index("seg"), lax.axis_index("seq")
    chip, core = me // CORES, me % CORES
    barrier = lax.optimization_barrier

    def to_chip(value, dx):
        pairs = [(i, (i + dx * CORES) % nseg) for i in range(nseg)]
        return lax.ppermute(value, "seg", pairs)

    def to_core(value):
        return lax.ppermute(value, "seg", [(i, i ^ 1) for i in range(nseg)])

    def to_seq(value, dz):
        return lax.ppermute(value, "seq", [(i, (i + dz) % nseq) for i in range(nseq)])

    def kernel(body, name, limit, cost, outs, scratch, *operands):
        smem = pl.BlockSpec(memory_space=pltpu.SMEM)
        vmem = pl.BlockSpec(memory_space=pltpu.VMEM)
        return pl.pallas_call(
            body,
            in_specs=[smem if o.ndim == 1 else vmem for o in operands],
            out_specs=[vmem] * len(outs),
            out_shape=[jax.ShapeDtypeStruct(*o) for o in outs],
            scratch_shapes=[pltpu.VMEM(*o) for o in scratch],
            compiler_params=pltpu.CompilerParams(vmem_limit_bytes=limit * MIB),
            cost_estimate=pl.CostEstimate(flops=0, bytes_accessed=cost, transcendentals=0),
            name=name,
        )(*operands)

    def summed(pieces):
        return kernel(sum_kernel, "sum", 12, 0, [((chunk // 2, 6 * feats), BF)], [], *pieces)[0]

    crossed = chips == 2 and lax.axis_size("groups") == 2
    shift = lax.axis_index("groups") if crossed else 0

    segs = jnp.arange(nseg, dtype=jnp.int32)
    slot_of = ((chip - segs // CORES) % chips) * CORES + (core + segs) % CORES
    back = (place - jnp.arange(nseq, dtype=jnp.int32)) % nseq
    dest = ((chip + shift + segs // CORES) % chips) * CORES + (core + segs) % CORES
    table = jnp.concatenate([slot_of, back, jnp.stack([dest[0] * hpd, dest[0]]), dest])
    table = table.astype(jnp.int32)
    dims = (nseg, nseq, hpd, feats, hid, tokens, chunk)

    wide = max(own, 128)
    deep = -(-3 * hpd * hid // width) * feats
    hbm = pl.BlockSpec(memory_space=pltpu.HBM)
    vmem = pl.BlockSpec(memory_space=pltpu.VMEM)
    outs = [((3 * own, chunk), BF), ((deep, width), BF), ((tokens + deep, width), BF)]
    outs += [((tokens + CORES * deep, width), BF)] * (chips - 1)
    operands = (rows, w_proj, out_cot[0], inner_start[0, 0])
    mine, pack, *ships = pl.pallas_call(
        functools.partial(prep_kernel, dims),
        in_specs=[pl.BlockSpec(memory_space=pltpu.SMEM)] + [hbm] * 4,
        out_specs=[vmem] * len(outs),
        out_shape=[jax.ShapeDtypeStruct(*o) for o in outs],
        scratch_shapes=[
            pltpu.VMEM((3, chunk, wide), BF),
            pltpu.VMEM((tokens, heads * feats), BF),
            pltpu.VMEM((2, heads, feats, hid), F32),
            pltpu.VMEM((heads * feats, tokens), BF),
            pltpu.SemaphoreType.DMA((5 + chips,)),
        ],
        compiler_params=pltpu.CompilerParams(vmem_limit_bytes=16 * MIB),
        cost_estimate=pl.CostEstimate(flops=0, bytes_accessed=0, transcendentals=0),
        name="prep",
    )(table, *[pltpu.with_memory_space_constraint(o, pltpu.HBM) for o in operands])
    near = to_core(ships[0])
    far = [to_chip(ships[dx], dx) for dx in range(1, chips)]
    wt = [mine] + [to_seq(mine, dz) for dz in range(1, nseq)]
    far, near, wt = barrier((far, near, wt))
    li = [rows, near]
    for value in far:
        li += [value, to_core(value)]

    def to_others(value):
        if crossed:
            return [lax.ppermute(value, "groups", [(0, 1), (1, 0)])]
        return [to_chip(value, -dx) for dx in range(1, chips)]

    def inner(head):
        return kernel(
            functools.partial(inner_kernel, dims, head),
            "inner",
            36,
            40 * MIB,
            [((3 * feats, chunk), BF if dz else F32) for dz in range(nseq)]
            + [((nseg, 3, feats, tokens), BF)]
            + [((chips - 1, 10 * feats, tokens), BF)]
            + [((CORES, 2, feats, hid), BF)],
            [
                ((nseg, 3, feats, tokens), BF),
                ((nseg, 2, feats, hid), BF),
                ((nseg, feats, tokens), BF),
                ((nseg, hid, tokens), BF),
                ((nseg, feats, tokens), BF),
                ((nseg, hid, tokens), F32),
                ((nseg, hid, tokens), F32),
                ((nseg, hid, tokens), BF),
                ((nseg, 2, feats, hid), F32),
            ],
            table,
            rates,
            *li,
            *wt,
            pack,
        )

    share = nseq // hpd
    grads, kept, sent, projs, away, pieces = [], [], [], [], [], None
    blocks = wt
    for head in range(hpd):
        away.append(to_others(jnp.stack(blocks[head * share : (head + 1) * share])))
        outs = inner(head)
        gp, gq, send, keep = outs[:nseq], outs[nseq], outs[nseq + 1], outs[nseq + 2]
        gp, send, away, blocks, pieces, sent = barrier((gp, send, away, blocks, pieces, sent))
        if pieces is not None:
            total = summed(pieces)
            projs += [total] + [to_chip(total, dx) for dx in range(1, chips)]
        pieces = [gp[0]] + [to_seq(gp[dz], dz) for dz in range(1, nseq)]
        sent += [to_chip(send[dx - 1], -dx) for dx in range(1, chips)]
        grads.append(gq)
        kept.append(keep)

    pieces, sent, projs = barrier((pieces, sent, projs))
    total = summed(pieces)
    projs += [total] + [to_chip(total, dx) for dx in range(1, chips)]

    others = [
        group[dx][i] for dx in range(chips - 1) for group in away for i in range(share)
    ]
    home, aside, leave = kernel(
        functools.partial(input_kernel, dims),
        "input",
        24,
        10 * MIB,
        [((tokens, width), F32), ((tokens, width), BF)]
        + [((hpd * chips, 2 * feats, hid), BF)],
        [],
        table,
        *grads,
        *kept,
        *sent,
        *wt,
        *others,
    )
    grad_input = home + to_core(aside).astype(F32)
    (grad_inner,) = kernel(
        functools.partial(weights_kernel, dims),
        "weights",
        8,
        10 * MIB,
        [((2, heads, feats, hid), F32)],
        [],
        table,
        *kept,
        *sent,
        to_core(leave),
    )
    (grad_proj,) = kernel(
        functools.partial(join_kernel, dims),
        "join",
        16,
        0,
        [((chunk, 3 * heads * feats), F32)],
        [],
        table,
        *projs,
        to_core(jnp.stack(projs)),
    )
    return (grad_input.astype(BF)[None], grad_proj, grad_inner[None, None])


def solution(mesh):
    placed = (
        P(("groups", "seq"), "seg", None),
        P(("groups", "seq"), "seg", None),
        P("seq", None),
        P(("groups", "seq"), "seg", None, None, None, None),
        P(),
    )
    return jax.shard_map(
        per_device,
        mesh=mesh,
        in_specs=placed,
        out_specs=(
            P(("groups", "seq"), "seg", None),
            P(("groups", "seq"), None),
            P(("groups", "seq"), "seg", None, None, None, None),
        ),
        check_vma=False,
    )
```

time: 131 us -> 119 us (0.908)
  starting transfers between devices: 26.9 us -> 17.9 us
  local copies, waits for them, and re-layouts: 3.73 us -> 0.23 us
  waiting for transfers between devices: 66.3 us -> 68.1 us
    ppermute x8 -> x5, waiting for transfers between devices: 22 us -> 2.45 us  [to_chip(): return lax.ppermute(value, 'seg', pairs)]
    ppermute x12 -> x9, waiting for transfers between devices: 42.6 us -> 55.7 us  [to_seq(): lax.ppermute(value, 'seq', [(i, (i + dz) % nseq) for i in range(nseq)])]
    ppermute x12 -> x9, starting transfers between devices: 15.2 us -> 8.11 us  [to_seq(): lax.ppermute(value, 'seq', [(i, (i + dz) % nseq) for i in range(nseq)])]
    ppermute x0 -> x2, waiting for transfers between devices: none -> 6.14 us  [to_others(): return [lax.ppermute(value, 'groups', [(0, 1), (1, 0)])]]
    unnamed x10 -> x4, local copies, waits for them, and re-layouts: 3.59 us -> 0.01 us
    ppermute x0 -> x2, starting transfers between devices: none -> 2.61 us  [to_others(): return [lax.ppermute(value, 'groups', [(0, 1), (1, 0)])]]
    ppermute x9 -> x5, starting transfers between devices: 6.3 us -> 3.73 us  [to_core(): return lax.ppermute(value, 'seg', [(i, i ^ 1) for i in range(nseg)])]
    ppermute x9 -> x5, waiting for transfers between devices: 1.62 us -> 3.87 us  [to_core(): return lax.ppermute(value, 'seg', [(i, i ^ 1) for i in range(nseg)])]
  transfers between devices with their start and end apart: 29 -> 21, of which waited for: 14 -> 12; matrix products, arithmetic and copies ran while one was open for 2% -> 0% of each run, Pallas kernels for 18% -> 23%
where the time goes in v5:
time: 119 us
  waiting for transfers between devices  68.1 us (57%)
  Pallas kernels  30.3 us (25%)
  starting transfers between devices  17.9 us (15%)
  other arithmetic  1.56 us (1%)
    ppermute x9, waiting for transfers between devices, to_seq(): lax.ppermute(value, 'seq', [(i, (i + dz) % nseq) for i in range(nseq)])  55.7 us
    pallas_call x7, Pallas kernels, kernel(): pl.pallas_call(body, in_specs=[smem if o.ndim == 1 else vmem for o in ope...  27.5 us
    ppermute x9, starting transfers between devices, to_seq(): lax.ppermute(value, 'seq', [(i, (i + dz) % nseq) for i in range(nseq)])  8.11 us
    ppermute x2, waiting for transfers between devices, to_others(): return [lax.ppermute(value, 'groups', [(0, 1), (1, 0)])]  6.14 us
    ppermute x5, waiting for transfers between devices, to_core(): return lax.ppermute(value, 'seg', [(i, i ^ 1) for i in range(nseg)])  3.87 us
    ppermute x5, starting transfers between devices, to_core(): return lax.ppermute(value, 'seg', [(i, i ^ 1) for i in range(nseg)])  3.73 us
    ppermute x5, starting transfers between devices, to_chip(): return lax.ppermute(value, 'seg', pairs)  3.39 us
    pallas_call x1, Pallas kernels, per_device(): pl.pallas_call(functools.partial(prep_kernel, dims), in_specs=[pl.BlockSp...  2.77 us
  transfers between devices with their start and end apart: 21, of which 12 were waited for; matrix products, arithmetic and copies ran while one was open for 0% of the time, Pallas kernels for 23%

profile of v5, /device:TPU:9, one launch (start us, length us, event | category | flops | bytes accessed | tf_op | source)
XLA Modules:
  0.0 118.9 jit_solution(14453245668328439406)
XLA Ops:
  0.7 0.1 concatenate.3.table
  0.9 2.8 %prep.1 = (bf16[384,512]{1,0:T(8,128)(2,1)S(1)}, bf16[64,2048]{1,0:T(8,128)(2,1)S(1)}, bf16[320,2048]{1,0:T(8,128)(2,1)S(1)}, bf16[384,2048]{1,0:T(8,128)(2,1)S(1)}) custom-call(s32[14]{0:T(128)S(1)} %concatenate.3.table, bf16[256,2048]{1,0:T(8,128)(2,1)} %bitcast.25, bf16[512,1536]{1,0:T(8,128)(2,1)} %w.1, bf16[256,512]{1,0:T(8,128)(2,1)} %bitcast.40, ...), custom_call_target="tpu_custom_call" | custom-call | tf_op jit(solution)/shard_map/prep/pallas_call | solution.py:330
  3.6 0.0 copy-start
  3.6 0.0 copy-start.1
  3.7 1.3 %collective-permute-start = (bf16[384,2048]{1,0:T(8,128)(2,1)S(1)}, bf16[384,2048]{1,0:T(8,128)(2,1)S(1)}, u32[]{:S(2)}, u32[]{:S(2)}) collective-permute-start(bf16[384,2048]{1,0:T(8,128)(2,1)S(1)} %get-tuple-element.58), channel_id=1, source_target_pairs={{0,2},{1,3},{2,0},{3,1},{4,6},{5,7},{6,4},{7,5},{8,10},{9,11},{10,... | collective-permute-start | bytes 4718600 | tf_op jit(solution)/shard_map/ppermute | solution.py:287
  4.9 0.9 collective-permute-start.1
  5.9 1.3 %collective-permute-start.2 = (bf16[384,512]{1,0:T(8,128)(2,1)S(1)}, bf16[384,512]{1,0:T(8,128)(2,1)S(1)}, u32[]{:S(2)}, u32[]{:S(2)}) collective-permute-start(bf16[384,512]{1,0:T(8,128)(2,1)S(1)} %get-tuple-element.63.refs_4_.refs_6_), channel_id=1, source_target_pairs={{0,4},{4,8},{8,12},{12,0},{1,5},{5,9},{9,13},{13,1},{2,6},{6,10},{... | collective-permute-start | bytes 1179656 | tf_op jit(solution)/shard_map/ppermute | solution.py:293
  7.2 1.0 collective-permute-start.3
  8.2 1.5 %collective-permute-start.4 = (bf16[384,512]{1,0:T(8,128)(2,1)S(1)}, bf16[384,512]{1,0:T(8,128)(2,1)S(1)}, u32[]{:S(2)}, u32[]{:S(2)}) collective-permute-start(bf16[384,512]{1,0:T(8,128)(2,1)S(1)} %get-tuple-element.63.refs_4_.refs_6_), channel_id=1, source_target_pairs={{0,12},{4,0},{8,4},{12,8},{1,13},{5,1},{9,5},{13,9},{2,14},{6,2},{... | collective-permute-start | bytes 1179656 | tf_op jit(solution)/shard_map/ppermute | solution.py:293
  9.7 7.0 %collective-permute-done.2.refs_5_.refs_7_ = bf16[384,512]{1,0:T(8,128)(2,1)S(1)} collective-permute-done((bf16[384,512]{1,0:T(8,128)(2,1)S(1)}, bf16[384,512]{1,0:T(8,128)(2,1)S(1)}, u32[]{:S(2)}, u32[]{:S(2)}) %collective-permute-start.2) | collective-permute-done | bytes 393248 | tf_op jit(solution)/shard_map/ppermute | solution.py:293
  16.6 24.4 %collective-permute-done.3.refs_6_.refs_8_ = bf16[384,512]{1,0:T(8,128)(2,1)S(1)} collective-permute-done((bf16[384,512]{1,0:T(8,128)(2,1)S(1)}, bf16[384,512]{1,0:T(8,128)(2,1)S(1)}, u32[]{:S(2)}, u32[]{:S(2)}) %collective-permute-start.3) | collective-permute-done | bytes 393248 | tf_op jit(solution)/shard_map/ppermute | solution.py:293
  41.0 2.1 %collective-permute-done.4.refs_7_.refs_9_ = bf16[384,512]{1,0:T(8,128)(2,1)S(1)} collective-permute-done((bf16[384,512]{1,0:T(8,128)(2,1)S(1)}, bf16[384,512]{1,0:T(8,128)(2,1)S(1)}, u32[]{:S(2)}, u32[]{:S(2)}) %collective-permute-start.4) | collective-permute-done | bytes 393248 | tf_op jit(solution)/shard_map/ppermute | solution.py:293
  43.1 0.0 collective-permute-done.1.refs_1_
  43.1 0.5 collective-permute-start.5
  43.6 0.1 pad_maximum_fusion
  43.7 1.3 %collective-permute-start.6 = (bf16[2,384,512]{2,1,0:T(8,128)(2,1)S(1)}, bf16[2,384,512]{2,1,0:T(8,128)(2,1)S(1)}, u32[]{:S(2)}, u32[]{:S(2)}) collective-permute-start(bf16[2,384,512]{2,1,0:T(8,128)(2,1)S(1)} %pad_maximum_fusion), channel_id=1, source_target_pairs={{0,16},{16,0},{1,17},{17,1},{2,18},{18,2},{3,19},{19,3},{4,20},{20... | collective-permute-start | bytes 2359304 | tf_op jit(solution)/shard_map/ppermute | solution.py:356
  45.0 1.7 %collective-permute-done.5.refs_3_ = bf16[384,2048]{1,0:T(8,128)(2,1)S(1)} collective-permute-done((bf16[384,2048]{1,0:T(8,128)(2,1)S(1)}, bf16[384,2048]{1,0:T(8,128)(2,1)S(1)}, u32[]{:S(2)}, u32[]{:S(2)}) %collective-permute-start.5) | collective-permute-done | bytes 1572896 | tf_op jit(solution)/shard_map/ppermute | solution.py:290
  46.6 10.1 %inner.2 = (f32[192,512]{1,0:T(8,128)S(1)}, bf16[192,512]{1,0:T(8,128)(2,1)S(1)}, bf16[192,512]{1,0:T(8,128)(2,1)S(1)}, bf16[192,512]{1,0:T(8,128)(2,1)S(1)}, bf...) custom-call(s32[14]{0:T(128)S(1)} %concatenate.3.table, ...), custom_call_target="tpu_custom_call" | custom-call | bytes 41943040 | tf_op jit(solution)/shard_map/inner/pallas_call | solution.py:298
  56.7 6.1 %collective-permute-done.6 = bf16[2,384,512]{2,1,0:T(8,128)(2,1)S(1)} collective-permute-done((bf16[2,384,512]{2,1,0:T(8,128)(2,1)S(1)}, bf16[2,384,512]{2,1,0:T(8,128)(2,1)S(1)}, u32[]{:S(2)}, u32[]{:S(2)}) %collective-permute-start.6) | collective-permute-done | bytes 786464 | tf_op jit(solution)/shard_map/ppermute | solution.py:356
  62.9 0.1 pad_maximum_fusion.1
  62.9 1.3 %collective-permute-start.7 = (bf16[2,384,512]{2,1,0:T(8,128)(2,1)S(1)}, bf16[2,384,512]{2,1,0:T(8,128)(2,1)S(1)}, u32[]{:S(2)}, u32[]{:S(2)}) collective-permute-start(bf16[2,384,512]{2,1,0:T(8,128)(2,1)S(1)} %pad_maximum_fusion.1), channel_id=1, source_target_pairs={{0,16},{16,0},{1,17},{17,1},{2,18},{18,2},{3,19},{19,3},{4,20},{20... | collective-permute-start | bytes 2359304 | tf_op jit(solution)/shard_map/ppermute | solution.py:356
  64.3 0.3 collective-permute-start.11
  64.5 1.4 %collective-permute-start.9 = (bf16[192,512]{1,0:T(8,128)(2,1)S(1)}, bf16[192,512]{1,0:T(8,128)(2,1)S(1)}, u32[]{:S(2)}, u32[]{:S(2)}) collective-permute-start(bf16[192,512]{1,0:T(8,128)(2,1)S(1)} %get-tuple-element.87), channel_id=1, source_target_pairs={{0,8},{4,12},{8,0},{12,4},{1,9},{5,13},{9,1},{13,5},{2,10},{6,14},... | collective-permute-start | bytes 589832 | tf_op jit(solution)/shard_map/ppermute | solution.py:293
  65.9 1.5 %collective-permute-start.10 = (bf16[192,512]{1,0:T(8,128)(2,1)S(1)}, bf16[192,512]{1,0:T(8,128)(2,1)S(1)}, u32[]{:S(2)}, u32[]{:S(2)}) collective-permute-start(bf16[192,512]{1,0:T(8,128)(2,1)S(1)} %get-tuple-element.88), channel_id=1, source_target_pairs={{0,12},{4,0},{8,4},{12,8},{1,13},{5,1},{9,5},{13,9},{2,14},{6,2},{... | collective-permute-start | bytes 589832 | tf_op jit(solution)/shard_map/ppermute | solution.py:293
  67.4 10.1 %inner.3 = (f32[192,512]{1,0:T(8,128)S(1)}, bf16[192,512]{1,0:T(8,128)(2,1)S(1)}, bf16[192,512]{1,0:T(8,128)(2,1)S(1)}, bf16[192,512]{1,0:T(8,128)(2,1)S(1)}, bf...) custom-call(s32[14]{0:T(128)S(1)} %concatenate.3.table, ...), custom_call_target="tpu_custom_call" | custom-call | bytes 41943040 | tf_op jit(solution)/shard_map/inner/pallas_call | solution.py:298
  77.5 2.8 %collective-permute-done.9.refs_2_ = bf16[192,512]{1,0:T(8,128)(2,1)S(1)} collective-permute-done((bf16[192,512]{1,0:T(8,128)(2,1)S(1)}, bf16[192,512]{1,0:T(8,128)(2,1)S(1)}, u32[]{:S(2)}, u32[]{:S(2)}) %collective-permute-start.9) | collective-permute-done | bytes 196640 | tf_op jit(solution)/shard_map/ppermute | solution.py:293
  80.2 3.7 %collective-permute-done.10.refs_3_ = bf16[192,512]{1,0:T(8,128)(2,1)S(1)} collective-permute-done((bf16[192,512]{1,0:T(8,128)(2,1)S(1)}, bf16[192,512]{1,0:T(8,128)(2,1)S(1)}, u32[]{:S(2)}, u32[]{:S(2)}) %collective-permute-start.10) | collective-permute-done | bytes 196640 | tf_op jit(solution)/shard_map/ppermute | solution.py:293
  83.9 1.2 %collective-permute-start.15 = (bf16[640,256]{1,0:T(8,128)(2,1)S(1)}, bf16[640,256]{1,0:T(8,128)(2,1)S(1)}, u32[]{:S(2)}, u32[]{:S(2)}) collective-permute-start(bf16[640,256]{1,0:T(8,128)(2,1)S(1)} %bitcast.36), channel_id=1, source_target_pairs={{0,2},{1,3},{2,0},{3,1},{4,6},{5,7},{6,4},{7,5},{8,10},{9,11},{10,... | collective-permute-start | bytes 983048 | tf_op jit(solution)/shard_map/ppermute | solution.py:287
  85.1 1.5 %collective-permute-start.14 = (bf16[192,512]{1,0:T(8,128)(2,1)S(1)}, bf16[192,512]{1,0:T(8,128)(2,1)S(1)}, u32[]{:S(2)}, u32[]{:S(2)}) collective-permute-start(bf16[192,512]{1,0:T(8,128)(2,1)S(1)} %get-tuple-element.93), channel_id=1, source_target_pairs={{0,12},{4,0},{8,4},{12,8},{1,13},{5,1},{9,5},{13,9},{2,14},{6,2},{... | collective-permute-start | bytes 589832 | tf_op jit(solution)/shard_map/ppermute | solution.py:293
  86.6 0.2 sum.2.refs_0_
  86.9 0.3 collective-permute-start.16
  87.2 0.1 slice_bitcast_fusion.2
  87.2 3.6 %collective-permute-done.12.refs_1_ = bf16[192,512]{1,0:T(8,128)(2,1)S(1)} collective-permute-done((bf16[192,512]{1,0:T(8,128)(2,1)S(1)}, bf16[192,512]{1,0:T(8,128)(2,1)S(1)}, u32[]{:S(2)}, u32[]{:S(2)}) %collective-permute-start.12) | collective-permute-done | bytes 196640 | tf_op jit(solution)/shard_map/ppermute | solution.py:293
  90.8 10.8 %collective-permute-done.13.refs_2_ = bf16[192,512]{1,0:T(8,128)(2,1)S(1)} collective-permute-done((bf16[192,512]{1,0:T(8,128)(2,1)S(1)}, bf16[192,512]{1,0:T(8,128)(2,1)S(1)}, u32[]{:S(2)}, u32[]{:S(2)}) %collective-permute-start.13) | collective-permute-done | bytes 196640 | tf_op jit(solution)/shard_map/ppermute | solution.py:293
  101.6 1.5 %collective-permute-done.14.refs_3_ = bf16[192,512]{1,0:T(8,128)(2,1)S(1)} collective-permute-done((bf16[192,512]{1,0:T(8,128)(2,1)S(1)}, bf16[192,512]{1,0:T(8,128)(2,1)S(1)}, u32[]{:S(2)}, u32[]{:S(2)}) %collective-permute-start.14) | collective-permute-done | bytes 196640 | tf_op jit(solution)/shard_map/ppermute | solution.py:293
  103.0 0.3 sum.3.refs_2_
  103.3 0.3 collective-permute-start.18
  103.6 0.1 slice_bitcast_fusion
  103.6 2.4 %input.1 = (f32[256,2048]{1,0:T(8,128)S(1)}, bf16[256,2048]{1,0:T(8,128)(2,1)S(1)}, bf16[4,128,256]{2,1,0:T(8,128)(2,1)S(1)}) custom-call(s32[14]{0:T(128)S(1)} %concatenate.3.table, bf16[4,3,64,256]{3,2,1,0:T(8,128)(2,1)S(1)} %get-tuple-element.68.refs_0_, bf16[4,3,64,256]{3,2,1,0:T(8,128)(2,1)S(1)} %get-tuple-element.69.refs_1_, ...), custom_call_target="tpu_custom_call" | custom-call | bytes 10485760 | tf_op jit(solution)/shard_map/input/pallas_call | solution.py:298
  106.0 0.8 collective-permute-start.17
  106.9 2.4 %collective-permute-done.18.refs_3_ = bf16[256,384]{1,0:T(8,128)(2,1)S(1)} collective-permute-done((bf16[256,384]{1,0:T(8,128)(2,1)S(1)}, bf16[256,384]{1,0:T(8,128)(2,1)S(1)}, u32[]{:S(2)}, u32[]{:S(2)}) %collective-permute-start.18) | collective-permute-done | bytes 196640 | tf_op jit(solution)/shard_map/ppermute | solution.py:287
  109.3 0.1 pad_maximum_fusion.2
  109.4 1.4 %collective-permute-start.19 = (bf16[4,256,384]{2,1,0:T(8,128)(2,1)S(1)}, bf16[4,256,384]{2,1,0:T(8,128)(2,1)S(1)}, u32[]{:S(2)}, u32[]{:S(2)}) collective-permute-start(bf16[4,256,384]{2,1,0:T(8,128)(2,1)S(1)} %pad_maximum_fusion.2), channel_id=1, source_target_pairs={{0,1},{1,0},{2,3},{3,2},{4,5},{5,4},{6,7},{7,6},{8,9},{9,8},{10,11... | collective-permute-start | bytes 2359304 | tf_op jit(solution)/shard_map/ppermute | solution.py:290
  110.8 0.1 collective-permute-start.20
  110.9 2.2 %collective-permute-done.20.refs_4_ = bf16[4,128,256]{2,1,0:T(8,128)(2,1)S(1)} collective-permute-done((bf16[4,128,256]{2,1,0:T(8,128)(2,1)S(1)}, bf16[4,128,256]{2,1,0:T(8,128)(2,1)S(1)}, u32[]{:S(2)}, u32[]{:S(2)}) %collective-permute-start.20) | collective-permute-done | bytes 262176 | tf_op jit(solution)/shard_map/ppermute | solution.py:290
  113.1 1.6 %weights.1 = f32[2,8,64,256]{3,2,1,0:T(8,128)} custom-call(s32[14]{0:T(128)S(1)} %concatenate.3.table, bf16[2,2,64,256]{3,2,1,0:T(8,128)(2,1)S(1)} %get-tuple-element.70.refs_2_.refs_0_, bf16[2,2,64,256]{3,2,1,0:T(8,128)(2,1)S(1)} %get-tuple-element.71.refs_3_.refs_1_, bf16[640,256]{1,0:T(8,128)(2,1)S(1)} %collective-permute-done.11.refs_4_.refs_2_, ...), custom_call_target="tpu_custom_call" | custom-call | bytes 10485760 | tf_op jit(solution)/shard_map/weights/pallas_call | solution.py:298
  114.7 2.9 %join.1 = f32[512,1536]{1,0:T(8,128)} custom-call(s32[14]{0:T(128)S(1)} %concatenate.3.table, bf16[256,384]{1,0:T(8,128)(2,1)S(1)} %sum.2.refs_0_, bf16[256,384]{1,0:T(8,128)(2,1)S(1)} %collective-permute-done.16.refs_1_, bf16[256,384]{1,0:T(8,128)(2,1)S(1)} %sum.3.refs_2_, bf16[256,384]{1,0:T(8,128)(2,1)S(1)} %collective-permute-done.18.refs_3_, ...), custom_call_target="tpu_custom_call" | custom-call | tf_op jit(solution)/shard_map/join/pallas_call | solution.py:298
  117.6 1.3 %fusion = bf16[1,256,2048]{2,1,0:T(8,128)(2,1)} fusion(f32[256,2048]{1,0:T(8,128)S(1)} %get-tuple-element.104, bf16[256,2048]{1,0:T(8,128)(2,1)S(1)} %collective-permute-done.17), kind=kLoop, calls=%fused_computation.1 | loop fusion | flops 1572864 | bytes 4194304 | tf_op jit(solution)/shard_map/broadcast_in_dim | solution.py:449
  (15 shorter events, 0.1 us)
Async XLA Ops:
  3.6 43.0 %copy-start = (bf16[1,256,2048]{2,1,0:T(8,128)(2,1)S(1)}, bf16[1,256,2048]{2,1,0:T(8,128)(2,1)}, u32[]{:S(2)}) copy-start(bf16[1,256,2048]{2,1,0:T(8,128)(2,1)} %param.5) | copy-start | bytes 3145732
  3.6 43.0 %copy-start.1 = (f32[8]{0:T(128)S(1)}, f32[8]{0:T(128)}, u32[]{:S(2)}) copy-start(f32[8]{0:T(128)} %rates.3) | copy-start | bytes 100
  3.7 39.5 %collective-permute-start = (bf16[384,2048]{1,0:T(8,128)(2,1)S(1)}, bf16[384,2048]{1,0:T(8,128)(2,1)S(1)}, u32[]{:S(2)}, u32[]{:S(2)}) collective-permute-start(bf16[384,2048]{1,0:T(8,128)(2,1)S(1)} %get-tuple-element.58), channel_id=1, source_target_pairs={{0,2},{1,3},{2,0},{3,1},{4,6},{5,7},{6,4},{7,5},{8,10},{9,11},{10,... | collective-permute-start | bytes 4718600 | tf_op jit(solution)/shard_map/ppermute | solution.py:287
  4.9 38.2 %collective-permute-start.1 = (bf16[320,2048]{1,0:T(8,128)(2,1)S(1)}, bf16[320,2048]{1,0:T(8,128)(2,1)S(1)}, u32[]{:S(2)}, u32[]{:S(2)}) collective-permute-start(bf16[320,2048]{1,0:T(8,128)(2,1)S(1)} %get-tuple-element.59), channel_id=1, source_target_pairs={{0,1},{1,0},{2,3},{3,2},{4,5},{5,4},{6,7},{7,6},{8,9},{9,8},{10,11... | collective-permute-start | bytes 3932168 | tf_op jit(solution)/shard_map/ppermute | solution.py:290
  5.9 10.7 %collective-permute-start.2 = (bf16[384,512]{1,0:T(8,128)(2,1)S(1)}, bf16[384,512]{1,0:T(8,128)(2,1)S(1)}, u32[]{:S(2)}, u32[]{:S(2)}) collective-permute-start(bf16[384,512]{1,0:T(8,128)(2,1)S(1)} %get-tuple-element.63.refs_4_.refs_6_), channel_id=1, source_target_pairs={{0,4},{4,8},{8,12},{12,0},{1,5},{5,9},{9,13},{13,1},{2,6},{6,10},{... | collective-permute-start | bytes 1179656 | tf_op jit(solution)/shard_map/ppermute | solution.py:293
  7.2 33.8 %collective-permute-start.3 = (bf16[384,512]{1,0:T(8,128)(2,1)S(1)}, bf16[384,512]{1,0:T(8,128)(2,1)S(1)}, u32[]{:S(2)}, u32[]{:S(2)}) collective-permute-start(bf16[384,512]{1,0:T(8,128)(2,1)S(1)} %get-tuple-element.63.refs_4_.refs_6_), channel_id=1, source_target_pairs={{0,8},{4,12},{8,0},{12,4},{1,9},{5,13},{9,1},{13,5},{2,10},{6,14},... | collective-permute-start | bytes 1179656 | tf_op jit(solution)/shard_map/ppermute | solution.py:293
  8.2 34.9 %collective-permute-start.4 = (bf16[384,512]{1,0:T(8,128)(2,1)S(1)}, bf16[384,512]{1,0:T(8,128)(2,1)S(1)}, u32[]{:S(2)}, u32[]{:S(2)}) collective-permute-start(bf16[384,512]{1,0:T(8,128)(2,1)S(1)} %get-tuple-element.63.refs_4_.refs_6_), channel_id=1, source_target_pairs={{0,12},{4,0},{8,4},{12,8},{1,13},{5,1},{9,5},{13,9},{2,14},{6,2},{... | collective-permute-start | bytes 1179656 | tf_op jit(solution)/shard_map/ppermute | solution.py:293
  43.1 3.5 %collective-permute-start.5 = (bf16[384,2048]{1,0:T(8,128)(2,1)S(1)}, bf16[384,2048]{1,0:T(8,128)(2,1)S(1)}, u32[]{:S(2)}, u32[]{:S(2)}) collective-permute-start(bf16[384,2048]{1,0:T(8,128)(2,1)S(1)} %collective-permute-done.refs_2_), channel_id=1, source_target_pairs={{0,1},{1,0},{2,3},{3,2},{4,5},{5,4},{6,7},{7,6},{8,9},{9,8},{10,11... | collective-permute-start | bytes 4718600 | tf_op jit(solution)/shard_map/ppermute | solution.py:290
  43.7 19.2 %collective-permute-start.6 = (bf16[2,384,512]{2,1,0:T(8,128)(2,1)S(1)}, bf16[2,384,512]{2,1,0:T(8,128)(2,1)S(1)}, u32[]{:S(2)}, u32[]{:S(2)}) collective-permute-start(bf16[2,384,512]{2,1,0:T(8,128)(2,1)S(1)} %pad_maximum_fusion), channel_id=1, source_target_pairs={{0,16},{16,0},{1,17},{17,1},{2,18},{18,2},{3,19},{19,3},{4,20},{20... | collective-permute-start | bytes 2359304 | tf_op jit(solution)/shard_map/ppermute | solution.py:356
  62.9 21.0 %collective-permute-start.7 = (bf16[2,384,512]{2,1,0:T(8,128)(2,1)S(1)}, bf16[2,384,512]{2,1,0:T(8,128)(2,1)S(1)}, u32[]{:S(2)}, u32[]{:S(2)}) collective-permute-start(bf16[2,384,512]{2,1,0:T(8,128)(2,1)S(1)} %pad_maximum_fusion.1), channel_id=1, source_target_pairs={{0,16},{16,0},{1,17},{17,1},{2,18},{18,2},{3,19},{19,3},{4,20},{20... | collective-permute-start | bytes 2359304 | tf_op jit(solution)/shard_map/ppermute | solution.py:356
  64.3 19.7 %collective-permute-start.11 = (bf16[640,256]{1,0:T(8,128)(2,1)S(1)}, bf16[640,256]{1,0:T(8,128)(2,1)S(1)}, u32[]{:S(2)}, u32[]{:S(2)}) collective-permute-start(bf16[640,256]{1,0:T(8,128)(2,1)S(1)} %bitcast.37), channel_id=1, source_target_pairs={{0,2},{1,3},{2,0},{3,1},{4,6},{5,7},{6,4},{7,5},{8,10},{9,11},{10,... | collective-permute-start | bytes 983048 | tf_op jit(solution)/shard_map/ppermute | solution.py:287
  64.5 13.0 %collective-permute-start.8 = (bf16[192,512]{1,0:T(8,128)(2,1)S(1)}, bf16[192,512]{1,0:T(8,128)(2,1)S(1)}, u32[]{:S(2)}, u32[]{:S(2)}) collective-permute-start(bf16[192,512]{1,0:T(8,128)(2,1)S(1)} %get-tuple-element.86), channel_id=1, source_target_pairs={{0,4},{4,8},{8,12},{12,0},{1,5},{5,9},{9,13},{13,1},{2,6},{6,10},{... | collective-permute-start | bytes 589832 | tf_op jit(solution)/shard_map/ppermute | solution.py:293
  64.5 15.7 %collective-permute-start.9 = (bf16[192,512]{1,0:T(8,128)(2,1)S(1)}, bf16[192,512]{1,0:T(8,128)(2,1)S(1)}, u32[]{:S(2)}, u32[]{:S(2)}) collective-permute-start(bf16[192,512]{1,0:T(8,128)(2,1)S(1)} %get-tuple-element.87), channel_id=1, source_target_pairs={{0,8},{4,12},{8,0},{12,4},{1,9},{5,13},{9,1},{13,5},{2,10},{6,14},... | collective-permute-start | bytes 589832 | tf_op jit(solution)/shard_map/ppermute | solution.py:293
  65.9 18.0 %collective-permute-start.10 = (bf16[192,512]{1,0:T(8,128)(2,1)S(1)}, bf16[192,512]{1,0:T(8,128)(2,1)S(1)}, u32[]{:S(2)}, u32[]{:S(2)}) collective-permute-start(bf16[192,512]{1,0:T(8,128)(2,1)S(1)} %get-tuple-element.88), channel_id=1, source_target_pairs={{0,12},{4,0},{8,4},{12,8},{1,13},{5,1},{9,5},{13,9},{2,14},{6,2},{... | collective-permute-start | bytes 589832 | tf_op jit(solution)/shard_map/ppermute | solution.py:293
  83.9 19.1 %collective-permute-start.15 = (bf16[640,256]{1,0:T(8,128)(2,1)S(1)}, bf16[640,256]{1,0:T(8,128)(2,1)S(1)}, u32[]{:S(2)}, u32[]{:S(2)}) collective-permute-start(bf16[640,256]{1,0:T(8,128)(2,1)S(1)} %bitcast.36), channel_id=1, source_target_pairs={{0,2},{1,3},{2,0},{3,1},{4,6},{5,7},{6,4},{7,5},{8,10},{9,11},{10,... | collective-permute-start | bytes 983048 | tf_op jit(solution)/shard_map/ppermute | solution.py:287
  85.1 5.7 %collective-permute-start.12 = (bf16[192,512]{1,0:T(8,128)(2,1)S(1)}, bf16[192,512]{1,0:T(8,128)(2,1)S(1)}, u32[]{:S(2)}, u32[]{:S(2)}) collective-permute-start(bf16[192,512]{1,0:T(8,128)(2,1)S(1)} %get-tuple-element.91), channel_id=1, source_target_pairs={{0,4},{4,8},{8,12},{12,0},{1,5},{5,9},{9,13},{13,1},{2,6},{6,10},{... | collective-permute-start | bytes 589832 | tf_op jit(solution)/shard_map/ppermute | solution.py:293
  85.1 16.4 %collective-permute-start.13 = (bf16[192,512]{1,0:T(8,128)(2,1)S(1)}, bf16[192,512]{1,0:T(8,128)(2,1)S(1)}, u32[]{:S(2)}, u32[]{:S(2)}) collective-permute-start(bf16[192,512]{1,0:T(8,128)(2,1)S(1)} %get-tuple-element.92), channel_id=1, source_target_pairs={{0,8},{4,12},{8,0},{12,4},{1,9},{5,13},{9,1},{13,5},{2,10},{6,14},... | collective-permute-start | bytes 589832 | tf_op jit(solution)/shard_map/ppermute | solution.py:293
  85.1 17.9 %collective-permute-start.14 = (bf16[192,512]{1,0:T(8,128)(2,1)S(1)}, bf16[192,512]{1,0:T(8,128)(2,1)S(1)}, u32[]{:S(2)}, u32[]{:S(2)}) collective-permute-start(bf16[192,512]{1,0:T(8,128)(2,1)S(1)} %get-tuple-element.93), channel_id=1, source_target_pairs={{0,12},{4,0},{8,4},{12,8},{1,13},{5,1},{9,5},{13,9},{2,14},{6,2},{... | collective-permute-start | bytes 589832 | tf_op jit(solution)/shard_map/ppermute | solution.py:293
  86.9 16.2 %collective-permute-start.16 = (bf16[256,384]{1,0:T(8,128)(2,1)S(1)}, bf16[256,384]{1,0:T(8,128)(2,1)S(1)}, u32[]{:S(2)}, u32[]{:S(2)}) collective-permute-start(bf16[256,384]{1,0:T(8,128)(2,1)S(1)} %sum.2.refs_0_), channel_id=1, source_target_pairs={{0,2},{1,3},{2,0},{3,1},{4,6},{5,7},{6,4},{7,5},{8,10},{9,11},{10,... | collective-permute-start | bytes 589832 | tf_op jit(solution)/shard_map/ppermute | solution.py:287
  103.3 6.0 %collective-permute-start.18 = (bf16[256,384]{1,0:T(8,128)(2,1)S(1)}, bf16[256,384]{1,0:T(8,128)(2,1)S(1)}, u32[]{:S(2)}, u32[]{:S(2)}) collective-permute-start(bf16[256,384]{1,0:T(8,128)(2,1)S(1)} %sum.3.refs_2_), channel_id=1, source_target_pairs={{0,2},{1,3},{2,0},{3,1},{4,6},{5,7},{6,4},{7,5},{8,10},{9,11},{10,... | collective-permute-start | bytes 589832 | tf_op jit(solution)/shard_map/ppermute | solution.py:287
  106.0 11.6 %collective-permute-start.17 = (bf16[256,2048]{1,0:T(8,128)(2,1)S(1)}, bf16[256,2048]{1,0:T(8,128)(2,1)S(1)}, u32[]{:S(2)}, u32[]{:S(2)}) collective-permute-start(bf16[256,2048]{1,0:T(8,128)(2,1)S(1)} %get-tuple-element.105), channel_id=1, source_target_pairs={{0,1},{1,0},{2,3},{3,2},{4,5},{5,4},{6,7},{7,6},{8,9},{9,8},{10,11... | collective-permute-start | bytes 3145736 | tf_op jit(solution)/shard_map/ppermute | solution.py:290
  109.4 5.3 %collective-permute-start.19 = (bf16[4,256,384]{2,1,0:T(8,128)(2,1)S(1)}, bf16[4,256,384]{2,1,0:T(8,128)(2,1)S(1)}, u32[]{:S(2)}, u32[]{:S(2)}) collective-permute-start(bf16[4,256,384]{2,1,0:T(8,128)(2,1)S(1)} %pad_maximum_fusion.2), channel_id=1, source_target_pairs={{0,1},{1,0},{2,3},{3,2},{4,5},{5,4},{6,7},{7,6},{8,9},{9,8},{10,11... | collective-permute-start | bytes 2359304 | tf_op jit(solution)/shard_map/ppermute | solution.py:290
  110.8 2.3 %collective-permute-start.20 = (bf16[4,128,256]{2,1,0:T(8,128)(2,1)S(1)}, bf16[4,128,256]{2,1,0:T(8,128)(2,1)S(1)}, u32[]{:S(2)}, u32[]{:S(2)}) collective-permute-start(bf16[4,128,256]{2,1,0:T(8,128)(2,1)S(1)} %get-tuple-element.112), channel_id=1, source_target_pairs={{0,1},{1,0},{2,3},{3,2},{4,5},{5,4},{6,7},{7,6},{8,9},{9,8},{10,11... | collective-permute-start | bytes 786440 | tf_op jit(solution)/shard_map/ppermute | solution.py:290

commit v6 on v5

--- a/solution.py
+++ b/solution.py
@@ -14,6 +14,7 @@
 GELU_A = 0.7978845608028654
 GELU_B = 0.044715
 MIB = 1024 * 1024
+TILE = 16
 
 
 def dot(a, b, ca, cb):
@@ -29,13 +30,16 @@
     return square, tanh, half, sech, slope
 
 
+def packed(row, deep, hid):
+    return row % deep, row // deep * hid
+
+
 def prep_kernel(dims, table, rows, w, cots, start, mine, pack, *refs):
     nseg, nseq, hpd, feats, hid, tokens, chunk = dims
     ships, refs = refs[: nseg // CORES], refs[nseg // CORES :]
     cut, held, weights, turned, sem = refs
     own = hpd * feats
     wide = cut.shape[2]
-    per = rows.shape[1] // hid
     deep = pack.shape[0]
     me = table[nseg + nseq + 1]
     base = me * own // wide * wide
@@ -69,8 +73,9 @@
                 value = weights[kind, dest * hpd + head].astype(BF)
             else:
                 value = turned[pl.ds(pl.multiple_of((dest * hpd + head) * feats, feats), feats)]
-            top, left = low + i // per * feats, i % per * hid
-            target[top : top + feats, left : left + hid] = value
+            for j in range(0, feats, TILE):
+                top, left = packed(i * feats + j, deep, hid)
+                target[low + top : low + top + TILE, left : left + hid] = value[j : j + TILE]
     for copy in copies[5:]:
         copy.wait()
 
@@ -87,16 +92,16 @@
     own = hpd * feats
     first = head * feats
 
-    per = li[0].shape[1] // hid
     deep = pack.shape[0]
 
     for slot in range(nseg):
         dx, dc = slot // CORES, slot % CORES
         source, low = (pack, 0) if slot == 0 else (li[slot], tokens + (deep * dc if dx else 0))
-        pieces = []
-        for i in range(head, 3 * hpd, hpd):
-            top, left = low + i // per * feats, i % per * hid
-            pieces.append(source[top : top + feats, left : left + hid])
+        for i, piece in enumerate((wts.at[slot, 0], wts.at[slot, 1], cts.at[slot])):
+            for j in range(0, feats, TILE):
+                top, left = packed((i * hpd + head) * feats + j, deep, hid)
+                value = source[low + top : low + top + TILE, left : left + hid]
+                piece[j : j + TILE] = value
         total = jnp.zeros((rows, tokens), F32)
         for back in range(nseq):
             at = pl.multiple_of(table[nseg + back] * chunk, chunk)
@@ -105,7 +110,6 @@
             )
             total += dot(left, li[slot][:tokens, pl.ds(at, chunk)], 1, 1)
         qkv[slot] = total.astype(BF).reshape(3, feats, tokens)
-        wts[slot, 0], wts[slot, 1], cts[slot] = pieces
     rate = rates[table[nseg + nseq] + head] * (1.0 / MB)
 
     def local(slot):
@@ -321,7 +325,7 @@
     dims = (nseg, nseq, hpd, feats, hid, tokens, chunk)
 
     wide = max(own, 128)
-    deep = -(-3 * hpd * hid // width) * feats
+    deep = -(-3 * own * hid // (width * TILE)) * TILE
     hbm = pl.BlockSpec(memory_space=pltpu.HBM)
     vmem = pl.BlockSpec(memory_space=pltpu.VMEM)
     outs = [((3 * own, chunk), BF), ((deep, width), BF), ((tokens + deep, width), BF)]
@@ -361,7 +365,7 @@
             functools.partial(inner_kernel, dims, head),
             "inner",
             36,
-            40 * MIB,
+            0,
             [((3 * feats, chunk), BF if dz else F32) for dz in range(nseq)]
             + [((nseg, 3, feats, tokens), BF)]
             + [((chips - 1, 10 * feats, tokens), BF)]
@@ -384,14 +388,13 @@
             pack,
         )
 
-    share = nseq // hpd
-    grads, kept, sent, projs, away, pieces = [], [], [], [], [], None
-    blocks = wt
+    away = to_others(jnp.stack(wt))
+    grads, kept, sent, projs, pieces = [], [], [], [], None
     for head in range(hpd):
-        away.append(to_others(jnp.stack(blocks[head * share : (head + 1) * share])))
         outs = inner(head)
         gp, gq, send, keep = outs[:nseq], outs[nseq], outs[nseq + 1], outs[nseq + 2]
-        gp, send, away, blocks, pieces, sent = barrier((gp, send, away, blocks, pieces, sent))
+        if head == hpd - 1:
+            gp, send, away, pieces, sent = barrier((gp, send, away, pieces, sent))
         if pieces is not None:
             total = summed(pieces)
             projs += [total] + [to_chip(total, dx) for dx in range(1, chips)]
@@ -404,9 +407,7 @@
     total = summed(pieces)
     projs += [total] + [to_chip(total, dx) for dx in range(1, chips)]
 
-    others = [
-        group[dx][i] for dx in range(chips - 1) for group in away for i in range(share)
-    ]
+    others = [value[i] for value in away for i in range(nseq)]
     home, aside, leave = kernel(
         functools.partial(input_kernel, dims),
         "input",
@@ -422,7 +423,9 @@
         *wt,
         *others,
     )
-    grad_input = home + to_core(aside).astype(F32)
+    aside, leave = to_core(aside), to_core(leave)
+    projs, aside, leave = barrier((projs, aside, leave))
+    grad_input = home + aside.astype(F32)
     (grad_inner,) = kernel(
         functools.partial(weights_kernel, dims),
         "weights",
@@ -433,7 +436,7 @@
         table,
         *kept,
         *sent,
-        to_core(leave),
+        leave,
     )
     (grad_proj,) = kernel(
         functools.partial(join_kernel, dims),

time: 119 us -> 116 us (0.975)
  waiting for transfers between devices: 68.1 us -> 64.6 us
    ppermute x9, waiting for transfers between devices: 55.7 us -> 48.4 us  [to_seq(): lax.ppermute(value, 'seq', [(i, (i + dz) % nseq) for i in range(nseq)])]
    ppermute x2 -> x1, waiting for transfers between devices: 6.14 us -> 10 us  [to_others(): return [lax.ppermute(value, 'groups', [(0, 1), (1, 0)])]]
    ppermute x5, waiting for transfers between devices: 3.87 us -> 1.35 us  [to_core(): return lax.ppermute(value, 'seg', [(i, i ^ 1) for i in range(nseg)])]
    ppermute x5, waiting for transfers between devices: 2.45 us -> 4.84 us  [to_chip(): return lax.ppermute(value, 'seg', pairs)]
    ppermute x9, starting transfers between devices: 8.11 us -> 9.46 us  [to_seq(): lax.ppermute(value, 'seq', [(i, (i + dz) % nseq) for i in range(nseq)])]
    ppermute x2 -> x1, starting transfers between devices: 2.61 us -> 1.3 us  [to_others(): return [lax.ppermute(value, 'groups', [(0, 1), (1, 0)])]]
  transfers between devices with their start and end apart: 21 -> 20, of which waited for: 12 -> 9; matrix products, arithmetic and copies ran while one was open for 0% -> 1% of each run, Pallas kernels for 23% -> 19%
where the time goes in v6:
time: 116 us
  waiting for transfers between devices  64.6 us (56%)
  Pallas kernels  30.3 us (26%)
  starting transfers between devices  18.6 us (16%)
  other arithmetic  1.61 us (1%)
    ppermute x9, waiting for transfers between devices, to_seq(): lax.ppermute(value, 'seq', [(i, (i + dz) % nseq) for i in range(nseq)])  48.4 us
    pallas_call x7, Pallas kernels, kernel(): pl.pallas_call(body, in_specs=[smem if o.ndim == 1 else vmem for o in ope...  27.5 us
    ppermute x1, waiting for transfers between devices, to_others(): return [lax.ppermute(value, 'groups', [(0, 1), (1, 0)])]  10 us
    ppermute x9, starting transfers between devices, to_seq(): lax.ppermute(value, 'seq', [(i, (i + dz) % nseq) for i in range(nseq)])  9.46 us
    ppermute x5, waiting for transfers between devices, to_chip(): return lax.ppermute(value, 'seg', pairs)  4.84 us
    ppermute x5, starting transfers between devices, to_chip(): return lax.ppermute(value, 'seg', pairs)  4.48 us
    ppermute x5, starting transfers between devices, to_core(): return lax.ppermute(value, 'seg', [(i, i ^ 1) for i in range(nseg)])  3.39 us
    pallas_call x1, Pallas kernels, per_device(): pl.pallas_call(functools.partial(prep_kernel, dims), in_specs=[pl.BlockSp...  2.77 us
  transfers between devices with their start and end apart: 20, of which 9 were waited for; matrix products, arithmetic and copies ran while one was open for 1% of the time, Pallas kernels for 19%

profile of v6, /device:TPU:9, one launch (start us, length us, event | category | flops | bytes accessed | tf_op | source)
XLA Modules:
  0.0 116.2 jit_solution(13782524738216566821)
XLA Ops:
  0.7 0.1 concatenate.3.table
  0.9 2.8 %prep.1 = (bf16[384,512]{1,0:T(8,128)(2,1)S(1)}, bf16[48,2048]{1,0:T(8,128)(2,1)S(1)}, bf16[304,2048]{1,0:T(8,128)(2,1)S(1)}, bf16[352,2048]{1,0:T(8,128)(2,1)S(1)}) custom-call(s32[14]{0:T(128)S(1)} %concatenate.3.table, bf16[256,2048]{1,0:T(8,128)(2,1)} %bitcast.25, bf16[512,1536]{1,0:T(8,128)(2,1)} %w.1, bf16[256,512]{1,0:T(8,128)(2,1)} %bitcast.40, ...), custom_call_target="tpu_custom_call" | custom-call | tf_op jit(solution)/shard_map/prep/pallas_call | solution.py:334
  3.6 1.3 %collective-permute-start = (bf16[352,2048]{1,0:T(8,128)(2,1)S(1)}, bf16[352,2048]{1,0:T(8,128)(2,1)S(1)}, u32[]{:S(2)}, u32[]{:S(2)}) collective-permute-start(bf16[352,2048]{1,0:T(8,128)(2,1)S(1)} %get-tuple-element.55), channel_id=1, source_target_pairs={{0,2},{1,3},{2,0},{3,1},{4,6},{5,7},{6,4},{7,5},{8,10},{9,11},{10,... | collective-permute-start | bytes 4325384 | tf_op jit(solution)/shard_map/ppermute | solution.py:291
  4.9 0.9 collective-permute-start.1
  5.9 1.3 %collective-permute-start.2 = (bf16[384,512]{1,0:T(8,128)(2,1)S(1)}, bf16[384,512]{1,0:T(8,128)(2,1)S(1)}, u32[]{:S(2)}, u32[]{:S(2)}) collective-permute-start(bf16[384,512]{1,0:T(8,128)(2,1)S(1)} %get-tuple-element.60.refs_4_.refs_6_), channel_id=1, source_target_pairs={{0,4},{4,8},{8,12},{12,0},{1,5},{5,9},{9,13},{13,1},{2,6},{6,10},{... | collective-permute-start | bytes 1179656 | tf_op jit(solution)/shard_map/ppermute | solution.py:297
  7.2 1.0 collective-permute-start.3
  8.2 1.5 %collective-permute-start.4 = (bf16[384,512]{1,0:T(8,128)(2,1)S(1)}, bf16[384,512]{1,0:T(8,128)(2,1)S(1)}, u32[]{:S(2)}, u32[]{:S(2)}) collective-permute-start(bf16[384,512]{1,0:T(8,128)(2,1)S(1)} %get-tuple-element.60.refs_4_.refs_6_), channel_id=1, source_target_pairs={{0,12},{4,0},{8,4},{12,8},{1,13},{5,1},{9,5},{13,9},{2,14},{6,2},{... | collective-permute-start | bytes 1179656 | tf_op jit(solution)/shard_map/ppermute | solution.py:297
  9.6 7.0 %collective-permute-done.2.refs_5_.refs_7_ = bf16[384,512]{1,0:T(8,128)(2,1)S(1)} collective-permute-done((bf16[384,512]{1,0:T(8,128)(2,1)S(1)}, bf16[384,512]{1,0:T(8,128)(2,1)S(1)}, u32[]{:S(2)}, u32[]{:S(2)}) %collective-permute-start.2) | collective-permute-done | bytes 393248 | tf_op jit(solution)/shard_map/ppermute | solution.py:297
  16.6 24.4 %collective-permute-done.3.refs_6_.refs_8_ = bf16[384,512]{1,0:T(8,128)(2,1)S(1)} collective-permute-done((bf16[384,512]{1,0:T(8,128)(2,1)S(1)}, bf16[384,512]{1,0:T(8,128)(2,1)S(1)}, u32[]{:S(2)}, u32[]{:S(2)}) %collective-permute-start.3) | collective-permute-done | bytes 393248 | tf_op jit(solution)/shard_map/ppermute | solution.py:297
  41.0 2.1 %collective-permute-done.4.refs_7_.refs_9_ = bf16[384,512]{1,0:T(8,128)(2,1)S(1)} collective-permute-done((bf16[384,512]{1,0:T(8,128)(2,1)S(1)}, bf16[384,512]{1,0:T(8,128)(2,1)S(1)}, u32[]{:S(2)}, u32[]{:S(2)}) %collective-permute-start.4) | collective-permute-done | bytes 393248 | tf_op jit(solution)/shard_map/ppermute | solution.py:297
  43.1 0.0 collective-permute-done.1.refs_1_
  43.1 0.0 collective-permute-done.refs_2_
  43.1 0.5 collective-permute-start.5
  43.6 0.2 pad_maximum_fusion
  43.8 1.3 %collective-permute-start.6 = (bf16[4,384,512]{2,1,0:T(8,128)(2,1)S(1)}, bf16[4,384,512]{2,1,0:T(8,128)(2,1)S(1)}, u32[]{:S(2)}, u32[]{:S(2)}) collective-permute-start(bf16[4,384,512]{2,1,0:T(8,128)(2,1)S(1)} %pad_maximum_fusion), channel_id=1, source_target_pairs={{0,16},{16,0},{1,17},{17,1},{2,18},{18,2},{3,19},{19,3},{4,20},{20... | collective-permute-start | bytes 4718600 | tf_op jit(solution)/shard_map/ppermute | solution.py:360
  45.1 1.3 %collective-permute-done.5.refs_3_ = bf16[352,2048]{1,0:T(8,128)(2,1)S(1)} collective-permute-done((bf16[352,2048]{1,0:T(8,128)(2,1)S(1)}, bf16[352,2048]{1,0:T(8,128)(2,1)S(1)}, u32[]{:S(2)}, u32[]{:S(2)}) %collective-permute-start.5) | collective-permute-done | bytes 1441824 | tf_op jit(solution)/shard_map/ppermute | solution.py:294
  46.4 10.1 %inner.2 = (f32[192,512]{1,0:T(8,128)S(1)}, bf16[192,512]{1,0:T(8,128)(2,1)S(1)}, bf16[192,512]{1,0:T(8,128)(2,1)S(1)}, bf16[192,512]{1,0:T(8,128)(2,1)S(1)}, bf...) custom-call(s32[14]{0:T(128)S(1)} %concatenate.3.table, ...), custom_call_target="tpu_custom_call" | custom-call | tf_op jit(solution)/shard_map/inner/pallas_call | solution.py:302
  56.5 0.3 collective-permute-start.10
  56.8 0.0 collective-permute-start.7
  56.8 1.4 %collective-permute-start.8 = (bf16[192,512]{1,0:T(8,128)(2,1)S(1)}, bf16[192,512]{1,0:T(8,128)(2,1)S(1)}, u32[]{:S(2)}, u32[]{:S(2)}) collective-permute-start(bf16[192,512]{1,0:T(8,128)(2,1)S(1)} %get-tuple-element.76), channel_id=1, source_target_pairs={{0,8},{4,12},{8,0},{12,4},{1,9},{5,13},{9,1},{13,5},{2,10},{6,14},... | collective-permute-start | bytes 589832 | tf_op jit(solution)/shard_map/ppermute | solution.py:297
  58.2 1.5 %collective-permute-start.9 = (bf16[192,512]{1,0:T(8,128)(2,1)S(1)}, bf16[192,512]{1,0:T(8,128)(2,1)S(1)}, u32[]{:S(2)}, u32[]{:S(2)}) collective-permute-start(bf16[192,512]{1,0:T(8,128)(2,1)S(1)} %get-tuple-element.77), channel_id=1, source_target_pairs={{0,12},{4,0},{8,4},{12,8},{1,13},{5,1},{9,5},{13,9},{2,14},{6,2},{... | collective-permute-start | bytes 589832 | tf_op jit(solution)/shard_map/ppermute | solution.py:297
  59.7 10.1 %inner.3 = (f32[192,512]{1,0:T(8,128)S(1)}, bf16[192,512]{1,0:T(8,128)(2,1)S(1)}, bf16[192,512]{1,0:T(8,128)(2,1)S(1)}, bf16[192,512]{1,0:T(8,128)(2,1)S(1)}, bf...) custom-call(s32[14]{0:T(128)S(1)} %concatenate.3.table, ...), custom_call_target="tpu_custom_call" | custom-call | tf_op jit(solution)/shard_map/inner/pallas_call | solution.py:302
  69.8 10.0 %collective-permute-done.6 = bf16[4,384,512]{2,1,0:T(8,128)(2,1)S(1)} collective-permute-done((bf16[4,384,512]{2,1,0:T(8,128)(2,1)S(1)}, bf16[4,384,512]{2,1,0:T(8,128)(2,1)S(1)}, u32[]{:S(2)}, u32[]{:S(2)}) %collective-permute-start.6) | collective-permute-done | bytes 1572896 | tf_op jit(solution)/shard_map/ppermute | solution.py:360
  79.8 0.0 collective-permute-done.7.refs_1_
  79.8 0.0 collective-permute-done.8.refs_2_
  79.8 0.0 collective-permute-done.9.refs_3_
  79.8 0.3 collective-permute-start.14
  80.2 0.0 collective-permute-start.11
  80.2 1.4 %collective-permute-start.12 = (bf16[192,512]{1,0:T(8,128)(2,1)S(1)}, bf16[192,512]{1,0:T(8,128)(2,1)S(1)}, u32[]{:S(2)}, u32[]{:S(2)}) collective-permute-start(bf16[192,512]{1,0:T(8,128)(2,1)S(1)} %get-tuple-element.81), channel_id=1, source_target_pairs={{0,8},{4,12},{8,0},{12,4},{1,9},{5,13},{9,1},{13,5},{2,10},{6,14},... | collective-permute-start | bytes 589832 | tf_op jit(solution)/shard_map/ppermute | solution.py:297
  81.5 1.5 %collective-permute-start.13 = (bf16[192,512]{1,0:T(8,128)(2,1)S(1)}, bf16[192,512]{1,0:T(8,128)(2,1)S(1)}, u32[]{:S(2)}, u32[]{:S(2)}) collective-permute-start(bf16[192,512]{1,0:T(8,128)(2,1)S(1)} %get-tuple-element.82), channel_id=1, source_target_pairs={{0,12},{4,0},{8,4},{12,8},{1,13},{5,1},{9,5},{13,9},{2,14},{6,2},{... | collective-permute-start | bytes 589832 | tf_op jit(solution)/shard_map/ppermute | solution.py:297
  83.0 0.2 sum.2.refs_0_
  83.3 1.3 %collective-permute-start.15 = (bf16[256,384]{1,0:T(8,128)(2,1)S(1)}, bf16[256,384]{1,0:T(8,128)(2,1)S(1)}, u32[]{:S(2)}, u32[]{:S(2)}) collective-permute-start(bf16[256,384]{1,0:T(8,128)(2,1)S(1)} %sum.2.refs_0_), channel_id=1, source_target_pairs={{0,2},{1,3},{2,0},{3,1},{4,6},{5,7},{6,4},{7,5},{8,10},{9,11},{10,... | collective-permute-start | bytes 589832 | tf_op jit(solution)/shard_map/ppermute | solution.py:291
  84.5 0.1 slice_bitcast_fusion
  84.7 0.8 collective-permute-done.11.refs_1_
  85.5 10.7 %collective-permute-done.12.refs_2_ = bf16[192,512]{1,0:T(8,128)(2,1)S(1)} collective-permute-done((bf16[192,512]{1,0:T(8,128)(2,1)S(1)}, bf16[192,512]{1,0:T(8,128)(2,1)S(1)}, u32[]{:S(2)}, u32[]{:S(2)}) %collective-permute-start.12) | collective-permute-done | bytes 196640 | tf_op jit(solution)/shard_map/ppermute | solution.py:297
  96.2 3.3 %collective-permute-done.13.refs_3_ = bf16[192,512]{1,0:T(8,128)(2,1)S(1)} collective-permute-done((bf16[192,512]{1,0:T(8,128)(2,1)S(1)}, bf16[192,512]{1,0:T(8,128)(2,1)S(1)}, u32[]{:S(2)}, u32[]{:S(2)}) %collective-permute-start.13) | collective-permute-done | bytes 196640 | tf_op jit(solution)/shard_map/ppermute | solution.py:297
  99.5 0.0 collective-permute-done.15.refs_1_
  99.6 2.4 %input.1 = (f32[256,2048]{1,0:T(8,128)S(1)}, bf16[256,2048]{1,0:T(8,128)(2,1)S(1)}, bf16[4,128,256]{2,1,0:T(8,128)(2,1)S(1)}) custom-call(s32[14]{0:T(128)S(1)} %concatenate.3.table, bf16[4,3,64,256]{3,2,1,0:T(8,128)(2,1)S(1)} %get-tuple-element.65.refs_0_, bf16[4,3,64,256]{3,2,1,0:T(8,128)(2,1)S(1)} %get-tuple-element.66.refs_1_, ...), custom_call_target="tpu_custom_call" | custom-call | bytes 10485760 | tf_op jit(solution)/shard_map/input/pallas_call | solution.py:302
  101.9 0.6 collective-permute-start.17
  102.5 0.1 collective-permute-start.18
  102.6 0.3 sum.3.refs_2_
  102.8 1.3 %collective-permute-start.16 = (bf16[256,384]{1,0:T(8,128)(2,1)S(1)}, bf16[256,384]{1,0:T(8,128)(2,1)S(1)}, u32[]{:S(2)}, u32[]{:S(2)}) collective-permute-start(bf16[256,384]{1,0:T(8,128)(2,1)S(1)} %sum.3.refs_2_), channel_id=1, source_target_pairs={{0,2},{1,3},{2,0},{3,1},{4,6},{5,7},{6,4},{7,5},{8,10},{9,11},{10,... | collective-permute-start | bytes 589832 | tf_op jit(solution)/shard_map/ppermute | solution.py:291
  104.1 4.8 %collective-permute-done.16.refs_3_ = bf16[256,384]{1,0:T(8,128)(2,1)S(1)} collective-permute-done((bf16[256,384]{1,0:T(8,128)(2,1)S(1)}, bf16[256,384]{1,0:T(8,128)(2,1)S(1)}, u32[]{:S(2)}, u32[]{:S(2)}) %collective-permute-start.16) | collective-permute-done | bytes 196640 | tf_op jit(solution)/shard_map/ppermute | solution.py:291
  108.9 0.1 pad_maximum_fusion.1
  109.1 1.3 %collective-permute-start.19 = (bf16[4,256,384]{2,1,0:T(8,128)(2,1)S(1)}, bf16[4,256,384]{2,1,0:T(8,128)(2,1)S(1)}, u32[]{:S(2)}, u32[]{:S(2)}) collective-permute-start(bf16[4,256,384]{2,1,0:T(8,128)(2,1)S(1)} %pad_maximum_fusion.1), channel_id=1, source_target_pairs={{0,1},{1,0},{2,3},{3,2},{4,5},{5,4},{6,7},{7,6},{8,9},{9,8},{10,11... | collective-permute-start | bytes 2359304 | tf_op jit(solution)/shard_map/ppermute | solution.py:294
  110.4 1.6 %weights.1 = f32[2,8,64,256]{3,2,1,0:T(8,128)} custom-call(s32[14]{0:T(128)S(1)} %concatenate.3.table, bf16[2,2,64,256]{3,2,1,0:T(8,128)(2,1)S(1)} %get-tuple-element.67.refs_2_.refs_0_, bf16[2,2,64,256]{3,2,1,0:T(8,128)(2,1)S(1)} %get-tuple-element.68.refs_3_.refs_1_, bf16[640,256]{1,0:T(8,128)(2,1)S(1)} %collective-permute-done.10.refs_4_.refs_2_, ...), custom_call_target="tpu_custom_call" | custom-call | bytes 10485760 | tf_op jit(solution)/shard_map/weights/pallas_call | solution.py:302
  112.0 1.3 %fusion = bf16[1,256,2048]{2,1,0:T(8,128)(2,1)} fusion(f32[256,2048]{1,0:T(8,128)S(1)} %get-tuple-element.92, bf16[256,2048]{1,0:T(8,128)(2,1)S(1)} %collective-permute-done.17), kind=kLoop, calls=%fused_computation.2 | loop fusion | flops 1572864 | bytes 4194304 | tf_op jit(solution)/shard_map/broadcast_in_dim | solution.py:452
  113.3 2.9 %join.1 = f32[512,1536]{1,0:T(8,128)} custom-call(s32[14]{0:T(128)S(1)} %concatenate.3.table, bf16[256,384]{1,0:T(8,128)(2,1)S(1)} %sum.2.refs_0_, bf16[256,384]{1,0:T(8,128)(2,1)S(1)} %collective-permute-done.15.refs_1_, bf16[256,384]{1,0:T(8,128)(2,1)S(1)} %sum.3.refs_2_, bf16[256,384]{1,0:T(8,128)(2,1)S(1)} %collective-permute-done.16.refs_3_, ...), custom_call_target="tpu_custom_call" | custom-call | tf_op jit(solution)/shard_map/join/pallas_call | solution.py:302
  (11 shorter events, 0.0 us)
Async XLA Ops:
  3.6 39.5 %collective-permute-start = (bf16[352,2048]{1,0:T(8,128)(2,1)S(1)}, bf16[352,2048]{1,0:T(8,128)(2,1)S(1)}, u32[]{:S(2)}, u32[]{:S(2)}) collective-permute-start(bf16[352,2048]{1,0:T(8,128)(2,1)S(1)} %get-tuple-element.55), channel_id=1, source_target_pairs={{0,2},{1,3},{2,0},{3,1},{4,6},{5,7},{6,4},{7,5},{8,10},{9,11},{10,... | collective-permute-start | bytes 4325384 | tf_op jit(solution)/shard_map/ppermute | solution.py:291
  4.9 38.2 %collective-permute-start.1 = (bf16[304,2048]{1,0:T(8,128)(2,1)S(1)}, bf16[304,2048]{1,0:T(8,128)(2,1)S(1)}, u32[]{:S(2)}, u32[]{:S(2)}) collective-permute-start(bf16[304,2048]{1,0:T(8,128)(2,1)S(1)} %get-tuple-element.56), channel_id=1, source_target_pairs={{0,1},{1,0},{2,3},{3,2},{4,5},{5,4},{6,7},{7,6},{8,9},{9,8},{10,11... | collective-permute-start | bytes 3735560 | tf_op jit(solution)/shard_map/ppermute | solution.py:294
  5.9 10.7 %collective-permute-start.2 = (bf16[384,512]{1,0:T(8,128)(2,1)S(1)}, bf16[384,512]{1,0:T(8,128)(2,1)S(1)}, u32[]{:S(2)}, u32[]{:S(2)}) collective-permute-start(bf16[384,512]{1,0:T(8,128)(2,1)S(1)} %get-tuple-element.60.refs_4_.refs_6_), channel_id=1, source_target_pairs={{0,4},{4,8},{8,12},{12,0},{1,5},{5,9},{9,13},{13,1},{2,6},{6,10},{... | collective-permute-start | bytes 1179656 | tf_op jit(solution)/shard_map/ppermute | solution.py:297
  7.2 33.8 %collective-permute-start.3 = (bf16[384,512]{1,0:T(8,128)(2,1)S(1)}, bf16[384,512]{1,0:T(8,128)(2,1)S(1)}, u32[]{:S(2)}, u32[]{:S(2)}) collective-permute-start(bf16[384,512]{1,0:T(8,128)(2,1)S(1)} %get-tuple-element.60.refs_4_.refs_6_), channel_id=1, source_target_pairs={{0,8},{4,12},{8,0},{12,4},{1,9},{5,13},{9,1},{13,5},{2,10},{6,14},... | collective-permute-start | bytes 1179656 | tf_op jit(solution)/shard_map/ppermute | solution.py:297
  8.2 34.9 %collective-permute-start.4 = (bf16[384,512]{1,0:T(8,128)(2,1)S(1)}, bf16[384,512]{1,0:T(8,128)(2,1)S(1)}, u32[]{:S(2)}, u32[]{:S(2)}) collective-permute-start(bf16[384,512]{1,0:T(8,128)(2,1)S(1)} %get-tuple-element.60.refs_4_.refs_6_), channel_id=1, source_target_pairs={{0,12},{4,0},{8,4},{12,8},{1,13},{5,1},{9,5},{13,9},{2,14},{6,2},{... | collective-permute-start | bytes 1179656 | tf_op jit(solution)/shard_map/ppermute | solution.py:297
  43.1 3.3 %collective-permute-start.5 = (bf16[352,2048]{1,0:T(8,128)(2,1)S(1)}, bf16[352,2048]{1,0:T(8,128)(2,1)S(1)}, u32[]{:S(2)}, u32[]{:S(2)}) collective-permute-start(bf16[352,2048]{1,0:T(8,128)(2,1)S(1)} %collective-permute-done.refs_2_), channel_id=1, source_target_pairs={{0,1},{1,0},{2,3},{3,2},{4,5},{5,4},{6,7},{7,6},{8,9},{9,8},{10,11... | collective-permute-start | bytes 4325384 | tf_op jit(solution)/shard_map/ppermute | solution.py:294
  43.6 2.9 %copy-start = (bf16[1,256,2048]{2,1,0:T(8,128)(2,1)S(1)}, bf16[1,256,2048]{2,1,0:T(8,128)(2,1)}, u32[]{:S(2)}) copy-start(bf16[1,256,2048]{2,1,0:T(8,128)(2,1)} %param.5) | copy-start | bytes 3145732
  43.6 2.9 %copy-start.1 = (f32[8]{0:T(128)S(1)}, f32[8]{0:T(128)}, u32[]{:S(2)}) copy-start(f32[8]{0:T(128)} %rates.3) | copy-start | bytes 100
  43.8 36.0 %collective-permute-start.6 = (bf16[4,384,512]{2,1,0:T(8,128)(2,1)S(1)}, bf16[4,384,512]{2,1,0:T(8,128)(2,1)S(1)}, u32[]{:S(2)}, u32[]{:S(2)}) collective-permute-start(bf16[4,384,512]{2,1,0:T(8,128)(2,1)S(1)} %pad_maximum_fusion), channel_id=1, source_target_pairs={{0,16},{16,0},{1,17},{17,1},{2,18},{18,2},{3,19},{19,3},{4,20},{20... | collective-permute-start | bytes 4718600 | tf_op jit(solution)/shard_map/ppermute | solution.py:360
  56.5 23.3 %collective-permute-start.10 = (bf16[640,256]{1,0:T(8,128)(2,1)S(1)}, bf16[640,256]{1,0:T(8,128)(2,1)S(1)}, u32[]{:S(2)}, u32[]{:S(2)}) collective-permute-start(bf16[640,256]{1,0:T(8,128)(2,1)S(1)} %bitcast.37), channel_id=1, source_target_pairs={{0,2},{1,3},{2,0},{3,1},{4,6},{5,7},{6,4},{7,5},{8,10},{9,11},{10,... | collective-permute-start | bytes 983048 | tf_op jit(solution)/shard_map/ppermute | solution.py:291
  56.8 23.0 %collective-permute-start.7 = (bf16[192,512]{1,0:T(8,128)(2,1)S(1)}, bf16[192,512]{1,0:T(8,128)(2,1)S(1)}, u32[]{:S(2)}, u32[]{:S(2)}) collective-permute-start(bf16[192,512]{1,0:T(8,128)(2,1)S(1)} %get-tuple-element.75), channel_id=1, source_target_pairs={{0,4},{4,8},{8,12},{12,0},{1,5},{5,9},{9,13},{13,1},{2,6},{6,10},{... | collective-permute-start | bytes 589832 | tf_op jit(solution)/shard_map/ppermute | solution.py:297
  56.8 23.0 %collective-permute-start.8 = (bf16[192,512]{1,0:T(8,128)(2,1)S(1)}, bf16[192,512]{1,0:T(8,128)(2,1)S(1)}, u32[]{:S(2)}, u32[]{:S(2)}) collective-permute-start(bf16[192,512]{1,0:T(8,128)(2,1)S(1)} %get-tuple-element.76), channel_id=1, source_target_pairs={{0,8},{4,12},{8,0},{12,4},{1,9},{5,13},{9,1},{13,5},{2,10},{6,14},... | collective-permute-start | bytes 589832 | tf_op jit(solution)/shard_map/ppermute | solution.py:297
  58.2 21.6 %collective-permute-start.9 = (bf16[192,512]{1,0:T(8,128)(2,1)S(1)}, bf16[192,512]{1,0:T(8,128)(2,1)S(1)}, u32[]{:S(2)}, u32[]{:S(2)}) collective-permute-start(bf16[192,512]{1,0:T(8,128)(2,1)S(1)} %get-tuple-element.77), channel_id=1, source_target_pairs={{0,12},{4,0},{8,4},{12,8},{1,13},{5,1},{9,5},{13,9},{2,14},{6,2},{... | collective-permute-start | bytes 589832 | tf_op jit(solution)/shard_map/ppermute | solution.py:297
  79.8 19.7 %collective-permute-start.14 = (bf16[640,256]{1,0:T(8,128)(2,1)S(1)}, bf16[640,256]{1,0:T(8,128)(2,1)S(1)}, u32[]{:S(2)}, u32[]{:S(2)}) collective-permute-start(bf16[640,256]{1,0:T(8,128)(2,1)S(1)} %bitcast.36), channel_id=1, source_target_pairs={{0,2},{1,3},{2,0},{3,1},{4,6},{5,7},{6,4},{7,5},{8,10},{9,11},{10,... | collective-permute-start | bytes 983048 | tf_op jit(solution)/shard_map/ppermute | solution.py:291
  80.2 5.3 %collective-permute-start.11 = (bf16[192,512]{1,0:T(8,128)(2,1)S(1)}, bf16[192,512]{1,0:T(8,128)(2,1)S(1)}, u32[]{:S(2)}, u32[]{:S(2)}) collective-permute-start(bf16[192,512]{1,0:T(8,128)(2,1)S(1)} %get-tuple-element.80), channel_id=1, source_target_pairs={{0,4},{4,8},{8,12},{12,0},{1,5},{5,9},{9,13},{13,1},{2,6},{6,10},{... | collective-permute-start | bytes 589832 | tf_op jit(solution)/shard_map/ppermute | solution.py:297
  80.2 16.0 %collective-permute-start.12 = (bf16[192,512]{1,0:T(8,128)(2,1)S(1)}, bf16[192,512]{1,0:T(8,128)(2,1)S(1)}, u32[]{:S(2)}, u32[]{:S(2)}) collective-permute-start(bf16[192,512]{1,0:T(8,128)(2,1)S(1)} %get-tuple-element.81), channel_id=1, source_target_pairs={{0,8},{4,12},{8,0},{12,4},{1,9},{5,13},{9,1},{13,5},{2,10},{6,14},... | collective-permute-start | bytes 589832 | tf_op jit(solution)/shard_map/ppermute | solution.py:297
  81.5 18.0 %collective-permute-start.13 = (bf16[192,512]{1,0:T(8,128)(2,1)S(1)}, bf16[192,512]{1,0:T(8,128)(2,1)S(1)}, u32[]{:S(2)}, u32[]{:S(2)}) collective-permute-start(bf16[192,512]{1,0:T(8,128)(2,1)S(1)} %get-tuple-element.82), channel_id=1, source_target_pairs={{0,12},{4,0},{8,4},{12,8},{1,13},{5,1},{9,5},{13,9},{2,14},{6,2},{... | collective-permute-start | bytes 589832 | tf_op jit(solution)/shard_map/ppermute | solution.py:297
  83.3 16.3 %collective-permute-start.15 = (bf16[256,384]{1,0:T(8,128)(2,1)S(1)}, bf16[256,384]{1,0:T(8,128)(2,1)S(1)}, u32[]{:S(2)}, u32[]{:S(2)}) collective-permute-start(bf16[256,384]{1,0:T(8,128)(2,1)S(1)} %sum.2.refs_0_), channel_id=1, source_target_pairs={{0,2},{1,3},{2,0},{3,1},{4,6},{5,7},{6,4},{7,5},{8,10},{9,11},{10,... | collective-permute-start | bytes 589832 | tf_op jit(solution)/shard_map/ppermute | solution.py:291
  101.9 7.0 %collective-permute-start.17 = (bf16[256,2048]{1,0:T(8,128)(2,1)S(1)}, bf16[256,2048]{1,0:T(8,128)(2,1)S(1)}, u32[]{:S(2)}, u32[]{:S(2)}) collective-permute-start(bf16[256,2048]{1,0:T(8,128)(2,1)S(1)} %get-tuple-element.99), channel_id=1, source_target_pairs={{0,1},{1,0},{2,3},{3,2},{4,5},{5,4},{6,7},{7,6},{8,9},{9,8},{10,11... | collective-permute-start | bytes 3145736 | tf_op jit(solution)/shard_map/ppermute | solution.py:294
  102.5 6.5 %collective-permute-start.18 = (bf16[4,128,256]{2,1,0:T(8,128)(2,1)S(1)}, bf16[4,128,256]{2,1,0:T(8,128)(2,1)S(1)}, u32[]{:S(2)}, u32[]{:S(2)}) collective-permute-start(bf16[4,128,256]{2,1,0:T(8,128)(2,1)S(1)} %get-tuple-element.100), channel_id=1, source_target_pairs={{0,1},{1,0},{2,3},{3,2},{4,5},{5,4},{6,7},{7,6},{8,9},{9,8},{10,11... | collective-permute-start | bytes 786440 | tf_op jit(solution)/shard_map/ppermute | solution.py:294
  102.8 6.1 %collective-permute-start.16 = (bf16[256,384]{1,0:T(8,128)(2,1)S(1)}, bf16[256,384]{1,0:T(8,128)(2,1)S(1)}, u32[]{:S(2)}, u32[]{:S(2)}) collective-permute-start(bf16[256,384]{1,0:T(8,128)(2,1)S(1)} %sum.3.refs_2_), channel_id=1, source_target_pairs={{0,2},{1,3},{2,0},{3,1},{4,6},{5,7},{6,4},{7,5},{8,10},{9,11},{10,... | collective-permute-start | bytes 589832 | tf_op jit(solution)/shard_map/ppermute | solution.py:291
  109.1 4.2 %collective-permute-start.19 = (bf16[4,256,384]{2,1,0:T(8,128)(2,1)S(1)}, bf16[4,256,384]{2,1,0:T(8,128)(2,1)S(1)}, u32[]{:S(2)}, u32[]{:S(2)}) collective-permute-start(bf16[4,256,384]{2,1,0:T(8,128)(2,1)S(1)} %pad_maximum_fusion.1), channel_id=1, source_target_pairs={{0,1},{1,0},{2,3},{3,2},{4,5},{5,4},{6,7},{7,6},{8,9},{9,8},{10,11... | collective-permute-start | bytes 2359304 | tf_op jit(solution)/shard_map/ppermute | solution.py:294

commit v7 on v6

--- a/solution.py
+++ b/solution.py
@@ -196,8 +196,8 @@
     gq, refs = refs[:hpd], refs[hpd:]
     kept, refs = refs[:hpd], refs[hpd:]
     sent, refs = refs[: hpd * (chips - 1)], refs[hpd * (chips - 1) :]
-    wt, refs = refs[: chips * nseq], refs[chips * nseq :]
-    home, aside, leave = refs
+    wt, refs = refs[:nseq], refs[nseq:]
+    away, (home, aside, leave) = refs[: chips - 1], refs[chips - 1 :]
     for dc in range(CORES):
         left = [gq[h][dc, p] for p in range(3) for h in range(hpd)]
         for dx in range(chips - 1):
@@ -207,7 +207,7 @@
         left = jnp.concatenate(left)
         for back in range(nseq):
             at = pl.multiple_of(table[nseg + back] * chunk, chunk)
-            right = jnp.concatenate([wt[dx * nseq + back][...] for dx in range(chips)])
+            right = jnp.concatenate([wt[back][...]] + [value[back] for value in away])
             value = dot(left, right, 0, 0)
             out = (home, aside)[dc]
             out[:, pl.ds(at, chunk)] = value.astype(out.dtype)
@@ -394,7 +394,7 @@
         outs = inner(head)
         gp, gq, send, keep = outs[:nseq], outs[nseq], outs[nseq + 1], outs[nseq + 2]
         if head == hpd - 1:
-            gp, send, away, pieces, sent = barrier((gp, send, away, pieces, sent))
+            gp, send, pieces, sent = barrier((gp, send, pieces, sent))
         if pieces is not None:
             total = summed(pieces)
             projs += [total] + [to_chip(total, dx) for dx in range(1, chips)]
@@ -403,11 +403,6 @@
         grads.append(gq)
         kept.append(keep)
 
-    pieces, sent, projs = barrier((pieces, sent, projs))
-    total = summed(pieces)
-    projs += [total] + [to_chip(total, dx) for dx in range(1, chips)]
-
-    others = [value[i] for value in away for i in range(nseq)]
     home, aside, leave = kernel(
         functools.partial(input_kernel, dims),
         "input",
@@ -421,11 +416,14 @@
         *kept,
         *sent,
         *wt,
-        *others,
+        *away,
     )
+    pieces, projs, home, aside, leave = barrier((pieces, projs, home, aside, leave))
+
+    total = summed(pieces)
+    projs += [total] + [to_chip(total, dx) for dx in range(1, chips)]
     aside, leave = to_core(aside), to_core(leave)
-    projs, aside, leave = barrier((projs, aside, leave))
-    grad_input = home + aside.astype(F32)
+    grad_input = (home + aside.astype(F32)).astype(BF)
     (grad_inner,) = kernel(
         functools.partial(weights_kernel, dims),
         "weights",
@@ -438,6 +436,7 @@
         *sent,
         leave,
     )
+    projs, grad_input, grad_inner = barrier((projs, grad_input, grad_inner))
     (grad_proj,) = kernel(
         functools.partial(join_kernel, dims),
         "join",
@@ -449,7 +448,7 @@
         *projs,
         to_core(jnp.stack(projs)),
     )
-    return (grad_input.astype(BF)[None], grad_proj, grad_inner[None, None])
+    return (grad_input[None], grad_proj, grad_inner[None, None])
 
 
 def solution(mesh):

time: 116 us -> 109 us (0.940)
  waiting for transfers between devices: 64.6 us -> 59.7 us
  starting transfers between devices: 18.6 us -> 16.4 us
    ppermute x1, waiting for transfers between devices: 10 us -> 0.38 us  [to_others(): return [lax.ppermute(value, 'groups', [(0, 1), (1, 0)])]]
    ppermute x5, waiting for transfers between devices: 1.35 us -> 5.33 us  [to_core(): return lax.ppermute(value, 'seg', [(i, i ^ 1) for i in range(nseg)])]
    convert_element_type x0 -> x1, other arithmetic: none -> 1.26 us  [per_device(): grad_input = (home + aside.astype(F32)).astype(BF)]
    broadcast_in_dim x1 -> x0, other arithmetic: 1.26 us -> none  [per_device(): return (grad_input.astype(BF)[None], grad_proj, grad_inner[None, None])]
  transfers between devices with their start and end apart: 20 -> 20, of which waited for: 9 -> 13; matrix products, arithmetic and copies ran while one was open for 1% -> 1% of each run, Pallas kernels for 19% -> 23%
where the time goes in v7:
time: 109 us
  waiting for transfers between devices  59.7 us (55%)
  Pallas kernels  30.3 us (28%)
  starting transfers between devices  16.4 us (15%)
  other arithmetic  1.61 us (1%)
    ppermute x9, waiting for transfers between devices, to_seq(): lax.ppermute(value, 'seq', [(i, (i + dz) % nseq) for i in range(nseq)])  48.2 us
    pallas_call x7, Pallas kernels, kernel(): pl.pallas_call(body, in_specs=[smem if o.ndim == 1 else vmem for o in ope...  27.5 us
    ppermute x9, starting transfers between devices, to_seq(): lax.ppermute(value, 'seq', [(i, (i + dz) % nseq) for i in range(nseq)])  8.34 us
    ppermute x5, waiting for transfers between devices, to_chip(): return lax.ppermute(value, 'seg', pairs)  5.78 us
    ppermute x5, waiting for transfers between devices, to_core(): return lax.ppermute(value, 'seg', [(i, i ^ 1) for i in range(nseg)])  5.33 us
    ppermute x5, starting transfers between devices, to_chip(): return lax.ppermute(value, 'seg', pairs)  3.39 us
    ppermute x5, starting transfers between devices, to_core(): return lax.ppermute(value, 'seg', [(i, i ^ 1) for i in range(nseg)])  3.33 us
    pallas_call x1, Pallas kernels, per_device(): pl.pallas_call(functools.partial(prep_kernel, dims), in_specs=[pl.BlockSp...  2.77 us
  transfers between devices with their start and end apart: 20, of which 13 were waited for; matrix products, arithmetic and copies ran while one was open for 1% of the time, Pallas kernels for 23%

profile of v7, /device:TPU:9, one launch (start us, length us, event | category | flops | bytes accessed | tf_op | source)
XLA Modules:
  0.0 108.9 jit_solution(12937810294375820039)
XLA Ops:
  0.7 0.1 concatenate.3.table
  0.9 2.8 %prep.1 = (bf16[384,512]{1,0:T(8,128)(2,1)S(1)}, bf16[48,2048]{1,0:T(8,128)(2,1)S(1)}, bf16[304,2048]{1,0:T(8,128)(2,1)S(1)}, bf16[352,2048]{1,0:T(8,128)(2,1)S(1)}) custom-call(s32[14]{0:T(128)S(1)} %concatenate.3.table, bf16[256,2048]{1,0:T(8,128)(2,1)} %bitcast.16, bf16[512,1536]{1,0:T(8,128)(2,1)} %w.1, bf16[256,512]{1,0:T(8,128)(2,1)} %bitcast.32, ...), custom_call_target="tpu_custom_call" | custom-call | tf_op jit(solution)/shard_map/prep/pallas_call | solution.py:334
  3.6 1.3 %collective-permute-start = (bf16[352,2048]{1,0:T(8,128)(2,1)S(1)}, bf16[352,2048]{1,0:T(8,128)(2,1)S(1)}, u32[]{:S(2)}, u32[]{:S(2)}) collective-permute-start(bf16[352,2048]{1,0:T(8,128)(2,1)S(1)} %get-tuple-element.55), channel_id=1, source_target_pairs={{0,2},{1,3},{2,0},{3,1},{4,6},{5,7},{6,4},{7,5},{8,10},{9,11},{10,... | collective-permute-start | bytes 4325384 | tf_op jit(solution)/shard_map/ppermute | solution.py:291
  4.9 0.9 collective-permute-start.1
  5.9 1.3 %collective-permute-start.2 = (bf16[384,512]{1,0:T(8,128)(2,1)S(1)}, bf16[384,512]{1,0:T(8,128)(2,1)S(1)}, u32[]{:S(2)}, u32[]{:S(2)}) collective-permute-start(bf16[384,512]{1,0:T(8,128)(2,1)S(1)} %get-tuple-element.60.refs_4_.refs_6_), channel_id=1, source_target_pairs={{0,4},{4,8},{8,12},{12,0},{1,5},{5,9},{9,13},{13,1},{2,6},{6,10},{... | collective-permute-start | bytes 1179656 | tf_op jit(solution)/shard_map/ppermute | solution.py:297
  7.2 1.0 collective-permute-start.3
  8.2 1.5 %collective-permute-start.4 = (bf16[384,512]{1,0:T(8,128)(2,1)S(1)}, bf16[384,512]{1,0:T(8,128)(2,1)S(1)}, u32[]{:S(2)}, u32[]{:S(2)}) collective-permute-start(bf16[384,512]{1,0:T(8,128)(2,1)S(1)} %get-tuple-element.60.refs_4_.refs_6_), channel_id=1, source_target_pairs={{0,12},{4,0},{8,4},{12,8},{1,13},{5,1},{9,5},{13,9},{2,14},{6,2},{... | collective-permute-start | bytes 1179656 | tf_op jit(solution)/shard_map/ppermute | solution.py:297
  9.6 7.0 %collective-permute-done.2.refs_5_.refs_7_ = bf16[384,512]{1,0:T(8,128)(2,1)S(1)} collective-permute-done((bf16[384,512]{1,0:T(8,128)(2,1)S(1)}, bf16[384,512]{1,0:T(8,128)(2,1)S(1)}, u32[]{:S(2)}, u32[]{:S(2)}) %collective-permute-start.2) | collective-permute-done | bytes 393248 | tf_op jit(solution)/shard_map/ppermute | solution.py:297
  16.6 24.4 %collective-permute-done.3.refs_6_.refs_8_ = bf16[384,512]{1,0:T(8,128)(2,1)S(1)} collective-permute-done((bf16[384,512]{1,0:T(8,128)(2,1)S(1)}, bf16[384,512]{1,0:T(8,128)(2,1)S(1)}, u32[]{:S(2)}, u32[]{:S(2)}) %collective-permute-start.3) | collective-permute-done | bytes 393248 | tf_op jit(solution)/shard_map/ppermute | solution.py:297
  41.0 2.1 %collective-permute-done.4.refs_7_.refs_9_ = bf16[384,512]{1,0:T(8,128)(2,1)S(1)} collective-permute-done((bf16[384,512]{1,0:T(8,128)(2,1)S(1)}, bf16[384,512]{1,0:T(8,128)(2,1)S(1)}, u32[]{:S(2)}, u32[]{:S(2)}) %collective-permute-start.4) | collective-permute-done | bytes 393248 | tf_op jit(solution)/shard_map/ppermute | solution.py:297
  43.1 0.0 collective-permute-done.1.refs_1_
  43.1 0.0 collective-permute-done.refs_2_
  43.1 0.5 collective-permute-start.5
  43.6 0.2 pad_maximum_fusion
  43.8 1.3 %collective-permute-start.15 = (bf16[4,384,512]{2,1,0:T(8,128)(2,1)S(1)}, bf16[4,384,512]{2,1,0:T(8,128)(2,1)S(1)}, u32[]{:S(2)}, u32[]{:S(2)}) collective-permute-start(bf16[4,384,512]{2,1,0:T(8,128)(2,1)S(1)} %pad_maximum_fusion), channel_id=1, source_target_pairs={{0,16},{16,0},{1,17},{17,1},{2,18},{18,2},{3,19},{19,3},{4,20},{20... | collective-permute-start | bytes 4718600 | tf_op jit(solution)/shard_map/ppermute | solution.py:360
  45.1 1.3 %collective-permute-done.5.refs_3_ = bf16[352,2048]{1,0:T(8,128)(2,1)S(1)} collective-permute-done((bf16[352,2048]{1,0:T(8,128)(2,1)S(1)}, bf16[352,2048]{1,0:T(8,128)(2,1)S(1)}, u32[]{:S(2)}, u32[]{:S(2)}) %collective-permute-start.5) | collective-permute-done | bytes 1441824 | tf_op jit(solution)/shard_map/ppermute | solution.py:294
  46.4 10.1 %inner.3 = (f32[192,512]{1,0:T(8,128)S(1)}, bf16[192,512]{1,0:T(8,128)(2,1)S(1)}, bf16[192,512]{1,0:T(8,128)(2,1)S(1)}, bf16[192,512]{1,0:T(8,128)(2,1)S(1)}, bf...) custom-call(s32[14]{0:T(128)S(1)} %concatenate.3.table, ...), custom_call_target="tpu_custom_call" | custom-call | tf_op jit(solution)/shard_map/inner/pallas_call | solution.py:302
  56.5 0.3 collective-permute-start.9
  56.8 1.4 %collective-permute-start.7 = (bf16[192,512]{1,0:T(8,128)(2,1)S(1)}, bf16[192,512]{1,0:T(8,128)(2,1)S(1)}, u32[]{:S(2)}, u32[]{:S(2)}) collective-permute-start(bf16[192,512]{1,0:T(8,128)(2,1)S(1)} %get-tuple-element.72), channel_id=1, source_target_pairs={{0,8},{4,12},{8,0},{12,4},{1,9},{5,13},{9,1},{13,5},{2,10},{6,14},... | collective-permute-start | bytes 589832 | tf_op jit(solution)/shard_map/ppermute | solution.py:297
  58.2 1.5 %collective-permute-start.8 = (bf16[192,512]{1,0:T(8,128)(2,1)S(1)}, bf16[192,512]{1,0:T(8,128)(2,1)S(1)}, u32[]{:S(2)}, u32[]{:S(2)}) collective-permute-start(bf16[192,512]{1,0:T(8,128)(2,1)S(1)} %get-tuple-element.73), channel_id=1, source_target_pairs={{0,12},{4,0},{8,4},{12,8},{1,13},{5,1},{9,5},{13,9},{2,14},{6,2},{... | collective-permute-start | bytes 589832 | tf_op jit(solution)/shard_map/ppermute | solution.py:297
  59.7 10.1 %inner.2 = (f32[192,512]{1,0:T(8,128)S(1)}, bf16[192,512]{1,0:T(8,128)(2,1)S(1)}, bf16[192,512]{1,0:T(8,128)(2,1)S(1)}, bf16[192,512]{1,0:T(8,128)(2,1)S(1)}, bf...) custom-call(s32[14]{0:T(128)S(1)} %concatenate.3.table, ...), custom_call_target="tpu_custom_call" | custom-call | tf_op jit(solution)/shard_map/inner/pallas_call | solution.py:302
  69.8 0.0 collective-permute-done.6.refs_1_
  69.8 3.6 %collective-permute-done.7.refs_2_ = bf16[192,512]{1,0:T(8,128)(2,1)S(1)} collective-permute-done((bf16[192,512]{1,0:T(8,128)(2,1)S(1)}, bf16[192,512]{1,0:T(8,128)(2,1)S(1)}, u32[]{:S(2)}, u32[]{:S(2)}) %collective-permute-start.7) | collective-permute-done | bytes 196640 | tf_op jit(solution)/shard_map/ppermute | solution.py:297
  73.4 2.9 %collective-permute-done.8.refs_3_ = bf16[192,512]{1,0:T(8,128)(2,1)S(1)} collective-permute-done((bf16[192,512]{1,0:T(8,128)(2,1)S(1)}, bf16[192,512]{1,0:T(8,128)(2,1)S(1)}, u32[]{:S(2)}, u32[]{:S(2)}) %collective-permute-start.8) | collective-permute-done | bytes 196640 | tf_op jit(solution)/shard_map/ppermute | solution.py:297
  76.3 0.0 collective-permute-done.9.refs_4_.refs_2_
  76.3 1.2 %collective-permute-start.14 = (bf16[640,256]{1,0:T(8,128)(2,1)S(1)}, bf16[640,256]{1,0:T(8,128)(2,1)S(1)}, u32[]{:S(2)}, u32[]{:S(2)}) collective-permute-start(bf16[640,256]{1,0:T(8,128)(2,1)S(1)} %bitcast.27), channel_id=1, source_target_pairs={{0,2},{1,3},{2,0},{3,1},{4,6},{5,7},{6,4},{7,5},{8,10},{9,11},{10,... | collective-permute-start | bytes 983048 | tf_op jit(solution)/shard_map/ppermute | solution.py:291
  77.5 0.0 collective-permute-start.10
  77.5 0.3 collective-permute-start.11
  77.7 1.5 %collective-permute-start.12 = (bf16[192,512]{1,0:T(8,128)(2,1)S(1)}, bf16[192,512]{1,0:T(8,128)(2,1)S(1)}, u32[]{:S(2)}, u32[]{:S(2)}) collective-permute-start(bf16[192,512]{1,0:T(8,128)(2,1)S(1)} %get-tuple-element.78), channel_id=1, source_target_pairs={{0,12},{4,0},{8,4},{12,8},{1,13},{5,1},{9,5},{13,9},{2,14},{6,2},{... | collective-permute-start | bytes 589832 | tf_op jit(solution)/shard_map/ppermute | solution.py:297
  79.2 0.2 sum.2.refs_0_
  79.4 0.4 collective-permute-done.15.refs_10_
  79.8 0.3 collective-permute-start.13
  80.1 5.0 %collective-permute-done.14.refs_5_.refs_3_ = bf16[640,256]{1,0:T(8,128)(2,1)S(1)} collective-permute-done((bf16[640,256]{1,0:T(8,128)(2,1)S(1)}, bf16[640,256]{1,0:T(8,128)(2,1)S(1)}, u32[]{:S(2)}, u32[]{:S(2)}) %collective-permute-start.14) | collective-permute-done | bytes 327712 | tf_op jit(solution)/shard_map/ppermute | solution.py:291
  85.0 2.4 %input.1 = (f32[256,2048]{1,0:T(8,128)S(1)}, bf16[256,2048]{1,0:T(8,128)(2,1)S(1)}, bf16[4,128,256]{2,1,0:T(8,128)(2,1)S(1)}) custom-call(s32[14]{0:T(128)S(1)} %concatenate.3.table, bf16[4,3,64,256]{3,2,1,0:T(8,128)(2,1)S(1)} %get-tuple-element.83.refs_0_, bf16[4,3,64,256]{3,2,1,0:T(8,128)(2,1)S(1)} %get-tuple-element.84.refs_1_, ...), custom_call_target="tpu_custom_call" | custom-call | bytes 10485760 | tf_op jit(solution)/shard_map/input/pallas_call | solution.py:302
  87.4 6.5 %collective-permute-done.11.refs_2_ = bf16[192,512]{1,0:T(8,128)(2,1)S(1)} collective-permute-done((bf16[192,512]{1,0:T(8,128)(2,1)S(1)}, bf16[192,512]{1,0:T(8,128)(2,1)S(1)}, u32[]{:S(2)}, u32[]{:S(2)}) %collective-permute-start.11) | collective-permute-done | bytes 196640 | tf_op jit(solution)/shard_map/ppermute | solution.py:297
  93.9 1.8 %collective-permute-done.12.refs_3_ = bf16[192,512]{1,0:T(8,128)(2,1)S(1)} collective-permute-done((bf16[192,512]{1,0:T(8,128)(2,1)S(1)}, bf16[192,512]{1,0:T(8,128)(2,1)S(1)}, u32[]{:S(2)}, u32[]{:S(2)}) %collective-permute-start.12) | collective-permute-done | bytes 196640 | tf_op jit(solution)/shard_map/ppermute | solution.py:297
  95.7 0.5 collective-permute-start.17
  96.2 0.0 collective-permute-start.18
  96.2 0.3 sum.3.refs_2_
  96.5 0.3 collective-permute-start.16
  96.8 2.1 %collective-permute-done.18.refs_4_ = bf16[4,128,256]{2,1,0:T(8,128)(2,1)S(1)} collective-permute-done((bf16[4,128,256]{2,1,0:T(8,128)(2,1)S(1)}, bf16[4,128,256]{2,1,0:T(8,128)(2,1)S(1)}, u32[]{:S(2)}, u32[]{:S(2)}) %collective-permute-start.18) | collective-permute-done | bytes 262176 | tf_op jit(solution)/shard_map/ppermute | solution.py:294
  98.9 1.6 %weights.1 = f32[2,8,64,256]{3,2,1,0:T(8,128)} custom-call(s32[14]{0:T(128)S(1)} %concatenate.3.table, bf16[2,2,64,256]{3,2,1,0:T(8,128)(2,1)S(1)} %get-tuple-element.85.refs_2_.refs_0_, bf16[2,2,64,256]{3,2,1,0:T(8,128)(2,1)S(1)} %get-tuple-element.86.refs_3_.refs_1_, bf16[640,256]{1,0:T(8,128)(2,1)S(1)} %collective-permute-done.9.refs_4_.refs_2_, ...), custom_call_target="tpu_custom_call" | custom-call | bytes 10485760 | tf_op jit(solution)/shard_map/weights/pallas_call | solution.py:302
  100.5 1.3 %add_convert_fusion = bf16[256,2048]{1,0:T(8,128)(2,1)} fusion(f32[256,2048]{1,0:T(8,128)S(1)} %get-tuple-element.98, bf16[256,2048]{1,0:T(8,128)(2,1)S(1)} %collective-permute-done.17), kind=kLoop, calls=%fused_computation | loop fusion | flops 1572864 | bytes 4194304 | tf_op jit(solution)/shard_map/convert_element_type | solution.py:426
  101.7 0.8 collective-permute-done.16.refs_3_
  102.5 0.1 pad_maximum_fusion.1
  102.7 1.4 %collective-permute-start.19 = (bf16[4,256,384]{2,1,0:T(8,128)(2,1)S(1)}, bf16[4,256,384]{2,1,0:T(8,128)(2,1)S(1)}, u32[]{:S(2)}, u32[]{:S(2)}) collective-permute-start(bf16[4,256,384]{2,1,0:T(8,128)(2,1)S(1)} %pad_maximum_fusion.1), channel_id=1, source_target_pairs={{0,1},{1,0},{2,3},{3,2},{4,5},{5,4},{6,7},{7,6},{8,9},{9,8},{10,11... | collective-permute-start | bytes 2359304 | tf_op jit(solution)/shard_map/ppermute | solution.py:294
  104.1 1.9 %collective-permute-done.19.refs_4_ = bf16[4,256,384]{2,1,0:T(8,128)(2,1)S(1)} collective-permute-done((bf16[4,256,384]{2,1,0:T(8,128)(2,1)S(1)}, bf16[4,256,384]{2,1,0:T(8,128)(2,1)S(1)}, u32[]{:S(2)}, u32[]{:S(2)}) %collective-permute-start.19) | collective-permute-done | bytes 786464 | tf_op jit(solution)/shard_map/ppermute | solution.py:294
  106.0 2.9 %join.1 = f32[512,1536]{1,0:T(8,128)} custom-call(s32[14]{0:T(128)S(1)} %concatenate.3.table, bf16[256,384]{1,0:T(8,128)(2,1)S(1)} %sum.2.refs_0_, bf16[256,384]{1,0:T(8,128)(2,1)S(1)} %collective-permute-done.13.refs_1_, bf16[256,384]{1,0:T(8,128)(2,1)S(1)} %sum.3.refs_2_, bf16[256,384]{1,0:T(8,128)(2,1)S(1)} %collective-permute-done.16.refs_3_, ...), custom_call_target="tpu_custom_call" | custom-call | tf_op jit(solution)/shard_map/join/pallas_call | solution.py:302
  (10 shorter events, 0.0 us)
Async XLA Ops:
  3.6 39.5 %collective-permute-start = (bf16[352,2048]{1,0:T(8,128)(2,1)S(1)}, bf16[352,2048]{1,0:T(8,128)(2,1)S(1)}, u32[]{:S(2)}, u32[]{:S(2)}) collective-permute-start(bf16[352,2048]{1,0:T(8,128)(2,1)S(1)} %get-tuple-element.55), channel_id=1, source_target_pairs={{0,2},{1,3},{2,0},{3,1},{4,6},{5,7},{6,4},{7,5},{8,10},{9,11},{10,... | collective-permute-start | bytes 4325384 | tf_op jit(solution)/shard_map/ppermute | solution.py:291
  4.9 38.2 %collective-permute-start.1 = (bf16[304,2048]{1,0:T(8,128)(2,1)S(1)}, bf16[304,2048]{1,0:T(8,128)(2,1)S(1)}, u32[]{:S(2)}, u32[]{:S(2)}) collective-permute-start(bf16[304,2048]{1,0:T(8,128)(2,1)S(1)} %get-tuple-element.56), channel_id=1, source_target_pairs={{0,1},{1,0},{2,3},{3,2},{4,5},{5,4},{6,7},{7,6},{8,9},{9,8},{10,11... | collective-permute-start | bytes 3735560 | tf_op jit(solution)/shard_map/ppermute | solution.py:294
  5.9 10.7 %collective-permute-start.2 = (bf16[384,512]{1,0:T(8,128)(2,1)S(1)}, bf16[384,512]{1,0:T(8,128)(2,1)S(1)}, u32[]{:S(2)}, u32[]{:S(2)}) collective-permute-start(bf16[384,512]{1,0:T(8,128)(2,1)S(1)} %get-tuple-element.60.refs_4_.refs_6_), channel_id=1, source_target_pairs={{0,4},{4,8},{8,12},{12,0},{1,5},{5,9},{9,13},{13,1},{2,6},{6,10},{... | collective-permute-start | bytes 1179656 | tf_op jit(solution)/shard_map/ppermute | solution.py:297
  7.2 33.8 %collective-permute-start.3 = (bf16[384,512]{1,0:T(8,128)(2,1)S(1)}, bf16[384,512]{1,0:T(8,128)(2,1)S(1)}, u32[]{:S(2)}, u32[]{:S(2)}) collective-permute-start(bf16[384,512]{1,0:T(8,128)(2,1)S(1)} %get-tuple-element.60.refs_4_.refs_6_), channel_id=1, source_target_pairs={{0,8},{4,12},{8,0},{12,4},{1,9},{5,13},{9,1},{13,5},{2,10},{6,14},... | collective-permute-start | bytes 1179656 | tf_op jit(solution)/shard_map/ppermute | solution.py:297
  8.2 34.9 %collective-permute-start.4 = (bf16[384,512]{1,0:T(8,128)(2,1)S(1)}, bf16[384,512]{1,0:T(8,128)(2,1)S(1)}, u32[]{:S(2)}, u32[]{:S(2)}) collective-permute-start(bf16[384,512]{1,0:T(8,128)(2,1)S(1)} %get-tuple-element.60.refs_4_.refs_6_), channel_id=1, source_target_pairs={{0,12},{4,0},{8,4},{12,8},{1,13},{5,1},{9,5},{13,9},{2,14},{6,2},{... | collective-permute-start | bytes 1179656 | tf_op jit(solution)/shard_map/ppermute | solution.py:297
  43.1 3.3 %collective-permute-start.5 = (bf16[352,2048]{1,0:T(8,128)(2,1)S(1)}, bf16[352,2048]{1,0:T(8,128)(2,1)S(1)}, u32[]{:S(2)}, u32[]{:S(2)}) collective-permute-start(bf16[352,2048]{1,0:T(8,128)(2,1)S(1)} %collective-permute-done.refs_2_), channel_id=1, source_target_pairs={{0,1},{1,0},{2,3},{3,2},{4,5},{5,4},{6,7},{7,6},{8,9},{9,8},{10,11... | collective-permute-start | bytes 4325384 | tf_op jit(solution)/shard_map/ppermute | solution.py:294
  43.6 2.9 %copy-start = (bf16[1,256,2048]{2,1,0:T(8,128)(2,1)S(1)}, bf16[1,256,2048]{2,1,0:T(8,128)(2,1)}, u32[]{:S(2)}) copy-start(bf16[1,256,2048]{2,1,0:T(8,128)(2,1)} %param.5) | copy-start | bytes 3145732
  43.6 2.9 %copy-start.1 = (f32[8]{0:T(128)S(1)}, f32[8]{0:T(128)}, u32[]{:S(2)}) copy-start(f32[8]{0:T(128)} %rates.3) | copy-start | bytes 100
  43.8 36.0 %collective-permute-start.15 = (bf16[4,384,512]{2,1,0:T(8,128)(2,1)S(1)}, bf16[4,384,512]{2,1,0:T(8,128)(2,1)S(1)}, u32[]{:S(2)}, u32[]{:S(2)}) collective-permute-start(bf16[4,384,512]{2,1,0:T(8,128)(2,1)S(1)} %pad_maximum_fusion), channel_id=1, source_target_pairs={{0,16},{16,0},{1,17},{17,1},{2,18},{18,2},{3,19},{19,3},{4,20},{20... | collective-permute-start | bytes 4718600 | tf_op jit(solution)/shard_map/ppermute | solution.py:360
  56.5 19.7 %collective-permute-start.9 = (bf16[640,256]{1,0:T(8,128)(2,1)S(1)}, bf16[640,256]{1,0:T(8,128)(2,1)S(1)}, u32[]{:S(2)}, u32[]{:S(2)}) collective-permute-start(bf16[640,256]{1,0:T(8,128)(2,1)S(1)} %bitcast.28), channel_id=1, source_target_pairs={{0,2},{1,3},{2,0},{3,1},{4,6},{5,7},{6,4},{7,5},{8,10},{9,11},{10,... | collective-permute-start | bytes 983048 | tf_op jit(solution)/shard_map/ppermute | solution.py:291
  56.8 12.9 %collective-permute-start.6 = (bf16[192,512]{1,0:T(8,128)(2,1)S(1)}, bf16[192,512]{1,0:T(8,128)(2,1)S(1)}, u32[]{:S(2)}, u32[]{:S(2)}) collective-permute-start(bf16[192,512]{1,0:T(8,128)(2,1)S(1)} %get-tuple-element.71), channel_id=1, source_target_pairs={{0,4},{4,8},{8,12},{12,0},{1,5},{5,9},{9,13},{13,1},{2,6},{6,10},{... | collective-permute-start | bytes 589832 | tf_op jit(solution)/shard_map/ppermute | solution.py:297
  56.8 16.5 %collective-permute-start.7 = (bf16[192,512]{1,0:T(8,128)(2,1)S(1)}, bf16[192,512]{1,0:T(8,128)(2,1)S(1)}, u32[]{:S(2)}, u32[]{:S(2)}) collective-permute-start(bf16[192,512]{1,0:T(8,128)(2,1)S(1)} %get-tuple-element.72), channel_id=1, source_target_pairs={{0,8},{4,12},{8,0},{12,4},{1,9},{5,13},{9,1},{13,5},{2,10},{6,14},... | collective-permute-start | bytes 589832 | tf_op jit(solution)/shard_map/ppermute | solution.py:297
  58.2 18.0 %collective-permute-start.8 = (bf16[192,512]{1,0:T(8,128)(2,1)S(1)}, bf16[192,512]{1,0:T(8,128)(2,1)S(1)}, u32[]{:S(2)}, u32[]{:S(2)}) collective-permute-start(bf16[192,512]{1,0:T(8,128)(2,1)S(1)} %get-tuple-element.73), channel_id=1, source_target_pairs={{0,12},{4,0},{8,4},{12,8},{1,13},{5,1},{9,5},{13,9},{2,14},{6,2},{... | collective-permute-start | bytes 589832 | tf_op jit(solution)/shard_map/ppermute | solution.py:297
  76.3 8.8 %collective-permute-start.14 = (bf16[640,256]{1,0:T(8,128)(2,1)S(1)}, bf16[640,256]{1,0:T(8,128)(2,1)S(1)}, u32[]{:S(2)}, u32[]{:S(2)}) collective-permute-start(bf16[640,256]{1,0:T(8,128)(2,1)S(1)} %bitcast.27), channel_id=1, source_target_pairs={{0,2},{1,3},{2,0},{3,1},{4,6},{5,7},{6,4},{7,5},{8,10},{9,11},{10,... | collective-permute-start | bytes 983048 | tf_op jit(solution)/shard_map/ppermute | solution.py:291
  77.5 9.9 %collective-permute-start.10 = (bf16[192,512]{1,0:T(8,128)(2,1)S(1)}, bf16[192,512]{1,0:T(8,128)(2,1)S(1)}, u32[]{:S(2)}, u32[]{:S(2)}) collective-permute-start(bf16[192,512]{1,0:T(8,128)(2,1)S(1)} %get-tuple-element.76), channel_id=1, source_target_pairs={{0,4},{4,8},{8,12},{12,0},{1,5},{5,9},{9,13},{13,1},{2,6},{6,10},{... | collective-permute-start | bytes 589832 | tf_op jit(solution)/shard_map/ppermute | solution.py:297
  77.5 16.4 %collective-permute-start.11 = (bf16[192,512]{1,0:T(8,128)(2,1)S(1)}, bf16[192,512]{1,0:T(8,128)(2,1)S(1)}, u32[]{:S(2)}, u32[]{:S(2)}) collective-permute-start(bf16[192,512]{1,0:T(8,128)(2,1)S(1)} %get-tuple-element.77), channel_id=1, source_target_pairs={{0,8},{4,12},{8,0},{12,4},{1,9},{5,13},{9,1},{13,5},{2,10},{6,14},... | collective-permute-start | bytes 589832 | tf_op jit(solution)/shard_map/ppermute | solution.py:297
  77.7 18.0 %collective-permute-start.12 = (bf16[192,512]{1,0:T(8,128)(2,1)S(1)}, bf16[192,512]{1,0:T(8,128)(2,1)S(1)}, u32[]{:S(2)}, u32[]{:S(2)}) collective-permute-start(bf16[192,512]{1,0:T(8,128)(2,1)S(1)} %get-tuple-element.78), channel_id=1, source_target_pairs={{0,12},{4,0},{8,4},{12,8},{1,13},{5,1},{9,5},{13,9},{2,14},{6,2},{... | collective-permute-start | bytes 589832 | tf_op jit(solution)/shard_map/ppermute | solution.py:297
  79.8 15.9 %collective-permute-start.13 = (bf16[256,384]{1,0:T(8,128)(2,1)S(1)}, bf16[256,384]{1,0:T(8,128)(2,1)S(1)}, u32[]{:S(2)}, u32[]{:S(2)}) collective-permute-start(bf16[256,384]{1,0:T(8,128)(2,1)S(1)} %sum.2.refs_0_), channel_id=1, source_target_pairs={{0,2},{1,3},{2,0},{3,1},{4,6},{5,7},{6,4},{7,5},{8,10},{9,11},{10,... | collective-permute-start | bytes 589832 | tf_op jit(solution)/shard_map/ppermute | solution.py:291
  95.7 4.7 %collective-permute-start.17 = (bf16[256,2048]{1,0:T(8,128)(2,1)S(1)}, bf16[256,2048]{1,0:T(8,128)(2,1)S(1)}, u32[]{:S(2)}, u32[]{:S(2)}) collective-permute-start(bf16[256,2048]{1,0:T(8,128)(2,1)S(1)} %get-tuple-element.99), channel_id=1, source_target_pairs={{0,1},{1,0},{2,3},{3,2},{4,5},{5,4},{6,7},{7,6},{8,9},{9,8},{10,11... | collective-permute-start | bytes 3145736 | tf_op jit(solution)/shard_map/ppermute | solution.py:294
  96.2 2.7 %collective-permute-start.18 = (bf16[4,128,256]{2,1,0:T(8,128)(2,1)S(1)}, bf16[4,128,256]{2,1,0:T(8,128)(2,1)S(1)}, u32[]{:S(2)}, u32[]{:S(2)}) collective-permute-start(bf16[4,128,256]{2,1,0:T(8,128)(2,1)S(1)} %get-tuple-element.100), channel_id=1, source_target_pairs={{0,1},{1,0},{2,3},{3,2},{4,5},{5,4},{6,7},{7,6},{8,9},{9,8},{10,11... | collective-permute-start | bytes 786440 | tf_op jit(solution)/shard_map/ppermute | solution.py:294
  96.5 6.0 %collective-permute-start.16 = (bf16[256,384]{1,0:T(8,128)(2,1)S(1)}, bf16[256,384]{1,0:T(8,128)(2,1)S(1)}, u32[]{:S(2)}, u32[]{:S(2)}) collective-permute-start(bf16[256,384]{1,0:T(8,128)(2,1)S(1)} %sum.3.refs_2_), channel_id=1, source_target_pairs={{0,2},{1,3},{2,0},{3,1},{4,6},{5,7},{6,4},{7,5},{8,10},{9,11},{10,... | collective-permute-start | bytes 589832 | tf_op jit(solution)/shard_map/ppermute | solution.py:291
  102.7 3.3 %collective-permute-start.19 = (bf16[4,256,384]{2,1,0:T(8,128)(2,1)S(1)}, bf16[4,256,384]{2,1,0:T(8,128)(2,1)S(1)}, u32[]{:S(2)}, u32[]{:S(2)}) collective-permute-start(bf16[4,256,384]{2,1,0:T(8,128)(2,1)S(1)} %pad_maximum_fusion.1), channel_id=1, source_target_pairs={{0,1},{1,0},{2,3},{3,2},{4,5},{5,4},{6,7},{7,6},{8,9},{9,8},{10,11... | collective-permute-start | bytes 2359304 | tf_op jit(solution)/shard_map/ppermute | solution.py:294

commit v8 on v7

--- a/solution.py
+++ b/solution.py
@@ -1,4 +1,5 @@
 import functools
+from itertools import zip_longest
 
 import jax
 import jax.numpy as jnp
@@ -15,6 +16,7 @@
 GELU_B = 0.044715
 MIB = 1024 * 1024
 TILE = 16
+GROUP = 4
 
 
 def dot(a, b, ca, cb):
@@ -87,7 +89,7 @@
     wt, refs = refs[:nseq], refs[nseq:]
     pack, refs = refs[0], refs[1:]
     gp, refs = refs[:nseq], refs[nseq:]
-    gq, sent, kept, qkv, wts, cts, ht, rt, g1, g2p, gu, gab = refs
+    gq, sent, kept, qkv, wts, cts, ht, rt, g1, g2p, gu, gab, res = refs
     rows = 3 * feats
     own = hpd * feats
     first = head * feats
@@ -117,69 +119,79 @@
         q_b, k_b, v_b = qkv[slot, 0], qkv[slot, 1], qkv[slot, 2]
         c_b = cts[slot]
         u = dot(a_b, k_b, 0, 0)
+        yield
         square, tanh, half, sech, slope = gelu_parts(u)
         h_b = (u * half).astype(BF)
+        yield
         slope1 = half + 0.5 * u * sech * slope
         second = sech * (GELU_A + (6.0 * GELU_A * GELU_B) * square - u * tanh * slope * slope)
         ht[slot] = h_b
         g1[slot] = slope1
         resid = k_b.astype(F32) - v_b.astype(F32) + dot(b_b, h_b, 1, 0)
         r_b = resid.astype(BF)
+        yield
         rt[slot] = r_b
         p = dot(b_b, r_b, 0, 0)
         g2p[slot] = second * p
         gu_b = (slope1 * p).astype(BF)
         gu[slot] = gu_b
+        yield
         new_a = (a_b.astype(F32) - rate * dot(k_b, gu_b, 1, 1)).astype(BF)
         new_b = (b_b.astype(F32) - rate * dot(r_b, h_b, 1, 1)).astype(BF)
         uq = dot(new_a, q_b, 0, 0)
+        yield
         square, tanh, half, sech, slope = gelu_parts(uq)
         hq_b = (uq * half).astype(BF)
         guq_b = ((half + 0.5 * uq * sech * slope) * dot(new_b, c_b, 0, 0)).astype(BF)
         gab[slot, 0] = dot(q_b, guq_b, 1, 1)
+        yield
         gab[slot, 1] = dot(c_b, hq_b, 1, 1)
         gq[slot, 0] = (c_b.astype(F32) + dot(new_a, guq_b, 1, 0)).astype(BF)
 
-    for slot in range(nseg):
-        local(slot)
-
-    def step(turn, carry):
+    for low in range(0, nseg, GROUP):
+        for _ in zip_longest(*[local(slot) for slot in range(low, min(low + GROUP, nseg))]):
+            pass
+
+    def end(slot, k_b, a_b, ta_b, gu_b, dr, dgu_b, c_a, c_b):
+        left = jnp.concatenate([a_b, ta_b], 1)
+        gk = dr + dot(left, jnp.concatenate([dgu_b, gu_b], 0), 1, 0)
+        gq[slot, 1] = (-rate * gk).astype(BF)
+        gq[slot, 2] = (rate * dr).astype(BF)
+        res[slot, 0] = c_a.astype(BF)
+        res[slot, 1] = c_b.astype(BF)
+
+    c_a = c_b = jnp.zeros((feats, hid), F32)
+    late = None
+    for turn in range(nseg):
         slot = table[nseg - 1 - turn]
-        t_a = carry[0] + gab[slot, 0]
-        t_b = carry[1] + gab[slot, 1]
+        t_a = c_a + gab[slot, 0]
+        t_b = c_b + gab[slot, 1]
         a_b, b_b = wts[slot, 0], wts[slot, 1]
         k_b = qkv[slot, 1]
         h_b, r_b, gu_b = ht[slot], rt[slot], gu[slot]
         ta_b, tb_b = t_a.astype(BF), t_b.astype(BF)
         du = dot(ta_b, k_b, 0, 0)
+        dr_h, dp_r = dot(tb_b, h_b, 1, 0), dot(tb_b, r_b, 0, 0)
+        if late is not None:
+            end(*late)
         dh_b = (g1[slot] * du).astype(BF)
-        dr = dot(b_b, dh_b, 1, 0) + dot(tb_b, h_b, 1, 0)
+        dr = dot(b_b, dh_b, 1, 0) + dr_h
         dr_b = dr.astype(BF)
-        dp = dot(b_b, dr_b, 0, 0) + dot(tb_b, r_b, 0, 0)
+        dp = dot(b_b, dr_b, 0, 0) + dp_r
+        c_b = t_b - rate * (dot(dr_b, h_b, 1, 1) + dot(r_b, dh_b, 1, 1))
         dgu_b = (g2p[slot] * du + g1[slot] * dp).astype(BF)
         c_a = t_a - rate * dot(k_b, dgu_b, 1, 1)
-        c_b = t_b - rate * (dot(dr_b, h_b, 1, 1) + dot(r_b, dh_b, 1, 1))
-        left = jnp.concatenate([a_b, ta_b], 1)
-        gk = dr + dot(left, jnp.concatenate([dgu_b, gu_b], 0), 1, 0)
-        gq[slot, 1] = (-rate * gk).astype(BF)
-        gq[slot, 2] = (rate * dr).astype(BF)
-        wts[slot, 0] = c_a.astype(BF)
-        wts[slot, 1] = c_b.astype(BF)
-        return (c_a, c_b)
-
-    zero = jnp.zeros((feats, hid), F32)
-    carry = (zero, zero)
-    for turn in range(nseg):
-        carry = step(turn, carry)
+        late = (slot, k_b, a_b, ta_b, gu_b, dr, dgu_b, c_a, c_b)
+    end(*late)
 
     for slot in range(nseg):
         dx, dc = slot // CORES, slot % CORES
         if dx == 0:
-            kept[dc] = wts[slot]
+            kept[dc] = res[slot]
         else:
             sent[dx - 1, dc * rows : (dc + 1) * rows] = gq[slot].reshape(rows, tokens)
             at = CORES * rows + dc * 2 * feats
-            sent[dx - 1, at : at + 2 * feats] = wts[slot].reshape(2 * feats, hid)
+            sent[dx - 1, at : at + 2 * feats] = res[slot].reshape(2 * feats, hid)
     for dz in range(nseq):
         at = pl.multiple_of(table[nseg + (nseq - dz) % nseq] * chunk, chunk)
         total = jnp.zeros((rows, chunk), F32)
@@ -380,6 +392,7 @@
                 ((nseg, hid, tokens), F32),
                 ((nseg, hid, tokens), BF),
                 ((nseg, 2, feats, hid), F32),
+                ((nseg, 2, feats, hid), BF),
             ],
             table,
             rates,
@@ -393,8 +406,8 @@
     for head in range(hpd):
         outs = inner(head)
         gp, gq, send, keep = outs[:nseq], outs[nseq], outs[nseq + 1], outs[nseq + 2]
-        if head == hpd - 1:
-            gp, send, pieces, sent = barrier((gp, send, pieces, sent))
+        if pieces is not None:
+            gp, send, pieces[1], sent = barrier((gp, send, pieces[1], sent))
         if pieces is not None:
             total = summed(pieces)
             projs += [total] + [to_chip(total, dx) for dx in range(1, chips)]

time: 109 us -> 107 us (0.982)
  the two profiles are of different devices: /device:TPU:9 before, /device:TPU:0 now
where the time goes in v8:
time: 107 us
  waiting for transfers between devices  42.9 us (40%)
  starting transfers between devices  34.5 us (32%)
  Pallas kernels  26.8 us (25%)
  other arithmetic  1.61 us (2%)
    ppermute x9, waiting for transfers between devices, to_seq(): lax.ppermute(value, 'seq', [(i, (i + dz) % nseq) for i in range(nseq)])  35.7 us
    pallas_call x7, Pallas kernels, kernel(): pl.pallas_call(body, in_specs=[smem if o.ndim == 1 else vmem for o in ope...  24 us
    ppermute x9, starting transfers between devices, to_seq(): lax.ppermute(value, 'seq', [(i, (i + dz) % nseq) for i in range(nseq)])  23.5 us
    ppermute x5, starting transfers between devices, to_chip(): return lax.ppermute(value, 'seg', pairs)  8.58 us
    ppermute x5, waiting for transfers between devices, to_core(): return lax.ppermute(value, 'seg', [(i, i ^ 1) for i in range(nseg)])  4.17 us
    ppermute x5, waiting for transfers between devices, to_chip(): return lax.ppermute(value, 'seg', pairs)  3.04 us
    pallas_call x1, Pallas kernels, per_device(): pl.pallas_call(functools.partial(prep_kernel, dims), in_specs=[pl.BlockSp...  2.77 us
  transfers between devices with their start and end apart: 20, of which 10 were waited for; matrix products, arithmetic and copies ran while one was open for 1% of the time, Pallas kernels for 20%

profile of v8, /device:TPU:0, one launch (start us, length us, event | category | flops | bytes accessed | tf_op | source)
XLA Modules:
  0.0 106.7 jit_solution(1452509674573535101)
XLA Ops:
  0.7 0.1 concatenate.3.table
  0.9 2.8 %prep.1 = (bf16[384,512]{1,0:T(8,128)(2,1)S(1)}, bf16[48,2048]{1,0:T(8,128)(2,1)S(1)}, bf16[304,2048]{1,0:T(8,128)(2,1)S(1)}, bf16[352,2048]{1,0:T(8,128)(2,1)S(1)}) custom-call(s32[14]{0:T(128)S(1)} %concatenate.3.table, bf16[256,2048]{1,0:T(8,128)(2,1)} %bitcast.16, bf16[512,1536]{1,0:T(8,128)(2,1)} %w.1, bf16[256,512]{1,0:T(8,128)(2,1)} %bitcast.32, ...), custom_call_target="tpu_custom_call" | custom-call | tf_op jit(solution)/shard_map/prep/pallas_call | solution.py:346
  3.6 3.0 %collective-permute-start = (bf16[352,2048]{1,0:T(8,128)(2,1)S(1)}, bf16[352,2048]{1,0:T(8,128)(2,1)S(1)}, u32[]{:S(2)}, u32[]{:S(2)}) collective-permute-start(bf16[352,2048]{1,0:T(8,128)(2,1)S(1)} %get-tuple-element.52), channel_id=1, source_target_pairs={{0,2},{1,3},{2,0},{3,1},{4,6},{5,7},{6,4},{7,5},{8,10},{9,11},{10,... | collective-permute-start | bytes 4325384 | tf_op jit(solution)/shard_map/ppermute | solution.py:303
  6.6 0.0 collective-permute-start.1
  6.6 1.6 %collective-permute-start.2 = (bf16[384,512]{1,0:T(8,128)(2,1)S(1)}, bf16[384,512]{1,0:T(8,128)(2,1)S(1)}, u32[]{:S(2)}, u32[]{:S(2)}) collective-permute-start(bf16[384,512]{1,0:T(8,128)(2,1)S(1)} %get-tuple-element.57.refs_4_.refs_6_), channel_id=1, source_target_pairs={{0,4},{4,8},{8,12},{12,0},{1,5},{5,9},{9,13},{13,1},{2,6},{6,10},{... | collective-permute-start | bytes 1179656 | tf_op jit(solution)/shard_map/ppermute | solution.py:309
  8.2 2.6 %collective-permute-start.3 = (bf16[384,512]{1,0:T(8,128)(2,1)S(1)}, bf16[384,512]{1,0:T(8,128)(2,1)S(1)}, u32[]{:S(2)}, u32[]{:S(2)}) collective-permute-start(bf16[384,512]{1,0:T(8,128)(2,1)S(1)} %get-tuple-element.57.refs_4_.refs_6_), channel_id=1, source_target_pairs={{0,8},{4,12},{8,0},{12,4},{1,9},{5,13},{9,1},{13,5},{2,10},{6,14},... | collective-permute-start | bytes 1179656 | tf_op jit(solution)/shard_map/ppermute | solution.py:309
  10.8 1.3 %collective-permute-start.4 = (bf16[384,512]{1,0:T(8,128)(2,1)S(1)}, bf16[384,512]{1,0:T(8,128)(2,1)S(1)}, u32[]{:S(2)}, u32[]{:S(2)}) collective-permute-start(bf16[384,512]{1,0:T(8,128)(2,1)S(1)} %get-tuple-element.57.refs_4_.refs_6_), channel_id=1, source_target_pairs={{0,12},{4,0},{8,4},{12,8},{1,13},{5,1},{9,5},{13,9},{2,14},{6,2},{... | collective-permute-start | bytes 1179656 | tf_op jit(solution)/shard_map/ppermute | solution.py:309
  12.2 8.3 %collective-permute-done.2.refs_5_.refs_7_ = bf16[384,512]{1,0:T(8,128)(2,1)S(1)} collective-permute-done((bf16[384,512]{1,0:T(8,128)(2,1)S(1)}, bf16[384,512]{1,0:T(8,128)(2,1)S(1)}, u32[]{:S(2)}, u32[]{:S(2)}) %collective-permute-start.2) | collective-permute-done | bytes 393248 | tf_op jit(solution)/shard_map/ppermute | solution.py:309
  20.5 16.5 %collective-permute-done.3.refs_6_.refs_8_ = bf16[384,512]{1,0:T(8,128)(2,1)S(1)} collective-permute-done((bf16[384,512]{1,0:T(8,128)(2,1)S(1)}, bf16[384,512]{1,0:T(8,128)(2,1)S(1)}, u32[]{:S(2)}, u32[]{:S(2)}) %collective-permute-start.3) | collective-permute-done | bytes 393248 | tf_op jit(solution)/shard_map/ppermute | solution.py:309
  37.0 0.0 collective-permute-done.1.refs_1_
  37.0 1.2 %collective-permute-done.refs_2_ = bf16[352,2048]{1,0:T(8,128)(2,1)S(1)} collective-permute-done((bf16[352,2048]{1,0:T(8,128)(2,1)S(1)}, bf16[352,2048]{1,0:T(8,128)(2,1)S(1)}, u32[]{:S(2)}, u32[]{:S(2)}) %collective-permute-start) | collective-permute-done | bytes 1441824 | tf_op jit(solution)/shard_map/ppermute | solution.py:303
  38.2 0.0 collective-permute-start.5
  38.2 0.2 pad_maximum_fusion
  38.4 1.8 %collective-permute-start.15 = (bf16[4,384,512]{2,1,0:T(8,128)(2,1)S(1)}, bf16[4,384,512]{2,1,0:T(8,128)(2,1)S(1)}, u32[]{:S(2)}, u32[]{:S(2)}) collective-permute-start(bf16[4,384,512]{2,1,0:T(8,128)(2,1)S(1)} %pad_maximum_fusion), channel_id=1, source_target_pairs={{0,16},{16,0},{1,17},{17,1},{2,18},{18,2},{3,19},{19,3},{4,20},{20... | collective-permute-start | bytes 4718600 | tf_op jit(solution)/shard_map/ppermute | solution.py:372
  40.3 1.2 %collective-permute-done.5.refs_3_ = bf16[352,2048]{1,0:T(8,128)(2,1)S(1)} collective-permute-done((bf16[352,2048]{1,0:T(8,128)(2,1)S(1)}, bf16[352,2048]{1,0:T(8,128)(2,1)S(1)}, u32[]{:S(2)}, u32[]{:S(2)}) %collective-permute-start.5) | collective-permute-done | bytes 1441824 | tf_op jit(solution)/shard_map/ppermute | solution.py:306
  41.5 8.4 %inner.3 = (f32[192,512]{1,0:T(8,128)S(1)}, bf16[192,512]{1,0:T(8,128)(2,1)S(1)}, bf16[192,512]{1,0:T(8,128)(2,1)S(1)}, bf16[192,512]{1,0:T(8,128)(2,1)S(1)}, bf...) custom-call(s32[14]{0:T(128)S(1)} %concatenate.3.table, ...), custom_call_target="tpu_custom_call" | custom-call | tf_op jit(solution)/shard_map/inner/pallas_call | solution.py:314
  49.8 1.8 %collective-permute-start.7 = (bf16[640,256]{1,0:T(8,128)(2,1)S(1)}, bf16[640,256]{1,0:T(8,128)(2,1)S(1)}, u32[]{:S(2)}, u32[]{:S(2)}) collective-permute-start(bf16[640,256]{1,0:T(8,128)(2,1)S(1)} %bitcast.28), channel_id=1, source_target_pairs={{0,2},{1,3},{2,0},{3,1},{4,6},{5,7},{6,4},{7,5},{8,10},{9,11},{10,... | collective-permute-start | bytes 983048 | tf_op jit(solution)/shard_map/ppermute | solution.py:303
  51.6 6.5 %collective-permute-start.6 = (bf16[192,512]{1,0:T(8,128)(2,1)S(1)}, bf16[192,512]{1,0:T(8,128)(2,1)S(1)}, u32[]{:S(2)}, u32[]{:S(2)}) collective-permute-start(bf16[192,512]{1,0:T(8,128)(2,1)S(1)} %get-tuple-element.67), channel_id=1, source_target_pairs={{0,4},{4,8},{8,12},{12,0},{1,5},{5,9},{9,13},{13,1},{2,6},{6,10},{... | collective-permute-start | bytes 589832 | tf_op jit(solution)/shard_map/ppermute | solution.py:309
  58.1 1.7 %collective-permute-start.11 = (bf16[192,512]{1,0:T(8,128)(2,1)S(1)}, bf16[192,512]{1,0:T(8,128)(2,1)S(1)}, u32[]{:S(2)}, u32[]{:S(2)}) collective-permute-start(bf16[192,512]{1,0:T(8,128)(2,1)S(1)} %get-tuple-element.75), channel_id=1, source_target_pairs={{0,8},{4,12},{8,0},{12,4},{1,9},{5,13},{9,1},{13,5},{2,10},{6,14},... | collective-permute-start | bytes 589832 | tf_op jit(solution)/shard_map/ppermute | solution.py:309
  59.8 0.7 collective-permute-start.12
  60.5 8.3 %inner.2 = (f32[192,512]{1,0:T(8,128)S(1)}, bf16[192,512]{1,0:T(8,128)(2,1)S(1)}, bf16[192,512]{1,0:T(8,128)(2,1)S(1)}, bf16[192,512]{1,0:T(8,128)(2,1)S(1)}, bf...) custom-call(s32[14]{0:T(128)S(1)} %concatenate.3.table, ...), custom_call_target="tpu_custom_call" | custom-call | tf_op jit(solution)/shard_map/inner/pallas_call | solution.py:314
  68.8 0.0 collective-permute-done.6.refs_1_
  68.8 0.0 collective-permute-done.7.refs_4_.refs_2_
  68.8 1.5 %collective-permute-start.14 = (bf16[640,256]{1,0:T(8,128)(2,1)S(1)}, bf16[640,256]{1,0:T(8,128)(2,1)S(1)}, u32[]{:S(2)}, u32[]{:S(2)}) collective-permute-start(bf16[640,256]{1,0:T(8,128)(2,1)S(1)} %bitcast.27), channel_id=1, source_target_pairs={{0,2},{1,3},{2,0},{3,1},{4,6},{5,7},{6,4},{7,5},{8,10},{9,11},{10,... | collective-permute-start | bytes 983048 | tf_op jit(solution)/shard_map/ppermute | solution.py:303
  70.4 1.3 %collective-permute-start.8 = (bf16[192,512]{1,0:T(8,128)(2,1)S(1)}, bf16[192,512]{1,0:T(8,128)(2,1)S(1)}, u32[]{:S(2)}, u32[]{:S(2)}) collective-permute-start(bf16[192,512]{1,0:T(8,128)(2,1)S(1)} %get-tuple-element.70), channel_id=1, source_target_pairs={{0,4},{4,8},{8,12},{12,0},{1,5},{5,9},{9,13},{13,1},{2,6},{6,10},{... | collective-permute-start | bytes 589832 | tf_op jit(solution)/shard_map/ppermute | solution.py:309
  71.7 1.0 collective-permute-done.11.refs_2_
  72.7 0.3 collective-permute-start.9
  72.9 7.5 %collective-permute-start.10 = (bf16[192,512]{1,0:T(8,128)(2,1)S(1)}, bf16[192,512]{1,0:T(8,128)(2,1)S(1)}, u32[]{:S(2)}, u32[]{:S(2)}) collective-permute-start(bf16[192,512]{1,0:T(8,128)(2,1)S(1)} %get-tuple-element.72), channel_id=1, source_target_pairs={{0,12},{4,0},{8,4},{12,8},{1,13},{5,1},{9,5},{13,9},{2,14},{6,2},{... | collective-permute-start | bytes 589832 | tf_op jit(solution)/shard_map/ppermute | solution.py:309
  80.5 0.2 sum.2.refs_0_
  80.7 0.0 collective-permute-done.15.refs_10_
  80.7 0.7 collective-permute-start.13
  81.4 0.0 collective-permute-done.14.refs_5_.refs_3_
  81.4 2.4 %input.1 = (f32[256,2048]{1,0:T(8,128)S(1)}, bf16[256,2048]{1,0:T(8,128)(2,1)S(1)}, bf16[4,128,256]{2,1,0:T(8,128)(2,1)S(1)}) custom-call(s32[14]{0:T(128)S(1)} %concatenate.3.table, bf16[4,3,64,256]{3,2,1,0:T(8,128)(2,1)S(1)} %get-tuple-element.77.refs_0_, bf16[4,3,64,256]{3,2,1,0:T(8,128)(2,1)S(1)} %get-tuple-element.78.refs_1_, ...), custom_call_target="tpu_custom_call" | custom-call | bytes 10485760 | tf_op jit(solution)/shard_map/input/pallas_call | solution.py:314
  83.8 5.7 %collective-permute-done.9.refs_2_ = bf16[192,512]{1,0:T(8,128)(2,1)S(1)} collective-permute-done((bf16[192,512]{1,0:T(8,128)(2,1)S(1)}, bf16[192,512]{1,0:T(8,128)(2,1)S(1)}, u32[]{:S(2)}, u32[]{:S(2)}) %collective-permute-start.9) | collective-permute-done | bytes 196640 | tf_op jit(solution)/shard_map/ppermute | solution.py:309
  89.6 4.1 %collective-permute-done.10.refs_3_ = bf16[192,512]{1,0:T(8,128)(2,1)S(1)} collective-permute-done((bf16[192,512]{1,0:T(8,128)(2,1)S(1)}, bf16[192,512]{1,0:T(8,128)(2,1)S(1)}, u32[]{:S(2)}, u32[]{:S(2)}) %collective-permute-start.10) | collective-permute-done | bytes 196640 | tf_op jit(solution)/shard_map/ppermute | solution.py:309
  93.6 0.0 collective-permute-done.13.refs_1_
  93.6 0.0 collective-permute-start.17
  93.7 0.5 collective-permute-start.18
  94.2 0.3 sum.3.refs_2_
  94.4 1.6 %collective-permute-start.16 = (bf16[256,384]{1,0:T(8,128)(2,1)S(1)}, bf16[256,384]{1,0:T(8,128)(2,1)S(1)}, u32[]{:S(2)}, u32[]{:S(2)}) collective-permute-start(bf16[256,384]{1,0:T(8,128)(2,1)S(1)} %sum.3.refs_2_), channel_id=1, source_target_pairs={{0,2},{1,3},{2,0},{3,1},{4,6},{5,7},{6,4},{7,5},{8,10},{9,11},{10,... | collective-permute-start | bytes 589832 | tf_op jit(solution)/shard_map/ppermute | solution.py:303
  96.0 0.7 collective-permute-done.18.refs_4_
  96.7 1.6 %weights.1 = f32[2,8,64,256]{3,2,1,0:T(8,128)} custom-call(s32[14]{0:T(128)S(1)} %concatenate.3.table, bf16[2,2,64,256]{3,2,1,0:T(8,128)(2,1)S(1)} %get-tuple-element.79.refs_2_.refs_0_, bf16[2,2,64,256]{3,2,1,0:T(8,128)(2,1)S(1)} %get-tuple-element.80.refs_3_.refs_1_, bf16[640,256]{1,0:T(8,128)(2,1)S(1)} %collective-permute-done.7.refs_4_.refs_2_, ...), custom_call_target="tpu_custom_call" | custom-call | bytes 10485760 | tf_op jit(solution)/shard_map/weights/pallas_call | solution.py:314
  98.3 1.3 %add_convert_fusion = bf16[256,2048]{1,0:T(8,128)(2,1)} fusion(f32[256,2048]{1,0:T(8,128)S(1)} %get-tuple-element.92, bf16[256,2048]{1,0:T(8,128)(2,1)S(1)} %collective-permute-done.17), kind=kLoop, calls=%fused_computation | loop fusion | flops 1572864 | bytes 4194304 | tf_op jit(solution)/shard_map/convert_element_type | solution.py:439
  99.5 1.8 %collective-permute-done.16.refs_3_ = bf16[256,384]{1,0:T(8,128)(2,1)S(1)} collective-permute-done((bf16[256,384]{1,0:T(8,128)(2,1)S(1)}, bf16[256,384]{1,0:T(8,128)(2,1)S(1)}, u32[]{:S(2)}, u32[]{:S(2)}) %collective-permute-start.16) | collective-permute-done | bytes 196640 | tf_op jit(solution)/shard_map/ppermute | solution.py:303
  101.3 0.1 pad_maximum_fusion.1
  101.5 0.1 collective-permute-start.19
  101.5 2.3 %collective-permute-done.19.refs_4_ = bf16[4,256,384]{2,1,0:T(8,128)(2,1)S(1)} collective-permute-done((bf16[4,256,384]{2,1,0:T(8,128)(2,1)S(1)}, bf16[4,256,384]{2,1,0:T(8,128)(2,1)S(1)}, u32[]{:S(2)}, u32[]{:S(2)}) %collective-permute-start.19) | collective-permute-done | bytes 786464 | tf_op jit(solution)/shard_map/ppermute | solution.py:306
  103.8 2.9 %join.1 = f32[512,1536]{1,0:T(8,128)} custom-call(s32[14]{0:T(128)S(1)} %concatenate.3.table, bf16[256,384]{1,0:T(8,128)(2,1)S(1)} %sum.2.refs_0_, bf16[256,384]{1,0:T(8,128)(2,1)S(1)} %collective-permute-done.13.refs_1_, bf16[256,384]{1,0:T(8,128)(2,1)S(1)} %sum.3.refs_2_, bf16[256,384]{1,0:T(8,128)(2,1)S(1)} %collective-permute-done.16.refs_3_, ...), custom_call_target="tpu_custom_call" | custom-call | tf_op jit(solution)/shard_map/join/pallas_call | solution.py:314
  (10 shorter events, 0.0 us)
Async XLA Ops:
  3.6 34.6 %collective-permute-start = (bf16[352,2048]{1,0:T(8,128)(2,1)S(1)}, bf16[352,2048]{1,0:T(8,128)(2,1)S(1)}, u32[]{:S(2)}, u32[]{:S(2)}) collective-permute-start(bf16[352,2048]{1,0:T(8,128)(2,1)S(1)} %get-tuple-element.52), channel_id=1, source_target_pairs={{0,2},{1,3},{2,0},{3,1},{4,6},{5,7},{6,4},{7,5},{8,10},{9,11},{10,... | collective-permute-start | bytes 4325384 | tf_op jit(solution)/shard_map/ppermute | solution.py:303
  6.6 30.4 %collective-permute-start.1 = (bf16[304,2048]{1,0:T(8,128)(2,1)S(1)}, bf16[304,2048]{1,0:T(8,128)(2,1)S(1)}, u32[]{:S(2)}, u32[]{:S(2)}) collective-permute-start(bf16[304,2048]{1,0:T(8,128)(2,1)S(1)} %get-tuple-element.53), channel_id=1, source_target_pairs={{0,1},{1,0},{2,3},{3,2},{4,5},{5,4},{6,7},{7,6},{8,9},{9,8},{10,11... | collective-permute-start | bytes 3735560 | tf_op jit(solution)/shard_map/ppermute | solution.py:306
  6.6 13.8 %collective-permute-start.2 = (bf16[384,512]{1,0:T(8,128)(2,1)S(1)}, bf16[384,512]{1,0:T(8,128)(2,1)S(1)}, u32[]{:S(2)}, u32[]{:S(2)}) collective-permute-start(bf16[384,512]{1,0:T(8,128)(2,1)S(1)} %get-tuple-element.57.refs_4_.refs_6_), channel_id=1, source_target_pairs={{0,4},{4,8},{8,12},{12,0},{1,5},{5,9},{9,13},{13,1},{2,6},{6,10},{... | collective-permute-start | bytes 1179656 | tf_op jit(solution)/shard_map/ppermute | solution.py:309
  8.2 28.8 %collective-permute-start.3 = (bf16[384,512]{1,0:T(8,128)(2,1)S(1)}, bf16[384,512]{1,0:T(8,128)(2,1)S(1)}, u32[]{:S(2)}, u32[]{:S(2)}) collective-permute-start(bf16[384,512]{1,0:T(8,128)(2,1)S(1)} %get-tuple-element.57.refs_4_.refs_6_), channel_id=1, source_target_pairs={{0,8},{4,12},{8,0},{12,4},{1,9},{5,13},{9,1},{13,5},{2,10},{6,14},... | collective-permute-start | bytes 1179656 | tf_op jit(solution)/shard_map/ppermute | solution.py:309
  10.8 26.2 %collective-permute-start.4 = (bf16[384,512]{1,0:T(8,128)(2,1)S(1)}, bf16[384,512]{1,0:T(8,128)(2,1)S(1)}, u32[]{:S(2)}, u32[]{:S(2)}) collective-permute-start(bf16[384,512]{1,0:T(8,128)(2,1)S(1)} %get-tuple-element.57.refs_4_.refs_6_), channel_id=1, source_target_pairs={{0,12},{4,0},{8,4},{12,8},{1,13},{5,1},{9,5},{13,9},{2,14},{6,2},{... | collective-permute-start | bytes 1179656 | tf_op jit(solution)/shard_map/ppermute | solution.py:309
  38.2 3.2 %collective-permute-start.5 = (bf16[352,2048]{1,0:T(8,128)(2,1)S(1)}, bf16[352,2048]{1,0:T(8,128)(2,1)S(1)}, u32[]{:S(2)}, u32[]{:S(2)}) collective-permute-start(bf16[352,2048]{1,0:T(8,128)(2,1)S(1)} %collective-permute-done.refs_2_), channel_id=1, source_target_pairs={{0,1},{1,0},{2,3},{3,2},{4,5},{5,4},{6,7},{7,6},{8,9},{9,8},{10,11... | collective-permute-start | bytes 4325384 | tf_op jit(solution)/shard_map/ppermute | solution.py:306
  38.2 3.2 %copy-start = (bf16[1,256,2048]{2,1,0:T(8,128)(2,1)S(1)}, bf16[1,256,2048]{2,1,0:T(8,128)(2,1)}, u32[]{:S(2)}) copy-start(bf16[1,256,2048]{2,1,0:T(8,128)(2,1)} %param.5) | copy-start | bytes 3145732
  38.2 3.2 %copy-start.1 = (f32[8]{0:T(128)S(1)}, f32[8]{0:T(128)}, u32[]{:S(2)}) copy-start(f32[8]{0:T(128)} %rates.3) | copy-start | bytes 100
  38.4 42.3 %collective-permute-start.15 = (bf16[4,384,512]{2,1,0:T(8,128)(2,1)S(1)}, bf16[4,384,512]{2,1,0:T(8,128)(2,1)S(1)}, u32[]{:S(2)}, u32[]{:S(2)}) collective-permute-start(bf16[4,384,512]{2,1,0:T(8,128)(2,1)S(1)} %pad_maximum_fusion), channel_id=1, source_target_pairs={{0,16},{16,0},{1,17},{17,1},{2,18},{18,2},{3,19},{19,3},{4,20},{20... | collective-permute-start | bytes 4718600 | tf_op jit(solution)/shard_map/ppermute | solution.py:372
  49.8 19.0 %collective-permute-start.7 = (bf16[640,256]{1,0:T(8,128)(2,1)S(1)}, bf16[640,256]{1,0:T(8,128)(2,1)S(1)}, u32[]{:S(2)}, u32[]{:S(2)}) collective-permute-start(bf16[640,256]{1,0:T(8,128)(2,1)S(1)} %bitcast.28), channel_id=1, source_target_pairs={{0,2},{1,3},{2,0},{3,1},{4,6},{5,7},{6,4},{7,5},{8,10},{9,11},{10,... | collective-permute-start | bytes 983048 | tf_op jit(solution)/shard_map/ppermute | solution.py:303
  51.6 17.2 %collective-permute-start.6 = (bf16[192,512]{1,0:T(8,128)(2,1)S(1)}, bf16[192,512]{1,0:T(8,128)(2,1)S(1)}, u32[]{:S(2)}, u32[]{:S(2)}) collective-permute-start(bf16[192,512]{1,0:T(8,128)(2,1)S(1)} %get-tuple-element.67), channel_id=1, source_target_pairs={{0,4},{4,8},{8,12},{12,0},{1,5},{5,9},{9,13},{13,1},{2,6},{6,10},{... | collective-permute-start | bytes 589832 | tf_op jit(solution)/shard_map/ppermute | solution.py:309
  58.1 14.6 %collective-permute-start.11 = (bf16[192,512]{1,0:T(8,128)(2,1)S(1)}, bf16[192,512]{1,0:T(8,128)(2,1)S(1)}, u32[]{:S(2)}, u32[]{:S(2)}) collective-permute-start(bf16[192,512]{1,0:T(8,128)(2,1)S(1)} %get-tuple-element.75), channel_id=1, source_target_pairs={{0,8},{4,12},{8,0},{12,4},{1,9},{5,13},{9,1},{13,5},{2,10},{6,14},... | collective-permute-start | bytes 589832 | tf_op jit(solution)/shard_map/ppermute | solution.py:309
  59.8 13.2 %collective-permute-start.12 = (bf16[192,512]{1,0:T(8,128)(2,1)S(1)}, bf16[192,512]{1,0:T(8,128)(2,1)S(1)}, u32[]{:S(2)}, u32[]{:S(2)}) collective-permute-start(bf16[192,512]{1,0:T(8,128)(2,1)S(1)} %get-tuple-element.76), channel_id=1, source_target_pairs={{0,12},{4,0},{8,4},{12,8},{1,13},{5,1},{9,5},{13,9},{2,14},{6,2},{... | collective-permute-start | bytes 589832 | tf_op jit(solution)/shard_map/ppermute | solution.py:309
  68.8 12.6 %collective-permute-start.14 = (bf16[640,256]{1,0:T(8,128)(2,1)S(1)}, bf16[640,256]{1,0:T(8,128)(2,1)S(1)}, u32[]{:S(2)}, u32[]{:S(2)}) collective-permute-start(bf16[640,256]{1,0:T(8,128)(2,1)S(1)} %bitcast.27), channel_id=1, source_target_pairs={{0,2},{1,3},{2,0},{3,1},{4,6},{5,7},{6,4},{7,5},{8,10},{9,11},{10,... | collective-permute-start | bytes 983048 | tf_op jit(solution)/shard_map/ppermute | solution.py:303
  70.4 13.4 %collective-permute-start.8 = (bf16[192,512]{1,0:T(8,128)(2,1)S(1)}, bf16[192,512]{1,0:T(8,128)(2,1)S(1)}, u32[]{:S(2)}, u32[]{:S(2)}) collective-permute-start(bf16[192,512]{1,0:T(8,128)(2,1)S(1)} %get-tuple-element.70), channel_id=1, source_target_pairs={{0,4},{4,8},{8,12},{12,0},{1,5},{5,9},{9,13},{13,1},{2,6},{6,10},{... | collective-permute-start | bytes 589832 | tf_op jit(solution)/shard_map/ppermute | solution.py:309
  72.7 16.9 %collective-permute-start.9 = (bf16[192,512]{1,0:T(8,128)(2,1)S(1)}, bf16[192,512]{1,0:T(8,128)(2,1)S(1)}, u32[]{:S(2)}, u32[]{:S(2)}) collective-permute-start(bf16[192,512]{1,0:T(8,128)(2,1)S(1)} %get-tuple-element.71), channel_id=1, source_target_pairs={{0,8},{4,12},{8,0},{12,4},{1,9},{5,13},{9,1},{13,5},{2,10},{6,14},... | collective-permute-start | bytes 589832 | tf_op jit(solution)/shard_map/ppermute | solution.py:309
  72.9 20.7 %collective-permute-start.10 = (bf16[192,512]{1,0:T(8,128)(2,1)S(1)}, bf16[192,512]{1,0:T(8,128)(2,1)S(1)}, u32[]{:S(2)}, u32[]{:S(2)}) collective-permute-start(bf16[192,512]{1,0:T(8,128)(2,1)S(1)} %get-tuple-element.72), channel_id=1, source_target_pairs={{0,12},{4,0},{8,4},{12,8},{1,13},{5,1},{9,5},{13,9},{2,14},{6,2},{... | collective-permute-start | bytes 589832 | tf_op jit(solution)/shard_map/ppermute | solution.py:309
  80.7 12.9 %collective-permute-start.13 = (bf16[256,384]{1,0:T(8,128)(2,1)S(1)}, bf16[256,384]{1,0:T(8,128)(2,1)S(1)}, u32[]{:S(2)}, u32[]{:S(2)}) collective-permute-start(bf16[256,384]{1,0:T(8,128)(2,1)S(1)} %sum.2.refs_0_), channel_id=1, source_target_pairs={{0,2},{1,3},{2,0},{3,1},{4,6},{5,7},{6,4},{7,5},{8,10},{9,11},{10,... | collective-permute-start | bytes 589832 | tf_op jit(solution)/shard_map/ppermute | solution.py:303
  93.6 4.6 %collective-permute-start.17 = (bf16[256,2048]{1,0:T(8,128)(2,1)S(1)}, bf16[256,2048]{1,0:T(8,128)(2,1)S(1)}, u32[]{:S(2)}, u32[]{:S(2)}) collective-permute-start(bf16[256,2048]{1,0:T(8,128)(2,1)S(1)} %get-tuple-element.93), channel_id=1, source_target_pairs={{0,1},{1,0},{2,3},{3,2},{4,5},{5,4},{6,7},{7,6},{8,9},{9,8},{10,11... | collective-permute-start | bytes 3145736 | tf_op jit(solution)/shard_map/ppermute | solution.py:306
  93.7 3.0 %collective-permute-start.18 = (bf16[4,128,256]{2,1,0:T(8,128)(2,1)S(1)}, bf16[4,128,256]{2,1,0:T(8,128)(2,1)S(1)}, u32[]{:S(2)}, u32[]{:S(2)}) collective-permute-start(bf16[4,128,256]{2,1,0:T(8,128)(2,1)S(1)} %get-tuple-element.94), channel_id=1, source_target_pairs={{0,1},{1,0},{2,3},{3,2},{4,5},{5,4},{6,7},{7,6},{8,9},{9,8},{10,11... | collective-permute-start | bytes 786440 | tf_op jit(solution)/shard_map/ppermute | solution.py:306
  94.4 6.9 %collective-permute-start.16 = (bf16[256,384]{1,0:T(8,128)(2,1)S(1)}, bf16[256,384]{1,0:T(8,128)(2,1)S(1)}, u32[]{:S(2)}, u32[]{:S(2)}) collective-permute-start(bf16[256,384]{1,0:T(8,128)(2,1)S(1)} %sum.3.refs_2_), channel_id=1, source_target_pairs={{0,2},{1,3},{2,0},{3,1},{4,6},{5,7},{6,4},{7,5},{8,10},{9,11},{10,... | collective-permute-start | bytes 589832 | tf_op jit(solution)/shard_map/ppermute | solution.py:303
  101.5 2.4 %collective-permute-start.19 = (bf16[4,256,384]{2,1,0:T(8,128)(2,1)S(1)}, bf16[4,256,384]{2,1,0:T(8,128)(2,1)S(1)}, u32[]{:S(2)}, u32[]{:S(2)}) collective-permute-start(bf16[4,256,384]{2,1,0:T(8,128)(2,1)S(1)} %pad_maximum_fusion.1), channel_id=1, source_target_pairs={{0,1},{1,0},{2,3},{3,2},{4,5},{5,4},{6,7},{7,6},{8,9},{9,8},{10,11... | collective-permute-start | bytes 2359304 | tf_op jit(solution)/shard_map/ppermute | solution.py:306

commit v9 on v8

--- a/solution.py
+++ b/solution.py
@@ -89,10 +89,15 @@
     wt, refs = refs[:nseq], refs[nseq:]
     pack, refs = refs[0], refs[1:]
     gp, refs = refs[:nseq], refs[nseq:]
-    gq, sent, kept, qkv, wts, cts, ht, rt, g1, g2p, gu, gab, res = refs
+    gq, sent, kept, qkv, wts, cts, ht, rt, g1, g2p, gu, gab, res, wide = refs
     rows = 3 * feats
     own = hpd * feats
     first = head * feats
+    for back in range(nseq):
+        at = pl.multiple_of(table[nseg + back] * chunk, chunk)
+        for p in range(3):
+            block = wt[back][p * own + first : p * own + first + feats]
+            wide[p * feats : (p + 1) * feats, pl.ds(at, chunk)] = block
 
     deep = pack.shape[0]
 
@@ -104,13 +109,7 @@
                 top, left = packed((i * hpd + head) * feats + j, deep, hid)
                 value = source[low + top : low + top + TILE, left : left + hid]
                 piece[j : j + TILE] = value
-        total = jnp.zeros((rows, tokens), F32)
-        for back in range(nseq):
-            at = pl.multiple_of(table[nseg + back] * chunk, chunk)
-            left = jnp.concatenate(
-                [wt[back][p * own + first : p * own + first + feats] for p in range(3)]
-            )
-            total += dot(left, li[slot][:tokens, pl.ds(at, chunk)], 1, 1)
+        total = dot(wide[...], li[slot][:tokens], 1, 1)
         qkv[slot] = total.astype(BF).reshape(3, feats, tokens)
     rate = rates[table[nseg + nseq] + head] * (1.0 / MB)
 
@@ -242,25 +241,36 @@
 def join_kernel(dims, table, *refs):
     nseg, nseq, hpd, feats, hid, tokens, chunk = dims
     chips = nseg // CORES
-    far, near, out = refs[: hpd * chips], refs[hpd * chips], refs[hpd * chips + 1]
+    far, near, out, whole, sem = refs[: hpd * chips], *refs[hpd * chips :]
     wide = CORES * hpd * feats
     half = chunk // 2
     me = table[nseg + nseq + 1]
     chip = me // CORES
     even = me % CORES == 0
+    copies = []
     for dx in range(chips):
         source = (chip - dx + chips) % chips
         for side in range(2):
             cut = slice(side * 3 * feats, (side + 1) * 3 * feats)
             mine = [far[h * chips + dx][:, cut].astype(F32) for h in range(hpd)]
             other = [near[h * chips + dx, :, cut].astype(F32) for h in range(hpd)]
+            mine, other = (
+                [jnp.where(even, a, b) for a, b in zip(mine, other)],
+                [jnp.where(even, b, a) for a, b in zip(mine, other)],
+            )
             for part in range(3):
                 cut = slice(part * feats, (part + 1) * feats)
-                a = jnp.concatenate([value[:, cut] for value in mine + other], 1)
-                b = jnp.concatenate([value[:, cut] for value in other + mine], 1)
+                whole[dx, side, part] = jnp.concatenate([v[:, cut] for v in mine + other], 1)
                 at = pl.multiple_of((part * nseg * hpd * feats) + source * wide, wide)
-                rows = pl.ds(side * half, half)
-                out[rows, pl.ds(at, wide)] = jnp.where(even, a, b)
+                copy = pltpu.make_async_copy(
+                    whole.at[dx, side, part],
+                    out.at[pl.ds(side * half, half), pl.ds(at, wide)],
+                    sem.at[len(copies)],
+                )
+                copy.start()
+                copies.append(copy)
+    for copy in copies:
+        copy.wait()
 
 
 def weights_kernel(dims, table, *refs):
@@ -393,6 +403,7 @@
                 ((nseg, hid, tokens), BF),
                 ((nseg, 2, feats, hid), F32),
                 ((nseg, 2, feats, hid), BF),
+                ((3 * feats, width), BF),
             ],
             table,
             rates,
@@ -450,17 +461,20 @@
         leave,
     )
     projs, grad_input, grad_inner = barrier((projs, grad_input, grad_inner))
-    (grad_proj,) = kernel(
+    near = to_core(jnp.stack(projs))
+    grad_proj = pl.pallas_call(
         functools.partial(join_kernel, dims),
-        "join",
-        16,
-        0,
-        [((chunk, 3 * heads * feats), F32)],
-        [],
-        table,
-        *projs,
-        to_core(jnp.stack(projs)),
-    )
+        in_specs=[pl.BlockSpec(memory_space=pltpu.SMEM)] + [vmem] * (hpd * chips + 1),
+        out_specs=hbm,
+        out_shape=jax.ShapeDtypeStruct((chunk, 3 * heads * feats), F32),
+        scratch_shapes=[
+            pltpu.VMEM((chips, 2, 3, chunk // 2, CORES * own), F32),
+            pltpu.SemaphoreType.DMA((6 * chips,)),
+        ],
+        compiler_params=pltpu.CompilerParams(vmem_limit_bytes=16 * MIB),
+        cost_estimate=pl.CostEstimate(flops=0, bytes_accessed=0, transcendentals=0),
+        name="join",
+    )(table, *projs, near)
     return (grad_input[None], grad_proj, grad_inner[None, None])
 
 

time: 107 us -> 107 us (level)
    pallas_call x7 -> x6, Pallas kernels: 24 us -> 21.1 us  [kernel(): pl.pallas_call(body, in_specs=[smem if o.ndim == 1 else vmem for o in ope...]
    pallas_call x0 -> x1, Pallas kernels: none -> 2.49 us  [per_device(): pl.pallas_call(functools.partial(join_kernel, dims), in_specs=[pl.BlockSp...]
where the time goes in v9:
time: 107 us; the launch traced here: 106 us
  waiting for transfers between devices  42.8 us (40%)
  starting transfers between devices  34.5 us (32%)
  Pallas kernels  26.4 us (25%)
  other arithmetic  1.61 us (2%)
    ppermute x9, waiting for transfers between devices, to_seq(): lax.ppermute(value, 'seq', [(i, (i + dz) % nseq) for i in range(nseq)])  35.6 us
    ppermute x9, starting transfers between devices, to_seq(): lax.ppermute(value, 'seq', [(i, (i + dz) % nseq) for i in range(nseq)])  23.5 us
    pallas_call x6, Pallas kernels, kernel(): pl.pallas_call(body, in_specs=[smem if o.ndim == 1 else vmem for o in ope...  21.1 us
    ppermute x5, starting transfers between devices, to_chip(): return lax.ppermute(value, 'seg', pairs)  8.61 us
    ppermute x5, waiting for transfers between devices, to_core(): return lax.ppermute(value, 'seg', [(i, i ^ 1) for i in range(nseg)])  4.17 us
    ppermute x5, waiting for transfers between devices, to_chip(): return lax.ppermute(value, 'seg', pairs)  3.04 us
    pallas_call x1, Pallas kernels, per_device(): pl.pallas_call(functools.partial(prep_kernel, dims), in_specs=[pl.BlockSp...  2.77 us
    pallas_call x1, Pallas kernels, per_device(): pl.pallas_call(functools.partial(join_kernel, dims), in_specs=[pl.BlockSp...  2.49 us
  transfers between devices with their start and end apart: 20, of which 10 were waited for; matrix products, arithmetic and copies ran while one was open for 1% of the time, Pallas kernels for 20%

profile of v9, /device:TPU:0, one launch (start us, length us, event | category | flops | bytes accessed | tf_op | source)
XLA Modules:
  0.0 106.5 jit_solution(5266196119518262385)
XLA Ops:
  0.7 0.1 concatenate.3.table
  0.9 2.8 %prep.1 = (bf16[384,512]{1,0:T(8,128)(2,1)S(1)}, bf16[48,2048]{1,0:T(8,128)(2,1)S(1)}, bf16[304,2048]{1,0:T(8,128)(2,1)S(1)}, bf16[352,2048]{1,0:T(8,128)(2,1)S(1)}) custom-call(s32[14]{0:T(128)S(1)} %concatenate.3.table, bf16[256,2048]{1,0:T(8,128)(2,1)} %bitcast.16, bf16[512,1536]{1,0:T(8,128)(2,1)} %w.1, bf16[256,512]{1,0:T(8,128)(2,1)} %bitcast.32, ...), custom_call_target="tpu_custom_call" | custom-call | tf_op jit(solution)/shard_map/prep/pallas_call | solution.py:356
  3.6 3.0 %collective-permute-start = (bf16[352,2048]{1,0:T(8,128)(2,1)S(1)}, bf16[352,2048]{1,0:T(8,128)(2,1)S(1)}, u32[]{:S(2)}, u32[]{:S(2)}) collective-permute-start(bf16[352,2048]{1,0:T(8,128)(2,1)S(1)} %get-tuple-element.52), channel_id=1, source_target_pairs={{0,2},{1,3},{2,0},{3,1},{4,6},{5,7},{6,4},{7,5},{8,10},{9,11},{10,... | collective-permute-start | bytes 4325384 | tf_op jit(solution)/shard_map/ppermute | solution.py:313
  6.6 0.0 collective-permute-start.1
  6.6 1.6 %collective-permute-start.2 = (bf16[384,512]{1,0:T(8,128)(2,1)S(1)}, bf16[384,512]{1,0:T(8,128)(2,1)S(1)}, u32[]{:S(2)}, u32[]{:S(2)}) collective-permute-start(bf16[384,512]{1,0:T(8,128)(2,1)S(1)} %get-tuple-element.57.refs_4_.refs_6_), channel_id=1, source_target_pairs={{0,4},{4,8},{8,12},{12,0},{1,5},{5,9},{9,13},{13,1},{2,6},{6,10},{... | collective-permute-start | bytes 1179656 | tf_op jit(solution)/shard_map/ppermute | solution.py:319
  8.2 2.6 %collective-permute-start.3 = (bf16[384,512]{1,0:T(8,128)(2,1)S(1)}, bf16[384,512]{1,0:T(8,128)(2,1)S(1)}, u32[]{:S(2)}, u32[]{:S(2)}) collective-permute-start(bf16[384,512]{1,0:T(8,128)(2,1)S(1)} %get-tuple-element.57.refs_4_.refs_6_), channel_id=1, source_target_pairs={{0,8},{4,12},{8,0},{12,4},{1,9},{5,13},{9,1},{13,5},{2,10},{6,14},... | collective-permute-start | bytes 1179656 | tf_op jit(solution)/shard_map/ppermute | solution.py:319
  10.8 1.3 %collective-permute-start.4 = (bf16[384,512]{1,0:T(8,128)(2,1)S(1)}, bf16[384,512]{1,0:T(8,128)(2,1)S(1)}, u32[]{:S(2)}, u32[]{:S(2)}) collective-permute-start(bf16[384,512]{1,0:T(8,128)(2,1)S(1)} %get-tuple-element.57.refs_4_.refs_6_), channel_id=1, source_target_pairs={{0,12},{4,0},{8,4},{12,8},{1,13},{5,1},{9,5},{13,9},{2,14},{6,2},{... | collective-permute-start | bytes 1179656 | tf_op jit(solution)/shard_map/ppermute | solution.py:319
  12.2 8.3 %collective-permute-done.2.refs_5_.refs_7_ = bf16[384,512]{1,0:T(8,128)(2,1)S(1)} collective-permute-done((bf16[384,512]{1,0:T(8,128)(2,1)S(1)}, bf16[384,512]{1,0:T(8,128)(2,1)S(1)}, u32[]{:S(2)}, u32[]{:S(2)}) %collective-permute-start.2) | collective-permute-done | bytes 393248 | tf_op jit(solution)/shard_map/ppermute | solution.py:319
  20.5 16.5 %collective-permute-done.3.refs_6_.refs_8_ = bf16[384,512]{1,0:T(8,128)(2,1)S(1)} collective-permute-done((bf16[384,512]{1,0:T(8,128)(2,1)S(1)}, bf16[384,512]{1,0:T(8,128)(2,1)S(1)}, u32[]{:S(2)}, u32[]{:S(2)}) %collective-permute-start.3) | collective-permute-done | bytes 393248 | tf_op jit(solution)/shard_map/ppermute | solution.py:319
  37.0 0.0 collective-permute-done.4.refs_7_.refs_9_
  37.0 0.0 collective-permute-done.1.refs_1_
  37.0 1.2 %collective-permute-done.refs_2_ = bf16[352,2048]{1,0:T(8,128)(2,1)S(1)} collective-permute-done((bf16[352,2048]{1,0:T(8,128)(2,1)S(1)}, bf16[352,2048]{1,0:T(8,128)(2,1)S(1)}, u32[]{:S(2)}, u32[]{:S(2)}) %collective-permute-start) | collective-permute-done | bytes 1441824 | tf_op jit(solution)/shard_map/ppermute | solution.py:313
  38.2 0.2 pad_maximum_fusion
  38.4 1.8 %collective-permute-start.15 = (bf16[4,384,512]{2,1,0:T(8,128)(2,1)S(1)}, bf16[4,384,512]{2,1,0:T(8,128)(2,1)S(1)}, u32[]{:S(2)}, u32[]{:S(2)}) collective-permute-start(bf16[4,384,512]{2,1,0:T(8,128)(2,1)S(1)} %pad_maximum_fusion), channel_id=1, source_target_pairs={{0,16},{16,0},{1,17},{17,1},{2,18},{18,2},{3,19},{19,3},{4,20},{20... | collective-permute-start | bytes 4718600 | tf_op jit(solution)/shard_map/ppermute | solution.py:382
  40.3 1.2 %collective-permute-done.5.refs_3_ = bf16[352,2048]{1,0:T(8,128)(2,1)S(1)} collective-permute-done((bf16[352,2048]{1,0:T(8,128)(2,1)S(1)}, bf16[352,2048]{1,0:T(8,128)(2,1)S(1)}, u32[]{:S(2)}, u32[]{:S(2)}) %collective-permute-start.5) | collective-permute-done | bytes 1441824 | tf_op jit(solution)/shard_map/ppermute | solution.py:316
  41.5 8.4 %inner.3 = (f32[192,512]{1,0:T(8,128)S(1)}, bf16[192,512]{1,0:T(8,128)(2,1)S(1)}, bf16[192,512]{1,0:T(8,128)(2,1)S(1)}, bf16[192,512]{1,0:T(8,128)(2,1)S(1)}, bf...) custom-call(s32[14]{0:T(128)S(1)} %concatenate.3.table, ...), custom_call_target="tpu_custom_call" | custom-call | tf_op jit(solution)/shard_map/inner/pallas_call | solution.py:324
  49.8 1.8 %collective-permute-start.7 = (bf16[640,256]{1,0:T(8,128)(2,1)S(1)}, bf16[640,256]{1,0:T(8,128)(2,1)S(1)}, u32[]{:S(2)}, u32[]{:S(2)}) collective-permute-start(bf16[640,256]{1,0:T(8,128)(2,1)S(1)} %bitcast.28), channel_id=1, source_target_pairs={{0,2},{1,3},{2,0},{3,1},{4,6},{5,7},{6,4},{7,5},{8,10},{9,11},{10,... | collective-permute-start | bytes 983048 | tf_op jit(solution)/shard_map/ppermute | solution.py:313
  51.6 6.5 %collective-permute-start.6 = (bf16[192,512]{1,0:T(8,128)(2,1)S(1)}, bf16[192,512]{1,0:T(8,128)(2,1)S(1)}, u32[]{:S(2)}, u32[]{:S(2)}) collective-permute-start(bf16[192,512]{1,0:T(8,128)(2,1)S(1)} %get-tuple-element.67), channel_id=1, source_target_pairs={{0,4},{4,8},{8,12},{12,0},{1,5},{5,9},{9,13},{13,1},{2,6},{6,10},{... | collective-permute-start | bytes 589832 | tf_op jit(solution)/shard_map/ppermute | solution.py:319
  58.1 1.7 %collective-permute-start.11 = (bf16[192,512]{1,0:T(8,128)(2,1)S(1)}, bf16[192,512]{1,0:T(8,128)(2,1)S(1)}, u32[]{:S(2)}, u32[]{:S(2)}) collective-permute-start(bf16[192,512]{1,0:T(8,128)(2,1)S(1)} %get-tuple-element.75), channel_id=1, source_target_pairs={{0,8},{4,12},{8,0},{12,4},{1,9},{5,13},{9,1},{13,5},{2,10},{6,14},... | collective-permute-start | bytes 589832 | tf_op jit(solution)/shard_map/ppermute | solution.py:319
  59.8 0.7 collective-permute-start.12
  60.5 8.3 %inner.2 = (f32[192,512]{1,0:T(8,128)S(1)}, bf16[192,512]{1,0:T(8,128)(2,1)S(1)}, bf16[192,512]{1,0:T(8,128)(2,1)S(1)}, bf16[192,512]{1,0:T(8,128)(2,1)S(1)}, bf...) custom-call(s32[14]{0:T(128)S(1)} %concatenate.3.table, ...), custom_call_target="tpu_custom_call" | custom-call | tf_op jit(solution)/shard_map/inner/pallas_call | solution.py:324
  68.8 0.0 collective-permute-done.6.refs_1_
  68.9 1.6 %collective-permute-start.14 = (bf16[640,256]{1,0:T(8,128)(2,1)S(1)}, bf16[640,256]{1,0:T(8,128)(2,1)S(1)}, u32[]{:S(2)}, u32[]{:S(2)}) collective-permute-start(bf16[640,256]{1,0:T(8,128)(2,1)S(1)} %bitcast.27), channel_id=1, source_target_pairs={{0,2},{1,3},{2,0},{3,1},{4,6},{5,7},{6,4},{7,5},{8,10},{9,11},{10,... | collective-permute-start | bytes 983048 | tf_op jit(solution)/shard_map/ppermute | solution.py:313
  70.4 1.3 %collective-permute-start.8 = (bf16[192,512]{1,0:T(8,128)(2,1)S(1)}, bf16[192,512]{1,0:T(8,128)(2,1)S(1)}, u32[]{:S(2)}, u32[]{:S(2)}) collective-permute-start(bf16[192,512]{1,0:T(8,128)(2,1)S(1)} %get-tuple-element.70), channel_id=1, source_target_pairs={{0,4},{4,8},{8,12},{12,0},{1,5},{5,9},{9,13},{13,1},{2,6},{6,10},{... | collective-permute-start | bytes 589832 | tf_op jit(solution)/shard_map/ppermute | solution.py:319
  71.7 0.9 collective-permute-done.11.refs_2_
  72.7 0.3 collective-permute-start.9
  73.0 7.5 %collective-permute-start.10 = (bf16[192,512]{1,0:T(8,128)(2,1)S(1)}, bf16[192,512]{1,0:T(8,128)(2,1)S(1)}, u32[]{:S(2)}, u32[]{:S(2)}) collective-permute-start(bf16[192,512]{1,0:T(8,128)(2,1)S(1)} %get-tuple-element.72), channel_id=1, source_target_pairs={{0,12},{4,0},{8,4},{12,8},{1,13},{5,1},{9,5},{13,9},{2,14},{6,2},{... | collective-permute-start | bytes 589832 | tf_op jit(solution)/shard_map/ppermute | solution.py:319
  80.5 0.2 sum.2.refs_0_
  80.7 0.0 collective-permute-done.15.refs_10_
  80.8 0.7 collective-permute-start.13
  81.5 0.0 collective-permute-done.14.refs_5_.refs_3_
  81.5 2.4 %input.1 = (f32[256,2048]{1,0:T(8,128)S(1)}, bf16[256,2048]{1,0:T(8,128)(2,1)S(1)}, bf16[4,128,256]{2,1,0:T(8,128)(2,1)S(1)}) custom-call(s32[14]{0:T(128)S(1)} %concatenate.3.table, bf16[4,3,64,256]{3,2,1,0:T(8,128)(2,1)S(1)} %get-tuple-element.77.refs_0_, bf16[4,3,64,256]{3,2,1,0:T(8,128)(2,1)S(1)} %get-tuple-element.78.refs_1_, ...), custom_call_target="tpu_custom_call" | custom-call | bytes 10485760 | tf_op jit(solution)/shard_map/input/pallas_call | solution.py:324
  83.8 0.0 collective-permute-done.8.refs_1_
  83.8 5.7 %collective-permute-done.9.refs_2_ = bf16[192,512]{1,0:T(8,128)(2,1)S(1)} collective-permute-done((bf16[192,512]{1,0:T(8,128)(2,1)S(1)}, bf16[192,512]{1,0:T(8,128)(2,1)S(1)}, u32[]{:S(2)}, u32[]{:S(2)}) %collective-permute-start.9) | collective-permute-done | bytes 196640 | tf_op jit(solution)/shard_map/ppermute | solution.py:319
  89.6 4.1 %collective-permute-done.10.refs_3_ = bf16[192,512]{1,0:T(8,128)(2,1)S(1)} collective-permute-done((bf16[192,512]{1,0:T(8,128)(2,1)S(1)}, bf16[192,512]{1,0:T(8,128)(2,1)S(1)}, u32[]{:S(2)}, u32[]{:S(2)}) %collective-permute-start.10) | collective-permute-done | bytes 196640 | tf_op jit(solution)/shard_map/ppermute | solution.py:319
  93.6 0.0 collective-permute-done.13.refs_1_
  93.6 0.0 collective-permute-start.17
  93.7 0.5 collective-permute-start.18
  94.2 0.3 sum.3.refs_2_
  94.4 1.6 %collective-permute-start.16 = (bf16[256,384]{1,0:T(8,128)(2,1)S(1)}, bf16[256,384]{1,0:T(8,128)(2,1)S(1)}, u32[]{:S(2)}, u32[]{:S(2)}) collective-permute-start(bf16[256,384]{1,0:T(8,128)(2,1)S(1)} %sum.3.refs_2_), channel_id=1, source_target_pairs={{0,2},{1,3},{2,0},{3,1},{4,6},{5,7},{6,4},{7,5},{8,10},{9,11},{10,... | collective-permute-start | bytes 589832 | tf_op jit(solution)/shard_map/ppermute | solution.py:313
  96.0 0.7 collective-permute-done.18.refs_4_
  96.7 1.6 %weights.1 = f32[2,8,64,256]{3,2,1,0:T(8,128)} custom-call(s32[14]{0:T(128)S(1)} %concatenate.3.table, bf16[2,2,64,256]{3,2,1,0:T(8,128)(2,1)S(1)} %get-tuple-element.79.refs_2_.refs_0_, bf16[2,2,64,256]{3,2,1,0:T(8,128)(2,1)S(1)} %get-tuple-element.80.refs_3_.refs_1_, bf16[640,256]{1,0:T(8,128)(2,1)S(1)} %collective-permute-done.7.refs_4_.refs_2_, ...), custom_call_target="tpu_custom_call" | custom-call | bytes 10485760 | tf_op jit(solution)/shard_map/weights/pallas_call | solution.py:324
  98.3 1.3 %add_convert_fusion = bf16[256,2048]{1,0:T(8,128)(2,1)} fusion(f32[256,2048]{1,0:T(8,128)S(1)} %get-tuple-element.92, bf16[256,2048]{1,0:T(8,128)(2,1)S(1)} %collective-permute-done.17), kind=kLoop, calls=%fused_computation | loop fusion | flops 1572864 | bytes 4194304 | tf_op jit(solution)/shard_map/convert_element_type | solution.py:450
  99.5 1.8 %collective-permute-done.16.refs_3_ = bf16[256,384]{1,0:T(8,128)(2,1)S(1)} collective-permute-done((bf16[256,384]{1,0:T(8,128)(2,1)S(1)}, bf16[256,384]{1,0:T(8,128)(2,1)S(1)}, u32[]{:S(2)}, u32[]{:S(2)}) %collective-permute-start.16) | collective-permute-done | bytes 196640 | tf_op jit(solution)/shard_map/ppermute | solution.py:313
  101.3 0.1 pad_maximum_fusion.1
  101.5 0.1 collective-permute-start.19
  101.5 2.3 %collective-permute-done.19.refs_4_ = bf16[4,256,384]{2,1,0:T(8,128)(2,1)S(1)} collective-permute-done((bf16[4,256,384]{2,1,0:T(8,128)(2,1)S(1)}, bf16[4,256,384]{2,1,0:T(8,128)(2,1)S(1)}, u32[]{:S(2)}, u32[]{:S(2)}) %collective-permute-start.19) | collective-permute-done | bytes 786464 | tf_op jit(solution)/shard_map/ppermute | solution.py:316
  103.8 2.5 %join.1 = f32[512,1536]{1,0:T(8,128)} custom-call(s32[14]{0:T(128)S(1)} %concatenate.3.table, bf16[256,384]{1,0:T(8,128)(2,1)S(1)} %sum.2.refs_0_, bf16[256,384]{1,0:T(8,128)(2,1)S(1)} %collective-permute-done.13.refs_1_, bf16[256,384]{1,0:T(8,128)(2,1)S(1)} %sum.3.refs_2_, bf16[256,384]{1,0:T(8,128)(2,1)S(1)} %collective-permute-done.16.refs_3_, ...), custom_call_target="tpu_custom_call" | custom-call | tf_op jit(solution)/shard_map/join/pallas_call | solution.py:465
  (10 shorter events, 0.0 us)
Async XLA Ops:
  3.6 34.6 %collective-permute-start = (bf16[352,2048]{1,0:T(8,128)(2,1)S(1)}, bf16[352,2048]{1,0:T(8,128)(2,1)S(1)}, u32[]{:S(2)}, u32[]{:S(2)}) collective-permute-start(bf16[352,2048]{1,0:T(8,128)(2,1)S(1)} %get-tuple-element.52), channel_id=1, source_target_pairs={{0,2},{1,3},{2,0},{3,1},{4,6},{5,7},{6,4},{7,5},{8,10},{9,11},{10,... | collective-permute-start | bytes 4325384 | tf_op jit(solution)/shard_map/ppermute | solution.py:313
  6.6 30.4 %collective-permute-start.1 = (bf16[304,2048]{1,0:T(8,128)(2,1)S(1)}, bf16[304,2048]{1,0:T(8,128)(2,1)S(1)}, u32[]{:S(2)}, u32[]{:S(2)}) collective-permute-start(bf16[304,2048]{1,0:T(8,128)(2,1)S(1)} %get-tuple-element.53), channel_id=1, source_target_pairs={{0,1},{1,0},{2,3},{3,2},{4,5},{5,4},{6,7},{7,6},{8,9},{9,8},{10,11... | collective-permute-start | bytes 3735560 | tf_op jit(solution)/shard_map/ppermute | solution.py:316
  6.6 13.8 %collective-permute-start.2 = (bf16[384,512]{1,0:T(8,128)(2,1)S(1)}, bf16[384,512]{1,0:T(8,128)(2,1)S(1)}, u32[]{:S(2)}, u32[]{:S(2)}) collective-permute-start(bf16[384,512]{1,0:T(8,128)(2,1)S(1)} %get-tuple-element.57.refs_4_.refs_6_), channel_id=1, source_target_pairs={{0,4},{4,8},{8,12},{12,0},{1,5},{5,9},{9,13},{13,1},{2,6},{6,10},{... | collective-permute-start | bytes 1179656 | tf_op jit(solution)/shard_map/ppermute | solution.py:319
  8.2 28.8 %collective-permute-start.3 = (bf16[384,512]{1,0:T(8,128)(2,1)S(1)}, bf16[384,512]{1,0:T(8,128)(2,1)S(1)}, u32[]{:S(2)}, u32[]{:S(2)}) collective-permute-start(bf16[384,512]{1,0:T(8,128)(2,1)S(1)} %get-tuple-element.57.refs_4_.refs_6_), channel_id=1, source_target_pairs={{0,8},{4,12},{8,0},{12,4},{1,9},{5,13},{9,1},{13,5},{2,10},{6,14},... | collective-permute-start | bytes 1179656 | tf_op jit(solution)/shard_map/ppermute | solution.py:319
  10.8 26.2 %collective-permute-start.4 = (bf16[384,512]{1,0:T(8,128)(2,1)S(1)}, bf16[384,512]{1,0:T(8,128)(2,1)S(1)}, u32[]{:S(2)}, u32[]{:S(2)}) collective-permute-start(bf16[384,512]{1,0:T(8,128)(2,1)S(1)} %get-tuple-element.57.refs_4_.refs_6_), channel_id=1, source_target_pairs={{0,12},{4,0},{8,4},{12,8},{1,13},{5,1},{9,5},{13,9},{2,14},{6,2},{... | collective-permute-start | bytes 1179656 | tf_op jit(solution)/shard_map/ppermute | solution.py:319
  38.2 3.2 %collective-permute-start.5 = (bf16[352,2048]{1,0:T(8,128)(2,1)S(1)}, bf16[352,2048]{1,0:T(8,128)(2,1)S(1)}, u32[]{:S(2)}, u32[]{:S(2)}) collective-permute-start(bf16[352,2048]{1,0:T(8,128)(2,1)S(1)} %collective-permute-done.refs_2_), channel_id=1, source_target_pairs={{0,1},{1,0},{2,3},{3,2},{4,5},{5,4},{6,7},{7,6},{8,9},{9,8},{10,11... | collective-permute-start | bytes 4325384 | tf_op jit(solution)/shard_map/ppermute | solution.py:316
  38.2 3.2 %copy-start = (bf16[1,256,2048]{2,1,0:T(8,128)(2,1)S(1)}, bf16[1,256,2048]{2,1,0:T(8,128)(2,1)}, u32[]{:S(2)}) copy-start(bf16[1,256,2048]{2,1,0:T(8,128)(2,1)} %param.5) | copy-start | bytes 3145732
  38.2 3.2 %copy-start.1 = (f32[8]{0:T(128)S(1)}, f32[8]{0:T(128)}, u32[]{:S(2)}) copy-start(f32[8]{0:T(128)} %rates.3) | copy-start | bytes 100
  38.4 42.3 %collective-permute-start.15 = (bf16[4,384,512]{2,1,0:T(8,128)(2,1)S(1)}, bf16[4,384,512]{2,1,0:T(8,128)(2,1)S(1)}, u32[]{:S(2)}, u32[]{:S(2)}) collective-permute-start(bf16[4,384,512]{2,1,0:T(8,128)(2,1)S(1)} %pad_maximum_fusion), channel_id=1, source_target_pairs={{0,16},{16,0},{1,17},{17,1},{2,18},{18,2},{3,19},{19,3},{4,20},{20... | collective-permute-start | bytes 4718600 | tf_op jit(solution)/shard_map/ppermute | solution.py:382
  49.8 19.0 %collective-permute-start.7 = (bf16[640,256]{1,0:T(8,128)(2,1)S(1)}, bf16[640,256]{1,0:T(8,128)(2,1)S(1)}, u32[]{:S(2)}, u32[]{:S(2)}) collective-permute-start(bf16[640,256]{1,0:T(8,128)(2,1)S(1)} %bitcast.28), channel_id=1, source_target_pairs={{0,2},{1,3},{2,0},{3,1},{4,6},{5,7},{6,4},{7,5},{8,10},{9,11},{10,... | collective-permute-start | bytes 983048 | tf_op jit(solution)/shard_map/ppermute | solution.py:313
  51.6 17.2 %collective-permute-start.6 = (bf16[192,512]{1,0:T(8,128)(2,1)S(1)}, bf16[192,512]{1,0:T(8,128)(2,1)S(1)}, u32[]{:S(2)}, u32[]{:S(2)}) collective-permute-start(bf16[192,512]{1,0:T(8,128)(2,1)S(1)} %get-tuple-element.67), channel_id=1, source_target_pairs={{0,4},{4,8},{8,12},{12,0},{1,5},{5,9},{9,13},{13,1},{2,6},{6,10},{... | collective-permute-start | bytes 589832 | tf_op jit(solution)/shard_map/ppermute | solution.py:319
  58.1 14.6 %collective-permute-start.11 = (bf16[192,512]{1,0:T(8,128)(2,1)S(1)}, bf16[192,512]{1,0:T(8,128)(2,1)S(1)}, u32[]{:S(2)}, u32[]{:S(2)}) collective-permute-start(bf16[192,512]{1,0:T(8,128)(2,1)S(1)} %get-tuple-element.75), channel_id=1, source_target_pairs={{0,8},{4,12},{8,0},{12,4},{1,9},{5,13},{9,1},{13,5},{2,10},{6,14},... | collective-permute-start | bytes 589832 | tf_op jit(solution)/shard_map/ppermute | solution.py:319
  59.8 13.2 %collective-permute-start.12 = (bf16[192,512]{1,0:T(8,128)(2,1)S(1)}, bf16[192,512]{1,0:T(8,128)(2,1)S(1)}, u32[]{:S(2)}, u32[]{:S(2)}) collective-permute-start(bf16[192,512]{1,0:T(8,128)(2,1)S(1)} %get-tuple-element.76), channel_id=1, source_target_pairs={{0,12},{4,0},{8,4},{12,8},{1,13},{5,1},{9,5},{13,9},{2,14},{6,2},{... | collective-permute-start | bytes 589832 | tf_op jit(solution)/shard_map/ppermute | solution.py:319
  68.9 12.6 %collective-permute-start.14 = (bf16[640,256]{1,0:T(8,128)(2,1)S(1)}, bf16[640,256]{1,0:T(8,128)(2,1)S(1)}, u32[]{:S(2)}, u32[]{:S(2)}) collective-permute-start(bf16[640,256]{1,0:T(8,128)(2,1)S(1)} %bitcast.27), channel_id=1, source_target_pairs={{0,2},{1,3},{2,0},{3,1},{4,6},{5,7},{6,4},{7,5},{8,10},{9,11},{10,... | collective-permute-start | bytes 983048 | tf_op jit(solution)/shard_map/ppermute | solution.py:313
  70.4 13.4 %collective-permute-start.8 = (bf16[192,512]{1,0:T(8,128)(2,1)S(1)}, bf16[192,512]{1,0:T(8,128)(2,1)S(1)}, u32[]{:S(2)}, u32[]{:S(2)}) collective-permute-start(bf16[192,512]{1,0:T(8,128)(2,1)S(1)} %get-tuple-element.70), channel_id=1, source_target_pairs={{0,4},{4,8},{8,12},{12,0},{1,5},{5,9},{9,13},{13,1},{2,6},{6,10},{... | collective-permute-start | bytes 589832 | tf_op jit(solution)/shard_map/ppermute | solution.py:319
  72.7 16.9 %collective-permute-start.9 = (bf16[192,512]{1,0:T(8,128)(2,1)S(1)}, bf16[192,512]{1,0:T(8,128)(2,1)S(1)}, u32[]{:S(2)}, u32[]{:S(2)}) collective-permute-start(bf16[192,512]{1,0:T(8,128)(2,1)S(1)} %get-tuple-element.71), channel_id=1, source_target_pairs={{0,8},{4,12},{8,0},{12,4},{1,9},{5,13},{9,1},{13,5},{2,10},{6,14},... | collective-permute-start | bytes 589832 | tf_op jit(solution)/shard_map/ppermute | solution.py:319
  73.0 20.6 %collective-permute-start.10 = (bf16[192,512]{1,0:T(8,128)(2,1)S(1)}, bf16[192,512]{1,0:T(8,128)(2,1)S(1)}, u32[]{:S(2)}, u32[]{:S(2)}) collective-permute-start(bf16[192,512]{1,0:T(8,128)(2,1)S(1)} %get-tuple-element.72), channel_id=1, source_target_pairs={{0,12},{4,0},{8,4},{12,8},{1,13},{5,1},{9,5},{13,9},{2,14},{6,2},{... | collective-permute-start | bytes 589832 | tf_op jit(solution)/shard_map/ppermute | solution.py:319
  80.8 12.9 %collective-permute-start.13 = (bf16[256,384]{1,0:T(8,128)(2,1)S(1)}, bf16[256,384]{1,0:T(8,128)(2,1)S(1)}, u32[]{:S(2)}, u32[]{:S(2)}) collective-permute-start(bf16[256,384]{1,0:T(8,128)(2,1)S(1)} %sum.2.refs_0_), channel_id=1, source_target_pairs={{0,2},{1,3},{2,0},{3,1},{4,6},{5,7},{6,4},{7,5},{8,10},{9,11},{10,... | collective-permute-start | bytes 589832 | tf_op jit(solution)/shard_map/ppermute | solution.py:313
  93.6 4.6 %collective-permute-start.17 = (bf16[256,2048]{1,0:T(8,128)(2,1)S(1)}, bf16[256,2048]{1,0:T(8,128)(2,1)S(1)}, u32[]{:S(2)}, u32[]{:S(2)}) collective-permute-start(bf16[256,2048]{1,0:T(8,128)(2,1)S(1)} %get-tuple-element.93), channel_id=1, source_target_pairs={{0,1},{1,0},{2,3},{3,2},{4,5},{5,4},{6,7},{7,6},{8,9},{9,8},{10,11... | collective-permute-start | bytes 3145736 | tf_op jit(solution)/shard_map/ppermute | solution.py:316
  93.7 3.0 %collective-permute-start.18 = (bf16[4,128,256]{2,1,0:T(8,128)(2,1)S(1)}, bf16[4,128,256]{2,1,0:T(8,128)(2,1)S(1)}, u32[]{:S(2)}, u32[]{:S(2)}) collective-permute-start(bf16[4,128,256]{2,1,0:T(8,128)(2,1)S(1)} %get-tuple-element.94), channel_id=1, source_target_pairs={{0,1},{1,0},{2,3},{3,2},{4,5},{5,4},{6,7},{7,6},{8,9},{9,8},{10,11... | collective-permute-start | bytes 786440 | tf_op jit(solution)/shard_map/ppermute | solution.py:316
  94.4 6.9 %collective-permute-start.16 = (bf16[256,384]{1,0:T(8,128)(2,1)S(1)}, bf16[256,384]{1,0:T(8,128)(2,1)S(1)}, u32[]{:S(2)}, u32[]{:S(2)}) collective-permute-start(bf16[256,384]{1,0:T(8,128)(2,1)S(1)} %sum.3.refs_2_), channel_id=1, source_target_pairs={{0,2},{1,3},{2,0},{3,1},{4,6},{5,7},{6,4},{7,5},{8,10},{9,11},{10,... | collective-permute-start | bytes 589832 | tf_op jit(solution)/shard_map/ppermute | solution.py:313
  101.5 2.4 %collective-permute-start.19 = (bf16[4,256,384]{2,1,0:T(8,128)(2,1)S(1)}, bf16[4,256,384]{2,1,0:T(8,128)(2,1)S(1)}, u32[]{:S(2)}, u32[]{:S(2)}) collective-permute-start(bf16[4,256,384]{2,1,0:T(8,128)(2,1)S(1)} %pad_maximum_fusion.1), channel_id=1, source_target_pairs={{0,1},{1,0},{2,3},{3,2},{4,5},{5,4},{6,7},{7,6},{8,9},{9,8},{10,11... | collective-permute-start | bytes 2359304 | tf_op jit(solution)/shard_map/ppermute | solution.py:316

commit v10 on v9

--- a/solution.py
+++ b/solution.py
@@ -418,7 +418,7 @@
         outs = inner(head)
         gp, gq, send, keep = outs[:nseq], outs[nseq], outs[nseq + 1], outs[nseq + 2]
         if pieces is not None:
-            gp, send, pieces[1], sent = barrier((gp, send, pieces[1], sent))
+            gp, send, pieces[nseq // 2], sent = barrier((gp, send, pieces[nseq // 2], sent))
         if pieces is not None:
             total = summed(pieces)
             projs += [total] + [to_chip(total, dx) for dx in range(1, chips)]

time: 107 us -> 104 us (0.972)
  the two profiles are of different devices: /device:TPU:0 before, /device:TPU:9 now
where the time goes in v10:
time: 104 us
  waiting for transfers between devices  56.5 us (54%)
  Pallas kernels  26.4 us (25%)
  starting transfers between devices  18.1 us (17%)
  other arithmetic  1.61 us (2%)
    ppermute x9, waiting for transfers between devices, to_seq(): lax.ppermute(value, 'seq', [(i, (i + dz) % nseq) for i in range(nseq)])  46.7 us
    pallas_call x6, Pallas kernels, kernel(): pl.pallas_call(body, in_specs=[smem if o.ndim == 1 else vmem for o in ope...  21.1 us
    ppermute x9, starting transfers between devices, to_seq(): lax.ppermute(value, 'seq', [(i, (i + dz) % nseq) for i in range(nseq)])  10 us
    ppermute x5, waiting for transfers between devices, to_core(): return lax.ppermute(value, 'seg', [(i, i ^ 1) for i in range(nseg)])  5.31 us
    ppermute x1, waiting for transfers between devices, to_others(): return [lax.ppermute(value, 'groups', [(0, 1), (1, 0)])]  3.6 us
    ppermute x5, starting transfers between devices, to_chip(): return lax.ppermute(value, 'seg', pairs)  3.44 us
    ppermute x5, starting transfers between devices, to_core(): return lax.ppermute(value, 'seg', [(i, i ^ 1) for i in range(nseg)])  3.3 us
    pallas_call x1, Pallas kernels, per_device(): pl.pallas_call(functools.partial(prep_kernel, dims), in_specs=[pl.BlockSp...  2.77 us
  transfers between devices with their start and end apart: 20, of which 12 were waited for; matrix products, arithmetic and copies ran while one was open for 1% of the time, Pallas kernels for 20%

profile of v10, /device:TPU:9, one launch (start us, length us, event | category | flops | bytes accessed | tf_op | source)
XLA Modules:
  0.0 103.6 jit_solution(14189993709593262408)
XLA Ops:
  0.7 0.1 concatenate.3.table
  0.9 2.8 %prep.1 = (bf16[384,512]{1,0:T(8,128)(2,1)S(1)}, bf16[48,2048]{1,0:T(8,128)(2,1)S(1)}, bf16[304,2048]{1,0:T(8,128)(2,1)S(1)}, bf16[352,2048]{1,0:T(8,128)(2,1)S(1)}) custom-call(s32[14]{0:T(128)S(1)} %concatenate.3.table, bf16[256,2048]{1,0:T(8,128)(2,1)} %bitcast.16, bf16[512,1536]{1,0:T(8,128)(2,1)} %w.1, bf16[256,512]{1,0:T(8,128)(2,1)} %bitcast.32, ...), custom_call_target="tpu_custom_call" | custom-call | tf_op jit(solution)/shard_map/prep/pallas_call | solution.py:356
  3.6 1.3 %collective-permute-start = (bf16[352,2048]{1,0:T(8,128)(2,1)S(1)}, bf16[352,2048]{1,0:T(8,128)(2,1)S(1)}, u32[]{:S(2)}, u32[]{:S(2)}) collective-permute-start(bf16[352,2048]{1,0:T(8,128)(2,1)S(1)} %get-tuple-element.52), channel_id=1, source_target_pairs={{0,2},{1,3},{2,0},{3,1},{4,6},{5,7},{6,4},{7,5},{8,10},{9,11},{10,... | collective-permute-start | bytes 4325384 | tf_op jit(solution)/shard_map/ppermute | solution.py:313
  4.9 0.9 collective-permute-start.1
  5.9 1.3 %collective-permute-start.2 = (bf16[384,512]{1,0:T(8,128)(2,1)S(1)}, bf16[384,512]{1,0:T(8,128)(2,1)S(1)}, u32[]{:S(2)}, u32[]{:S(2)}) collective-permute-start(bf16[384,512]{1,0:T(8,128)(2,1)S(1)} %get-tuple-element.57.refs_4_.refs_6_), channel_id=1, source_target_pairs={{0,4},{4,8},{8,12},{12,0},{1,5},{5,9},{9,13},{13,1},{2,6},{6,10},{... | collective-permute-start | bytes 1179656 | tf_op jit(solution)/shard_map/ppermute | solution.py:319
  7.2 1.0 collective-permute-start.3
  8.2 1.5 %collective-permute-start.4 = (bf16[384,512]{1,0:T(8,128)(2,1)S(1)}, bf16[384,512]{1,0:T(8,128)(2,1)S(1)}, u32[]{:S(2)}, u32[]{:S(2)}) collective-permute-start(bf16[384,512]{1,0:T(8,128)(2,1)S(1)} %get-tuple-element.57.refs_4_.refs_6_), channel_id=1, source_target_pairs={{0,12},{4,0},{8,4},{12,8},{1,13},{5,1},{9,5},{13,9},{2,14},{6,2},{... | collective-permute-start | bytes 1179656 | tf_op jit(solution)/shard_map/ppermute | solution.py:319
  9.6 7.0 %collective-permute-done.2.refs_5_.refs_7_ = bf16[384,512]{1,0:T(8,128)(2,1)S(1)} collective-permute-done((bf16[384,512]{1,0:T(8,128)(2,1)S(1)}, bf16[384,512]{1,0:T(8,128)(2,1)S(1)}, u32[]{:S(2)}, u32[]{:S(2)}) %collective-permute-start.2) | collective-permute-done | bytes 393248 | tf_op jit(solution)/shard_map/ppermute | solution.py:319
  16.6 24.4 %collective-permute-done.3.refs_6_.refs_8_ = bf16[384,512]{1,0:T(8,128)(2,1)S(1)} collective-permute-done((bf16[384,512]{1,0:T(8,128)(2,1)S(1)}, bf16[384,512]{1,0:T(8,128)(2,1)S(1)}, u32[]{:S(2)}, u32[]{:S(2)}) %collective-permute-start.3) | collective-permute-done | bytes 393248 | tf_op jit(solution)/shard_map/ppermute | solution.py:319
  41.0 2.1 %collective-permute-done.4.refs_7_.refs_9_ = bf16[384,512]{1,0:T(8,128)(2,1)S(1)} collective-permute-done((bf16[384,512]{1,0:T(8,128)(2,1)S(1)}, bf16[384,512]{1,0:T(8,128)(2,1)S(1)}, u32[]{:S(2)}, u32[]{:S(2)}) %collective-permute-start.4) | collective-permute-done | bytes 393248 | tf_op jit(solution)/shard_map/ppermute | solution.py:319
  43.1 0.0 collective-permute-done.1.refs_1_
  43.1 0.0 collective-permute-done.refs_2_
  43.1 0.5 collective-permute-start.5
  43.6 0.2 pad_maximum_fusion
  43.8 1.3 %collective-permute-start.15 = (bf16[4,384,512]{2,1,0:T(8,128)(2,1)S(1)}, bf16[4,384,512]{2,1,0:T(8,128)(2,1)S(1)}, u32[]{:S(2)}, u32[]{:S(2)}) collective-permute-start(bf16[4,384,512]{2,1,0:T(8,128)(2,1)S(1)} %pad_maximum_fusion), channel_id=1, source_target_pairs={{0,16},{16,0},{1,17},{17,1},{2,18},{18,2},{3,19},{19,3},{4,20},{20... | collective-permute-start | bytes 4718600 | tf_op jit(solution)/shard_map/ppermute | solution.py:382
  45.1 1.3 %collective-permute-done.5.refs_3_ = bf16[352,2048]{1,0:T(8,128)(2,1)S(1)} collective-permute-done((bf16[352,2048]{1,0:T(8,128)(2,1)S(1)}, bf16[352,2048]{1,0:T(8,128)(2,1)S(1)}, u32[]{:S(2)}, u32[]{:S(2)}) %collective-permute-start.5) | collective-permute-done | bytes 1441824 | tf_op jit(solution)/shard_map/ppermute | solution.py:316
  46.4 8.3 %inner.3 = (f32[192,512]{1,0:T(8,128)S(1)}, bf16[192,512]{1,0:T(8,128)(2,1)S(1)}, bf16[192,512]{1,0:T(8,128)(2,1)S(1)}, bf16[192,512]{1,0:T(8,128)(2,1)S(1)}, bf...) custom-call(s32[14]{0:T(128)S(1)} %concatenate.3.table, ...), custom_call_target="tpu_custom_call" | custom-call | tf_op jit(solution)/shard_map/inner/pallas_call | solution.py:324
  54.8 0.3 collective-permute-start.7
  55.1 1.4 %collective-permute-start.6 = (bf16[192,512]{1,0:T(8,128)(2,1)S(1)}, bf16[192,512]{1,0:T(8,128)(2,1)S(1)}, u32[]{:S(2)}, u32[]{:S(2)}) collective-permute-start(bf16[192,512]{1,0:T(8,128)(2,1)S(1)} %get-tuple-element.67), channel_id=1, source_target_pairs={{0,8},{4,12},{8,0},{12,4},{1,9},{5,13},{9,1},{13,5},{2,10},{6,14},... | collective-permute-start | bytes 589832 | tf_op jit(solution)/shard_map/ppermute | solution.py:319
  56.5 0.0 collective-permute-start.11
  56.5 1.5 %collective-permute-start.12 = (bf16[192,512]{1,0:T(8,128)(2,1)S(1)}, bf16[192,512]{1,0:T(8,128)(2,1)S(1)}, u32[]{:S(2)}, u32[]{:S(2)}) collective-permute-start(bf16[192,512]{1,0:T(8,128)(2,1)S(1)} %get-tuple-element.76), channel_id=1, source_target_pairs={{0,12},{4,0},{8,4},{12,8},{1,13},{5,1},{9,5},{13,9},{2,14},{6,2},{... | collective-permute-start | bytes 589832 | tf_op jit(solution)/shard_map/ppermute | solution.py:319
  57.9 8.4 %inner.2 = (f32[192,512]{1,0:T(8,128)S(1)}, bf16[192,512]{1,0:T(8,128)(2,1)S(1)}, bf16[192,512]{1,0:T(8,128)(2,1)S(1)}, bf16[192,512]{1,0:T(8,128)(2,1)S(1)}, bf...) custom-call(s32[14]{0:T(128)S(1)} %concatenate.3.table, ...), custom_call_target="tpu_custom_call" | custom-call | tf_op jit(solution)/shard_map/inner/pallas_call | solution.py:324
  66.3 0.0 collective-permute-done.6.refs_2_
  66.3 0.0 collective-permute-done.7.refs_4_.refs_2_
  66.3 1.3 %collective-permute-start.14 = (bf16[640,256]{1,0:T(8,128)(2,1)S(1)}, bf16[640,256]{1,0:T(8,128)(2,1)S(1)}, u32[]{:S(2)}, u32[]{:S(2)}) collective-permute-start(bf16[640,256]{1,0:T(8,128)(2,1)S(1)} %bitcast.27), channel_id=1, source_target_pairs={{0,2},{1,3},{2,0},{3,1},{4,6},{5,7},{6,4},{7,5},{8,10},{9,11},{10,... | collective-permute-start | bytes 983048 | tf_op jit(solution)/shard_map/ppermute | solution.py:313
  67.6 0.0 collective-permute-start.8
  67.6 5.0 %collective-permute-done.11.refs_1_ = bf16[192,512]{1,0:T(8,128)(2,1)S(1)} collective-permute-done((bf16[192,512]{1,0:T(8,128)(2,1)S(1)}, bf16[192,512]{1,0:T(8,128)(2,1)S(1)}, u32[]{:S(2)}, u32[]{:S(2)}) %collective-permute-start.11) | collective-permute-done | bytes 196640 | tf_op jit(solution)/shard_map/ppermute | solution.py:319
  72.6 3.4 %collective-permute-start.10 = (bf16[192,512]{1,0:T(8,128)(2,1)S(1)}, bf16[192,512]{1,0:T(8,128)(2,1)S(1)}, u32[]{:S(2)}, u32[]{:S(2)}) collective-permute-start(bf16[192,512]{1,0:T(8,128)(2,1)S(1)} %get-tuple-element.72), channel_id=1, source_target_pairs={{0,12},{4,0},{8,4},{12,8},{1,13},{5,1},{9,5},{13,9},{2,14},{6,2},{... | collective-permute-start | bytes 589832 | tf_op jit(solution)/shard_map/ppermute | solution.py:319
  76.0 0.2 sum.2.refs_0_
  76.2 3.6 %collective-permute-done.15.refs_10_ = bf16[4,384,512]{2,1,0:T(8,128)(2,1)S(1)} collective-permute-done((bf16[4,384,512]{2,1,0:T(8,128)(2,1)S(1)}, bf16[4,384,512]{2,1,0:T(8,128)(2,1)S(1)}, u32[]{:S(2)}, u32[]{:S(2)}) %collective-permute-start.15) | collective-permute-done | bytes 1572896 | tf_op jit(solution)/shard_map/ppermute | solution.py:382
  79.8 0.3 collective-permute-start.13
  80.1 2.4 %input.1 = (f32[256,2048]{1,0:T(8,128)S(1)}, bf16[256,2048]{1,0:T(8,128)(2,1)S(1)}, bf16[4,128,256]{2,1,0:T(8,128)(2,1)S(1)}) custom-call(s32[14]{0:T(128)S(1)} %concatenate.3.table, bf16[4,3,64,256]{3,2,1,0:T(8,128)(2,1)S(1)} %get-tuple-element.77.refs_0_, bf16[4,3,64,256]{3,2,1,0:T(8,128)(2,1)S(1)} %get-tuple-element.78.refs_1_, ...), custom_call_target="tpu_custom_call" | custom-call | bytes 10485760 | tf_op jit(solution)/shard_map/input/pallas_call | solution.py:324
  82.5 2.6 %collective-permute-done.8.refs_1_ = bf16[192,512]{1,0:T(8,128)(2,1)S(1)} collective-permute-done((bf16[192,512]{1,0:T(8,128)(2,1)S(1)}, bf16[192,512]{1,0:T(8,128)(2,1)S(1)}, u32[]{:S(2)}, u32[]{:S(2)}) %collective-permute-start.8) | collective-permute-done | bytes 196640 | tf_op jit(solution)/shard_map/ppermute | solution.py:319
  85.1 4.4 %collective-permute-done.9.refs_2_ = bf16[192,512]{1,0:T(8,128)(2,1)S(1)} collective-permute-done((bf16[192,512]{1,0:T(8,128)(2,1)S(1)}, bf16[192,512]{1,0:T(8,128)(2,1)S(1)}, u32[]{:S(2)}, u32[]{:S(2)}) %collective-permute-start.9) | collective-permute-done | bytes 196640 | tf_op jit(solution)/shard_map/ppermute | solution.py:319
  89.4 1.3 %collective-permute-done.10.refs_3_ = bf16[192,512]{1,0:T(8,128)(2,1)S(1)} collective-permute-done((bf16[192,512]{1,0:T(8,128)(2,1)S(1)}, bf16[192,512]{1,0:T(8,128)(2,1)S(1)}, u32[]{:S(2)}, u32[]{:S(2)}) %collective-permute-start.10) | collective-permute-done | bytes 196640 | tf_op jit(solution)/shard_map/ppermute | solution.py:319
  90.7 0.0 collective-permute-done.13.refs_1_
  90.7 0.5 collective-permute-start.17
  91.2 0.0 collective-permute-start.18
  91.2 0.3 sum.3.refs_2_
  91.5 0.3 collective-permute-start.16
  91.8 2.1 %collective-permute-done.18.refs_4_ = bf16[4,128,256]{2,1,0:T(8,128)(2,1)S(1)} collective-permute-done((bf16[4,128,256]{2,1,0:T(8,128)(2,1)S(1)}, bf16[4,128,256]{2,1,0:T(8,128)(2,1)S(1)}, u32[]{:S(2)}, u32[]{:S(2)}) %collective-permute-start.18) | collective-permute-done | bytes 262176 | tf_op jit(solution)/shard_map/ppermute | solution.py:316
  93.8 1.6 %weights.1 = f32[2,8,64,256]{3,2,1,0:T(8,128)} custom-call(s32[14]{0:T(128)S(1)} %concatenate.3.table, bf16[2,2,64,256]{3,2,1,0:T(8,128)(2,1)S(1)} %get-tuple-element.79.refs_2_.refs_0_, bf16[2,2,64,256]{3,2,1,0:T(8,128)(2,1)S(1)} %get-tuple-element.80.refs_3_.refs_1_, bf16[640,256]{1,0:T(8,128)(2,1)S(1)} %collective-permute-done.7.refs_4_.refs_2_, ...), custom_call_target="tpu_custom_call" | custom-call | bytes 10485760 | tf_op jit(solution)/shard_map/weights/pallas_call | solution.py:324
  95.4 1.3 %add_convert_fusion = bf16[256,2048]{1,0:T(8,128)(2,1)} fusion(f32[256,2048]{1,0:T(8,128)S(1)} %get-tuple-element.92, bf16[256,2048]{1,0:T(8,128)(2,1)S(1)} %collective-permute-done.17), kind=kLoop, calls=%fused_computation | loop fusion | flops 1572864 | bytes 4194304 | tf_op jit(solution)/shard_map/convert_element_type | solution.py:450
  96.7 0.9 collective-permute-done.16.refs_3_
  97.5 0.1 pad_maximum_fusion.1
  97.7 1.4 %collective-permute-start.19 = (bf16[4,256,384]{2,1,0:T(8,128)(2,1)S(1)}, bf16[4,256,384]{2,1,0:T(8,128)(2,1)S(1)}, u32[]{:S(2)}, u32[]{:S(2)}) collective-permute-start(bf16[4,256,384]{2,1,0:T(8,128)(2,1)S(1)} %pad_maximum_fusion.1), channel_id=1, source_target_pairs={{0,1},{1,0},{2,3},{3,2},{4,5},{5,4},{6,7},{7,6},{8,9},{9,8},{10,11... | collective-permute-start | bytes 2359304 | tf_op jit(solution)/shard_map/ppermute | solution.py:316
  99.0 1.9 %collective-permute-done.19.refs_4_ = bf16[4,256,384]{2,1,0:T(8,128)(2,1)S(1)} collective-permute-done((bf16[4,256,384]{2,1,0:T(8,128)(2,1)S(1)}, bf16[4,256,384]{2,1,0:T(8,128)(2,1)S(1)}, u32[]{:S(2)}, u32[]{:S(2)}) %collective-permute-start.19) | collective-permute-done | bytes 786464 | tf_op jit(solution)/shard_map/ppermute | solution.py:316
  101.0 2.5 %join.1 = f32[512,1536]{1,0:T(8,128)} custom-call(s32[14]{0:T(128)S(1)} %concatenate.3.table, bf16[256,384]{1,0:T(8,128)(2,1)S(1)} %sum.2.refs_0_, bf16[256,384]{1,0:T(8,128)(2,1)S(1)} %collective-permute-done.13.refs_1_, bf16[256,384]{1,0:T(8,128)(2,1)S(1)} %sum.3.refs_2_, bf16[256,384]{1,0:T(8,128)(2,1)S(1)} %collective-permute-done.16.refs_3_, ...), custom_call_target="tpu_custom_call" | custom-call | tf_op jit(solution)/shard_map/join/pallas_call | solution.py:465
  (10 shorter events, 0.0 us)
Async XLA Ops:
  3.6 39.5 %collective-permute-start = (bf16[352,2048]{1,0:T(8,128)(2,1)S(1)}, bf16[352,2048]{1,0:T(8,128)(2,1)S(1)}, u32[]{:S(2)}, u32[]{:S(2)}) collective-permute-start(bf16[352,2048]{1,0:T(8,128)(2,1)S(1)} %get-tuple-element.52), channel_id=1, source_target_pairs={{0,2},{1,3},{2,0},{3,1},{4,6},{5,7},{6,4},{7,5},{8,10},{9,11},{10,... | collective-permute-start | bytes 4325384 | tf_op jit(solution)/shard_map/ppermute | solution.py:313
  4.9 38.2 %collective-permute-start.1 = (bf16[304,2048]{1,0:T(8,128)(2,1)S(1)}, bf16[304,2048]{1,0:T(8,128)(2,1)S(1)}, u32[]{:S(2)}, u32[]{:S(2)}) collective-permute-start(bf16[304,2048]{1,0:T(8,128)(2,1)S(1)} %get-tuple-element.53), channel_id=1, source_target_pairs={{0,1},{1,0},{2,3},{3,2},{4,5},{5,4},{6,7},{7,6},{8,9},{9,8},{10,11... | collective-permute-start | bytes 3735560 | tf_op jit(solution)/shard_map/ppermute | solution.py:316
  5.9 10.7 %collective-permute-start.2 = (bf16[384,512]{1,0:T(8,128)(2,1)S(1)}, bf16[384,512]{1,0:T(8,128)(2,1)S(1)}, u32[]{:S(2)}, u32[]{:S(2)}) collective-permute-start(bf16[384,512]{1,0:T(8,128)(2,1)S(1)} %get-tuple-element.57.refs_4_.refs_6_), channel_id=1, source_target_pairs={{0,4},{4,8},{8,12},{12,0},{1,5},{5,9},{9,13},{13,1},{2,6},{6,10},{... | collective-permute-start | bytes 1179656 | tf_op jit(solution)/shard_map/ppermute | solution.py:319
  7.2 33.8 %collective-permute-start.3 = (bf16[384,512]{1,0:T(8,128)(2,1)S(1)}, bf16[384,512]{1,0:T(8,128)(2,1)S(1)}, u32[]{:S(2)}, u32[]{:S(2)}) collective-permute-start(bf16[384,512]{1,0:T(8,128)(2,1)S(1)} %get-tuple-element.57.refs_4_.refs_6_), channel_id=1, source_target_pairs={{0,8},{4,12},{8,0},{12,4},{1,9},{5,13},{9,1},{13,5},{2,10},{6,14},... | collective-permute-start | bytes 1179656 | tf_op jit(solution)/shard_map/ppermute | solution.py:319
  8.2 34.9 %collective-permute-start.4 = (bf16[384,512]{1,0:T(8,128)(2,1)S(1)}, bf16[384,512]{1,0:T(8,128)(2,1)S(1)}, u32[]{:S(2)}, u32[]{:S(2)}) collective-permute-start(bf16[384,512]{1,0:T(8,128)(2,1)S(1)} %get-tuple-element.57.refs_4_.refs_6_), channel_id=1, source_target_pairs={{0,12},{4,0},{8,4},{12,8},{1,13},{5,1},{9,5},{13,9},{2,14},{6,2},{... | collective-permute-start | bytes 1179656 | tf_op jit(solution)/shard_map/ppermute | solution.py:319
  43.1 3.3 %collective-permute-start.5 = (bf16[352,2048]{1,0:T(8,128)(2,1)S(1)}, bf16[352,2048]{1,0:T(8,128)(2,1)S(1)}, u32[]{:S(2)}, u32[]{:S(2)}) collective-permute-start(bf16[352,2048]{1,0:T(8,128)(2,1)S(1)} %collective-permute-done.refs_2_), channel_id=1, source_target_pairs={{0,1},{1,0},{2,3},{3,2},{4,5},{5,4},{6,7},{7,6},{8,9},{9,8},{10,11... | collective-permute-start | bytes 4325384 | tf_op jit(solution)/shard_map/ppermute | solution.py:316
  43.6 2.9 %copy-start = (bf16[1,256,2048]{2,1,0:T(8,128)(2,1)S(1)}, bf16[1,256,2048]{2,1,0:T(8,128)(2,1)}, u32[]{:S(2)}) copy-start(bf16[1,256,2048]{2,1,0:T(8,128)(2,1)} %param.5) | copy-start | bytes 3145732
  43.6 2.9 %copy-start.1 = (f32[8]{0:T(128)S(1)}, f32[8]{0:T(128)}, u32[]{:S(2)}) copy-start(f32[8]{0:T(128)} %rates.3) | copy-start | bytes 100
  43.8 36.0 %collective-permute-start.15 = (bf16[4,384,512]{2,1,0:T(8,128)(2,1)S(1)}, bf16[4,384,512]{2,1,0:T(8,128)(2,1)S(1)}, u32[]{:S(2)}, u32[]{:S(2)}) collective-permute-start(bf16[4,384,512]{2,1,0:T(8,128)(2,1)S(1)} %pad_maximum_fusion), channel_id=1, source_target_pairs={{0,16},{16,0},{1,17},{17,1},{2,18},{18,2},{3,19},{19,3},{4,20},{20... | collective-permute-start | bytes 4718600 | tf_op jit(solution)/shard_map/ppermute | solution.py:382
  54.8 11.5 %collective-permute-start.7 = (bf16[640,256]{1,0:T(8,128)(2,1)S(1)}, bf16[640,256]{1,0:T(8,128)(2,1)S(1)}, u32[]{:S(2)}, u32[]{:S(2)}) collective-permute-start(bf16[640,256]{1,0:T(8,128)(2,1)S(1)} %bitcast.28), channel_id=1, source_target_pairs={{0,2},{1,3},{2,0},{3,1},{4,6},{5,7},{6,4},{7,5},{8,10},{9,11},{10,... | collective-permute-start | bytes 983048 | tf_op jit(solution)/shard_map/ppermute | solution.py:313
  55.1 11.2 %collective-permute-start.6 = (bf16[192,512]{1,0:T(8,128)(2,1)S(1)}, bf16[192,512]{1,0:T(8,128)(2,1)S(1)}, u32[]{:S(2)}, u32[]{:S(2)}) collective-permute-start(bf16[192,512]{1,0:T(8,128)(2,1)S(1)} %get-tuple-element.67), channel_id=1, source_target_pairs={{0,8},{4,12},{8,0},{12,4},{1,9},{5,13},{9,1},{13,5},{2,10},{6,14},... | collective-permute-start | bytes 589832 | tf_op jit(solution)/shard_map/ppermute | solution.py:319
  56.5 16.1 %collective-permute-start.11 = (bf16[192,512]{1,0:T(8,128)(2,1)S(1)}, bf16[192,512]{1,0:T(8,128)(2,1)S(1)}, u32[]{:S(2)}, u32[]{:S(2)}) collective-permute-start(bf16[192,512]{1,0:T(8,128)(2,1)S(1)} %get-tuple-element.74), channel_id=1, source_target_pairs={{0,4},{4,8},{8,12},{12,0},{1,5},{5,9},{9,13},{13,1},{2,6},{6,10},{... | collective-permute-start | bytes 589832 | tf_op jit(solution)/shard_map/ppermute | solution.py:319
  56.5 16.1 %collective-permute-start.12 = (bf16[192,512]{1,0:T(8,128)(2,1)S(1)}, bf16[192,512]{1,0:T(8,128)(2,1)S(1)}, u32[]{:S(2)}, u32[]{:S(2)}) collective-permute-start(bf16[192,512]{1,0:T(8,128)(2,1)S(1)} %get-tuple-element.76), channel_id=1, source_target_pairs={{0,12},{4,0},{8,4},{12,8},{1,13},{5,1},{9,5},{13,9},{2,14},{6,2},{... | collective-permute-start | bytes 589832 | tf_op jit(solution)/shard_map/ppermute | solution.py:319
  66.3 13.8 %collective-permute-start.14 = (bf16[640,256]{1,0:T(8,128)(2,1)S(1)}, bf16[640,256]{1,0:T(8,128)(2,1)S(1)}, u32[]{:S(2)}, u32[]{:S(2)}) collective-permute-start(bf16[640,256]{1,0:T(8,128)(2,1)S(1)} %bitcast.27), channel_id=1, source_target_pairs={{0,2},{1,3},{2,0},{3,1},{4,6},{5,7},{6,4},{7,5},{8,10},{9,11},{10,... | collective-permute-start | bytes 983048 | tf_op jit(solution)/shard_map/ppermute | solution.py:313
  67.6 17.5 %collective-permute-start.8 = (bf16[192,512]{1,0:T(8,128)(2,1)S(1)}, bf16[192,512]{1,0:T(8,128)(2,1)S(1)}, u32[]{:S(2)}, u32[]{:S(2)}) collective-permute-start(bf16[192,512]{1,0:T(8,128)(2,1)S(1)} %get-tuple-element.70), channel_id=1, source_target_pairs={{0,4},{4,8},{8,12},{12,0},{1,5},{5,9},{9,13},{13,1},{2,6},{6,10},{... | collective-permute-start | bytes 589832 | tf_op jit(solution)/shard_map/ppermute | solution.py:319
  72.6 16.9 %collective-permute-start.9 = (bf16[192,512]{1,0:T(8,128)(2,1)S(1)}, bf16[192,512]{1,0:T(8,128)(2,1)S(1)}, u32[]{:S(2)}, u32[]{:S(2)}) collective-permute-start(bf16[192,512]{1,0:T(8,128)(2,1)S(1)} %get-tuple-element.71), channel_id=1, source_target_pairs={{0,8},{4,12},{8,0},{12,4},{1,9},{5,13},{9,1},{13,5},{2,10},{6,14},... | collective-permute-start | bytes 589832 | tf_op jit(solution)/shard_map/ppermute | solution.py:319
  72.6 18.1 %collective-permute-start.10 = (bf16[192,512]{1,0:T(8,128)(2,1)S(1)}, bf16[192,512]{1,0:T(8,128)(2,1)S(1)}, u32[]{:S(2)}, u32[]{:S(2)}) collective-permute-start(bf16[192,512]{1,0:T(8,128)(2,1)S(1)} %get-tuple-element.72), channel_id=1, source_target_pairs={{0,12},{4,0},{8,4},{12,8},{1,13},{5,1},{9,5},{13,9},{2,14},{6,2},{... | collective-permute-start | bytes 589832 | tf_op jit(solution)/shard_map/ppermute | solution.py:319
  79.8 10.9 %collective-permute-start.13 = (bf16[256,384]{1,0:T(8,128)(2,1)S(1)}, bf16[256,384]{1,0:T(8,128)(2,1)S(1)}, u32[]{:S(2)}, u32[]{:S(2)}) collective-permute-start(bf16[256,384]{1,0:T(8,128)(2,1)S(1)} %sum.2.refs_0_), channel_id=1, source_target_pairs={{0,2},{1,3},{2,0},{3,1},{4,6},{5,7},{6,4},{7,5},{8,10},{9,11},{10,... | collective-permute-start | bytes 589832 | tf_op jit(solution)/shard_map/ppermute | solution.py:313
  90.7 4.7 %collective-permute-start.17 = (bf16[256,2048]{1,0:T(8,128)(2,1)S(1)}, bf16[256,2048]{1,0:T(8,128)(2,1)S(1)}, u32[]{:S(2)}, u32[]{:S(2)}) collective-permute-start(bf16[256,2048]{1,0:T(8,128)(2,1)S(1)} %get-tuple-element.93), channel_id=1, source_target_pairs={{0,1},{1,0},{2,3},{3,2},{4,5},{5,4},{6,7},{7,6},{8,9},{9,8},{10,11... | collective-permute-start | bytes 3145736 | tf_op jit(solution)/shard_map/ppermute | solution.py:316
  91.2 2.7 %collective-permute-start.18 = (bf16[4,128,256]{2,1,0:T(8,128)(2,1)S(1)}, bf16[4,128,256]{2,1,0:T(8,128)(2,1)S(1)}, u32[]{:S(2)}, u32[]{:S(2)}) collective-permute-start(bf16[4,128,256]{2,1,0:T(8,128)(2,1)S(1)} %get-tuple-element.94), channel_id=1, source_target_pairs={{0,1},{1,0},{2,3},{3,2},{4,5},{5,4},{6,7},{7,6},{8,9},{9,8},{10,11... | collective-permute-start | bytes 786440 | tf_op jit(solution)/shard_map/ppermute | solution.py:316
  91.5 6.1 %collective-permute-start.16 = (bf16[256,384]{1,0:T(8,128)(2,1)S(1)}, bf16[256,384]{1,0:T(8,128)(2,1)S(1)}, u32[]{:S(2)}, u32[]{:S(2)}) collective-permute-start(bf16[256,384]{1,0:T(8,128)(2,1)S(1)} %sum.3.refs_2_), channel_id=1, source_target_pairs={{0,2},{1,3},{2,0},{3,1},{4,6},{5,7},{6,4},{7,5},{8,10},{9,11},{10,... | collective-permute-start | bytes 589832 | tf_op jit(solution)/shard_map/ppermute | solution.py:313
  97.7 3.3 %collective-permute-start.19 = (bf16[4,256,384]{2,1,0:T(8,128)(2,1)S(1)}, bf16[4,256,384]{2,1,0:T(8,128)(2,1)S(1)}, u32[]{:S(2)}, u32[]{:S(2)}) collective-permute-start(bf16[4,256,384]{2,1,0:T(8,128)(2,1)S(1)} %pad_maximum_fusion.1), channel_id=1, source_target_pairs={{0,1},{1,0},{2,3},{3,2},{4,5},{5,4},{6,7},{7,6},{8,9},{9,8},{10,11... | collective-permute-start | bytes 2359304 | tf_op jit(solution)/shard_map/ppermute | solution.py:316

commit v11 on v10

--- a/solution.py
+++ b/solution.py
@@ -418,7 +418,7 @@
         outs = inner(head)
         gp, gq, send, keep = outs[:nseq], outs[nseq], outs[nseq + 1], outs[nseq + 2]
         if pieces is not None:
-            gp, send, pieces[nseq // 2], sent = barrier((gp, send, pieces[nseq // 2], sent))
+            gp, send, pieces[nseq // 2] = barrier((gp, send, pieces[nseq // 2]))
         if pieces is not None:
             total = summed(pieces)
             projs += [total] + [to_chip(total, dx) for dx in range(1, chips)]

time: 104 us -> 106 us (1.019)
  waiting for transfers between devices: 56.5 us -> 57.9 us
    ppermute x1, waiting for transfers between devices: 3.6 us -> 5.02 us  [to_others(): return [lax.ppermute(value, 'groups', [(0, 1), (1, 0)])]]
    ppermute x9, starting transfers between devices: 10 us -> 8.89 us  [to_seq(): lax.ppermute(value, 'seq', [(i, (i + dz) % nseq) for i in range(nseq)])]
  transfers between devices with their start and end apart: 20 -> 20, of which waited for: 12 -> 10; matrix products, arithmetic and copies ran while one was open for 1% -> 1% of each run, Pallas kernels for 20% -> 20%
where the time goes in v11:
time: 106 us; the launch traced here: 105 us
  waiting for transfers between devices  57.9 us (55%)
  Pallas kernels  26.4 us (25%)
  starting transfers between devices  17.7 us (17%)
  other arithmetic  1.61 us (2%)
    ppermute x9, waiting for transfers between devices, to_seq(): lax.ppermute(value, 'seq', [(i, (i + dz) % nseq) for i in range(nseq)])  46.7 us
    pallas_call x6, Pallas kernels, kernel(): pl.pallas_call(body, in_specs=[smem if o.ndim == 1 else vmem for o in ope...  21.1 us
    ppermute x9, starting transfers between devices, to_seq(): lax.ppermute(value, 'seq', [(i, (i + dz) % nseq) for i in range(nseq)])  8.89 us
    ppermute x5, waiting for transfers between devices, to_core(): return lax.ppermute(value, 'seg', [(i, i ^ 1) for i in range(nseg)])  5.27 us
    ppermute x1, waiting for transfers between devices, to_others(): return [lax.ppermute(value, 'groups', [(0, 1), (1, 0)])]  5.02 us
    ppermute x5, starting transfers between devices, to_core(): return lax.ppermute(value, 'seg', [(i, i ^ 1) for i in range(nseg)])  4.15 us
    ppermute x5, starting transfers between devices, to_chip(): return lax.ppermute(value, 'seg', pairs)  3.39 us
    pallas_call x1, Pallas kernels, per_device(): pl.pallas_call(functools.partial(prep_kernel, dims), in_specs=[pl.BlockSp...  2.77 us
  transfers between devices with their start and end apart: 20, of which 10 were waited for; matrix products, arithmetic and copies ran while one was open for 1% of the time, Pallas kernels for 20%

profile of v11, /device:TPU:9, one launch (start us, length us, event | category | flops | bytes accessed | tf_op | source)
XLA Modules:
  0.0 104.8 jit_solution(9229206681479672353)
XLA Ops:
  0.7 0.1 concatenate.3.table
  0.9 2.8 %prep.1 = (bf16[384,512]{1,0:T(8,128)(2,1)S(1)}, bf16[48,2048]{1,0:T(8,128)(2,1)S(1)}, bf16[304,2048]{1,0:T(8,128)(2,1)S(1)}, bf16[352,2048]{1,0:T(8,128)(2,1)S(1)}) custom-call(s32[14]{0:T(128)S(1)} %concatenate.3.table, bf16[256,2048]{1,0:T(8,128)(2,1)} %bitcast.16, bf16[512,1536]{1,0:T(8,128)(2,1)} %w.1, bf16[256,512]{1,0:T(8,128)(2,1)} %bitcast.32, ...), custom_call_target="tpu_custom_call" | custom-call | tf_op jit(solution)/shard_map/prep/pallas_call | solution.py:356
  3.6 1.3 %collective-permute-start = (bf16[352,2048]{1,0:T(8,128)(2,1)S(1)}, bf16[352,2048]{1,0:T(8,128)(2,1)S(1)}, u32[]{:S(2)}, u32[]{:S(2)}) collective-permute-start(bf16[352,2048]{1,0:T(8,128)(2,1)S(1)} %get-tuple-element.51), channel_id=1, source_target_pairs={{0,2},{1,3},{2,0},{3,1},{4,6},{5,7},{6,4},{7,5},{8,10},{9,11},{10,... | collective-permute-start | bytes 4325384 | tf_op jit(solution)/shard_map/ppermute | solution.py:313
  4.9 0.9 collective-permute-start.1
  5.9 1.3 %collective-permute-start.2 = (bf16[384,512]{1,0:T(8,128)(2,1)S(1)}, bf16[384,512]{1,0:T(8,128)(2,1)S(1)}, u32[]{:S(2)}, u32[]{:S(2)}) collective-permute-start(bf16[384,512]{1,0:T(8,128)(2,1)S(1)} %get-tuple-element.56.refs_4_.refs_6_), channel_id=1, source_target_pairs={{0,4},{4,8},{8,12},{12,0},{1,5},{5,9},{9,13},{13,1},{2,6},{6,10},{... | collective-permute-start | bytes 1179656 | tf_op jit(solution)/shard_map/ppermute | solution.py:319
  7.2 1.0 collective-permute-start.3
  8.2 1.5 %collective-permute-start.4 = (bf16[384,512]{1,0:T(8,128)(2,1)S(1)}, bf16[384,512]{1,0:T(8,128)(2,1)S(1)}, u32[]{:S(2)}, u32[]{:S(2)}) collective-permute-start(bf16[384,512]{1,0:T(8,128)(2,1)S(1)} %get-tuple-element.56.refs_4_.refs_6_), channel_id=1, source_target_pairs={{0,12},{4,0},{8,4},{12,8},{1,13},{5,1},{9,5},{13,9},{2,14},{6,2},{... | collective-permute-start | bytes 1179656 | tf_op jit(solution)/shard_map/ppermute | solution.py:319
  9.6 7.0 %collective-permute-done.2.refs_5_.refs_7_ = bf16[384,512]{1,0:T(8,128)(2,1)S(1)} collective-permute-done((bf16[384,512]{1,0:T(8,128)(2,1)S(1)}, bf16[384,512]{1,0:T(8,128)(2,1)S(1)}, u32[]{:S(2)}, u32[]{:S(2)}) %collective-permute-start.2) | collective-permute-done | bytes 393248 | tf_op jit(solution)/shard_map/ppermute | solution.py:319
  16.6 24.4 %collective-permute-done.3.refs_6_.refs_8_ = bf16[384,512]{1,0:T(8,128)(2,1)S(1)} collective-permute-done((bf16[384,512]{1,0:T(8,128)(2,1)S(1)}, bf16[384,512]{1,0:T(8,128)(2,1)S(1)}, u32[]{:S(2)}, u32[]{:S(2)}) %collective-permute-start.3) | collective-permute-done | bytes 393248 | tf_op jit(solution)/shard_map/ppermute | solution.py:319
  41.0 2.1 %collective-permute-done.4.refs_7_.refs_9_ = bf16[384,512]{1,0:T(8,128)(2,1)S(1)} collective-permute-done((bf16[384,512]{1,0:T(8,128)(2,1)S(1)}, bf16[384,512]{1,0:T(8,128)(2,1)S(1)}, u32[]{:S(2)}, u32[]{:S(2)}) %collective-permute-start.4) | collective-permute-done | bytes 393248 | tf_op jit(solution)/shard_map/ppermute | solution.py:319
  43.1 0.0 collective-permute-done.1.refs_1_
  43.1 0.0 collective-permute-done.refs_2_
  43.1 0.5 collective-permute-start.5
  43.6 0.2 pad_maximum_fusion
  43.8 1.3 %collective-permute-start.15 = (bf16[4,384,512]{2,1,0:T(8,128)(2,1)S(1)}, bf16[4,384,512]{2,1,0:T(8,128)(2,1)S(1)}, u32[]{:S(2)}, u32[]{:S(2)}) collective-permute-start(bf16[4,384,512]{2,1,0:T(8,128)(2,1)S(1)} %pad_maximum_fusion), channel_id=1, source_target_pairs={{0,16},{16,0},{1,17},{17,1},{2,18},{18,2},{3,19},{19,3},{4,20},{20... | collective-permute-start | bytes 4718600 | tf_op jit(solution)/shard_map/ppermute | solution.py:382
  45.1 1.3 %collective-permute-done.5.refs_3_ = bf16[352,2048]{1,0:T(8,128)(2,1)S(1)} collective-permute-done((bf16[352,2048]{1,0:T(8,128)(2,1)S(1)}, bf16[352,2048]{1,0:T(8,128)(2,1)S(1)}, u32[]{:S(2)}, u32[]{:S(2)}) %collective-permute-start.5) | collective-permute-done | bytes 1441824 | tf_op jit(solution)/shard_map/ppermute | solution.py:316
  46.4 8.3 %inner.3 = (f32[192,512]{1,0:T(8,128)S(1)}, bf16[192,512]{1,0:T(8,128)(2,1)S(1)}, bf16[192,512]{1,0:T(8,128)(2,1)S(1)}, bf16[192,512]{1,0:T(8,128)(2,1)S(1)}, bf...) custom-call(s32[14]{0:T(128)S(1)} %concatenate.3.table, ...), custom_call_target="tpu_custom_call" | custom-call | tf_op jit(solution)/shard_map/inner/pallas_call | solution.py:324
  54.8 1.4 %collective-permute-start.6 = (bf16[192,512]{1,0:T(8,128)(2,1)S(1)}, bf16[192,512]{1,0:T(8,128)(2,1)S(1)}, u32[]{:S(2)}, u32[]{:S(2)}) collective-permute-start(bf16[192,512]{1,0:T(8,128)(2,1)S(1)} %get-tuple-element.66), channel_id=1, source_target_pairs={{0,8},{4,12},{8,0},{12,4},{1,9},{5,13},{9,1},{13,5},{2,10},{6,14},... | collective-permute-start | bytes 589832 | tf_op jit(solution)/shard_map/ppermute | solution.py:319
  56.2 0.3 collective-permute-start.13
  56.5 1.5 %collective-permute-start.11 = (bf16[192,512]{1,0:T(8,128)(2,1)S(1)}, bf16[192,512]{1,0:T(8,128)(2,1)S(1)}, u32[]{:S(2)}, u32[]{:S(2)}) collective-permute-start(bf16[192,512]{1,0:T(8,128)(2,1)S(1)} %get-tuple-element.74), channel_id=1, source_target_pairs={{0,12},{4,0},{8,4},{12,8},{1,13},{5,1},{9,5},{13,9},{2,14},{6,2},{... | collective-permute-start | bytes 589832 | tf_op jit(solution)/shard_map/ppermute | solution.py:319
  57.9 8.4 %inner.2 = (f32[192,512]{1,0:T(8,128)S(1)}, bf16[192,512]{1,0:T(8,128)(2,1)S(1)}, bf16[192,512]{1,0:T(8,128)(2,1)S(1)}, bf16[192,512]{1,0:T(8,128)(2,1)S(1)}, bf...) custom-call(s32[14]{0:T(128)S(1)} %concatenate.3.table, ...), custom_call_target="tpu_custom_call" | custom-call | tf_op jit(solution)/shard_map/inner/pallas_call | solution.py:324
  66.3 0.0 collective-permute-done.6.refs_2_
  66.3 1.3 %collective-permute-start.14 = (bf16[640,256]{1,0:T(8,128)(2,1)S(1)}, bf16[640,256]{1,0:T(8,128)(2,1)S(1)}, u32[]{:S(2)}, u32[]{:S(2)}) collective-permute-start(bf16[640,256]{1,0:T(8,128)(2,1)S(1)} %bitcast.28), channel_id=1, source_target_pairs={{0,2},{1,3},{2,0},{3,1},{4,6},{5,7},{6,4},{7,5},{8,10},{9,11},{10,... | collective-permute-start | bytes 983048 | tf_op jit(solution)/shard_map/ppermute | solution.py:313
  67.6 4.7 %collective-permute-done.10.refs_1_ = bf16[192,512]{1,0:T(8,128)(2,1)S(1)} collective-permute-done((bf16[192,512]{1,0:T(8,128)(2,1)S(1)}, bf16[192,512]{1,0:T(8,128)(2,1)S(1)}, u32[]{:S(2)}, u32[]{:S(2)}) %collective-permute-start.10) | collective-permute-done | bytes 196640 | tf_op jit(solution)/shard_map/ppermute | solution.py:319
  72.3 2.2 %collective-permute-start.7 = (bf16[192,512]{1,0:T(8,128)(2,1)S(1)}, bf16[192,512]{1,0:T(8,128)(2,1)S(1)}, u32[]{:S(2)}, u32[]{:S(2)}) collective-permute-start(bf16[192,512]{1,0:T(8,128)(2,1)S(1)} %get-tuple-element.68), channel_id=1, source_target_pairs={{0,4},{4,8},{8,12},{12,0},{1,5},{5,9},{9,13},{13,1},{2,6},{6,10},{... | collective-permute-start | bytes 589832 | tf_op jit(solution)/shard_map/ppermute | solution.py:319
  74.5 0.0 collective-permute-done.11.refs_3_
  74.5 0.0 collective-permute-start.8
  74.5 0.3 sum.2.refs_0_
  74.8 5.0 %collective-permute-done.15.refs_10_ = bf16[4,384,512]{2,1,0:T(8,128)(2,1)S(1)} collective-permute-done((bf16[4,384,512]{2,1,0:T(8,128)(2,1)S(1)}, bf16[4,384,512]{2,1,0:T(8,128)(2,1)S(1)}, u32[]{:S(2)}, u32[]{:S(2)}) %collective-permute-start.15) | collective-permute-done | bytes 1572896 | tf_op jit(solution)/shard_map/ppermute | solution.py:382
  79.8 0.0 collective-permute-start.9
  79.8 0.0 collective-permute-done.13.refs_4_.refs_2_
  79.8 0.3 collective-permute-start.12
  80.1 0.0 collective-permute-done.14.refs_5_.refs_3_
  80.1 2.4 %input.1 = (f32[256,2048]{1,0:T(8,128)S(1)}, bf16[256,2048]{1,0:T(8,128)(2,1)S(1)}, bf16[4,128,256]{2,1,0:T(8,128)(2,1)S(1)}) custom-call(s32[14]{0:T(128)S(1)} %concatenate.3.table, bf16[4,3,64,256]{3,2,1,0:T(8,128)(2,1)S(1)} %get-tuple-element.75.refs_0_, bf16[4,3,64,256]{3,2,1,0:T(8,128)(2,1)S(1)} %get-tuple-element.76.refs_1_, ...), custom_call_target="tpu_custom_call" | custom-call | bytes 10485760 | tf_op jit(solution)/shard_map/input/pallas_call | solution.py:324
  82.5 8.5 %collective-permute-done.8.refs_2_ = bf16[192,512]{1,0:T(8,128)(2,1)S(1)} collective-permute-done((bf16[192,512]{1,0:T(8,128)(2,1)S(1)}, bf16[192,512]{1,0:T(8,128)(2,1)S(1)}, u32[]{:S(2)}, u32[]{:S(2)}) %collective-permute-start.8) | collective-permute-done | bytes 196640 | tf_op jit(solution)/shard_map/ppermute | solution.py:319
  91.0 0.0 collective-permute-done.9.refs_3_
  91.0 1.3 %collective-permute-start.17 = (bf16[256,2048]{1,0:T(8,128)(2,1)S(1)}, bf16[256,2048]{1,0:T(8,128)(2,1)S(1)}, u32[]{:S(2)}, u32[]{:S(2)}) collective-permute-start(bf16[256,2048]{1,0:T(8,128)(2,1)S(1)} %get-tuple-element.91), channel_id=1, source_target_pairs={{0,1},{1,0},{2,3},{3,2},{4,5},{5,4},{6,7},{7,6},{8,9},{9,8},{10,11... | collective-permute-start | bytes 3145736 | tf_op jit(solution)/shard_map/ppermute | solution.py:316
  92.3 0.1 collective-permute-start.18
  92.4 0.3 sum.3.refs_2_
  92.6 0.3 collective-permute-start.16
  93.0 2.0 %collective-permute-done.18.refs_4_ = bf16[4,128,256]{2,1,0:T(8,128)(2,1)S(1)} collective-permute-done((bf16[4,128,256]{2,1,0:T(8,128)(2,1)S(1)}, bf16[4,128,256]{2,1,0:T(8,128)(2,1)S(1)}, u32[]{:S(2)}, u32[]{:S(2)}) %collective-permute-start.18) | collective-permute-done | bytes 262176 | tf_op jit(solution)/shard_map/ppermute | solution.py:316
  95.0 1.6 %weights.1 = f32[2,8,64,256]{3,2,1,0:T(8,128)} custom-call(s32[14]{0:T(128)S(1)} %concatenate.3.table, bf16[2,2,64,256]{3,2,1,0:T(8,128)(2,1)S(1)} %get-tuple-element.77.refs_2_.refs_0_, bf16[2,2,64,256]{3,2,1,0:T(8,128)(2,1)S(1)} %get-tuple-element.78.refs_3_.refs_1_, bf16[640,256]{1,0:T(8,128)(2,1)S(1)} %collective-permute-done.13.refs_4_.refs_2_, ...), custom_call_target="tpu_custom_call" | custom-call | bytes 10485760 | tf_op jit(solution)/shard_map/weights/pallas_call | solution.py:324
  96.6 1.3 %add_convert_fusion = bf16[256,2048]{1,0:T(8,128)(2,1)} fusion(f32[256,2048]{1,0:T(8,128)S(1)} %get-tuple-element.90, bf16[256,2048]{1,0:T(8,128)(2,1)S(1)} %collective-permute-done.17), kind=kLoop, calls=%fused_computation | loop fusion | flops 1572864 | bytes 4194304 | tf_op jit(solution)/shard_map/convert_element_type | solution.py:450
  97.8 0.9 collective-permute-done.16.refs_3_
  98.7 0.1 pad_maximum_fusion.1
  98.9 1.3 %collective-permute-start.19 = (bf16[4,256,384]{2,1,0:T(8,128)(2,1)S(1)}, bf16[4,256,384]{2,1,0:T(8,128)(2,1)S(1)}, u32[]{:S(2)}, u32[]{:S(2)}) collective-permute-start(bf16[4,256,384]{2,1,0:T(8,128)(2,1)S(1)} %pad_maximum_fusion.1), channel_id=1, source_target_pairs={{0,1},{1,0},{2,3},{3,2},{4,5},{5,4},{6,7},{7,6},{8,9},{9,8},{10,11... | collective-permute-start | bytes 2359304 | tf_op jit(solution)/shard_map/ppermute | solution.py:316
  100.2 1.9 %collective-permute-done.19.refs_4_ = bf16[4,256,384]{2,1,0:T(8,128)(2,1)S(1)} collective-permute-done((bf16[4,256,384]{2,1,0:T(8,128)(2,1)S(1)}, bf16[4,256,384]{2,1,0:T(8,128)(2,1)S(1)}, u32[]{:S(2)}, u32[]{:S(2)}) %collective-permute-start.19) | collective-permute-done | bytes 786464 | tf_op jit(solution)/shard_map/ppermute | solution.py:316
  102.1 2.5 %join.1 = f32[512,1536]{1,0:T(8,128)} custom-call(s32[14]{0:T(128)S(1)} %concatenate.3.table, bf16[256,384]{1,0:T(8,128)(2,1)S(1)} %sum.2.refs_0_, bf16[256,384]{1,0:T(8,128)(2,1)S(1)} %collective-permute-done.12.refs_1_, bf16[256,384]{1,0:T(8,128)(2,1)S(1)} %sum.3.refs_2_, bf16[256,384]{1,0:T(8,128)(2,1)S(1)} %collective-permute-done.16.refs_3_, ...), custom_call_target="tpu_custom_call" | custom-call | tf_op jit(solution)/shard_map/join/pallas_call | solution.py:465
  (10 shorter events, 0.0 us)
Async XLA Ops:
  3.6 39.5 %collective-permute-start = (bf16[352,2048]{1,0:T(8,128)(2,1)S(1)}, bf16[352,2048]{1,0:T(8,128)(2,1)S(1)}, u32[]{:S(2)}, u32[]{:S(2)}) collective-permute-start(bf16[352,2048]{1,0:T(8,128)(2,1)S(1)} %get-tuple-element.51), channel_id=1, source_target_pairs={{0,2},{1,3},{2,0},{3,1},{4,6},{5,7},{6,4},{7,5},{8,10},{9,11},{10,... | collective-permute-start | bytes 4325384 | tf_op jit(solution)/shard_map/ppermute | solution.py:313
  4.9 38.2 %collective-permute-start.1 = (bf16[304,2048]{1,0:T(8,128)(2,1)S(1)}, bf16[304,2048]{1,0:T(8,128)(2,1)S(1)}, u32[]{:S(2)}, u32[]{:S(2)}) collective-permute-start(bf16[304,2048]{1,0:T(8,128)(2,1)S(1)} %get-tuple-element.52), channel_id=1, source_target_pairs={{0,1},{1,0},{2,3},{3,2},{4,5},{5,4},{6,7},{7,6},{8,9},{9,8},{10,11... | collective-permute-start | bytes 3735560 | tf_op jit(solution)/shard_map/ppermute | solution.py:316
  5.9 10.7 %collective-permute-start.2 = (bf16[384,512]{1,0:T(8,128)(2,1)S(1)}, bf16[384,512]{1,0:T(8,128)(2,1)S(1)}, u32[]{:S(2)}, u32[]{:S(2)}) collective-permute-start(bf16[384,512]{1,0:T(8,128)(2,1)S(1)} %get-tuple-element.56.refs_4_.refs_6_), channel_id=1, source_target_pairs={{0,4},{4,8},{8,12},{12,0},{1,5},{5,9},{9,13},{13,1},{2,6},{6,10},{... | collective-permute-start | bytes 1179656 | tf_op jit(solution)/shard_map/ppermute | solution.py:319
  7.2 33.8 %collective-permute-start.3 = (bf16[384,512]{1,0:T(8,128)(2,1)S(1)}, bf16[384,512]{1,0:T(8,128)(2,1)S(1)}, u32[]{:S(2)}, u32[]{:S(2)}) collective-permute-start(bf16[384,512]{1,0:T(8,128)(2,1)S(1)} %get-tuple-element.56.refs_4_.refs_6_), channel_id=1, source_target_pairs={{0,8},{4,12},{8,0},{12,4},{1,9},{5,13},{9,1},{13,5},{2,10},{6,14},... | collective-permute-start | bytes 1179656 | tf_op jit(solution)/shard_map/ppermute | solution.py:319
  8.2 34.9 %collective-permute-start.4 = (bf16[384,512]{1,0:T(8,128)(2,1)S(1)}, bf16[384,512]{1,0:T(8,128)(2,1)S(1)}, u32[]{:S(2)}, u32[]{:S(2)}) collective-permute-start(bf16[384,512]{1,0:T(8,128)(2,1)S(1)} %get-tuple-element.56.refs_4_.refs_6_), channel_id=1, source_target_pairs={{0,12},{4,0},{8,4},{12,8},{1,13},{5,1},{9,5},{13,9},{2,14},{6,2},{... | collective-permute-start | bytes 1179656 | tf_op jit(solution)/shard_map/ppermute | solution.py:319
  43.1 3.3 %collective-permute-start.5 = (bf16[352,2048]{1,0:T(8,128)(2,1)S(1)}, bf16[352,2048]{1,0:T(8,128)(2,1)S(1)}, u32[]{:S(2)}, u32[]{:S(2)}) collective-permute-start(bf16[352,2048]{1,0:T(8,128)(2,1)S(1)} %collective-permute-done.refs_2_), channel_id=1, source_target_pairs={{0,1},{1,0},{2,3},{3,2},{4,5},{5,4},{6,7},{7,6},{8,9},{9,8},{10,11... | collective-permute-start | bytes 4325384 | tf_op jit(solution)/shard_map/ppermute | solution.py:316
  43.6 2.9 %copy-start = (bf16[1,256,2048]{2,1,0:T(8,128)(2,1)S(1)}, bf16[1,256,2048]{2,1,0:T(8,128)(2,1)}, u32[]{:S(2)}) copy-start(bf16[1,256,2048]{2,1,0:T(8,128)(2,1)} %param.5) | copy-start | bytes 3145732
  43.6 2.9 %copy-start.1 = (f32[8]{0:T(128)S(1)}, f32[8]{0:T(128)}, u32[]{:S(2)}) copy-start(f32[8]{0:T(128)} %rates.3) | copy-start | bytes 100
  43.8 36.0 %collective-permute-start.15 = (bf16[4,384,512]{2,1,0:T(8,128)(2,1)S(1)}, bf16[4,384,512]{2,1,0:T(8,128)(2,1)S(1)}, u32[]{:S(2)}, u32[]{:S(2)}) collective-permute-start(bf16[4,384,512]{2,1,0:T(8,128)(2,1)S(1)} %pad_maximum_fusion), channel_id=1, source_target_pairs={{0,16},{16,0},{1,17},{17,1},{2,18},{18,2},{3,19},{19,3},{4,20},{20... | collective-permute-start | bytes 4718600 | tf_op jit(solution)/shard_map/ppermute | solution.py:382
  54.8 11.5 %collective-permute-start.6 = (bf16[192,512]{1,0:T(8,128)(2,1)S(1)}, bf16[192,512]{1,0:T(8,128)(2,1)S(1)}, u32[]{:S(2)}, u32[]{:S(2)}) collective-permute-start(bf16[192,512]{1,0:T(8,128)(2,1)S(1)} %get-tuple-element.66), channel_id=1, source_target_pairs={{0,8},{4,12},{8,0},{12,4},{1,9},{5,13},{9,1},{13,5},{2,10},{6,14},... | collective-permute-start | bytes 589832 | tf_op jit(solution)/shard_map/ppermute | solution.py:319
  56.2 23.6 %collective-permute-start.13 = (bf16[640,256]{1,0:T(8,128)(2,1)S(1)}, bf16[640,256]{1,0:T(8,128)(2,1)S(1)}, u32[]{:S(2)}, u32[]{:S(2)}) collective-permute-start(bf16[640,256]{1,0:T(8,128)(2,1)S(1)} %bitcast.27), channel_id=1, source_target_pairs={{0,2},{1,3},{2,0},{3,1},{4,6},{5,7},{6,4},{7,5},{8,10},{9,11},{10,... | collective-permute-start | bytes 983048 | tf_op jit(solution)/shard_map/ppermute | solution.py:313
  56.5 15.9 %collective-permute-start.10 = (bf16[192,512]{1,0:T(8,128)(2,1)S(1)}, bf16[192,512]{1,0:T(8,128)(2,1)S(1)}, u32[]{:S(2)}, u32[]{:S(2)}) collective-permute-start(bf16[192,512]{1,0:T(8,128)(2,1)S(1)} %get-tuple-element.72), channel_id=1, source_target_pairs={{0,4},{4,8},{8,12},{12,0},{1,5},{5,9},{9,13},{13,1},{2,6},{6,10},{... | collective-permute-start | bytes 589832 | tf_op jit(solution)/shard_map/ppermute | solution.py:319
  56.5 18.1 %collective-permute-start.11 = (bf16[192,512]{1,0:T(8,128)(2,1)S(1)}, bf16[192,512]{1,0:T(8,128)(2,1)S(1)}, u32[]{:S(2)}, u32[]{:S(2)}) collective-permute-start(bf16[192,512]{1,0:T(8,128)(2,1)S(1)} %get-tuple-element.74), channel_id=1, source_target_pairs={{0,12},{4,0},{8,4},{12,8},{1,13},{5,1},{9,5},{13,9},{2,14},{6,2},{... | collective-permute-start | bytes 589832 | tf_op jit(solution)/shard_map/ppermute | solution.py:319
  66.3 13.8 %collective-permute-start.14 = (bf16[640,256]{1,0:T(8,128)(2,1)S(1)}, bf16[640,256]{1,0:T(8,128)(2,1)S(1)}, u32[]{:S(2)}, u32[]{:S(2)}) collective-permute-start(bf16[640,256]{1,0:T(8,128)(2,1)S(1)} %bitcast.28), channel_id=1, source_target_pairs={{0,2},{1,3},{2,0},{3,1},{4,6},{5,7},{6,4},{7,5},{8,10},{9,11},{10,... | collective-permute-start | bytes 983048 | tf_op jit(solution)/shard_map/ppermute | solution.py:313
  72.3 10.1 %collective-permute-start.7 = (bf16[192,512]{1,0:T(8,128)(2,1)S(1)}, bf16[192,512]{1,0:T(8,128)(2,1)S(1)}, u32[]{:S(2)}, u32[]{:S(2)}) collective-permute-start(bf16[192,512]{1,0:T(8,128)(2,1)S(1)} %get-tuple-element.68), channel_id=1, source_target_pairs={{0,4},{4,8},{8,12},{12,0},{1,5},{5,9},{9,13},{13,1},{2,6},{6,10},{... | collective-permute-start | bytes 589832 | tf_op jit(solution)/shard_map/ppermute | solution.py:319
  74.5 16.4 %collective-permute-start.8 = (bf16[192,512]{1,0:T(8,128)(2,1)S(1)}, bf16[192,512]{1,0:T(8,128)(2,1)S(1)}, u32[]{:S(2)}, u32[]{:S(2)}) collective-permute-start(bf16[192,512]{1,0:T(8,128)(2,1)S(1)} %get-tuple-element.69), channel_id=1, source_target_pairs={{0,8},{4,12},{8,0},{12,4},{1,9},{5,13},{9,1},{13,5},{2,10},{6,14},... | collective-permute-start | bytes 589832 | tf_op jit(solution)/shard_map/ppermute | solution.py:319
  79.8 11.2 %collective-permute-start.9 = (bf16[192,512]{1,0:T(8,128)(2,1)S(1)}, bf16[192,512]{1,0:T(8,128)(2,1)S(1)}, u32[]{:S(2)}, u32[]{:S(2)}) collective-permute-start(bf16[192,512]{1,0:T(8,128)(2,1)S(1)} %get-tuple-element.70), channel_id=1, source_target_pairs={{0,12},{4,0},{8,4},{12,8},{1,13},{5,1},{9,5},{13,9},{2,14},{6,2},{... | collective-permute-start | bytes 589832 | tf_op jit(solution)/shard_map/ppermute | solution.py:319
  79.8 11.2 %collective-permute-start.12 = (bf16[256,384]{1,0:T(8,128)(2,1)S(1)}, bf16[256,384]{1,0:T(8,128)(2,1)S(1)}, u32[]{:S(2)}, u32[]{:S(2)}) collective-permute-start(bf16[256,384]{1,0:T(8,128)(2,1)S(1)} %sum.2.refs_0_), channel_id=1, source_target_pairs={{0,2},{1,3},{2,0},{3,1},{4,6},{5,7},{6,4},{7,5},{8,10},{9,11},{10,... | collective-permute-start | bytes 589832 | tf_op jit(solution)/shard_map/ppermute | solution.py:313
  91.0 5.6 %collective-permute-start.17 = (bf16[256,2048]{1,0:T(8,128)(2,1)S(1)}, bf16[256,2048]{1,0:T(8,128)(2,1)S(1)}, u32[]{:S(2)}, u32[]{:S(2)}) collective-permute-start(bf16[256,2048]{1,0:T(8,128)(2,1)S(1)} %get-tuple-element.91), channel_id=1, source_target_pairs={{0,1},{1,0},{2,3},{3,2},{4,5},{5,4},{6,7},{7,6},{8,9},{9,8},{10,11... | collective-permute-start | bytes 3145736 | tf_op jit(solution)/shard_map/ppermute | solution.py:316
  92.3 2.7 %collective-permute-start.18 = (bf16[4,128,256]{2,1,0:T(8,128)(2,1)S(1)}, bf16[4,128,256]{2,1,0:T(8,128)(2,1)S(1)}, u32[]{:S(2)}, u32[]{:S(2)}) collective-permute-start(bf16[4,128,256]{2,1,0:T(8,128)(2,1)S(1)} %get-tuple-element.92), channel_id=1, source_target_pairs={{0,1},{1,0},{2,3},{3,2},{4,5},{5,4},{6,7},{7,6},{8,9},{9,8},{10,11... | collective-permute-start | bytes 786440 | tf_op jit(solution)/shard_map/ppermute | solution.py:316
  92.6 6.1 %collective-permute-start.16 = (bf16[256,384]{1,0:T(8,128)(2,1)S(1)}, bf16[256,384]{1,0:T(8,128)(2,1)S(1)}, u32[]{:S(2)}, u32[]{:S(2)}) collective-permute-start(bf16[256,384]{1,0:T(8,128)(2,1)S(1)} %sum.3.refs_2_), channel_id=1, source_target_pairs={{0,2},{1,3},{2,0},{3,1},{4,6},{5,7},{6,4},{7,5},{8,10},{9,11},{10,... | collective-permute-start | bytes 589832 | tf_op jit(solution)/shard_map/ppermute | solution.py:313
  98.9 3.3 %collective-permute-start.19 = (bf16[4,256,384]{2,1,0:T(8,128)(2,1)S(1)}, bf16[4,256,384]{2,1,0:T(8,128)(2,1)S(1)}, u32[]{:S(2)}, u32[]{:S(2)}) collective-permute-start(bf16[4,256,384]{2,1,0:T(8,128)(2,1)S(1)} %pad_maximum_fusion.1), channel_id=1, source_target_pairs={{0,1},{1,0},{2,3},{3,2},{4,5},{5,4},{6,7},{7,6},{8,9},{9,8},{10,11... | collective-permute-start | bytes 2359304 | tf_op jit(solution)/shard_map/ppermute | solution.py:316
